TPU v7x, 32 devices: a whole 2x2x4 slice. The times are simulated.
32 devices in a mesh: parts: 2 (over y), train: 4 (over z), layer: 2 (over x), sub: 2 (over core).
Axes of the slice: x: 2, y: 2, z: 4, core: 2. Of those that a mesh axis runs over, the one named last changes fastest.
Arguments:
- inputs: bfloat16 [2, 2048, 4096], P('layer', ('parts', 'train')), parts along dimension 1, may hold values from -6 to 6
- out_grads: bfloat16 [2, 2048, 4096], P('layer', ('parts', 'train')), parts along dimension 1, may hold values from -6 to 6
- proj_in: bfloat16 [2, 64, 4096], P('layer'), may hold values from -0.09375 to 0.09375
- proj_out: bfloat16 [2, 64, 4096], P('layer'), may hold values from -0.09375 to 0.09375
- basis_in: float32 [2, 64, 64], P('layer'), may hold values from -0.75 to 0.75
- basis_out: float32 [2, 64, 64], P('layer'), may hold values from -0.75 to 0.75
- eigen: float32 [2, 64, 64], P('layer'), may hold values from 0.25 to 4
- queries: bfloat16 [2, 2048, 4096], P('layer', ('parts', 'train', 'sub')), parts along dimension 1, may hold values from -0.0234375 to 0.0234375
Outputs:
- scores: float32 [2048, 4, 2, 128], P(('parts', 'train', 'layer'), None, 'sub'), parts along dimension 0
There are 2 independent parts, one for each index of `parts`. A program takes and returns all parts, laid end to end along the dimension named above; an argument that names none is the same for every part. Nothing has to cross between parts.
All inputs are finite; a program needn't handle non-finite values.
Results may differ from a plain program's by a relative error of at most 0.01.
Values may be sent and summed in bfloat16 or wider, within the bound.
No kernel may reach another device: no remote copies, remote signals or barrier semaphores. Data moves between devices by JAX's collectives and lax.ppermute only.
A program may use at most 128 MiB of HBM per device.

v0:
```python
import jax
import jax.numpy as jnp
from jax import lax
from jax.sharding import PartitionSpec as P


def precondition(query_block, basis_in, basis_out, eigen):
    count = query_block.shape[0]
    rank_size = basis_in.shape[0]
    matrices = query_block.astype(jnp.float32).reshape(count, rank_size, rank_size)
    damping = 0.1 * jnp.mean(eigen)
    half_turn = jnp.einsum("ia,qij->qaj", basis_out, matrices, precision=lax.Precision.HIGHEST)
    rotated = jnp.einsum("qaj,jb->qab", half_turn, basis_in, precision=lax.Precision.HIGHEST)
    scaled = rotated / (eigen + damping)
    back_left = jnp.einsum("ia,qab->qib", basis_out, scaled, precision=lax.Precision.HIGHEST)
    back_full = jnp.einsum("qib,jb->qij", back_left, basis_in, precision=lax.Precision.HIGHEST)
    return back_full.astype(jnp.bfloat16).reshape(count, rank_size * rank_size)


def outer_grads(factor_out, factor_in):
    row_count, rank_size = factor_out.shape
    product = factor_out.astype(jnp.float32)[:, :, None] * factor_in.astype(jnp.float32)[:, None, :]
    return product.astype(jnp.bfloat16).reshape(row_count, rank_size * rank_size)


def body(inputs, out_grads, proj_in, proj_out, basis_in, basis_out, eigen, queries):
    query_dev = queries.shape[1]
    train_size = lax.axis_size("train")
    feat_in = jnp.dot(inputs[0], proj_in[0].T, preferred_element_type=jnp.float32).astype(
        jnp.bfloat16
    )
    feat_out = jnp.dot(out_grads[0], proj_out[0].T, preferred_element_type=jnp.float32).astype(
        jnp.bfloat16
    )
    precond = precondition(queries[0], basis_in[0], basis_out[0], eigen[0])
    token_grads = outer_grads(feat_out, feat_in)
    partial_value = jnp.dot(
        token_grads,
        lax.all_gather(precond, "train", axis=0, tiled=True).T,
        preferred_element_type=jnp.float32,
    )
    owned_rows = lax.psum_scatter(partial_value, "layer", scatter_dimension=0, tiled=True)
    return owned_rows.reshape(owned_rows.shape[0], train_size, 1, query_dev)


def solution(mesh):
    placed = (
        P("layer", ("parts", "train"), None),
        P("layer", ("parts", "train"), None),
        P("layer", None, None),
        P("layer", None, None),
        P("layer", None, None),
        P("layer", None, None),
        P("layer", None, None),
        P("layer", ("parts", "train", "sub"), None),
    )
    return jax.shard_map(
        body,
        mesh=mesh,
        in_specs=placed,
        out_specs=P(("parts", "train", "layer"), None, "sub", None),
        check_vma=False,
    )
```

profile of v0, /device:TPU:0, one launch (start us, length us, event | category | flops | bytes accessed | tf_op | source)
XLA Modules:
  0.0 152.4 jit_solution(7589246257589771881)
XLA Ops:
  6.5 0.0 copy-start
  6.5 0.0 all-gather.2.cloned.1.call-start
  6.5 1.8 %copy.14 = bf16[1,128,4096]{1,2,0:T(8,128)(2,1)S(1)} copy(bf16[1,128,4096]{2,1,0:T(8,128)(2,1)} %param.15) | data formatting | bytes 2097152 | tf_op args[7]
  8.3 0.0 copy-start.5
  8.3 0.0 copy-start.6
  8.3 4.5 %copy.15 = bf16[128,64,64]{1,2,0:T(8,128)(2,1)} copy(bf16[128,64,64]{0,2,1:T(8,128)(2,1)S(1)} %bitcast.48) | data formatting | bytes 2097152 | tf_op jit(solution)/shard_map/reshape | solution.py:10
  12.8 0.0 copy-done.5
  12.8 0.6 reduce_sum.9
  14.1 0.0 copy-done.6
  14.1 0.0 copy-start.4
  14.1 3.4 %fusion.29 = f32[128,64,64]{2,1,0:T(8,128)S(1)} fusion(bf16[128,64,64]{1,2,0:T(8,128)(2,1)} %copy.15, f32[1,64,64]{2,1,0:T(8,128)S(1)} %copy-done.6), kind=kOutput, calls=%fused_computation.21 | convolution fusion | flops 402653184 | bytes 3162112 | tf_op jit(solution)/shard_map/ia,qij->qaj/dot_general | solution.py:12
  17.6 0.0 copy-done.4
  17.6 6.7 %fusion = f32[128,64,64]{2,1,0:T(8,128)S(1)} fusion(f32[128,64,64]{2,1,0:T(8,128)S(1)} %fusion.29, f32[1,64,64]{2,1,0:T(8,128)S(1)} %copy-done.4), kind=kOutput, calls=%fused_computation | convolution fusion | flops 402653184 | bytes 4210688 | tf_op jit(solution)/shard_map/qaj,jb->qab/dot_general | solution.py:13
  24.3 8.4 %fusion.4 = f32[128,64,64]{1,2,0:T(8,128)} fusion(f32[128,64,64]{2,1,0:T(8,128)S(1)} %fusion, f32[64,64]{1,0:T(8,128)S(1)} %add_bitcast_fusion, f32[1,64,64]{2,1,0:T(8,128)S(1)} %copy-done.6), kind=kOutput, calls=%fused_computation.5 | convolution fusion | flops 403177472 | bytes 4227072 | tf_op jit(solution)/shard_map/ia,qab->qib/dot_general | solution.py:15
  32.7 5.3 %copy.18 = f32[128,64,64]{0,2,1:T(8,128)} copy(f32[128,64,64]{1,2,0:T(8,128)} %fusion.4) | data formatting | bytes 4194304 | tf_op jit(solution)/shard_map/ia,qab->qib/transpose | solution.py:15
  37.9 4.7 %convolution_convert_fusion = bf16[128,64,64]{0,2,1:T(8,128)(2,1)} fusion(f32[128,64,64]{0,2,1:T(8,128)} %copy.18, f32[1,64,64]{2,1,0:T(8,128)S(1)} %copy-done.4), kind=kOutput, calls=%fused_computation.11 | convolution fusion | flops 403177472 | bytes 3162112 | tf_op jit(solution)/shard_map/qib,jb->qij/dot_general | solution.py:16
  42.6 0.0 copy-start.3
  42.6 0.0 all-gather.2.cloned.1.call-update
  42.6 0.0 reduce-scatter.2.cloned.1.call-start
  42.7 0.0 copy-done
  42.7 0.0 copy-done.2
  42.7 0.0 copy-start.1
  42.7 0.8 fusion.15
  43.5 0.2 copy-done.3
  43.6 0.7 copy-done.1
  44.4 0.8 fusion.21
  45.1 2.0 %multiply_convert_fusion = bf16[256,64,64]{0,2,1:T(8,128)(2,1)} fusion(f32[256,64]{0,1:T(8,128)S(1)} %fusion.21, f32[256,64]{0,1:T(8,128)S(1)} %fusion.15), kind=kLoop, calls=%fused_computation.4 | loop fusion | flops 2097152 | bytes 2228224 | tf_op jit(solution)/shard_map/convert_element_type | solution.py:23
  47.2 78.9 %all-gather.2.cloned.1.call-done = bf16[512,4096]{0,1:T(8,128)(2,1)} async-done(((bf16[128,4096]{0,1:T(8,128)(2,1)}), bf16[512,4096]{0,1:T(8,128)(2,1)}) %all-gather.2.cloned.1.call-update) | async-done | bytes 4194320 | tf_op jit(solution)/shard_map/all_gather | solution.py:39
  126.0 4.9 %fusion.31 = f32[256,512]{1,0:T(8,128)} fusion(bf16[256,4096]{0,1:T(8,128)(2,1)} %bitcast.49, bf16[512,4096]{0,1:T(8,128)(2,1)} %all-gather.2.cloned.1.call-done), kind=kOutput, calls=%fused_computation.24 | convolution fusion | flops 1073741824 | bytes 6815744 | tf_op jit(solution)/shard_map/dot_general | solution.py:37
  131.0 0.0 reduce-scatter.2.cloned.1.call-update
  131.0 12.9 %reduce-scatter.2.cloned.1.call-done = f32[128,512]{1,0:T(8,128)} async-done(((f32[256,512]{1,0:T(8,128)}), f32[128,512]{1,0:T(8,128)}) %reduce-scatter.2.cloned.1.call-update) | async-done | bytes 262160 | tf_op jit(solution)/shard_map/reduce_scatter | solution.py:42
  143.9 1.7 %reshape.19 = f32[128,4,1,128]{3,1,0,2:T(4,128)} reshape(f32[128,512]{1,0:T(8,128)} %reduce-scatter.2.cloned.1.call-done) | data formatting | bytes 524288 | tf_op jit(solution)/shard_map/reshape | solution.py:43
  (2 shorter events, 0.0 us)
Async XLA Ops:
  6.5 36.1 %copy-start = (bf16[1,256,4096]{2,1,0:T(8,128)(2,1)S(1)}, bf16[1,256,4096]{2,1,0:T(8,128)(2,1)}, u32[]{:S(2)}) copy-start(bf16[1,256,4096]{2,1,0:T(8,128)(2,1)} %param.9) | copy-start | bytes 6291460
  6.5 119.5 %all-gather.2.cloned.1.call-start = ((), (), s32[]{:S(2)}) async-start(), calls=%async_computation.1 | async-start | bytes 5242880 | tf_op jit(solution)/shard_map/all_gather | solution.py:39
  8.3 4.5 %copy-start.5 = (f32[1,64,64]{2,1,0:T(8,128)S(1)}, f32[1,64,64]{2,1,0:T(8,128)}, u32[]{:S(2)}) copy-start(f32[1,64,64]{2,1,0:T(8,128)} %param.14) | copy-start | bytes 49156
  8.3 5.8 %copy-start.6 = (f32[1,64,64]{2,1,0:T(8,128)S(1)}, f32[1,64,64]{2,1,0:T(8,128)}, u32[]{:S(2)}) copy-start(f32[1,64,64]{2,1,0:T(8,128)} %param.13) | copy-start | bytes 49156
  14.1 3.5 %copy-start.4 = (f32[1,64,64]{2,1,0:T(8,128)S(1)}, f32[1,64,64]{2,1,0:T(8,128)}, u32[]{:S(2)}) copy-start(f32[1,64,64]{2,1,0:T(8,128)} %param.12) | copy-start | bytes 49156
  37.9 4.7 %copy-start.2 = (bf16[1,64,4096]{2,1,0:T(8,128)(2,1)S(1)}, bf16[1,64,4096]{2,1,0:T(8,128)(2,1)}, u32[]{:S(2)}) copy-start(bf16[1,64,4096]{2,1,0:T(8,128)(2,1)} %param.11) | copy-start | bytes 1572868
  42.6 1.0 copy-start.3
  42.6 101.2 %reduce-scatter.2.cloned.1.call-start = ((), (), s32[]{:S(2)}) async-start(), calls=%async_computation.2 | async-start | bytes 786432 | tf_op jit(solution)/shard_map/reduce_scatter | solution.py:42
  42.7 1.7 %copy-start.1 = (bf16[1,256,4096]{2,1,0:T(8,128)(2,1)S(1)}, bf16[1,256,4096]{2,1,0:T(8,128)(2,1)}, u32[]{:S(2)}) copy-start(bf16[1,256,4096]{2,1,0:T(8,128)(2,1)} %param.8) | copy-start | bytes 6291460
Sparse Core Ops, SparseCore 0:
  42.7 83.2 all-gather.1
  131.1 12.7 reduce-scatter.1
where the time goes:
time: 153 us; the launch traced here: 152 us
  waiting for transfers between devices  91.8 us (60%)
  matrix products  29.6 us (19%)
  local copies, waits for them, and re-layouts  14.2 us (9%)
  between operations  14.2 us (9%)
  other arithmetic  2.66 us (2%)
    all_gather x1, waiting for transfers between devices, body(): lax.all_gather(precond, 'train', axis=0, tiled=True)  78.9 us
    reduce_scatter x1, waiting for transfers between devices, body(): lax.psum_scatter(partial_value, 'layer', scatter_dimension=0, tiled=True)  12.9 us
    dot_general x1, matrix products, precondition(): jnp.einsum('ia,qab->qib', basis_out, scaled, precision=lax.Precision.HIGH...  8.39 us
    dot_general x1, matrix products, precondition(): jnp.einsum('qaj,jb->qab', half_turn, basis_in, precision=lax.Precision.HI...  6.68 us
    transpose x1, local copies, waits for them, and re-layouts, precondition(): jnp.einsum('ia,qab->qib', basis_out, scaled, precision=lax.Precision.HIGH...  5.28 us
    dot_general x1, matrix products, body(): jnp.dot(token_grads, lax.all_gather(precond, 'train', axis=0, tiled=True)...  4.9 us
    dot_general x1, matrix products, precondition(): jnp.einsum('qib,jb->qij', back_left, basis_in, precision=lax.Precision.HI...  4.66 us
    reshape x1, local copies, waits for them, and re-layouts, precondition(): query_block.astype(jnp.float32).reshape(count, rank_size, rank_size)  4.51 us
  transfers between devices with their start and end apart: 2, of which 2 were waited for; matrix products, arithmetic and copies ran while one was open for 2% of the time, Pallas kernels for 0%

commit v1 on v0

v1 whole, which is shorter than its diff:
```python
import functools

import jax
import jax.numpy as jnp
from jax import lax
from jax.experimental import pallas as pl
from jax.experimental.pallas import tpu as pltpu
from jax.sharding import PartitionSpec as P

F32 = jnp.float32
BF16 = jnp.bfloat16
PACK = 4


def nt(left, right, precision=None):
    return lax.dot_general(
        left, right, (((1,), (1,)), ((), ())), precision=precision, preferred_element_type=F32
    )


def block_diagonal(matrix):
    rank = matrix.shape[0]
    wide = jnp.concatenate([matrix] * PACK, axis=1)
    tall = jnp.concatenate([wide] * PACK, axis=0)
    rows = lax.broadcasted_iota(jnp.int32, tall.shape, 0) // rank
    columns = lax.broadcasted_iota(jnp.int32, tall.shape, 1) // rank
    return jnp.where(rows == columns, tall, 0.0)


def features_kernel(chunks, inputs_hbm, grads_hbm, proj_in_hbm, proj_out_hbm, basis_in, basis_out,
                    feats, inputs, grads, proj_in, proj_out, sems):
    rank = basis_in.shape[0]
    step = inputs.shape[1] // chunks
    pairs = ((inputs_hbm, inputs), (proj_in_hbm, proj_in), (grads_hbm, grads), (proj_out_hbm, proj_out))

    def copy(which, chunk):
        source, target = pairs[which]
        columns = pl.ds(chunk * step, step)
        return pltpu.make_async_copy(
            source.at[0, :, columns], target.at[:, columns], sems.at[which, chunk]
        )

    for side in (0, 2):
        for chunk in range(chunks):
            copy(side, chunk).start()
            copy(side + 1, chunk).start()
    for side, rows, proj, basis in ((0, inputs, proj_in, basis_in), (2, grads, proj_out, basis_out)):
        total = None
        for chunk in range(chunks):
            copy(side, chunk).wait()
            copy(side + 1, chunk).wait()
            columns = slice(chunk * step, (chunk + 1) * step)
            term = nt(rows[:, columns], proj[:, columns])
            total = term if total is None else total + term
        turned = nt(basis[...].T, total, lax.Precision.HIGHEST)
        feats[side // 2 * rank:(side // 2 + 1) * rank, :] = turned.astype(BF16)


def score_block(feats, weights, rank):
    tokens = feats.shape[1]
    side_in = feats[:rank, :].astype(F32)
    side_out = feats[rank:, :].reshape(rank // 16, 16, tokens)
    total = None
    for part in range(rank // PACK):
        products = []
        for b in range(part * PACK, (part + 1) * PACK):
            row = jnp.broadcast_to(side_in[b:b + 1, :], (16, tokens)).astype(BF16)
            products.append((side_out * row[None]).reshape(rank, tokens))
        width = PACK * rank
        term = jnp.dot(
            weights[:, part * width:(part + 1) * width],
            jnp.concatenate(products, axis=0),
            preferred_element_type=F32,
        )
        total = term if total is None else total + term
    return total.T


def queries_kernel(queries, basis_in, basis_out, eigen, weights, half):
    rank = basis_in.shape[0]
    width = PACK * rank
    groups = rank // PACK
    right = block_diagonal(basis_in[...].T).astype(BF16)
    for part in range(groups):
        half[part * width:(part + 1) * width, :] = nt(
            right, queries[:, part * width:(part + 1) * width]
        )
    left = block_diagonal(basis_out[...]).astype(BF16)
    spectrum = eigen[...]
    inverse = (1.0 / (spectrum + 0.1 * jnp.mean(spectrum))).T
    for part in range(groups):
        columns = range(part * PACK, (part + 1) * PACK)
        matrix = jnp.concatenate(
            [half[pl.ds(b, rank, stride=rank), :] for b in columns], axis=0
        )
        turned = jnp.dot(matrix.T.astype(BF16), left, preferred_element_type=F32)
        scale = jnp.concatenate([inverse[b:b + 1, :] for b in columns], axis=1)
        weights[:, part * width:(part + 1) * width] = (turned * scale).astype(BF16)


def scores_kernel(train_size, layer_size, rank, weights, *refs):
    feats, blocks = refs[:-1], refs[-1]
    here = lax.axis_index("train")
    rows = blocks.shape[1]
    for offset in range(train_size):
        scores = score_block(feats[offset][...], weights, rank).astype(BF16)
        owner = lax.rem(here + offset, train_size)
        for layer in range(layer_size):
            blocks[owner * layer_size + layer] = scores[layer * rows:(layer + 1) * rows, :]


def sum_kernel(train_size, layer_size, blocks, out):
    rows = blocks.shape[1]
    for source in range(train_size):
        total = blocks[source * layer_size].astype(F32)
        for layer in range(1, layer_size):
            total = total + blocks[source * layer_size + layer].astype(F32)
        out[pl.ds(source, rows, stride=train_size), :] = total


def body(inputs, out_grads, proj_in, proj_out, basis_in, basis_out, eigen, queries):
    train_size, layer_size = lax.axis_size("train"), lax.axis_size("layer")
    tokens, width = inputs.shape[1:]
    count, entries = queries.shape[1:]
    rank = proj_in.shape[1]
    chunks = 4
    vmem, hbm = pl.BlockSpec(memory_space=pltpu.VMEM), pl.BlockSpec(memory_space=pl.ANY)
    params = pltpu.CompilerParams(vmem_limit_bytes=32 << 20)

    feats = pl.pallas_call(
        functools.partial(features_kernel, chunks),
        out_shape=jax.ShapeDtypeStruct((2 * rank, tokens), BF16),
        in_specs=[hbm] * 4 + [vmem] * 2,
        out_specs=vmem,
        scratch_shapes=[
            pltpu.VMEM((tokens, width), BF16),
            pltpu.VMEM((tokens, width), BF16),
            pltpu.VMEM((rank, width), BF16),
            pltpu.VMEM((rank, width), BF16),
            pltpu.SemaphoreType.DMA((4, chunks)),
        ],
        compiler_params=params,
        cost_estimate=pl.CostEstimate(
            flops=4 * tokens * rank * width, bytes_accessed=4 * width * (tokens + rank), transcendentals=0
        ),
        name="features",
    )(inputs, out_grads, proj_in, proj_out, basis_in[0], basis_out[0])

    gathered = [feats] + [
        lax.ppermute(
            feats, "train", [((j + offset) % train_size, j) for j in range(train_size)]
        )
        for offset in range(1, train_size)
    ]

    weights = pl.pallas_call(
        queries_kernel,
        out_shape=jax.ShapeDtypeStruct((count, entries), BF16),
        in_specs=[vmem] * 4,
        out_specs=vmem,
        scratch_shapes=[pltpu.VMEM((entries, count), F32)],
        compiler_params=params,
        cost_estimate=pl.CostEstimate(
            flops=4 * PACK * count * entries * rank, bytes_accessed=4 * count * entries, transcendentals=0
        ),
        name="queries",
    )(queries[0], basis_in[0], basis_out[0], eigen[0])

    rows = tokens // layer_size
    blocks = pl.pallas_call(
        functools.partial(scores_kernel, train_size, layer_size, rank),
        out_shape=jax.ShapeDtypeStruct((train_size * layer_size, rows, count), BF16),
        in_specs=[vmem] * (train_size + 1),
        out_specs=vmem,
        compiler_params=params,
        cost_estimate=pl.CostEstimate(
            flops=2 * train_size * tokens * entries * count, bytes_accessed=2 * count * entries, transcendentals=0
        ),
        name="scores",
    )(weights, *gathered)

    arrived = lax.all_to_all(blocks, ("train", "layer"), 0, 0, tiled=True)

    total = pl.pallas_call(
        functools.partial(sum_kernel, train_size, layer_size),
        out_shape=jax.ShapeDtypeStruct((rows * train_size, count), F32),
        in_specs=[vmem],
        out_specs=vmem,
        compiler_params=params,
        name="sum",
    )(arrived)
    return total.reshape(rows, train_size, 1, count)


def solution(mesh):
    placed = (
        P("layer", ("parts", "train"), None),
        P("layer", ("parts", "train"), None),
        P("layer", None, None),
        P("layer", None, None),
        P("layer", None, None),
        P("layer", None, None),
        P("layer", None, None),
        P("layer", ("parts", "train", "sub"), None),
    )
    return jax.shard_map(
        body,
        mesh=mesh,
        in_specs=placed,
        out_specs=P(("parts", "train", "layer"), None, "sub", None),
        check_vma=False,
    )
```

time: 153 us -> 36.9 us (0.24)
  waiting for transfers between devices: 91.8 us -> 1.22 us
  matrix products: 29.6 us -> 0 us
  between operations: 14.2 us -> 0.05 us
  blocking collectives: 0 us -> 13.3 us
  Pallas kernels: 0 us -> 8.13 us
  local copies, waits for them, and re-layouts: 14.2 us -> 6.79 us
  starting transfers between devices: 0.04 us -> 7.02 us
  other arithmetic: 2.66 us -> 0 us
    all_gather x1 -> x0, waiting for transfers between devices: 78.9 us -> none  [body(): lax.all_gather(precond, 'train', axis=0, tiled=True)]
    dot_general x7 -> x0, matrix products: 29.6 us -> none  [the longest x1 8.39 us: precondition(): jnp.einsum('ia,qab->qib', basis_out, scaled, precision=lax.Precision.HIGH...]
    all_to_all x0 -> x1, blocking collectives: none -> 13.3 us  [body(): arrived = lax.all_to_all(blocks, ('train', 'layer'), 0, 0, tiled=True)]
    reduce_scatter x1 -> x0, waiting for transfers between devices: 12.9 us -> none  [body(): lax.psum_scatter(partial_value, 'layer', scatter_dimension=0, tiled=True)]
    pallas_call x0 -> x4, Pallas kernels: none -> 8.13 us  [the longest x1 3.95 us: body(): pl.pallas_call(functools.partial(features_kernel, chunks), out_shape=jax....]
    ppermute x0 -> x3, starting transfers between devices: none -> 7.02 us  [body(): lax.ppermute(feats, 'train', [((j + offset) % train_size, j) for j in ran...]
    reshape x2 -> x0, local copies, waits for them, and re-layouts: 6.24 us -> none  [the longest x1 4.51 us: precondition(): query_block.astype(jnp.float32).reshape(count, rank_size, rank_size)]
    transpose x1 -> x0, local copies, waits for them, and re-layouts: 5.28 us -> none  [precondition(): jnp.einsum('ia,qab->qib', basis_out, scaled, precision=lax.Precision.HIGH...]
  transfers between devices with their start and end apart: 2 -> 3, of which waited for: 2 -> 2; matrix products, arithmetic and copies ran while one was open for 2% -> 0% of each run, Pallas kernels for 0% -> 6%
where the time goes in v1:
time: 36.9 us; the launch traced here: 36.5 us
  blocking collectives  13.3 us (36%)
  Pallas kernels  8.13 us (22%)
  starting transfers between devices  7.02 us (19%)
  local copies, waits for them, and re-layouts  6.79 us (18%)
  waiting for transfers between devices  1.22 us (3%)
    all_to_all x1, blocking collectives, body(): arrived = lax.all_to_all(blocks, ('train', 'layer'), 0, 0, tiled=True)  13.3 us
    ppermute x3, starting transfers between devices, body(): lax.ppermute(feats, 'train', [((j + offset) % train_size, j) for j in ran...  7.02 us
    unnamed x20, local copies, waits for them, and re-layouts  6.79 us
    pallas_call x1, Pallas kernels, body(): pl.pallas_call(functools.partial(features_kernel, chunks), out_shape=jax....  3.95 us
    pallas_call x1, Pallas kernels, body(): pl.pallas_call(queries_kernel, out_shape=jax.ShapeDtypeStruct((count, ent...  2.12 us
    pallas_call x1, Pallas kernels, body(): pl.pallas_call(functools.partial(scores_kernel, train_size, layer_size, r...  1.32 us
    ppermute x3, waiting for transfers between devices, body(): lax.ppermute(feats, 'train', [((j + offset) % train_size, j) for j in ran...  1.22 us
    pallas_call x1, Pallas kernels, body(): pl.pallas_call(functools.partial(sum_kernel, train_size, layer_size), out...  0.74 us
  transfers between devices with their start and end apart: 3, of which 2 were waited for; matrix products, arithmetic and copies ran while one was open for 0% of the time, Pallas kernels for 6%

profile of v1, /device:TPU:0, one launch (start us, length us, event | category | flops | bytes accessed | tf_op | source)
XLA Modules:
  0.0 36.5 jit_solution(18212450455027177636)
XLA Ops:
  0.0 0.0 copy-start
  0.0 1.6 %copy-done = bf16[1,256,4096]{2,1,0:T(8,128)(2,1)S(1)} copy-done((bf16[1,256,4096]{2,1,0:T(8,128)(2,1)S(1)}, bf16[1,256,4096]{2,1,0:T(8,128)(2,1)}, u32[]{:S(2)}) %copy-start) | copy-done | bytes 2097176
  1.6 0.0 copy-start.1
  1.6 1.6 %copy-done.1 = bf16[1,256,4096]{2,1,0:T(8,128)(2,1)S(1)} copy-done((bf16[1,256,4096]{2,1,0:T(8,128)(2,1)S(1)}, bf16[1,256,4096]{2,1,0:T(8,128)(2,1)}, u32[]{:S(2)}) %copy-start.1) | copy-done | bytes 2097176
  3.2 0.0 copy-start.3
  3.2 1.0 %copy-done.3 = bf16[1,64,4096]{2,1,0:T(8,128)(2,1)S(1)} copy-done((bf16[1,64,4096]{2,1,0:T(8,128)(2,1)S(1)}, bf16[1,64,4096]{2,1,0:T(8,128)(2,1)}, u32[]{:S(2)}) %copy-start.3) | copy-done | bytes 524312
  4.2 0.0 copy-start.4
  4.2 1.0 %copy-done.4 = bf16[1,64,4096]{2,1,0:T(8,128)(2,1)S(1)} copy-done((bf16[1,64,4096]{2,1,0:T(8,128)(2,1)S(1)}, bf16[1,64,4096]{2,1,0:T(8,128)(2,1)}, u32[]{:S(2)}) %copy-start.4) | copy-done | bytes 524312
  5.3 0.0 copy-start.5
  5.3 0.8 %copy-done.5 = f32[1,64,64]{2,1,0:T(8,128)S(1)} copy-done((f32[1,64,64]{2,1,0:T(8,128)S(1)}, f32[1,64,64]{2,1,0:T(8,128)}, u32[]{:S(2)}) %copy-start.5) | copy-done | bytes 16408
  6.0 0.0 copy-start.7
  6.0 0.8 %copy-done.7 = f32[1,64,64]{2,1,0:T(8,128)S(1)} copy-done((f32[1,64,64]{2,1,0:T(8,128)S(1)}, f32[1,64,64]{2,1,0:T(8,128)}, u32[]{:S(2)}) %copy-start.7) | copy-done | bytes 16408
  6.8 0.0 copy-start.2
  6.8 0.0 copy-start.6
  6.8 0.0 copy-start.8
  6.8 0.0 copy-start.9
  6.8 3.9 %features.1.refs_0_ = bf16[128,256]{1,0:T(8,128)(2,1)S(1)} custom-call(bf16[1,256,4096]{2,1,0:T(8,128)(2,1)S(1)} %copy-done, bf16[1,256,4096]{2,1,0:T(8,128)(2,1)S(1)} %copy-done.1, bf16[1,64,4096]{2,1,0:T(8,128)(2,1)S(1)} %copy-done.3, bf16[1,64,4096]{2,1,0:T(8,128)(2,1)S(1)} %copy-done.4, f32[64,64]{1,0:T(8,128)S(1)} %bitcast.8, f32[64,64]{1,0:T(8,128)S(1)} %bitcast.10), custom_call_target="tpu_custom_call" | custom-call | flops 268435456 | bytes 5242880 | tf_op jit(solution)/shard_map/features/pallas_call | solution.py:130
  10.8 3.1 %collective-permute-start.2 = (bf16[128,256]{1,0:T(8,128)(2,1)S(1)}, bf16[128,256]{1,0:T(8,128)(2,1)S(1)}, u32[]{:S(2)}, u32[]{:S(2)}) collective-permute-start(bf16[128,256]{1,0:T(8,128)(2,1)S(1)} %features.1.refs_0_), channel_id=1, source_target_pairs={{12,0},{0,4},{4,8},{8,12},{13,1},{1,5},{5,9},{9,13},{14,2},{2,6},{... | collective-permute-start | bytes 196616 | tf_op jit(solution)/shard_map/ppermute | solution.py:150
  13.8 2.6 %collective-permute-start.1 = (bf16[128,256]{1,0:T(8,128)(2,1)S(1)}, bf16[128,256]{1,0:T(8,128)(2,1)S(1)}, u32[]{:S(2)}, u32[]{:S(2)}) collective-permute-start(bf16[128,256]{1,0:T(8,128)(2,1)S(1)} %features.1.refs_0_), channel_id=1, source_target_pairs={{8,0},{12,4},{0,8},{4,12},{9,1},{13,5},{1,9},{5,13},{10,2},{14,6},... | collective-permute-start | bytes 196616 | tf_op jit(solution)/shard_map/ppermute | solution.py:150
  16.4 1.3 %collective-permute-start = (bf16[128,256]{1,0:T(8,128)(2,1)S(1)}, bf16[128,256]{1,0:T(8,128)(2,1)S(1)}, u32[]{:S(2)}, u32[]{:S(2)}) collective-permute-start(bf16[128,256]{1,0:T(8,128)(2,1)S(1)} %features.1.refs_0_), channel_id=1, source_target_pairs={{4,0},{8,4},{12,8},{0,12},{5,1},{9,5},{13,9},{1,13},{6,2},{10,6},{... | collective-permute-start | bytes 196616 | tf_op jit(solution)/shard_map/ppermute | solution.py:150
  17.8 0.0 copy-done.2
  17.8 0.0 copy-done.6
  17.8 0.0 copy-done.8
  17.8 0.0 copy-done.9
  17.8 2.1 %queries.1.weights = bf16[128,4096]{1,0:T(8,128)(2,1)S(1)} custom-call(bf16[128,4096]{1,0:T(8,128)(2,1)S(1)} %bitcast.7, f32[64,64]{1,0:T(8,128)S(1)} %bitcast.9, f32[64,64]{1,0:T(8,128)S(1)} %bitcast.11, f32[64,64]{1,0:T(8,128)S(1)} %bitcast.12), custom_call_target="tpu_custom_call" | custom-call | flops 536870912 | bytes 2097152 | tf_op jit(solution)/shard_map/queries/pallas_call | solution.py:156
  19.9 0.0 collective-permute-done.2.refs_3_
  19.9 1.0 %collective-permute-done.1.refs_2_ = bf16[128,256]{1,0:T(8,128)(2,1)S(1)} collective-permute-done((bf16[128,256]{1,0:T(8,128)(2,1)S(1)}, bf16[128,256]{1,0:T(8,128)(2,1)S(1)}, u32[]{:S(2)}, u32[]{:S(2)}) %collective-permute-start.1) | collective-permute-done | bytes 65568 | tf_op jit(solution)/shard_map/ppermute | solution.py:150
  20.9 0.2 collective-permute-done.refs_1_
  21.1 1.3 %scores.1 = bf16[8,128,128]{2,1,0:T(8,128)(2,1)S(1)} custom-call(bf16[128,4096]{1,0:T(8,128)(2,1)S(1)} %queries.1.weights, bf16[128,256]{1,0:T(8,128)(2,1)S(1)} %features.1.refs_0_, bf16[128,256]{1,0:T(8,128)(2,1)S(1)} %collective-permute-done.refs_1_, bf16[128,256]{1,0:T(8,128)(2,1)S(1)} %collective-permute-done.1.refs_2_, ...), custom_call_target="tpu_custom_call" | custom-call | flops 1073741824 | bytes 1048576 | tf_op jit(solution)/shard_map/scores/pallas_call | solution.py:170
  22.5 13.3 %all_to_all.5.blocks = bf16[8,128,128]{2,1,0:T(8,128)(2,1)S(1)} all-to-all(bf16[8,128,128]{2,1,0:T(8,128)(2,1)S(1)} %scores.1), channel_id=1, replica_groups=mesh['parts'=2,'train'=4,'layer'=2,'sub'=2] {'train','layer'}, dimensions={0} | all-to-all | bytes 524288 | tf_op jit(solution)/shard_map/all_to_all | solution.py:182
  35.7 0.7 %sum.1 = f32[512,128]{1,0:T(8,128)} custom-call(bf16[8,128,128]{2,1,0:T(8,128)(2,1)S(1)} %all_to_all.5.blocks), custom_call_target="tpu_custom_call" | custom-call | tf_op jit(solution)/shard_map/sum/pallas_call | solution.py:184
Async XLA Ops:
  0.0 1.6 %copy-start = (bf16[1,256,4096]{2,1,0:T(8,128)(2,1)S(1)}, bf16[1,256,4096]{2,1,0:T(8,128)(2,1)}, u32[]{:S(2)}) copy-start(bf16[1,256,4096]{2,1,0:T(8,128)(2,1)} %inputs_hbm.1) | copy-start | bytes 6291460
  1.6 1.6 %copy-start.1 = (bf16[1,256,4096]{2,1,0:T(8,128)(2,1)S(1)}, bf16[1,256,4096]{2,1,0:T(8,128)(2,1)}, u32[]{:S(2)}) copy-start(bf16[1,256,4096]{2,1,0:T(8,128)(2,1)} %grads_hbm.1) | copy-start | bytes 6291460
  3.2 1.0 %copy-start.3 = (bf16[1,64,4096]{2,1,0:T(8,128)(2,1)S(1)}, bf16[1,64,4096]{2,1,0:T(8,128)(2,1)}, u32[]{:S(2)}) copy-start(bf16[1,64,4096]{2,1,0:T(8,128)(2,1)} %proj_in_hbm.1) | copy-start | bytes 1572868
  4.2 1.0 %copy-start.4 = (bf16[1,64,4096]{2,1,0:T(8,128)(2,1)S(1)}, bf16[1,64,4096]{2,1,0:T(8,128)(2,1)}, u32[]{:S(2)}) copy-start(bf16[1,64,4096]{2,1,0:T(8,128)(2,1)} %proj_out_hbm.1) | copy-start | bytes 1572868
  5.3 0.8 %copy-start.5 = (f32[1,64,64]{2,1,0:T(8,128)S(1)}, f32[1,64,64]{2,1,0:T(8,128)}, u32[]{:S(2)}) copy-start(f32[1,64,64]{2,1,0:T(8,128)} %param.12) | copy-start | bytes 49156
  6.0 0.8 %copy-start.7 = (f32[1,64,64]{2,1,0:T(8,128)S(1)}, f32[1,64,64]{2,1,0:T(8,128)}, u32[]{:S(2)}) copy-start(f32[1,64,64]{2,1,0:T(8,128)} %param.13) | copy-start | bytes 49156
  6.8 11.0 %copy-start.2 = (bf16[1,128,4096]{2,1,0:T(8,128)(2,1)S(1)}, bf16[1,128,4096]{2,1,0:T(8,128)(2,1)}, u32[]{:S(2)}) copy-start(bf16[1,128,4096]{2,1,0:T(8,128)(2,1)} %param.15) | copy-start | bytes 3145732
  6.8 11.0 %copy-start.6 = (f32[1,64,64]{2,1,0:T(8,128)S(1)}, f32[1,64,64]{2,1,0:T(8,128)}, u32[]{:S(2)}) copy-start(f32[1,64,64]{2,1,0:T(8,128)} %param.12) | copy-start | bytes 49156
  6.8 11.0 %copy-start.8 = (f32[1,64,64]{2,1,0:T(8,128)S(1)}, f32[1,64,64]{2,1,0:T(8,128)}, u32[]{:S(2)}) copy-start(f32[1,64,64]{2,1,0:T(8,128)} %param.13) | copy-start | bytes 49156
  6.8 11.0 %copy-start.9 = (f32[1,64,64]{2,1,0:T(8,128)S(1)}, f32[1,64,64]{2,1,0:T(8,128)}, u32[]{:S(2)}) copy-start(f32[1,64,64]{2,1,0:T(8,128)} %param.14) | copy-start | bytes 49156
  10.8 9.2 %collective-permute-start.2 = (bf16[128,256]{1,0:T(8,128)(2,1)S(1)}, bf16[128,256]{1,0:T(8,128)(2,1)S(1)}, u32[]{:S(2)}, u32[]{:S(2)}) collective-permute-start(bf16[128,256]{1,0:T(8,128)(2,1)S(1)} %features.1.refs_0_), channel_id=1, source_target_pairs={{12,0},{0,4},{4,8},{8,12},{13,1},{1,5},{5,9},{9,13},{14,2},{2,6},{... | collective-permute-start | bytes 196616 | tf_op jit(solution)/shard_map/ppermute | solution.py:150
  13.8 7.1 %collective-permute-start.1 = (bf16[128,256]{1,0:T(8,128)(2,1)S(1)}, bf16[128,256]{1,0:T(8,128)(2,1)S(1)}, u32[]{:S(2)}, u32[]{:S(2)}) collective-permute-start(bf16[128,256]{1,0:T(8,128)(2,1)S(1)} %features.1.refs_0_), channel_id=1, source_target_pairs={{8,0},{12,4},{0,8},{4,12},{9,1},{13,5},{1,9},{5,13},{10,2},{14,6},... | collective-permute-start | bytes 196616 | tf_op jit(solution)/shard_map/ppermute | solution.py:150
  16.4 4.7 %collective-permute-start = (bf16[128,256]{1,0:T(8,128)(2,1)S(1)}, bf16[128,256]{1,0:T(8,128)(2,1)S(1)}, u32[]{:S(2)}, u32[]{:S(2)}) collective-permute-start(bf16[128,256]{1,0:T(8,128)(2,1)S(1)} %features.1.refs_0_), channel_id=1, source_target_pairs={{4,0},{8,4},{12,8},{0,12},{5,1},{9,5},{13,9},{1,13},{6,2},{10,6},{... | collective-permute-start | bytes 196616 | tf_op jit(solution)/shard_map/ppermute | solution.py:150

commit v2 on v1

--- a/solution.py
+++ b/solution.py
@@ -27,33 +27,38 @@
     return jnp.where(rows == columns, tall, 0.0)
 
 
-def features_kernel(chunks, inputs_hbm, grads_hbm, proj_in_hbm, proj_out_hbm, basis_in, basis_out,
-                    feats, inputs, grads, proj_in, proj_out, sems):
+def features_kernel(chunks, *refs):
+    sources, feats, targets, sems = refs[:6], refs[6], refs[7:13], refs[13]
+    inputs, grads, proj_in, proj_out, basis_in, basis_out = targets
     rank = basis_in.shape[0]
     step = inputs.shape[1] // chunks
-    pairs = ((inputs_hbm, inputs), (proj_in_hbm, proj_in), (grads_hbm, grads), (proj_out_hbm, proj_out))
 
     def copy(which, chunk):
-        source, target = pairs[which]
+        source, target = sources[which], targets[which]
+        if which >= 4:
+            return pltpu.make_async_copy(source.at[0], target, sems.at[which, 0])
         columns = pl.ds(chunk * step, step)
         return pltpu.make_async_copy(
             source.at[0, :, columns], target.at[:, columns], sems.at[which, chunk]
         )
 
-    for side in (0, 2):
+    sides = ((0, 2, 4), (1, 3, 5))
+    for side in sides:
         for chunk in range(chunks):
-            copy(side, chunk).start()
-            copy(side + 1, chunk).start()
-    for side, rows, proj, basis in ((0, inputs, proj_in, basis_in), (2, grads, proj_out, basis_out)):
+            copy(side[0], chunk).start()
+            copy(side[1], chunk).start()
+        copy(side[2], 0).start()
+    for place, (tokens, proj, basis) in enumerate(sides):
         total = None
         for chunk in range(chunks):
-            copy(side, chunk).wait()
-            copy(side + 1, chunk).wait()
+            copy(tokens, chunk).wait()
+            copy(proj, chunk).wait()
             columns = slice(chunk * step, (chunk + 1) * step)
-            term = nt(rows[:, columns], proj[:, columns])
+            term = nt(targets[tokens][:, columns], targets[proj][:, columns])
             total = term if total is None else total + term
-        turned = nt(basis[...].T, total, lax.Precision.HIGHEST)
-        feats[side // 2 * rank:(side // 2 + 1) * rank, :] = turned.astype(BF16)
+        copy(basis, 0).wait()
+        turned = nt(targets[basis][...].T, total, lax.Precision.HIGHEST)
+        feats[place * rank:(place + 1) * rank, :] = turned.astype(BF16)
 
 
 def score_block(feats, weights, rank):
@@ -99,23 +104,29 @@
 
 
 def scores_kernel(train_size, layer_size, rank, weights, *refs):
-    feats, blocks = refs[:-1], refs[-1]
-    here = lax.axis_index("train")
-    rows = blocks.shape[1]
+    feats, blocks, scores = refs[:train_size], refs[train_size:-1], refs[-1]
+    place, layer = lax.axis_index("train"), lax.axis_index("layer")
+    rows = blocks[0].shape[1]
     for offset in range(train_size):
-        scores = score_block(feats[offset][...], weights, rank).astype(BF16)
-        owner = lax.rem(here + offset, train_size)
-        for layer in range(layer_size):
-            blocks[owner * layer_size + layer] = scores[layer * rows:(layer + 1) * rows, :]
-
-
-def sum_kernel(train_size, layer_size, blocks, out):
+        scores[...] = score_block(feats[offset][...], weights, rank)
+        owner = lax.rem(place + offset, train_size)
+        for k, block in enumerate(blocks):
+            first = pl.multiple_of(lax.rem(layer + k, layer_size) * rows, rows)
+            block[owner] = scores[pl.ds(first, rows), :].astype(block.dtype)
+
+
+def layers_kernel(own, *refs):
+    others, out = refs[:-1], refs[-1]
+    total = own[...]
+    for other in others:
+        total = total + other[...].astype(F32)
+    out[...] = total.astype(BF16)
+
+
+def place_kernel(train_size, blocks, out):
     rows = blocks.shape[1]
     for source in range(train_size):
-        total = blocks[source * layer_size].astype(F32)
-        for layer in range(1, layer_size):
-            total = total + blocks[source * layer_size + layer].astype(F32)
-        out[pl.ds(source, rows, stride=train_size), :] = total
+        out[pl.ds(source, rows, stride=train_size), :] = blocks[source].astype(F32)
 
 
 def body(inputs, out_grads, proj_in, proj_out, basis_in, basis_out, eigen, queries):
@@ -124,27 +135,32 @@
     count, entries = queries.shape[1:]
     rank = proj_in.shape[1]
     chunks = 4
-    vmem, hbm = pl.BlockSpec(memory_space=pltpu.VMEM), pl.BlockSpec(memory_space=pl.ANY)
+    vmem, hbm = pl.BlockSpec(memory_space=pltpu.VMEM), pl.BlockSpec(memory_space=pltpu.HBM)
     params = pltpu.CompilerParams(vmem_limit_bytes=32 << 20)
 
     feats = pl.pallas_call(
         functools.partial(features_kernel, chunks),
         out_shape=jax.ShapeDtypeStruct((2 * rank, tokens), BF16),
-        in_specs=[hbm] * 4 + [vmem] * 2,
+        in_specs=[hbm] * 6,
         out_specs=vmem,
         scratch_shapes=[
             pltpu.VMEM((tokens, width), BF16),
             pltpu.VMEM((tokens, width), BF16),
             pltpu.VMEM((rank, width), BF16),
             pltpu.VMEM((rank, width), BF16),
-            pltpu.SemaphoreType.DMA((4, chunks)),
+            pltpu.VMEM((rank, rank), F32),
+            pltpu.VMEM((rank, rank), F32),
+            pltpu.SemaphoreType.DMA((6, chunks)),
         ],
         compiler_params=params,
         cost_estimate=pl.CostEstimate(
             flops=4 * tokens * rank * width, bytes_accessed=4 * width * (tokens + rank), transcendentals=0
         ),
         name="features",
-    )(inputs, out_grads, proj_in, proj_out, basis_in[0], basis_out[0])
+    )(*[
+        pltpu.with_memory_space_constraint(value, pltpu.HBM)
+        for value in (inputs, out_grads, proj_in, proj_out, basis_in, basis_out)
+    ])
 
     gathered = [feats] + [
         lax.ppermute(
@@ -167,11 +183,15 @@
     )(queries[0], basis_in[0], basis_out[0], eigen[0])
 
     rows = tokens // layer_size
-    blocks = pl.pallas_call(
+    own, *away = pl.pallas_call(
         functools.partial(scores_kernel, train_size, layer_size, rank),
-        out_shape=jax.ShapeDtypeStruct((train_size * layer_size, rows, count), BF16),
+        out_shape=[
+            jax.ShapeDtypeStruct((train_size, rows, count), BF16 if k else F32)
+            for k in range(layer_size)
+        ],
         in_specs=[vmem] * (train_size + 1),
-        out_specs=vmem,
+        out_specs=[vmem] * layer_size,
+        scratch_shapes=[pltpu.VMEM((tokens, count), F32)],
         compiler_params=params,
         cost_estimate=pl.CostEstimate(
             flops=2 * train_size * tokens * entries * count, bytes_accessed=2 * count * entries, transcendentals=0
@@ -179,15 +199,28 @@
         name="scores",
     )(weights, *gathered)
 
-    arrived = lax.all_to_all(blocks, ("train", "layer"), 0, 0, tiled=True)
+    others = [
+        lax.ppermute(block, "layer", [(l, (l + k) % layer_size) for l in range(layer_size)])
+        for k, block in enumerate(away, 1)
+    ]
+    summed = pl.pallas_call(
+        layers_kernel,
+        out_shape=jax.ShapeDtypeStruct((train_size, rows, count), BF16),
+        in_specs=[vmem] * layer_size,
+        out_specs=vmem,
+        compiler_params=params,
+        name="layers",
+    )(own, *others)
+
+    arrived = lax.all_to_all(summed, "train", 0, 0, tiled=True)
 
     total = pl.pallas_call(
-        functools.partial(sum_kernel, train_size, layer_size),
+        functools.partial(place_kernel, train_size),
         out_shape=jax.ShapeDtypeStruct((rows * train_size, count), F32),
         in_specs=[vmem],
         out_specs=vmem,
         compiler_params=params,
-        name="sum",
+        name="place",
     )(arrived)
     return total.reshape(rows, train_size, 1, count)
 

time: 36.9 us -> 32.7 us (0.89)
  local copies, waits for them, and re-layouts: 6.79 us -> 0.01 us
  waiting for transfers between devices: 1.22 us -> 4.65 us
  blocking collectives: 13.3 us -> 10 us
  starting transfers between devices: 7.02 us -> 8.65 us
  Pallas kernels: 8.13 us -> 9.15 us
    unnamed x20 -> x8, local copies, waits for them, and re-layouts: 6.79 us -> 0.01 us
    ppermute x0 -> x1, waiting for transfers between devices: none -> 3.44 us  [body(): lax.ppermute(block, 'layer', [(l, (l + k) % layer_size) for l in range(la...]
    all_to_all x1, blocking collectives: 13.3 us -> 10 us  [body(): arrived = lax.all_to_all(summed, 'train', 0, 0, tiled=True)]
    ppermute x0 -> x1, starting transfers between devices: none -> 1.62 us  [body(): lax.ppermute(block, 'layer', [(l, (l + k) % layer_size) for l in range(la...]
    pallas_call x1, Pallas kernels: 3.95 us -> 4.87 us  [body(): pl.pallas_call(functools.partial(features_kernel, chunks), out_shape=jax....]
    pallas_call x1 -> x2, Pallas kernels: 0.74 us -> 0.76 us  [the longest x1 0.73 us: body(): pl.pallas_call(functools.partial(place_kernel, train_size), out_shape=jax...]
  transfers between devices with their start and end apart: 3 -> 4, of which waited for: 2 -> 3; matrix products, arithmetic and copies ran while one was open for 0% -> 0% of each run, Pallas kernels for 6% -> 7%
where the time goes in v2:
time: 32.7 us; the launch traced here: 32.5 us
  blocking collectives  10 us (31%)
  Pallas kernels  9.15 us (28%)
  starting transfers between devices  8.65 us (26%)
  waiting for transfers between devices  4.65 us (14%)
    all_to_all x1, blocking collectives, body(): arrived = lax.all_to_all(summed, 'train', 0, 0, tiled=True)  10 us
    ppermute x3, starting transfers between devices, body(): lax.ppermute(feats, 'train', [((j + offset) % train_size, j) for j in ran...  7.03 us
    pallas_call x1, Pallas kernels, body(): pl.pallas_call(functools.partial(features_kernel, chunks), out_shape=jax....  4.87 us
    ppermute x1, waiting for transfers between devices, body(): lax.ppermute(block, 'layer', [(l, (l + k) % layer_size) for l in range(la...  3.44 us
    pallas_call x1, Pallas kernels, body(): pl.pallas_call(queries_kernel, out_shape=jax.ShapeDtypeStruct((count, ent...  2.12 us
    ppermute x1, starting transfers between devices, body(): lax.ppermute(block, 'layer', [(l, (l + k) % layer_size) for l in range(la...  1.62 us
    pallas_call x1, Pallas kernels, body(): pl.pallas_call(functools.partial(scores_kernel, train_size, layer_size, r...  1.41 us
    ppermute x3, waiting for transfers between devices, body(): lax.ppermute(feats, 'train', [((j + offset) % train_size, j) for j in ran...  1.21 us
  transfers between devices with their start and end apart: 4, of which 3 were waited for; matrix products, arithmetic and copies ran while one was open for 0% of the time, Pallas kernels for 7%

profile of v2, /device:TPU:0, one launch (start us, length us, event | category | flops | bytes accessed | tf_op | source)
XLA Modules:
  0.0 32.5 jit_solution(1810358024655031272)
XLA Ops:
  0.0 0.0 copy-start.2
  0.0 0.0 copy-start.1
  0.0 0.0 copy-start
  0.0 0.0 copy-start.3
  0.0 4.9 %features.1.refs_0_ = bf16[128,256]{1,0:T(8,128)(2,1)S(1)} custom-call(bf16[1,256,4096]{2,1,0:T(8,128)(2,1)} %refs_0_.1, bf16[1,256,4096]{2,1,0:T(8,128)(2,1)} %refs_1_.1, bf16[1,64,4096]{2,1,0:T(8,128)(2,1)} %refs_2_.1, bf16[1,64,4096]{2,1,0:T(8,128)(2,1)} %refs_3_.1, f32[1,64,64]{2,1,0:T(8,128)} %refs_4_.1, f32[1,64,64]{2,1,0:T(8,128)} %refs_5_.1), custom_call_target="tpu_custom_call" | custom-call | flops 268435456 | bytes 5242880 | tf_op jit(solution)/shard_map/features/pallas_call | solution.py:141
  4.9 3.1 %collective-permute-start.2 = (bf16[128,256]{1,0:T(8,128)(2,1)S(1)}, bf16[128,256]{1,0:T(8,128)(2,1)S(1)}, u32[]{:S(2)}, u32[]{:S(2)}) collective-permute-start(bf16[128,256]{1,0:T(8,128)(2,1)S(1)} %features.1.refs_0_), channel_id=1, source_target_pairs={{12,0},{0,4},{4,8},{8,12},{13,1},{1,5},{5,9},{9,13},{14,2},{2,6},{... | collective-permute-start | bytes 196616 | tf_op jit(solution)/shard_map/ppermute | solution.py:166
  8.0 2.6 %collective-permute-start.1 = (bf16[128,256]{1,0:T(8,128)(2,1)S(1)}, bf16[128,256]{1,0:T(8,128)(2,1)S(1)}, u32[]{:S(2)}, u32[]{:S(2)}) collective-permute-start(bf16[128,256]{1,0:T(8,128)(2,1)S(1)} %features.1.refs_0_), channel_id=1, source_target_pairs={{8,0},{12,4},{0,8},{4,12},{9,1},{13,5},{1,9},{5,13},{10,2},{14,6},... | collective-permute-start | bytes 196616 | tf_op jit(solution)/shard_map/ppermute | solution.py:166
  10.6 1.4 %collective-permute-start = (bf16[128,256]{1,0:T(8,128)(2,1)S(1)}, bf16[128,256]{1,0:T(8,128)(2,1)S(1)}, u32[]{:S(2)}, u32[]{:S(2)}) collective-permute-start(bf16[128,256]{1,0:T(8,128)(2,1)S(1)} %features.1.refs_0_), channel_id=1, source_target_pairs={{4,0},{8,4},{12,8},{0,12},{5,1},{9,5},{13,9},{1,13},{6,2},{10,6},{... | collective-permute-start | bytes 196616 | tf_op jit(solution)/shard_map/ppermute | solution.py:166
  11.9 0.0 copy-done.2
  11.9 0.0 copy-done.1
  11.9 0.0 copy-done
  11.9 0.0 copy-done.3
  11.9 2.1 %queries.1.weights = bf16[128,4096]{1,0:T(8,128)(2,1)S(1)} custom-call(bf16[128,4096]{1,0:T(8,128)(2,1)S(1)} %bitcast.7, f32[64,64]{1,0:T(8,128)S(1)} %bitcast.8, f32[64,64]{1,0:T(8,128)S(1)} %bitcast.9, f32[64,64]{1,0:T(8,128)S(1)} %bitcast.10), custom_call_target="tpu_custom_call" | custom-call | flops 536870912 | bytes 2097152 | tf_op jit(solution)/shard_map/queries/pallas_call | solution.py:172
  14.1 0.0 collective-permute-done.2.refs_3_
  14.1 1.0 %collective-permute-done.1.refs_2_ = bf16[128,256]{1,0:T(8,128)(2,1)S(1)} collective-permute-done((bf16[128,256]{1,0:T(8,128)(2,1)S(1)}, bf16[128,256]{1,0:T(8,128)(2,1)S(1)}, u32[]{:S(2)}, u32[]{:S(2)}) %collective-permute-start.1) | collective-permute-done | bytes 65568 | tf_op jit(solution)/shard_map/ppermute | solution.py:166
  15.1 0.2 collective-permute-done.refs_1_
  15.3 1.4 %scores.1 = (f32[4,128,128]{2,1,0:T(8,128)S(1)}, bf16[4,128,128]{2,1,0:T(8,128)(2,1)S(1)}) custom-call(bf16[128,4096]{1,0:T(8,128)(2,1)S(1)} %queries.1.weights, bf16[128,256]{1,0:T(8,128)(2,1)S(1)} %features.1.refs_0_, bf16[128,256]{1,0:T(8,128)(2,1)S(1)} %collective-permute-done.refs_1_, bf16[128,256]{1,0:T(8,128)(2,1)S(1)} %collective-permute-done.1.refs_2_, ...), custom_call_target="tpu_custom_call" | custom-call | flops 1073741824 | bytes 1048576 | tf_op jit(solution)/shard_map/scores/pallas_call | solution.py:186
  16.7 1.6 %collective-permute-start.3 = (bf16[4,128,128]{2,1,0:T(8,128)(2,1)S(1)}, bf16[4,128,128]{2,1,0:T(8,128)(2,1)S(1)}, u32[]{:S(2)}, u32[]{:S(2)}) collective-permute-start(bf16[4,128,128]{2,1,0:T(8,128)(2,1)S(1)} %get-tuple-element.8), channel_id=1, source_target_pairs={{0,2},{2,0},{1,3},{3,1},{4,6},{6,4},{5,7},{7,5},{8,10},{10,8},{9,1... | collective-permute-start | bytes 393224 | tf_op jit(solution)/shard_map/ppermute | solution.py:203
  18.3 3.4 %collective-permute-done.3.refs_0_ = bf16[4,128,128]{2,1,0:T(8,128)(2,1)S(1)} collective-permute-done((bf16[4,128,128]{2,1,0:T(8,128)(2,1)S(1)}, bf16[4,128,128]{2,1,0:T(8,128)(2,1)S(1)}, u32[]{:S(2)}, u32[]{:S(2)}) %collective-permute-start.3) | collective-permute-done | bytes 131104 | tf_op jit(solution)/shard_map/ppermute | solution.py:203
  21.8 10.0 %all_to_all.5.blocks = bf16[4,128,128]{2,1,0:T(8,128)(2,1)S(1)} all-to-all(bf16[4,128,128]{2,1,0:T(8,128)(2,1)S(1)} %layers.1), channel_id=1, replica_groups=mesh['parts'=2,'train'=4,'layer'=2,'sub'=2] {'train'}, dimensions={0} | all-to-all | bytes 262144 | tf_op jit(solution)/shard_map/all_to_all | solution.py:215
  31.8 0.7 %place.1 = f32[512,128]{1,0:T(8,128)} custom-call(bf16[4,128,128]{2,1,0:T(8,128)(2,1)S(1)} %all_to_all.5.blocks), custom_call_target="tpu_custom_call" | custom-call | tf_op jit(solution)/shard_map/place/pallas_call | solution.py:217
  (1 shorter events, 0.0 us)
Async XLA Ops:
  0.0 11.9 %copy-start.2 = (f32[1,64,64]{2,1,0:T(8,128)S(1)}, f32[1,64,64]{2,1,0:T(8,128)}, u32[]{:S(2)}) copy-start(f32[1,64,64]{2,1,0:T(8,128)} %refs_5_.1) | copy-start | bytes 49156
  0.0 11.9 %copy-start.1 = (f32[1,64,64]{2,1,0:T(8,128)S(1)}, f32[1,64,64]{2,1,0:T(8,128)}, u32[]{:S(2)}) copy-start(f32[1,64,64]{2,1,0:T(8,128)} %refs_4_.1) | copy-start | bytes 49156
  0.0 11.9 %copy-start = (bf16[1,128,4096]{2,1,0:T(8,128)(2,1)S(1)}, bf16[1,128,4096]{2,1,0:T(8,128)(2,1)}, u32[]{:S(2)}) copy-start(bf16[1,128,4096]{2,1,0:T(8,128)(2,1)} %param.15) | copy-start | bytes 3145732
  0.0 11.9 %copy-start.3 = (f32[1,64,64]{2,1,0:T(8,128)S(1)}, f32[1,64,64]{2,1,0:T(8,128)}, u32[]{:S(2)}) copy-start(f32[1,64,64]{2,1,0:T(8,128)} %param.14) | copy-start | bytes 49156
  4.9 9.2 %collective-permute-start.2 = (bf16[128,256]{1,0:T(8,128)(2,1)S(1)}, bf16[128,256]{1,0:T(8,128)(2,1)S(1)}, u32[]{:S(2)}, u32[]{:S(2)}) collective-permute-start(bf16[128,256]{1,0:T(8,128)(2,1)S(1)} %features.1.refs_0_), channel_id=1, source_target_pairs={{12,0},{0,4},{4,8},{8,12},{13,1},{1,5},{5,9},{9,13},{14,2},{2,6},{... | collective-permute-start | bytes 196616 | tf_op jit(solution)/shard_map/ppermute | solution.py:166
  8.0 7.1 %collective-permute-start.1 = (bf16[128,256]{1,0:T(8,128)(2,1)S(1)}, bf16[128,256]{1,0:T(8,128)(2,1)S(1)}, u32[]{:S(2)}, u32[]{:S(2)}) collective-permute-start(bf16[128,256]{1,0:T(8,128)(2,1)S(1)} %features.1.refs_0_), channel_id=1, source_target_pairs={{8,0},{12,4},{0,8},{4,12},{9,1},{13,5},{1,9},{5,13},{10,2},{14,6},... | collective-permute-start | bytes 196616 | tf_op jit(solution)/shard_map/ppermute | solution.py:166
  10.6 4.7 %collective-permute-start = (bf16[128,256]{1,0:T(8,128)(2,1)S(1)}, bf16[128,256]{1,0:T(8,128)(2,1)S(1)}, u32[]{:S(2)}, u32[]{:S(2)}) collective-permute-start(bf16[128,256]{1,0:T(8,128)(2,1)S(1)} %features.1.refs_0_), channel_id=1, source_target_pairs={{4,0},{8,4},{12,8},{0,12},{5,1},{9,5},{13,9},{1,13},{6,2},{10,6},{... | collective-permute-start | bytes 196616 | tf_op jit(solution)/shard_map/ppermute | solution.py:166
  16.7 5.1 %collective-permute-start.3 = (bf16[4,128,128]{2,1,0:T(8,128)(2,1)S(1)}, bf16[4,128,128]{2,1,0:T(8,128)(2,1)S(1)}, u32[]{:S(2)}, u32[]{:S(2)}) collective-permute-start(bf16[4,128,128]{2,1,0:T(8,128)(2,1)S(1)} %get-tuple-element.8), channel_id=1, source_target_pairs={{0,2},{2,0},{1,3},{3,1},{4,6},{6,4},{5,7},{7,5},{8,10},{10,8},{9,1... | collective-permute-start | bytes 393224 | tf_op jit(solution)/shard_map/ppermute | solution.py:203

commit v3 on v2

--- a/solution.py
+++ b/solution.py
@@ -12,10 +12,13 @@
 PACK = 4
 
 
-def nt(left, right, precision=None):
-    return lax.dot_general(
-        left, right, (((1,), (1,)), ((), ())), precision=precision, preferred_element_type=F32
-    )
+def nt(left, right):
+    return lax.dot_general(left, right, (((1,), (1,)), ((), ())), preferred_element_type=F32)
+
+
+def two_terms(matrix):
+    high = matrix.astype(BF16)
+    return jnp.concatenate([high, (matrix - high.astype(F32)).astype(BF16)], axis=1)
 
 
 def block_diagonal(matrix):
@@ -54,10 +57,14 @@
             copy(tokens, chunk).wait()
             copy(proj, chunk).wait()
             columns = slice(chunk * step, (chunk + 1) * step)
-            term = nt(targets[tokens][:, columns], targets[proj][:, columns])
+            term = nt(targets[proj][:, columns], targets[tokens][:, columns])
             total = term if total is None else total + term
         copy(basis, 0).wait()
-        turned = nt(targets[basis][...].T, total, lax.Precision.HIGHEST)
+        turned = jnp.dot(
+            two_terms(targets[basis][...].T),
+            jnp.concatenate([total.astype(BF16)] * 2, axis=0),
+            preferred_element_type=F32,
+        )
         feats[place * rank:(place + 1) * rank, :] = turned.astype(BF16)
 
 
@@ -103,30 +110,37 @@
         weights[:, part * width:(part + 1) * width] = (turned * scale).astype(BF16)
 
 
-def scores_kernel(train_size, layer_size, rank, weights, *refs):
-    feats, blocks, scores = refs[:train_size], refs[train_size:-1], refs[-1]
-    place, layer = lax.axis_index("train"), lax.axis_index("layer")
-    rows = blocks[0].shape[1]
-    for offset in range(train_size):
-        scores[...] = score_block(feats[offset][...], weights, rank)
-        owner = lax.rem(place + offset, train_size)
-        for k, block in enumerate(blocks):
+def scores_kernel(layer_size, rank, groups, weights, *refs):
+    feats = refs[:groups]
+    own, away, scores = refs[-layer_size - 1], refs[-layer_size:-1], refs[-1]
+    layer = lax.axis_index("layer")
+    rows = own.shape[1]
+    for i, feat in enumerate(feats):
+        scores[...] = score_block(feat[...], weights, rank)
+        for k, block in enumerate((own, *away)):
             first = pl.multiple_of(lax.rem(layer + k, layer_size) * rows, rows)
-            block[owner] = scores[pl.ds(first, rows), :].astype(block.dtype)
-
-
-def layers_kernel(own, *refs):
-    others, out = refs[:-1], refs[-1]
-    total = own[...]
+            block[i] = scores[pl.ds(first, rows), :].astype(block.dtype)
+
+
+def layers_kernel(layer_size, groups, own, *refs):
+    others, outs = refs[:layer_size - 1], refs[-groups:]
+    for i, out in enumerate(outs):
+        total = own[i]
+        for other in others:
+            total = total + other[i].astype(F32)
+        out[...] = total.astype(BF16)
+
+
+def place_kernel(train_size, layer_size, own, *refs):
+    others, arrived, out = refs[:layer_size - 1], refs[layer_size - 1:-1], refs[-1]
+    here = lax.axis_index("train")
+    rows = own.shape[1]
+    total = own[0]
     for other in others:
-        total = total + other[...].astype(F32)
-    out[...] = total.astype(BF16)
-
-
-def place_kernel(train_size, blocks, out):
-    rows = blocks.shape[1]
-    for source in range(train_size):
-        out[pl.ds(source, rows, stride=train_size), :] = blocks[source].astype(F32)
+        total = total + other[0].astype(F32)
+    out[pl.ds(here, rows, stride=train_size), :] = total
+    for offset, block in enumerate(arrived, 1):
+        out[pl.ds(here ^ offset, rows, stride=train_size), :] = block[...].astype(F32)
 
 
 def body(inputs, out_grads, proj_in, proj_out, basis_in, basis_out, eigen, queries):
@@ -136,6 +150,7 @@
     rank = proj_in.shape[1]
     chunks = 4
     vmem, hbm = pl.BlockSpec(memory_space=pltpu.VMEM), pl.BlockSpec(memory_space=pltpu.HBM)
+    anywhere = pl.BlockSpec(memory_space=pl.ANY)
     params = pltpu.CompilerParams(vmem_limit_bytes=32 << 20)
 
     feats = pl.pallas_call(
@@ -162,12 +177,10 @@
         for value in (inputs, out_grads, proj_in, proj_out, basis_in, basis_out)
     ])
 
-    gathered = [feats] + [
-        lax.ppermute(
-            feats, "train", [((j + offset) % train_size, j) for j in range(train_size)]
-        )
-        for offset in range(1, train_size)
-    ]
+    def exchange(value, offset):
+        return lax.ppermute(value, "train", [(j, j ^ offset) for j in range(train_size)])
+
+    gathered = [feats] + [exchange(feats, offset) for offset in range(1, train_size)]
 
     weights = pl.pallas_call(
         queries_kernel,
@@ -183,45 +196,58 @@
     )(queries[0], basis_in[0], basis_out[0], eigen[0])
 
     rows = tokens // layer_size
-    own, *away = pl.pallas_call(
-        functools.partial(scores_kernel, train_size, layer_size, rank),
-        out_shape=[
-            jax.ShapeDtypeStruct((train_size, rows, count), BF16 if k else F32)
-            for k in range(layer_size)
-        ],
-        in_specs=[vmem] * (train_size + 1),
-        out_specs=[vmem] * layer_size,
-        scratch_shapes=[pltpu.VMEM((tokens, count), F32)],
-        compiler_params=params,
-        cost_estimate=pl.CostEstimate(
-            flops=2 * train_size * tokens * entries * count, bytes_accessed=2 * count * entries, transcendentals=0
-        ),
-        name="scores",
-    )(weights, *gathered)
-
-    others = [
-        lax.ppermute(block, "layer", [(l, (l + k) % layer_size) for l in range(layer_size)])
-        for k, block in enumerate(away, 1)
-    ]
-    summed = pl.pallas_call(
-        layers_kernel,
-        out_shape=jax.ShapeDtypeStruct((train_size, rows, count), BF16),
-        in_specs=[vmem] * layer_size,
-        out_specs=vmem,
-        compiler_params=params,
-        name="layers",
-    )(own, *others)
-
-    arrived = lax.all_to_all(summed, "train", 0, 0, tiled=True)
+
+    def scored(offsets, after):
+        own, *away = pl.pallas_call(
+            functools.partial(scores_kernel, layer_size, rank, len(offsets)),
+            out_shape=[
+                jax.ShapeDtypeStruct((len(offsets), rows, count), BF16 if k else F32)
+                for k in range(layer_size)
+            ],
+            in_specs=[vmem] * (len(offsets) + 1) + [anywhere] * len(after),
+            out_specs=[vmem] * layer_size,
+            scratch_shapes=[pltpu.VMEM((tokens, count), F32)],
+            compiler_params=params,
+            cost_estimate=pl.CostEstimate(
+                flops=2 * len(offsets) * tokens * entries * count,
+                bytes_accessed=2 * count * entries,
+                transcendentals=0,
+            ),
+            name="scores",
+        )(weights, *[gathered[offset] for offset in offsets], *after)
+        return own, [
+            lax.ppermute(block, "layer", [(l, (l + k) % layer_size) for l in range(layer_size)])
+            for k, block in enumerate(away, 1)
+        ]
+
+    half = train_size // 2
+    far, near = range(train_size - 1, half - 1, -1), range(half - 1, 0, -1)
+    own, others = scored([0], [])
+    far_terms = scored(far, [own])
+    near_terms = scored(near, [far_terms[0]])
+    arrived = [None] * train_size
+    after = []
+    for offsets, (mine, theirs) in ((far, far_terms), (near, near_terms)):
+        summed = pl.pallas_call(
+            functools.partial(layers_kernel, layer_size, len(offsets)),
+            out_shape=[jax.ShapeDtypeStruct((rows, count), BF16)] * len(offsets),
+            in_specs=[vmem] * layer_size + [anywhere] * len(after),
+            out_specs=[vmem] * len(offsets),
+            compiler_params=params,
+            name="layers",
+        )(mine, *theirs, *after)
+        after = summed[-1:]
+        for offset, block in zip(offsets, summed):
+            arrived[offset] = exchange(block, offset)
 
     total = pl.pallas_call(
-        functools.partial(place_kernel, train_size),
+        functools.partial(place_kernel, train_size, layer_size),
         out_shape=jax.ShapeDtypeStruct((rows * train_size, count), F32),
-        in_specs=[vmem],
+        in_specs=[vmem] * (layer_size + train_size - 1),
         out_specs=vmem,
         compiler_params=params,
         name="place",
-    )(arrived)
+    )(own, *others, *arrived[1:])
     return total.reshape(rows, train_size, 1, count)
 
 

time: 32.7 us -> 29.6 us (0.905)
  blocking collectives: 10 us -> 0 us
  starting transfers between devices: 8.65 us -> 14.4 us
  waiting for transfers between devices: 4.65 us -> 5.55 us
  Pallas kernels: 9.15 us -> 9.48 us
    all_to_all x1 -> x0, blocking collectives: 10 us -> none  [body(): arrived = lax.all_to_all(summed, 'train', 0, 0, tiled=True)]
    ppermute x4 -> x9, starting transfers between devices: 8.65 us -> 14.4 us  [the longest x6 10.7 us: exchange(): lax.ppermute(value, 'train', [(j, j ^ offset) for j in range(train_size)])]
    ppermute x4 -> x9, waiting for transfers between devices: 4.65 us -> 5.55 us  [the longest x6 5.41 us: exchange(): lax.ppermute(value, 'train', [(j, j ^ offset) for j in range(train_size)])]
    pallas_call x3 -> x6, Pallas kernels: 2.16 us -> 2.69 us  [the longest x3 1.94 us: scored(): pl.pallas_call(functools.partial(scores_kernel, layer_size, rank, len(off...]
  transfers between devices with their start and end apart: 4 -> 9, of which waited for: 3 -> 5; matrix products, arithmetic and copies ran while one was open for 0% -> 0% of each run, Pallas kernels for 7% -> 14%
where the time goes in v3:
time: 29.6 us; the launch traced here: 29.5 us
  starting transfers between devices  14.4 us (49%)
  Pallas kernels  9.48 us (32%)
  waiting for transfers between devices  5.55 us (19%)
    ppermute x6, starting transfers between devices, exchange(): lax.ppermute(value, 'train', [(j, j ^ offset) for j in range(train_size)])  10.7 us
    ppermute x6, waiting for transfers between devices, exchange(): lax.ppermute(value, 'train', [(j, j ^ offset) for j in range(train_size)])  5.41 us
    pallas_call x1, Pallas kernels, body(): pl.pallas_call(functools.partial(features_kernel, chunks), out_shape=jax....  4.67 us
    ppermute x3, starting transfers between devices, scored(): lax.ppermute(block, 'layer', [(l, (l + k) % layer_size) for l in range(la...  3.66 us
    pallas_call x1, Pallas kernels, body(): pl.pallas_call(queries_kernel, out_shape=jax.ShapeDtypeStruct((count, ent...  2.11 us
    pallas_call x3, Pallas kernels, scored(): pl.pallas_call(functools.partial(scores_kernel, layer_size, rank, len(off...  1.94 us
    pallas_call x1, Pallas kernels, body(): pl.pallas_call(functools.partial(place_kernel, train_size, layer_size), o...  0.73 us
  transfers between devices with their start and end apart: 9, of which 5 were waited for; matrix products, arithmetic and copies ran while one was open for 0% of the time, Pallas kernels for 14%

profile of v3, /device:TPU:0, one launch (start us, length us, event | category | flops | bytes accessed | tf_op | source)
XLA Modules:
  0.0 29.5 jit_solution(4096058634660951245)
XLA Ops:
  0.0 0.0 copy-start.2
  0.0 0.0 copy-start.1
  0.0 0.0 copy-start
  0.0 0.0 copy-start.3
  0.0 4.7 %features.1.refs_0_ = bf16[128,256]{1,0:T(8,128)(2,1)S(1)} custom-call(bf16[1,256,4096]{2,1,0:T(8,128)(2,1)} %refs_0_.1, bf16[1,256,4096]{2,1,0:T(8,128)(2,1)} %refs_1_.1, bf16[1,64,4096]{2,1,0:T(8,128)(2,1)} %refs_2_.1, bf16[1,64,4096]{2,1,0:T(8,128)(2,1)} %refs_3_.1, f32[1,64,64]{2,1,0:T(8,128)} %refs_4_.1, f32[1,64,64]{2,1,0:T(8,128)} %refs_5_.1), custom_call_target="tpu_custom_call" | custom-call | flops 268435456 | bytes 5242880 | tf_op jit(solution)/shard_map/features/pallas_call | solution.py:156
  4.7 4.1 %collective-permute-start.3 = (bf16[128,256]{1,0:T(8,128)(2,1)S(1)}, bf16[128,256]{1,0:T(8,128)(2,1)S(1)}, u32[]{:S(2)}, u32[]{:S(2)}) collective-permute-start(bf16[128,256]{1,0:T(8,128)(2,1)S(1)} %features.1.refs_0_), channel_id=1, source_target_pairs={{0,8},{4,12},{8,0},{12,4},{1,9},{5,13},{9,1},{13,5},{2,10},{6,14},... | collective-permute-start | bytes 196616 | tf_op jit(solution)/shard_map/ppermute | solution.py:181
  8.8 1.3 %collective-permute-start.2 = (bf16[128,256]{1,0:T(8,128)(2,1)S(1)}, bf16[128,256]{1,0:T(8,128)(2,1)S(1)}, u32[]{:S(2)}, u32[]{:S(2)}) collective-permute-start(bf16[128,256]{1,0:T(8,128)(2,1)S(1)} %features.1.refs_0_), channel_id=1, source_target_pairs={{0,12},{4,8},{8,4},{12,0},{1,13},{5,9},{9,5},{13,1},{2,14},{6,10},... | collective-permute-start | bytes 196616 | tf_op jit(solution)/shard_map/ppermute | solution.py:181
  10.2 0.2 collective-permute-start.1
  10.4 0.0 copy-done.2
  10.4 0.0 copy-done.1
  10.4 0.0 copy-done
  10.4 0.0 copy-done.3
  10.4 2.1 %queries.1.weights = bf16[128,4096]{1,0:T(8,128)(2,1)S(1)} custom-call(bf16[128,4096]{1,0:T(8,128)(2,1)S(1)} %bitcast.7, f32[64,64]{1,0:T(8,128)S(1)} %bitcast.8, f32[64,64]{1,0:T(8,128)S(1)} %bitcast.9, f32[64,64]{1,0:T(8,128)S(1)} %bitcast.10), custom_call_target="tpu_custom_call" | custom-call | flops 536870912 | bytes 2097152 | tf_op jit(solution)/shard_map/queries/pallas_call | solution.py:185
  12.5 0.5 %scores.3 = (f32[1,128,128]{2,1,0:T(8,128)S(1)}, bf16[1,128,128]{2,1,0:T(8,128)(2,1)S(1)}) custom-call(bf16[128,4096]{1,0:T(8,128)(2,1)S(1)} %queries.1.weights, bf16[128,256]{1,0:T(8,128)(2,1)S(1)} %features.1.refs_0_), custom_call_target="tpu_custom_call" | custom-call | flops 268435456 | bytes 1048576 | tf_op jit(solution)/shard_map/scores/pallas_call | solution.py:201
  13.1 0.0 collective-permute-done.3.refs_1_
  13.1 2.0 %collective-permute-done.2.refs_0_ = bf16[128,256]{1,0:T(8,128)(2,1)S(1)} collective-permute-done((bf16[128,256]{1,0:T(8,128)(2,1)S(1)}, bf16[128,256]{1,0:T(8,128)(2,1)S(1)}, u32[]{:S(2)}, u32[]{:S(2)}) %collective-permute-start.2) | collective-permute-done | bytes 65568 | tf_op jit(solution)/shard_map/ppermute | solution.py:181
  15.0 0.9 %scores.4 = (f32[2,128,128]{2,1,0:T(8,128)S(1)}, bf16[2,128,128]{2,1,0:T(8,128)(2,1)S(1)}) custom-call(bf16[128,4096]{1,0:T(8,128)(2,1)S(1)} %queries.1.weights, bf16[128,256]{1,0:T(8,128)(2,1)S(1)} %collective-permute-done.2.refs_0_, bf16[128,256]{1,0:T(8,128)(2,1)S(1)} %collective-permute-done.3.refs_1_, f32[1,128,128]{2,1,0:T(8,128)S(1)} %get-tuple-element.13.refs_2_.own), custom_call_target="tpu_custom_call" | custom-call | flops 536870912 | bytes 1048576 | tf_op jit(solution)/shard_map/scores/pallas_call | solution.py:201
  15.9 1.6 %collective-permute-start.5 = (bf16[2,128,128]{2,1,0:T(8,128)(2,1)S(1)}, bf16[2,128,128]{2,1,0:T(8,128)(2,1)S(1)}, u32[]{:S(2)}, u32[]{:S(2)}) collective-permute-start(bf16[2,128,128]{2,1,0:T(8,128)(2,1)S(1)} %get-tuple-element.18), channel_id=1, source_target_pairs={{0,2},{2,0},{1,3},{3,1},{4,6},{6,4},{5,7},{7,5},{8,10},{10,8},{9,1... | collective-permute-start | bytes 196616 | tf_op jit(solution)/shard_map/ppermute | solution.py:219
  17.5 0.0 collective-permute-done.1.refs_0_
  17.5 0.5 %scores.5 = (f32[1,128,128]{2,1,0:T(8,128)S(1)}, bf16[1,128,128]{2,1,0:T(8,128)(2,1)S(1)}) custom-call(bf16[128,4096]{1,0:T(8,128)(2,1)S(1)} %queries.1.weights, bf16[128,256]{1,0:T(8,128)(2,1)S(1)} %collective-permute-done.1.refs_0_, f32[2,128,128]{2,1,0:T(8,128)S(1)} %get-tuple-element.15.refs_1_.own), custom_call_target="tpu_custom_call" | custom-call | flops 268435456 | bytes 1048576 | tf_op jit(solution)/shard_map/scores/pallas_call | solution.py:201
  18.0 0.6 %collective-permute-start.4 = (bf16[1,128,128]{2,1,0:T(8,128)(2,1)S(1)}, bf16[1,128,128]{2,1,0:T(8,128)(2,1)S(1)}, u32[]{:S(2)}, u32[]{:S(2)}) collective-permute-start(bf16[1,128,128]{2,1,0:T(8,128)(2,1)S(1)} %get-tuple-element.17), channel_id=1, source_target_pairs={{0,2},{2,0},{1,3},{3,1},{4,6},{6,4},{5,7},{7,5},{8,10},{10,8},{9,1... | collective-permute-start | bytes 98312 | tf_op jit(solution)/shard_map/ppermute | solution.py:219
  18.6 1.5 %collective-permute-start = (bf16[1,128,128]{2,1,0:T(8,128)(2,1)S(1)}, bf16[1,128,128]{2,1,0:T(8,128)(2,1)S(1)}, u32[]{:S(2)}, u32[]{:S(2)}) collective-permute-start(bf16[1,128,128]{2,1,0:T(8,128)(2,1)S(1)} %get-tuple-element.14), channel_id=1, source_target_pairs={{0,2},{2,0},{1,3},{3,1},{4,6},{6,4},{5,7},{7,5},{8,10},{10,8},{9,1... | collective-permute-start | bytes 98312 | tf_op jit(solution)/shard_map/ppermute | solution.py:219
  20.1 0.1 collective-permute-done.5.refs_0_
  20.3 3.4 %collective-permute-start.8 = (bf16[128,128]{1,0:T(8,128)(2,1)S(1)}, bf16[128,128]{1,0:T(8,128)(2,1)S(1)}, u32[]{:S(2)}, u32[]{:S(2)}) collective-permute-start(bf16[128,128]{1,0:T(8,128)(2,1)S(1)} %get-tuple-element.20), channel_id=1, source_target_pairs={{0,12},{4,8},{8,4},{12,0},{1,13},{5,9},{9,5},{13,1},{2,14},{6,10},... | collective-permute-start | bytes 98312 | tf_op jit(solution)/shard_map/ppermute | solution.py:181
  23.6 0.0 collective-permute-done.4.refs_0_
  23.6 0.3 collective-permute-start.6
  23.9 1.4 %collective-permute-start.7 = (bf16[128,128]{1,0:T(8,128)(2,1)S(1)}, bf16[128,128]{1,0:T(8,128)(2,1)S(1)}, u32[]{:S(2)}, u32[]{:S(2)}) collective-permute-start(bf16[128,128]{1,0:T(8,128)(2,1)S(1)} %get-tuple-element.19.refs_1_), channel_id=1, source_target_pairs={{0,8},{4,12},{8,0},{12,4},{1,9},{5,13},{9,1},{13,5},{2,10},{6,14},... | collective-permute-start | bytes 98312 | tf_op jit(solution)/shard_map/ppermute | solution.py:181
  25.3 0.0 collective-permute-done.refs_0_
  25.3 1.1 %collective-permute-done.8.refs_3_ = bf16[128,128]{1,0:T(8,128)(2,1)S(1)} collective-permute-done((bf16[128,128]{1,0:T(8,128)(2,1)S(1)}, bf16[128,128]{1,0:T(8,128)(2,1)S(1)}, u32[]{:S(2)}, u32[]{:S(2)}) %collective-permute-start.8) | collective-permute-done | bytes 32800 | tf_op jit(solution)/shard_map/ppermute | solution.py:181
  26.4 1.2 %collective-permute-done.6.refs_1_ = bf16[128,128]{1,0:T(8,128)(2,1)S(1)} collective-permute-done((bf16[128,128]{1,0:T(8,128)(2,1)S(1)}, bf16[128,128]{1,0:T(8,128)(2,1)S(1)}, u32[]{:S(2)}, u32[]{:S(2)}) %collective-permute-start.6) | collective-permute-done | bytes 32800 | tf_op jit(solution)/shard_map/ppermute | solution.py:181
  27.6 1.1 %collective-permute-done.7.refs_2_ = bf16[128,128]{1,0:T(8,128)(2,1)S(1)} collective-permute-done((bf16[128,128]{1,0:T(8,128)(2,1)S(1)}, bf16[128,128]{1,0:T(8,128)(2,1)S(1)}, u32[]{:S(2)}, u32[]{:S(2)}) %collective-permute-start.7) | collective-permute-done | bytes 32800 | tf_op jit(solution)/shard_map/ppermute | solution.py:181
  28.7 0.7 %place.1 = f32[512,128]{1,0:T(8,128)} custom-call(f32[1,128,128]{2,1,0:T(8,128)S(1)} %get-tuple-element.13.refs_2_.own, bf16[1,128,128]{2,1,0:T(8,128)(2,1)S(1)} %collective-permute-done.refs_0_, bf16[128,128]{1,0:T(8,128)(2,1)S(1)} %collective-permute-done.6.refs_1_, bf16[128,128]{1,0:T(8,128)(2,1)S(1)} %collective-permute-done.7.refs_2_, ...), custom_call_target="tpu_custom_call" | custom-call | tf_op jit(solution)/shard_map/place/pallas_call | solution.py:243
  (2 shorter events, 0.0 us)
Async XLA Ops:
  0.0 10.4 %copy-start.2 = (f32[1,64,64]{2,1,0:T(8,128)S(1)}, f32[1,64,64]{2,1,0:T(8,128)}, u32[]{:S(2)}) copy-start(f32[1,64,64]{2,1,0:T(8,128)} %refs_5_.1) | copy-start | bytes 49156
  0.0 10.4 %copy-start.1 = (f32[1,64,64]{2,1,0:T(8,128)S(1)}, f32[1,64,64]{2,1,0:T(8,128)}, u32[]{:S(2)}) copy-start(f32[1,64,64]{2,1,0:T(8,128)} %refs_4_.1) | copy-start | bytes 49156
  0.0 10.4 %copy-start = (bf16[1,128,4096]{2,1,0:T(8,128)(2,1)S(1)}, bf16[1,128,4096]{2,1,0:T(8,128)(2,1)}, u32[]{:S(2)}) copy-start(bf16[1,128,4096]{2,1,0:T(8,128)(2,1)} %param.15) | copy-start | bytes 3145732
  0.0 10.4 %copy-start.3 = (f32[1,64,64]{2,1,0:T(8,128)S(1)}, f32[1,64,64]{2,1,0:T(8,128)}, u32[]{:S(2)}) copy-start(f32[1,64,64]{2,1,0:T(8,128)} %param.14) | copy-start | bytes 49156
  4.7 8.4 %collective-permute-start.3 = (bf16[128,256]{1,0:T(8,128)(2,1)S(1)}, bf16[128,256]{1,0:T(8,128)(2,1)S(1)}, u32[]{:S(2)}, u32[]{:S(2)}) collective-permute-start(bf16[128,256]{1,0:T(8,128)(2,1)S(1)} %features.1.refs_0_), channel_id=1, source_target_pairs={{0,8},{4,12},{8,0},{12,4},{1,9},{5,13},{9,1},{13,5},{2,10},{6,14},... | collective-permute-start | bytes 196616 | tf_op jit(solution)/shard_map/ppermute | solution.py:181
  8.8 6.2 %collective-permute-start.2 = (bf16[128,256]{1,0:T(8,128)(2,1)S(1)}, bf16[128,256]{1,0:T(8,128)(2,1)S(1)}, u32[]{:S(2)}, u32[]{:S(2)}) collective-permute-start(bf16[128,256]{1,0:T(8,128)(2,1)S(1)} %features.1.refs_0_), channel_id=1, source_target_pairs={{0,12},{4,8},{8,4},{12,0},{1,13},{5,9},{9,5},{13,1},{2,14},{6,10},... | collective-permute-start | bytes 196616 | tf_op jit(solution)/shard_map/ppermute | solution.py:181
  10.2 7.3 %collective-permute-start.1 = (bf16[128,256]{1,0:T(8,128)(2,1)S(1)}, bf16[128,256]{1,0:T(8,128)(2,1)S(1)}, u32[]{:S(2)}, u32[]{:S(2)}) collective-permute-start(bf16[128,256]{1,0:T(8,128)(2,1)S(1)} %features.1.refs_0_), channel_id=1, source_target_pairs={{0,4},{4,0},{8,12},{12,8},{1,5},{5,1},{9,13},{13,9},{2,6},{6,2},{1... | collective-permute-start | bytes 196616 | tf_op jit(solution)/shard_map/ppermute | solution.py:181
  15.9 4.3 %collective-permute-start.5 = (bf16[2,128,128]{2,1,0:T(8,128)(2,1)S(1)}, bf16[2,128,128]{2,1,0:T(8,128)(2,1)S(1)}, u32[]{:S(2)}, u32[]{:S(2)}) collective-permute-start(bf16[2,128,128]{2,1,0:T(8,128)(2,1)S(1)} %get-tuple-element.18), channel_id=1, source_target_pairs={{0,2},{2,0},{1,3},{3,1},{4,6},{6,4},{5,7},{7,5},{8,10},{10,8},{9,1... | collective-permute-start | bytes 196616 | tf_op jit(solution)/shard_map/ppermute | solution.py:219
  18.0 5.6 %collective-permute-start.4 = (bf16[1,128,128]{2,1,0:T(8,128)(2,1)S(1)}, bf16[1,128,128]{2,1,0:T(8,128)(2,1)S(1)}, u32[]{:S(2)}, u32[]{:S(2)}) collective-permute-start(bf16[1,128,128]{2,1,0:T(8,128)(2,1)S(1)} %get-tuple-element.17), channel_id=1, source_target_pairs={{0,2},{2,0},{1,3},{3,1},{4,6},{6,4},{5,7},{7,5},{8,10},{10,8},{9,1... | collective-permute-start | bytes 98312 | tf_op jit(solution)/shard_map/ppermute | solution.py:219
  18.6 6.7 %collective-permute-start = (bf16[1,128,128]{2,1,0:T(8,128)(2,1)S(1)}, bf16[1,128,128]{2,1,0:T(8,128)(2,1)S(1)}, u32[]{:S(2)}, u32[]{:S(2)}) collective-permute-start(bf16[1,128,128]{2,1,0:T(8,128)(2,1)S(1)} %get-tuple-element.14), channel_id=1, source_target_pairs={{0,2},{2,0},{1,3},{3,1},{4,6},{6,4},{5,7},{7,5},{8,10},{10,8},{9,1... | collective-permute-start | bytes 98312 | tf_op jit(solution)/shard_map/ppermute | solution.py:219
  20.3 6.1 %collective-permute-start.8 = (bf16[128,128]{1,0:T(8,128)(2,1)S(1)}, bf16[128,128]{1,0:T(8,128)(2,1)S(1)}, u32[]{:S(2)}, u32[]{:S(2)}) collective-permute-start(bf16[128,128]{1,0:T(8,128)(2,1)S(1)} %get-tuple-element.20), channel_id=1, source_target_pairs={{0,12},{4,8},{8,4},{12,0},{1,13},{5,9},{9,5},{13,1},{2,14},{6,10},... | collective-permute-start | bytes 98312 | tf_op jit(solution)/shard_map/ppermute | solution.py:181
  23.6 4.0 %collective-permute-start.6 = (bf16[128,128]{1,0:T(8,128)(2,1)S(1)}, bf16[128,128]{1,0:T(8,128)(2,1)S(1)}, u32[]{:S(2)}, u32[]{:S(2)}) collective-permute-start(bf16[128,128]{1,0:T(8,128)(2,1)S(1)} %layers.3), channel_id=1, source_target_pairs={{0,4},{4,0},{8,12},{12,8},{1,5},{5,1},{9,13},{13,9},{2,6},{6,2},{1... | collective-permute-start | bytes 98312 | tf_op jit(solution)/shard_map/ppermute | solution.py:181
  23.9 4.8 %collective-permute-start.7 = (bf16[128,128]{1,0:T(8,128)(2,1)S(1)}, bf16[128,128]{1,0:T(8,128)(2,1)S(1)}, u32[]{:S(2)}, u32[]{:S(2)}) collective-permute-start(bf16[128,128]{1,0:T(8,128)(2,1)S(1)} %get-tuple-element.19.refs_1_), channel_id=1, source_target_pairs={{0,8},{4,12},{8,0},{12,4},{1,9},{5,13},{9,1},{13,5},{2,10},{6,14},... | collective-permute-start | bytes 98312 | tf_op jit(solution)/shard_map/ppermute | solution.py:181

commit v4 on v3

--- a/solution.py
+++ b/solution.py
@@ -34,15 +34,18 @@
     sources, feats, targets, sems = refs[:6], refs[6], refs[7:13], refs[13]
     inputs, grads, proj_in, proj_out, basis_in, basis_out = targets
     rank = basis_in.shape[0]
-    step = inputs.shape[1] // chunks
+    tokens, width = inputs.shape
+    step = width // chunks
+    first = pl.multiple_of(lax.axis_index("sub") * tokens, tokens)
 
     def copy(which, chunk):
         source, target = sources[which], targets[which]
         if which >= 4:
             return pltpu.make_async_copy(source.at[0], target, sems.at[which, 0])
         columns = pl.ds(chunk * step, step)
+        rows = pl.ds(first, tokens) if which < 2 else slice(None)
         return pltpu.make_async_copy(
-            source.at[0, :, columns], target.at[:, columns], sems.at[which, chunk]
+            source.at[0, rows, columns], target.at[:, columns], sems.at[which, chunk]
         )
 
     sides = ((0, 2, 4), (1, 3, 5))
@@ -51,13 +54,13 @@
             copy(side[0], chunk).start()
             copy(side[1], chunk).start()
         copy(side[2], 0).start()
-    for place, (tokens, proj, basis) in enumerate(sides):
+    for place, (rows, proj, basis) in enumerate(sides):
         total = None
         for chunk in range(chunks):
-            copy(tokens, chunk).wait()
+            copy(rows, chunk).wait()
             copy(proj, chunk).wait()
             columns = slice(chunk * step, (chunk + 1) * step)
-            term = nt(targets[proj][:, columns], targets[tokens][:, columns])
+            term = nt(targets[proj][:, columns], targets[rows][:, columns])
             total = term if total is None else total + term
         copy(basis, 0).wait()
         turned = jnp.dot(
@@ -66,6 +69,11 @@
             preferred_element_type=F32,
         )
         feats[place * rank:(place + 1) * rank, :] = turned.astype(BF16)
+
+
+def pack_kernel(*refs):
+    for i, ref in enumerate(refs[:-2]):
+        refs[-1][i] = ref[...]
 
 
 def score_block(feats, weights, rank):
@@ -110,16 +118,16 @@
         weights[:, part * width:(part + 1) * width] = (turned * scale).astype(BF16)
 
 
-def scores_kernel(layer_size, rank, groups, weights, *refs):
-    feats = refs[:groups]
+def scores_kernel(layer_size, rank, offsets, weights, mine, theirs, *refs):
     own, away, scores = refs[-layer_size - 1], refs[-layer_size:-1], refs[-1]
-    layer = lax.axis_index("layer")
-    rows = own.shape[1]
-    for i, feat in enumerate(feats):
-        scores[...] = score_block(feat[...], weights, rank)
+    layer, core = lax.axis_index("layer"), lax.axis_index("sub")
+    rows, half = own.shape[1], mine.shape[2]
+    for i, offset in enumerate(offsets):
+        feats = jnp.concatenate([mine[offset], theirs[offset]], axis=1)
+        scores[...] = score_block(feats, weights, rank)
         for k, block in enumerate((own, *away)):
-            first = pl.multiple_of(lax.rem(layer + k, layer_size) * rows, rows)
-            block[i] = scores[pl.ds(first, rows), :].astype(block.dtype)
+            first = lax.rem(lax.rem(layer + k, layer_size) * rows + core * half, 2 * half)
+            block[i] = scores[pl.ds(pl.multiple_of(first, rows), rows), :].astype(block.dtype)
 
 
 def layers_kernel(layer_size, groups, own, *refs):
@@ -128,19 +136,14 @@
         total = own[i]
         for other in others:
             total = total + other[i].astype(F32)
-        out[...] = total.astype(BF16)
-
-
-def place_kernel(train_size, layer_size, own, *refs):
-    others, arrived, out = refs[:layer_size - 1], refs[layer_size - 1:-1], refs[-1]
+        out[...] = total.astype(out.dtype)
+
+
+def place_kernel(train_size, *refs):
+    arrived, out = refs[:-1], refs[-1]
     here = lax.axis_index("train")
-    rows = own.shape[1]
-    total = own[0]
-    for other in others:
-        total = total + other[0].astype(F32)
-    out[pl.ds(here, rows, stride=train_size), :] = total
-    for offset, block in enumerate(arrived, 1):
-        out[pl.ds(here ^ offset, rows, stride=train_size), :] = block[...].astype(F32)
+    for offset, block in enumerate(arrived):
+        out[pl.ds(here ^ offset, block.shape[0], stride=train_size), :] = block[...].astype(F32)
 
 
 def body(inputs, out_grads, proj_in, proj_out, basis_in, basis_out, eigen, queries):
@@ -148,6 +151,7 @@
     tokens, width = inputs.shape[1:]
     count, entries = queries.shape[1:]
     rank = proj_in.shape[1]
+    half = tokens // 2
     chunks = 4
     vmem, hbm = pl.BlockSpec(memory_space=pltpu.VMEM), pl.BlockSpec(memory_space=pltpu.HBM)
     anywhere = pl.BlockSpec(memory_space=pl.ANY)
@@ -155,12 +159,12 @@
 
     feats = pl.pallas_call(
         functools.partial(features_kernel, chunks),
-        out_shape=jax.ShapeDtypeStruct((2 * rank, tokens), BF16),
+        out_shape=jax.ShapeDtypeStruct((2 * rank, half), BF16),
         in_specs=[hbm] * 6,
         out_specs=vmem,
         scratch_shapes=[
-            pltpu.VMEM((tokens, width), BF16),
-            pltpu.VMEM((tokens, width), BF16),
+            pltpu.VMEM((half, width), BF16),
+            pltpu.VMEM((half, width), BF16),
             pltpu.VMEM((rank, width), BF16),
             pltpu.VMEM((rank, width), BF16),
             pltpu.VMEM((rank, rank), F32),
@@ -169,7 +173,7 @@
         ],
         compiler_params=params,
         cost_estimate=pl.CostEstimate(
-            flops=4 * tokens * rank * width, bytes_accessed=4 * width * (tokens + rank), transcendentals=0
+            flops=4 * half * rank * width, bytes_accessed=4 * width * (half + rank), transcendentals=0
         ),
         name="features",
     )(*[
@@ -195,16 +199,26 @@
         name="queries",
     )(queries[0], basis_in[0], basis_out[0], eigen[0])
 
+    mine = pl.pallas_call(
+        pack_kernel,
+        out_shape=jax.ShapeDtypeStruct((train_size, 2 * rank, half), BF16),
+        in_specs=[vmem] * train_size + [anywhere],
+        out_specs=vmem,
+        compiler_params=params,
+        name="pack",
+    )(*gathered, weights)
+    theirs = lax.ppermute(mine, "sub", [(0, 1), (1, 0)])
+
     rows = tokens // layer_size
 
     def scored(offsets, after):
         own, *away = pl.pallas_call(
-            functools.partial(scores_kernel, layer_size, rank, len(offsets)),
+            functools.partial(scores_kernel, layer_size, rank, offsets),
             out_shape=[
                 jax.ShapeDtypeStruct((len(offsets), rows, count), BF16 if k else F32)
                 for k in range(layer_size)
             ],
-            in_specs=[vmem] * (len(offsets) + 1) + [anywhere] * len(after),
+            in_specs=[vmem] * 3 + [anywhere] * len(after),
             out_specs=[vmem] * layer_size,
             scratch_shapes=[pltpu.VMEM((tokens, count), F32)],
             compiler_params=params,
@@ -214,40 +228,41 @@
                 transcendentals=0,
             ),
             name="scores",
-        )(weights, *[gathered[offset] for offset in offsets], *after)
+        )(weights, mine, theirs, *after)
         return own, [
             lax.ppermute(block, "layer", [(l, (l + k) % layer_size) for l in range(layer_size)])
             for k, block in enumerate(away, 1)
         ]
 
-    half = train_size // 2
-    far, near = range(train_size - 1, half - 1, -1), range(half - 1, 0, -1)
-    own, others = scored([0], [])
-    far_terms = scored(far, [own])
-    near_terms = scored(near, [far_terms[0]])
-    arrived = [None] * train_size
-    after = []
-    for offsets, (mine, theirs) in ((far, far_terms), (near, near_terms)):
-        summed = pl.pallas_call(
+    def summed(offsets, own, others, after):
+        return pl.pallas_call(
             functools.partial(layers_kernel, layer_size, len(offsets)),
-            out_shape=[jax.ShapeDtypeStruct((rows, count), BF16)] * len(offsets),
+            out_shape=[jax.ShapeDtypeStruct((rows, count), BF16 if offset else F32) for offset in offsets],
             in_specs=[vmem] * layer_size + [anywhere] * len(after),
             out_specs=[vmem] * len(offsets),
             compiler_params=params,
             name="layers",
-        )(mine, *theirs, *after)
-        after = summed[-1:]
-        for offset, block in zip(offsets, summed):
-            arrived[offset] = exchange(block, offset)
+        )(own, *others, *after)
+
+    far = tuple(range(train_size - 1, train_size // 2 - 1, -1))
+    near = tuple(range(train_size // 2 - 1, -1, -1))
+    far_terms = scored(far, [])
+    near_terms = scored(near, far_terms[:1])
+    far_sums = summed(far, *far_terms, [])
+    near_sums = summed(near, *near_terms, far_sums[:1])
+    arrived = {
+        offset: exchange(block, offset) if offset else block
+        for offset, block in (*zip(far, far_sums), *zip(near, near_sums))
+    }
 
     total = pl.pallas_call(
-        functools.partial(place_kernel, train_size, layer_size),
+        functools.partial(place_kernel, train_size),
         out_shape=jax.ShapeDtypeStruct((rows * train_size, count), F32),
-        in_specs=[vmem] * (layer_size + train_size - 1),
+        in_specs=[vmem] * train_size,
         out_specs=vmem,
         compiler_params=params,
         name="place",
-    )(own, *others, *arrived[1:])
+    )(*[arrived[offset] for offset in range(train_size)])
     return total.reshape(rows, train_size, 1, count)
 
 

time: 29.6 us -> 31.4 us (1.061)
  waiting for transfers between devices: 5.55 us -> 10.7 us
  starting transfers between devices: 14.4 us -> 12.4 us
  Pallas kernels: 9.48 us -> 7.98 us
    ppermute x3 -> x2, waiting for transfers between devices: 0.14 us -> 3.71 us  [scored(): lax.ppermute(block, 'layer', [(l, (l + k) % layer_size) for l in range(la...]
    ppermute x3 -> x2, starting transfers between devices: 3.66 us -> 2.16 us  [scored(): lax.ppermute(block, 'layer', [(l, (l + k) % layer_size) for l in range(la...]
    ppermute x0 -> x1, waiting for transfers between devices: none -> 1.33 us  [body(): theirs = lax.ppermute(mine, 'sub', [(0, 1), (1, 0)])]
    pallas_call x1, Pallas kernels: 4.67 us -> 3.45 us  [body(): pl.pallas_call(functools.partial(features_kernel, chunks), out_shape=jax....]
    ppermute x6, starting transfers between devices: 10.7 us -> 10.2 us  [exchange(): lax.ppermute(value, 'train', [(j, j ^ offset) for j in range(train_size)])]
  transfers between devices with their start and end apart: 9 -> 9, of which waited for: 5 -> 6; matrix products, arithmetic and copies ran while one was open for 0% -> 0% of each run, Pallas kernels for 14% -> 9%
where the time goes in v4:
time: 31.4 us; the launch traced here: 31.2 us
  starting transfers between devices  12.4 us (39%)
  waiting for transfers between devices  10.7 us (34%)
  Pallas kernels  7.98 us (25%)
    ppermute x6, starting transfers between devices, exchange(): lax.ppermute(value, 'train', [(j, j ^ offset) for j in range(train_size)])  10.2 us
    ppermute x6, waiting for transfers between devices, exchange(): lax.ppermute(value, 'train', [(j, j ^ offset) for j in range(train_size)])  5.66 us
    ppermute x2, waiting for transfers between devices, scored(): lax.ppermute(block, 'layer', [(l, (l + k) % layer_size) for l in range(la...  3.71 us
    pallas_call x1, Pallas kernels, body(): pl.pallas_call(functools.partial(features_kernel, chunks), out_shape=jax....  3.45 us
    ppermute x2, starting transfers between devices, scored(): lax.ppermute(block, 'layer', [(l, (l + k) % layer_size) for l in range(la...  2.16 us
    pallas_call x1, Pallas kernels, body(): pl.pallas_call(queries_kernel, out_shape=jax.ShapeDtypeStruct((count, ent...  2.11 us
    pallas_call x2, Pallas kernels, scored(): pl.pallas_call(functools.partial(scores_kernel, layer_size, rank, offsets...  1.65 us
    ppermute x1, waiting for transfers between devices, body(): theirs = lax.ppermute(mine, 'sub', [(0, 1), (1, 0)])  1.33 us
  transfers between devices with their start and end apart: 9, of which 6 were waited for; matrix products, arithmetic and copies ran while one was open for 0% of the time, Pallas kernels for 9%

profile of v4, /device:TPU:0, one launch (start us, length us, event | category | flops | bytes accessed | tf_op | source)
XLA Modules:
  0.0 31.2 jit_solution(17629895736558881520)
XLA Ops:
  0.0 0.0 copy-start.2
  0.0 0.0 copy-start.1
  0.0 0.0 copy-start
  0.0 0.0 copy-start.3
  0.0 3.4 %features.1.refs_0_ = bf16[128,128]{1,0:T(8,128)(2,1)S(1)} custom-call(bf16[1,256,4096]{2,1,0:T(8,128)(2,1)} %refs_0_.1, bf16[1,256,4096]{2,1,0:T(8,128)(2,1)} %refs_1_.1, bf16[1,64,4096]{2,1,0:T(8,128)(2,1)} %refs_2_.1, bf16[1,64,4096]{2,1,0:T(8,128)(2,1)} %refs_3_.1, f32[1,64,64]{2,1,0:T(8,128)} %refs_4_.1, f32[1,64,64]{2,1,0:T(8,128)} %refs_5_.1), custom_call_target="tpu_custom_call" | custom-call | flops 134217728 | bytes 3145728 | tf_op jit(solution)/shard_map/features/pallas_call | solution.py:160
  3.5 5.1 %collective-permute-start.2 = (bf16[128,128]{1,0:T(8,128)(2,1)S(1)}, bf16[128,128]{1,0:T(8,128)(2,1)S(1)}, u32[]{:S(2)}, u32[]{:S(2)}) collective-permute-start(bf16[128,128]{1,0:T(8,128)(2,1)S(1)} %features.1.refs_0_), channel_id=1, source_target_pairs={{0,12},{4,8},{8,4},{12,0},{1,13},{5,9},{9,5},{13,1},{2,14},{6,10},... | collective-permute-start | bytes 98312 | tf_op jit(solution)/shard_map/ppermute | solution.py:185
  8.6 0.0 collective-permute-start.1
  8.6 0.6 %collective-permute-start = (bf16[128,128]{1,0:T(8,128)(2,1)S(1)}, bf16[128,128]{1,0:T(8,128)(2,1)S(1)}, u32[]{:S(2)}, u32[]{:S(2)}) collective-permute-start(bf16[128,128]{1,0:T(8,128)(2,1)S(1)} %features.1.refs_0_), channel_id=1, source_target_pairs={{0,4},{4,0},{8,12},{12,8},{1,5},{5,1},{9,13},{13,9},{2,6},{6,2},{1... | collective-permute-start | bytes 98312 | tf_op jit(solution)/shard_map/ppermute | solution.py:185
  9.2 0.0 copy-done.2
  9.2 0.0 copy-done.1
  9.2 0.0 copy-done
  9.2 0.0 copy-done.3
  9.2 2.1 %queries.1.refs_4_.weights = bf16[128,4096]{1,0:T(8,128)(2,1)S(1)} custom-call(bf16[128,4096]{1,0:T(8,128)(2,1)S(1)} %bitcast.7, f32[64,64]{1,0:T(8,128)S(1)} %bitcast.8, f32[64,64]{1,0:T(8,128)S(1)} %bitcast.9, f32[64,64]{1,0:T(8,128)S(1)} %bitcast.10), custom_call_target="tpu_custom_call" | custom-call | flops 536870912 | bytes 2097152 | tf_op jit(solution)/shard_map/queries/pallas_call | solution.py:189
  11.4 0.0 collective-permute-done.2.refs_3_
  11.4 2.0 %collective-permute-done.1.refs_2_ = bf16[128,128]{1,0:T(8,128)(2,1)S(1)} collective-permute-done((bf16[128,128]{1,0:T(8,128)(2,1)S(1)}, bf16[128,128]{1,0:T(8,128)(2,1)S(1)}, u32[]{:S(2)}, u32[]{:S(2)}) %collective-permute-start.1) | collective-permute-done | bytes 32800 | tf_op jit(solution)/shard_map/ppermute | solution.py:185
  13.4 0.0 collective-permute-done.refs_1_
  13.4 0.1 collective-permute-start.3
  13.5 1.3 %collective-permute-done.3.theirs = bf16[4,128,128]{2,1,0:T(8,128)(2,1)S(1)} collective-permute-done((bf16[4,128,128]{2,1,0:T(8,128)(2,1)S(1)}, bf16[4,128,128]{2,1,0:T(8,128)(2,1)S(1)}, u32[]{:S(2)}, u32[]{:S(2)}) %collective-permute-start.3) | collective-permute-done | bytes 131104 | tf_op jit(solution)/shard_map/ppermute | solution.py:210
  14.8 0.8 %scores.2 = (f32[2,128,128]{2,1,0:T(8,128)S(1)}, bf16[2,128,128]{2,1,0:T(8,128)(2,1)S(1)}) custom-call(bf16[128,4096]{1,0:T(8,128)(2,1)S(1)} %queries.1.refs_4_.weights, bf16[4,128,128]{2,1,0:T(8,128)(2,1)S(1)} %pack.1.mine, bf16[4,128,128]{2,1,0:T(8,128)(2,1)S(1)} %collective-permute-done.3.theirs), custom_call_target="tpu_custom_call" | custom-call | flops 536870912 | bytes 1048576 | tf_op jit(solution)/shard_map/scores/pallas_call | solution.py:215
  15.7 1.6 %collective-permute-start.5 = (bf16[2,128,128]{2,1,0:T(8,128)(2,1)S(1)}, bf16[2,128,128]{2,1,0:T(8,128)(2,1)S(1)}, u32[]{:S(2)}, u32[]{:S(2)}) collective-permute-start(bf16[2,128,128]{2,1,0:T(8,128)(2,1)S(1)} %get-tuple-element.16), channel_id=1, source_target_pairs={{0,2},{2,0},{1,3},{3,1},{4,6},{6,4},{5,7},{7,5},{8,10},{10,8},{9,1... | collective-permute-start | bytes 196616 | tf_op jit(solution)/shard_map/ppermute | solution.py:233
  17.2 0.8 %scores.3 = (f32[2,128,128]{2,1,0:T(8,128)S(1)}, bf16[2,128,128]{2,1,0:T(8,128)(2,1)S(1)}) custom-call(bf16[128,4096]{1,0:T(8,128)(2,1)S(1)} %queries.1.refs_4_.weights, bf16[4,128,128]{2,1,0:T(8,128)(2,1)S(1)} %pack.1.mine, bf16[4,128,128]{2,1,0:T(8,128)(2,1)S(1)} %collective-permute-done.3.theirs, f32[2,128,128]{2,1,0:T(8,128)S(1)} %get-tuple-element.13.refs_0_.own), custom_call_target="tpu_custom_call" | custom-call | flops 536870912 | bytes 1048576 | tf_op jit(solution)/shard_map/scores/pallas_call | solution.py:215
  18.1 0.6 %collective-permute-start.4 = (bf16[2,128,128]{2,1,0:T(8,128)(2,1)S(1)}, bf16[2,128,128]{2,1,0:T(8,128)(2,1)S(1)}, u32[]{:S(2)}, u32[]{:S(2)}) collective-permute-start(bf16[2,128,128]{2,1,0:T(8,128)(2,1)S(1)} %get-tuple-element.15), channel_id=1, source_target_pairs={{0,2},{2,0},{1,3},{3,1},{4,6},{6,4},{5,7},{7,5},{8,10},{10,8},{9,1... | collective-permute-start | bytes 196616 | tf_op jit(solution)/shard_map/ppermute | solution.py:233
  18.7 1.3 %collective-permute-done.5.refs_0_ = bf16[2,128,128]{2,1,0:T(8,128)(2,1)S(1)} collective-permute-done((bf16[2,128,128]{2,1,0:T(8,128)(2,1)S(1)}, bf16[2,128,128]{2,1,0:T(8,128)(2,1)S(1)}, u32[]{:S(2)}, u32[]{:S(2)}) %collective-permute-start.5) | collective-permute-done | bytes 65568 | tf_op jit(solution)/shard_map/ppermute | solution.py:233
  20.0 2.4 %collective-permute-done.4.refs_0_ = bf16[2,128,128]{2,1,0:T(8,128)(2,1)S(1)} collective-permute-done((bf16[2,128,128]{2,1,0:T(8,128)(2,1)S(1)}, bf16[2,128,128]{2,1,0:T(8,128)(2,1)S(1)}, u32[]{:S(2)}, u32[]{:S(2)}) %collective-permute-start.4) | collective-permute-done | bytes 65568 | tf_op jit(solution)/shard_map/ppermute | solution.py:233
  22.4 0.1 collective-permute-start.6
  22.5 2.3 %collective-permute-start.7 = (bf16[128,128]{1,0:T(8,128)(2,1)S(1)}, bf16[128,128]{1,0:T(8,128)(2,1)S(1)}, u32[]{:S(2)}, u32[]{:S(2)}) collective-permute-start(bf16[128,128]{1,0:T(8,128)(2,1)S(1)} %get-tuple-element.20), channel_id=1, source_target_pairs={{0,8},{4,12},{8,0},{12,4},{1,9},{5,13},{9,1},{13,5},{2,10},{6,14},... | collective-permute-start | bytes 98312 | tf_op jit(solution)/shard_map/ppermute | solution.py:185
  24.8 2.1 %collective-permute-start.8 = (bf16[128,128]{1,0:T(8,128)(2,1)S(1)}, bf16[128,128]{1,0:T(8,128)(2,1)S(1)}, u32[]{:S(2)}, u32[]{:S(2)}) collective-permute-start(bf16[128,128]{1,0:T(8,128)(2,1)S(1)} %get-tuple-element.17.refs_1_), channel_id=1, source_target_pairs={{0,12},{4,8},{8,4},{12,0},{1,13},{5,9},{9,5},{13,1},{2,14},{6,10},... | collective-permute-start | bytes 98312 | tf_op jit(solution)/shard_map/ppermute | solution.py:185
  26.9 0.0 collective-permute-done.6.refs_1_
  26.9 0.6 %collective-permute-done.7.refs_2_ = bf16[128,128]{1,0:T(8,128)(2,1)S(1)} collective-permute-done((bf16[128,128]{1,0:T(8,128)(2,1)S(1)}, bf16[128,128]{1,0:T(8,128)(2,1)S(1)}, u32[]{:S(2)}, u32[]{:S(2)}) %collective-permute-start.7) | collective-permute-done | bytes 32800 | tf_op jit(solution)/shard_map/ppermute | solution.py:185
  27.4 3.1 %collective-permute-done.8.refs_3_ = bf16[128,128]{1,0:T(8,128)(2,1)S(1)} collective-permute-done((bf16[128,128]{1,0:T(8,128)(2,1)S(1)}, bf16[128,128]{1,0:T(8,128)(2,1)S(1)}, u32[]{:S(2)}, u32[]{:S(2)}) %collective-permute-start.8) | collective-permute-done | bytes 32800 | tf_op jit(solution)/shard_map/ppermute | solution.py:185
  30.5 0.7 %place.1 = f32[512,128]{1,0:T(8,128)} custom-call(f32[128,128]{1,0:T(8,128)S(1)} %get-tuple-element.18.refs_0_, bf16[128,128]{1,0:T(8,128)(2,1)S(1)} %collective-permute-done.6.refs_1_, bf16[128,128]{1,0:T(8,128)(2,1)S(1)} %collective-permute-done.7.refs_2_, bf16[128,128]{1,0:T(8,128)(2,1)S(1)} %collective-permute-done.8.refs_3_), custom_call_target="tpu_custom_call" | custom-call | tf_op jit(solution)/shard_map/place/pallas_call | solution.py:258
  (3 shorter events, 0.0 us)
Async XLA Ops:
  0.0 9.2 %copy-start.2 = (f32[1,64,64]{2,1,0:T(8,128)S(1)}, f32[1,64,64]{2,1,0:T(8,128)}, u32[]{:S(2)}) copy-start(f32[1,64,64]{2,1,0:T(8,128)} %refs_5_.1) | copy-start | bytes 49156
  0.0 9.2 %copy-start.1 = (f32[1,64,64]{2,1,0:T(8,128)S(1)}, f32[1,64,64]{2,1,0:T(8,128)}, u32[]{:S(2)}) copy-start(f32[1,64,64]{2,1,0:T(8,128)} %refs_4_.1) | copy-start | bytes 49156
  0.0 9.2 %copy-start = (bf16[1,128,4096]{2,1,0:T(8,128)(2,1)S(1)}, bf16[1,128,4096]{2,1,0:T(8,128)(2,1)}, u32[]{:S(2)}) copy-start(bf16[1,128,4096]{2,1,0:T(8,128)(2,1)} %param.15) | copy-start | bytes 3145732
  0.0 9.2 %copy-start.3 = (f32[1,64,64]{2,1,0:T(8,128)S(1)}, f32[1,64,64]{2,1,0:T(8,128)}, u32[]{:S(2)}) copy-start(f32[1,64,64]{2,1,0:T(8,128)} %param.14) | copy-start | bytes 49156
  3.5 7.9 %collective-permute-start.2 = (bf16[128,128]{1,0:T(8,128)(2,1)S(1)}, bf16[128,128]{1,0:T(8,128)(2,1)S(1)}, u32[]{:S(2)}, u32[]{:S(2)}) collective-permute-start(bf16[128,128]{1,0:T(8,128)(2,1)S(1)} %features.1.refs_0_), channel_id=1, source_target_pairs={{0,12},{4,8},{8,4},{12,0},{1,13},{5,9},{9,5},{13,1},{2,14},{6,10},... | collective-permute-start | bytes 98312 | tf_op jit(solution)/shard_map/ppermute | solution.py:185
  8.6 4.8 %collective-permute-start.1 = (bf16[128,128]{1,0:T(8,128)(2,1)S(1)}, bf16[128,128]{1,0:T(8,128)(2,1)S(1)}, u32[]{:S(2)}, u32[]{:S(2)}) collective-permute-start(bf16[128,128]{1,0:T(8,128)(2,1)S(1)} %features.1.refs_0_), channel_id=1, source_target_pairs={{0,8},{4,12},{8,0},{12,4},{1,9},{5,13},{9,1},{13,5},{2,10},{6,14},... | collective-permute-start | bytes 98312 | tf_op jit(solution)/shard_map/ppermute | solution.py:185
  8.6 4.8 %collective-permute-start = (bf16[128,128]{1,0:T(8,128)(2,1)S(1)}, bf16[128,128]{1,0:T(8,128)(2,1)S(1)}, u32[]{:S(2)}, u32[]{:S(2)}) collective-permute-start(bf16[128,128]{1,0:T(8,128)(2,1)S(1)} %features.1.refs_0_), channel_id=1, source_target_pairs={{0,4},{4,0},{8,12},{12,8},{1,5},{5,1},{9,13},{13,9},{2,6},{6,2},{1... | collective-permute-start | bytes 98312 | tf_op jit(solution)/shard_map/ppermute | solution.py:185
  13.4 1.4 %collective-permute-start.3 = (bf16[4,128,128]{2,1,0:T(8,128)(2,1)S(1)}, bf16[4,128,128]{2,1,0:T(8,128)(2,1)S(1)}, u32[]{:S(2)}, u32[]{:S(2)}) collective-permute-start(bf16[4,128,128]{2,1,0:T(8,128)(2,1)S(1)} %pack.1.mine), channel_id=1, source_target_pairs={{0,1},{1,0},{2,3},{3,2},{4,5},{5,4},{6,7},{7,6},{8,9},{9,8},{10,11... | collective-permute-start | bytes 393224 | tf_op jit(solution)/shard_map/ppermute | solution.py:210
  15.7 4.3 %collective-permute-start.5 = (bf16[2,128,128]{2,1,0:T(8,128)(2,1)S(1)}, bf16[2,128,128]{2,1,0:T(8,128)(2,1)S(1)}, u32[]{:S(2)}, u32[]{:S(2)}) collective-permute-start(bf16[2,128,128]{2,1,0:T(8,128)(2,1)S(1)} %get-tuple-element.16), channel_id=1, source_target_pairs={{0,2},{2,0},{1,3},{3,1},{4,6},{6,4},{5,7},{7,5},{8,10},{10,8},{9,1... | collective-permute-start | bytes 196616 | tf_op jit(solution)/shard_map/ppermute | solution.py:233
  18.1 4.3 %collective-permute-start.4 = (bf16[2,128,128]{2,1,0:T(8,128)(2,1)S(1)}, bf16[2,128,128]{2,1,0:T(8,128)(2,1)S(1)}, u32[]{:S(2)}, u32[]{:S(2)}) collective-permute-start(bf16[2,128,128]{2,1,0:T(8,128)(2,1)S(1)} %get-tuple-element.15), channel_id=1, source_target_pairs={{0,2},{2,0},{1,3},{3,1},{4,6},{6,4},{5,7},{7,5},{8,10},{10,8},{9,1... | collective-permute-start | bytes 196616 | tf_op jit(solution)/shard_map/ppermute | solution.py:233
  22.4 4.5 %collective-permute-start.6 = (bf16[128,128]{1,0:T(8,128)(2,1)S(1)}, bf16[128,128]{1,0:T(8,128)(2,1)S(1)}, u32[]{:S(2)}, u32[]{:S(2)}) collective-permute-start(bf16[128,128]{1,0:T(8,128)(2,1)S(1)} %get-tuple-element.19), channel_id=1, source_target_pairs={{0,4},{4,0},{8,12},{12,8},{1,5},{5,1},{9,13},{13,9},{2,6},{6,2},{1... | collective-permute-start | bytes 98312 | tf_op jit(solution)/shard_map/ppermute | solution.py:185
  22.5 4.9 %collective-permute-start.7 = (bf16[128,128]{1,0:T(8,128)(2,1)S(1)}, bf16[128,128]{1,0:T(8,128)(2,1)S(1)}, u32[]{:S(2)}, u32[]{:S(2)}) collective-permute-start(bf16[128,128]{1,0:T(8,128)(2,1)S(1)} %get-tuple-element.20), channel_id=1, source_target_pairs={{0,8},{4,12},{8,0},{12,4},{1,9},{5,13},{9,1},{13,5},{2,10},{6,14},... | collective-permute-start | bytes 98312 | tf_op jit(solution)/shard_map/ppermute | solution.py:185
  24.8 5.7 %collective-permute-start.8 = (bf16[128,128]{1,0:T(8,128)(2,1)S(1)}, bf16[128,128]{1,0:T(8,128)(2,1)S(1)}, u32[]{:S(2)}, u32[]{:S(2)}) collective-permute-start(bf16[128,128]{1,0:T(8,128)(2,1)S(1)} %get-tuple-element.17.refs_1_), channel_id=1, source_target_pairs={{0,12},{4,8},{8,4},{12,0},{1,13},{5,9},{9,5},{13,1},{2,14},{6,10},... | collective-permute-start | bytes 98312 | tf_op jit(solution)/shard_map/ppermute | solution.py:185

commit v5 on v4

--- a/solution.py
+++ b/solution.py
@@ -32,37 +32,35 @@
 
 def features_kernel(chunks, *refs):
     sources, feats, targets, sems = refs[:6], refs[6], refs[7:13], refs[13]
-    inputs, grads, proj_in, proj_out, basis_in, basis_out = targets
-    rank = basis_in.shape[0]
-    tokens, width = inputs.shape
+    tokens, width = targets[0].shape
+    rank = targets[2].shape[0]
     step = width // chunks
     first = pl.multiple_of(lax.axis_index("sub") * tokens, tokens)
 
-    def copy(which, chunk):
-        source, target = sources[which], targets[which]
-        if which >= 4:
-            return pltpu.make_async_copy(source.at[0], target, sems.at[which, 0])
+    def copy(which, chunk=None):
+        source, target = sources[which].at[0], targets[which]
+        if chunk is None:
+            return pltpu.make_async_copy(source, target, sems.at[which, 0])
         columns = pl.ds(chunk * step, step)
-        rows = pl.ds(first, tokens) if which < 2 else slice(None)
         return pltpu.make_async_copy(
-            source.at[0, rows, columns], target.at[:, columns], sems.at[which, chunk]
+            source.at[pl.ds(first, tokens), columns], target.at[:, columns], sems.at[which, chunk]
         )
 
     sides = ((0, 2, 4), (1, 3, 5))
-    for side in sides:
+    for rows, proj, basis in sides:
+        copy(proj).start()
         for chunk in range(chunks):
-            copy(side[0], chunk).start()
-            copy(side[1], chunk).start()
-        copy(side[2], 0).start()
+            copy(rows, chunk).start()
+        copy(basis).start()
     for place, (rows, proj, basis) in enumerate(sides):
+        copy(proj).wait()
         total = None
         for chunk in range(chunks):
             copy(rows, chunk).wait()
-            copy(proj, chunk).wait()
             columns = slice(chunk * step, (chunk + 1) * step)
             term = nt(targets[proj][:, columns], targets[rows][:, columns])
             total = term if total is None else total + term
-        copy(basis, 0).wait()
+        copy(basis).wait()
         turned = jnp.dot(
             two_terms(targets[basis][...].T),
             jnp.concatenate([total.astype(BF16)] * 2, axis=0),
@@ -71,9 +69,9 @@
         feats[place * rank:(place + 1) * rank, :] = turned.astype(BF16)
 
 
-def pack_kernel(*refs):
-    for i, ref in enumerate(refs[:-2]):
-        refs[-1][i] = ref[...]
+def pack_kernel(order, *refs):
+    for offset, ref in zip(order, refs):
+        refs[-1][offset] = ref[...]
 
 
 def score_block(feats, weights, rank):
@@ -130,19 +128,17 @@
             block[i] = scores[pl.ds(pl.multiple_of(first, rows), rows), :].astype(block.dtype)
 
 
-def layers_kernel(layer_size, groups, own, *refs):
-    others, outs = refs[:layer_size - 1], refs[-groups:]
-    for i, out in enumerate(outs):
-        total = own[i]
-        for other in others:
-            total = total + other[i].astype(F32)
-        out[...] = total.astype(out.dtype)
+def layers_kernel(layer_size, which, own, *refs):
+    total = own[which]
+    for other in refs[:layer_size - 1]:
+        total = total + other[which].astype(F32)
+    refs[-1][...] = total.astype(refs[-1].dtype)
 
 
 def place_kernel(train_size, *refs):
     arrived, out = refs[:-1], refs[-1]
     here = lax.axis_index("train")
-    for offset, block in enumerate(arrived):
+    for offset, block in enumerate(reversed(arrived)):
         out[pl.ds(here ^ offset, block.shape[0], stride=train_size), :] = block[...].astype(F32)
 
 
@@ -152,7 +148,7 @@
     count, entries = queries.shape[1:]
     rank = proj_in.shape[1]
     half = tokens // 2
-    chunks = 4
+    chunks = 2
     vmem, hbm = pl.BlockSpec(memory_space=pltpu.VMEM), pl.BlockSpec(memory_space=pltpu.HBM)
     anywhere = pl.BlockSpec(memory_space=pl.ANY)
     params = pltpu.CompilerParams(vmem_limit_bytes=32 << 20)
@@ -184,7 +180,9 @@
     def exchange(value, offset):
         return lax.ppermute(value, "train", [(j, j ^ offset) for j in range(train_size)])
 
-    gathered = [feats] + [exchange(feats, offset) for offset in range(1, train_size)]
+    middle = train_size // 2
+    order = (0, *range(1, middle), *range(train_size - 1, middle - 1, -1))
+    gathered = [exchange(feats, offset) if offset else feats for offset in order]
 
     weights = pl.pallas_call(
         queries_kernel,
@@ -200,7 +198,7 @@
     )(queries[0], basis_in[0], basis_out[0], eigen[0])
 
     mine = pl.pallas_call(
-        pack_kernel,
+        functools.partial(pack_kernel, order),
         out_shape=jax.ShapeDtypeStruct((train_size, 2 * rank, half), BF16),
         in_specs=[vmem] * train_size + [anywhere],
         out_specs=vmem,
@@ -234,26 +232,25 @@
             for k, block in enumerate(away, 1)
         ]
 
-    def summed(offsets, own, others, after):
+    def summed(which, offset, own, others, after):
         return pl.pallas_call(
-            functools.partial(layers_kernel, layer_size, len(offsets)),
-            out_shape=[jax.ShapeDtypeStruct((rows, count), BF16 if offset else F32) for offset in offsets],
+            functools.partial(layers_kernel, layer_size, which),
+            out_shape=jax.ShapeDtypeStruct((rows, count), BF16 if offset else F32),
             in_specs=[vmem] * layer_size + [anywhere] * len(after),
-            out_specs=[vmem] * len(offsets),
+            out_specs=vmem,
             compiler_params=params,
             name="layers",
         )(own, *others, *after)
 
-    far = tuple(range(train_size - 1, train_size // 2 - 1, -1))
-    near = tuple(range(train_size // 2 - 1, -1, -1))
+    far, near = tuple(range(train_size - 1, middle - 1, -1)), tuple(range(middle))
     far_terms = scored(far, [])
     near_terms = scored(near, far_terms[:1])
-    far_sums = summed(far, *far_terms, [])
-    near_sums = summed(near, *near_terms, far_sums[:1])
-    arrived = {
-        offset: exchange(block, offset) if offset else block
-        for offset, block in (*zip(far, far_sums), *zip(near, near_sums))
-    }
+    arrived, after = {}, []
+    for offsets, terms in ((far, far_terms), (near, near_terms)):
+        for which, offset in enumerate(offsets):
+            block = summed(which, offset, *terms, after)
+            after = [block]
+            arrived[offset] = exchange(block, offset) if offset else block
 
     total = pl.pallas_call(
         functools.partial(place_kernel, train_size),
@@ -262,7 +259,7 @@
         out_specs=vmem,
         compiler_params=params,
         name="place",
-    )(*[arrived[offset] for offset in range(train_size)])
+    )(*[arrived[offset] for offset in reversed(range(train_size))])
     return total.reshape(rows, train_size, 1, count)
 
 

time: 31.4 us -> 27.8 us (0.89)
  waiting for transfers between devices: 10.7 us -> 7.21 us
    ppermute x2, waiting for transfers between devices: 3.71 us -> 1.54 us  [scored(): lax.ppermute(block, 'layer', [(l, (l + k) % layer_size) for l in range(la...]
    ppermute x6, waiting for transfers between devices: 5.66 us -> 4.34 us  [exchange(): lax.ppermute(value, 'train', [(j, j ^ offset) for j in range(train_size)])]
  transfers between devices with their start and end apart: 9 -> 9, of which waited for: 6 -> 5; matrix products, arithmetic and copies ran while one was open for 0% -> 0% of each run, Pallas kernels for 9% -> 11%
where the time goes in v5:
time: 27.8 us; the launch traced here: 27.7 us
  starting transfers between devices  12.3 us (44%)
  Pallas kernels  8.04 us (29%)
  waiting for transfers between devices  7.21 us (26%)
    ppermute x6, starting transfers between devices, exchange(): lax.ppermute(value, 'train', [(j, j ^ offset) for j in range(train_size)])  10.1 us
    ppermute x6, waiting for transfers between devices, exchange(): lax.ppermute(value, 'train', [(j, j ^ offset) for j in range(train_size)])  4.34 us
    pallas_call x1, Pallas kernels, body(): pl.pallas_call(functools.partial(features_kernel, chunks), out_shape=jax....  3.49 us
    ppermute x2, starting transfers between devices, scored(): lax.ppermute(block, 'layer', [(l, (l + k) % layer_size) for l in range(la...  2.16 us
    pallas_call x1, Pallas kernels, body(): pl.pallas_call(queries_kernel, out_shape=jax.ShapeDtypeStruct((count, ent...  2.12 us
    pallas_call x2, Pallas kernels, scored(): pl.pallas_call(functools.partial(scores_kernel, layer_size, rank, offsets...  1.65 us
    ppermute x2, waiting for transfers between devices, scored(): lax.ppermute(block, 'layer', [(l, (l + k) % layer_size) for l in range(la...  1.54 us
    ppermute x1, waiting for transfers between devices, body(): theirs = lax.ppermute(mine, 'sub', [(0, 1), (1, 0)])  1.33 us
  transfers between devices with their start and end apart: 9, of which 5 were waited for; matrix products, arithmetic and copies ran while one was open for 0% of the time, Pallas kernels for 11%

profile of v5, /device:TPU:0, one launch (start us, length us, event | category | flops | bytes accessed | tf_op | source)
XLA Modules:
  0.0 27.7 jit_solution(14169338522296267132)
XLA Ops:
  0.0 0.0 copy-start.2
  0.0 0.0 copy-start.1
  0.0 0.0 copy-start
  0.0 0.0 copy-start.3
  0.0 3.5 %features.1.refs_0_ = bf16[128,128]{1,0:T(8,128)(2,1)S(1)} custom-call(bf16[1,256,4096]{2,1,0:T(8,128)(2,1)} %refs_0_.1, bf16[1,256,4096]{2,1,0:T(8,128)(2,1)} %refs_1_.1, bf16[1,64,4096]{2,1,0:T(8,128)(2,1)} %refs_2_.1, bf16[1,64,4096]{2,1,0:T(8,128)(2,1)} %refs_3_.1, f32[1,64,64]{2,1,0:T(8,128)} %refs_4_.1, f32[1,64,64]{2,1,0:T(8,128)} %refs_5_.1), custom_call_target="tpu_custom_call" | custom-call | flops 134217728 | bytes 3145728 | tf_op jit(solution)/shard_map/features/pallas_call | solution.py:156
  3.5 4.1 %collective-permute-start.2 = (bf16[128,128]{1,0:T(8,128)(2,1)S(1)}, bf16[128,128]{1,0:T(8,128)(2,1)S(1)}, u32[]{:S(2)}, u32[]{:S(2)}) collective-permute-start(bf16[128,128]{1,0:T(8,128)(2,1)S(1)} %features.1.refs_0_), channel_id=1, source_target_pairs={{0,8},{4,12},{8,0},{12,4},{1,9},{5,13},{9,1},{13,5},{2,10},{6,14},... | collective-permute-start | bytes 98312 | tf_op jit(solution)/shard_map/ppermute | solution.py:181
  7.6 1.3 %collective-permute-start.1 = (bf16[128,128]{1,0:T(8,128)(2,1)S(1)}, bf16[128,128]{1,0:T(8,128)(2,1)S(1)}, u32[]{:S(2)}, u32[]{:S(2)}) collective-permute-start(bf16[128,128]{1,0:T(8,128)(2,1)S(1)} %features.1.refs_0_), channel_id=1, source_target_pairs={{0,12},{4,8},{8,4},{12,0},{1,13},{5,9},{9,5},{13,1},{2,14},{6,10},... | collective-permute-start | bytes 98312 | tf_op jit(solution)/shard_map/ppermute | solution.py:181
  9.0 0.2 collective-permute-start
  9.2 0.0 copy-done.2
  9.2 0.0 copy-done.1
  9.2 0.0 copy-done
  9.2 0.0 copy-done.3
  9.2 2.1 %queries.1.refs_4_.weights = bf16[128,4096]{1,0:T(8,128)(2,1)S(1)} custom-call(bf16[128,4096]{1,0:T(8,128)(2,1)S(1)} %bitcast.7, f32[64,64]{1,0:T(8,128)S(1)} %bitcast.8, f32[64,64]{1,0:T(8,128)S(1)} %bitcast.9, f32[64,64]{1,0:T(8,128)S(1)} %bitcast.10), custom_call_target="tpu_custom_call" | custom-call | flops 536870912 | bytes 2097152 | tf_op jit(solution)/shard_map/queries/pallas_call | solution.py:187
  11.3 0.0 collective-permute-done.2.refs_3_
  11.4 2.0 %collective-permute-done.1.refs_2_ = bf16[128,128]{1,0:T(8,128)(2,1)S(1)} collective-permute-done((bf16[128,128]{1,0:T(8,128)(2,1)S(1)}, bf16[128,128]{1,0:T(8,128)(2,1)S(1)}, u32[]{:S(2)}, u32[]{:S(2)}) %collective-permute-start.1) | collective-permute-done | bytes 32800 | tf_op jit(solution)/shard_map/ppermute | solution.py:181
  13.3 0.0 collective-permute-done.refs_1_
  13.4 0.1 collective-permute-start.3
  13.4 1.3 %collective-permute-done.3.theirs = bf16[4,128,128]{2,1,0:T(8,128)(2,1)S(1)} collective-permute-done((bf16[4,128,128]{2,1,0:T(8,128)(2,1)S(1)}, bf16[4,128,128]{2,1,0:T(8,128)(2,1)S(1)}, u32[]{:S(2)}, u32[]{:S(2)}) %collective-permute-start.3) | collective-permute-done | bytes 131104 | tf_op jit(solution)/shard_map/ppermute | solution.py:208
  14.8 0.8 %scores.2 = (f32[2,128,128]{2,1,0:T(8,128)S(1)}, bf16[2,128,128]{2,1,0:T(8,128)(2,1)S(1)}) custom-call(bf16[128,4096]{1,0:T(8,128)(2,1)S(1)} %queries.1.refs_4_.weights, bf16[4,128,128]{2,1,0:T(8,128)(2,1)S(1)} %pack.1.mine, bf16[4,128,128]{2,1,0:T(8,128)(2,1)S(1)} %collective-permute-done.3.theirs), custom_call_target="tpu_custom_call" | custom-call | flops 536870912 | bytes 1048576 | tf_op jit(solution)/shard_map/scores/pallas_call | solution.py:213
  15.6 1.6 %collective-permute-start.4 = (bf16[2,128,128]{2,1,0:T(8,128)(2,1)S(1)}, bf16[2,128,128]{2,1,0:T(8,128)(2,1)S(1)}, u32[]{:S(2)}, u32[]{:S(2)}) collective-permute-start(bf16[2,128,128]{2,1,0:T(8,128)(2,1)S(1)} %get-tuple-element.10), channel_id=1, source_target_pairs={{0,2},{2,0},{1,3},{3,1},{4,6},{6,4},{5,7},{7,5},{8,10},{10,8},{9,1... | collective-permute-start | bytes 196616 | tf_op jit(solution)/shard_map/ppermute | solution.py:231
  17.2 0.8 %scores.3 = (f32[2,128,128]{2,1,0:T(8,128)S(1)}, bf16[2,128,128]{2,1,0:T(8,128)(2,1)S(1)}) custom-call(bf16[128,4096]{1,0:T(8,128)(2,1)S(1)} %queries.1.refs_4_.weights, bf16[4,128,128]{2,1,0:T(8,128)(2,1)S(1)} %pack.1.mine, bf16[4,128,128]{2,1,0:T(8,128)(2,1)S(1)} %collective-permute-done.3.theirs, f32[2,128,128]{2,1,0:T(8,128)S(1)} %get-tuple-element.9.own.refs_0_), custom_call_target="tpu_custom_call" | custom-call | flops 536870912 | bytes 1048576 | tf_op jit(solution)/shard_map/scores/pallas_call | solution.py:213
  18.0 0.6 %collective-permute-start.7 = (bf16[2,128,128]{2,1,0:T(8,128)(2,1)S(1)}, bf16[2,128,128]{2,1,0:T(8,128)(2,1)S(1)}, u32[]{:S(2)}, u32[]{:S(2)}) collective-permute-start(bf16[2,128,128]{2,1,0:T(8,128)(2,1)S(1)} %get-tuple-element.12), channel_id=1, source_target_pairs={{0,2},{2,0},{1,3},{3,1},{4,6},{6,4},{5,7},{7,5},{8,10},{10,8},{9,1... | collective-permute-start | bytes 196616 | tf_op jit(solution)/shard_map/ppermute | solution.py:231
  18.6 1.3 %collective-permute-done.4.refs_0_ = bf16[2,128,128]{2,1,0:T(8,128)(2,1)S(1)} collective-permute-done((bf16[2,128,128]{2,1,0:T(8,128)(2,1)S(1)}, bf16[2,128,128]{2,1,0:T(8,128)(2,1)S(1)}, u32[]{:S(2)}, u32[]{:S(2)}) %collective-permute-start.4) | collective-permute-done | bytes 65568 | tf_op jit(solution)/shard_map/ppermute | solution.py:231
  19.9 2.1 %collective-permute-start.5 = (bf16[128,128]{1,0:T(8,128)(2,1)S(1)}, bf16[128,128]{1,0:T(8,128)(2,1)S(1)}, u32[]{:S(2)}, u32[]{:S(2)}) collective-permute-start(bf16[128,128]{1,0:T(8,128)(2,1)S(1)} %layers.4.refs_1_), channel_id=1, source_target_pairs={{0,12},{4,8},{8,4},{12,0},{1,13},{5,9},{9,5},{13,1},{2,14},{6,10},... | collective-permute-start | bytes 98312 | tf_op jit(solution)/shard_map/ppermute | solution.py:181
  22.0 0.1 collective-permute-start.6
  22.1 0.2 collective-permute-done.7.refs_0_
  22.4 2.2 %collective-permute-start.8 = (bf16[128,128]{1,0:T(8,128)(2,1)S(1)}, bf16[128,128]{1,0:T(8,128)(2,1)S(1)}, u32[]{:S(2)}, u32[]{:S(2)}) collective-permute-start(bf16[128,128]{1,0:T(8,128)(2,1)S(1)} %layers.7), channel_id=1, source_target_pairs={{0,4},{4,0},{8,12},{12,8},{1,5},{5,1},{9,13},{13,9},{2,6},{6,2},{1... | collective-permute-start | bytes 98312 | tf_op jit(solution)/shard_map/ppermute | solution.py:181
  24.6 2.3 %collective-permute-done.6.refs_1_ = bf16[128,128]{1,0:T(8,128)(2,1)S(1)} collective-permute-done((bf16[128,128]{1,0:T(8,128)(2,1)S(1)}, bf16[128,128]{1,0:T(8,128)(2,1)S(1)}, u32[]{:S(2)}, u32[]{:S(2)}) %collective-permute-start.6) | collective-permute-done | bytes 32800 | tf_op jit(solution)/shard_map/ppermute | solution.py:181
  26.9 0.0 collective-permute-done.5.refs_0_
  26.9 0.0 collective-permute-done.8.refs_2_
  26.9 0.7 %place.1 = f32[512,128]{1,0:T(8,128)} custom-call(bf16[128,128]{1,0:T(8,128)(2,1)S(1)} %collective-permute-done.5.refs_0_, bf16[128,128]{1,0:T(8,128)(2,1)S(1)} %collective-permute-done.6.refs_1_, bf16[128,128]{1,0:T(8,128)(2,1)S(1)} %collective-permute-done.8.refs_2_, f32[128,128]{1,0:T(8,128)S(1)} %layers.6.refs_1_.refs_3_), custom_call_target="tpu_custom_call" | custom-call | tf_op jit(solution)/shard_map/place/pallas_call | solution.py:255
  (5 shorter events, 0.0 us)
Async XLA Ops:
  0.0 9.2 %copy-start.2 = (f32[1,64,64]{2,1,0:T(8,128)S(1)}, f32[1,64,64]{2,1,0:T(8,128)}, u32[]{:S(2)}) copy-start(f32[1,64,64]{2,1,0:T(8,128)} %refs_5_.1) | copy-start | bytes 49156
  0.0 9.2 %copy-start.1 = (f32[1,64,64]{2,1,0:T(8,128)S(1)}, f32[1,64,64]{2,1,0:T(8,128)}, u32[]{:S(2)}) copy-start(f32[1,64,64]{2,1,0:T(8,128)} %refs_4_.1) | copy-start | bytes 49156
  0.0 9.2 %copy-start = (bf16[1,128,4096]{2,1,0:T(8,128)(2,1)S(1)}, bf16[1,128,4096]{2,1,0:T(8,128)(2,1)}, u32[]{:S(2)}) copy-start(bf16[1,128,4096]{2,1,0:T(8,128)(2,1)} %param.15) | copy-start | bytes 3145732
  0.0 9.2 %copy-start.3 = (f32[1,64,64]{2,1,0:T(8,128)S(1)}, f32[1,64,64]{2,1,0:T(8,128)}, u32[]{:S(2)}) copy-start(f32[1,64,64]{2,1,0:T(8,128)} %param.14) | copy-start | bytes 49156
  3.5 7.8 %collective-permute-start.2 = (bf16[128,128]{1,0:T(8,128)(2,1)S(1)}, bf16[128,128]{1,0:T(8,128)(2,1)S(1)}, u32[]{:S(2)}, u32[]{:S(2)}) collective-permute-start(bf16[128,128]{1,0:T(8,128)(2,1)S(1)} %features.1.refs_0_), channel_id=1, source_target_pairs={{0,8},{4,12},{8,0},{12,4},{1,9},{5,13},{9,1},{13,5},{2,10},{6,14},... | collective-permute-start | bytes 98312 | tf_op jit(solution)/shard_map/ppermute | solution.py:181
  7.6 5.7 %collective-permute-start.1 = (bf16[128,128]{1,0:T(8,128)(2,1)S(1)}, bf16[128,128]{1,0:T(8,128)(2,1)S(1)}, u32[]{:S(2)}, u32[]{:S(2)}) collective-permute-start(bf16[128,128]{1,0:T(8,128)(2,1)S(1)} %features.1.refs_0_), channel_id=1, source_target_pairs={{0,12},{4,8},{8,4},{12,0},{1,13},{5,9},{9,5},{13,1},{2,14},{6,10},... | collective-permute-start | bytes 98312 | tf_op jit(solution)/shard_map/ppermute | solution.py:181
  9.0 4.4 %collective-permute-start = (bf16[128,128]{1,0:T(8,128)(2,1)S(1)}, bf16[128,128]{1,0:T(8,128)(2,1)S(1)}, u32[]{:S(2)}, u32[]{:S(2)}) collective-permute-start(bf16[128,128]{1,0:T(8,128)(2,1)S(1)} %features.1.refs_0_), channel_id=1, source_target_pairs={{0,4},{4,0},{8,12},{12,8},{1,5},{5,1},{9,13},{13,9},{2,6},{6,2},{1... | collective-permute-start | bytes 98312 | tf_op jit(solution)/shard_map/ppermute | solution.py:181
  13.4 1.4 %collective-permute-start.3 = (bf16[4,128,128]{2,1,0:T(8,128)(2,1)S(1)}, bf16[4,128,128]{2,1,0:T(8,128)(2,1)S(1)}, u32[]{:S(2)}, u32[]{:S(2)}) collective-permute-start(bf16[4,128,128]{2,1,0:T(8,128)(2,1)S(1)} %pack.1.mine), channel_id=1, source_target_pairs={{0,1},{1,0},{2,3},{3,2},{4,5},{5,4},{6,7},{7,6},{8,9},{9,8},{10,11... | collective-permute-start | bytes 393224 | tf_op jit(solution)/shard_map/ppermute | solution.py:208
  15.6 4.3 %collective-permute-start.4 = (bf16[2,128,128]{2,1,0:T(8,128)(2,1)S(1)}, bf16[2,128,128]{2,1,0:T(8,128)(2,1)S(1)}, u32[]{:S(2)}, u32[]{:S(2)}) collective-permute-start(bf16[2,128,128]{2,1,0:T(8,128)(2,1)S(1)} %get-tuple-element.10), channel_id=1, source_target_pairs={{0,2},{2,0},{1,3},{3,1},{4,6},{6,4},{5,7},{7,5},{8,10},{10,8},{9,1... | collective-permute-start | bytes 196616 | tf_op jit(solution)/shard_map/ppermute | solution.py:231
  18.0 4.3 %collective-permute-start.7 = (bf16[2,128,128]{2,1,0:T(8,128)(2,1)S(1)}, bf16[2,128,128]{2,1,0:T(8,128)(2,1)S(1)}, u32[]{:S(2)}, u32[]{:S(2)}) collective-permute-start(bf16[2,128,128]{2,1,0:T(8,128)(2,1)S(1)} %get-tuple-element.12), channel_id=1, source_target_pairs={{0,2},{2,0},{1,3},{3,1},{4,6},{6,4},{5,7},{7,5},{8,10},{10,8},{9,1... | collective-permute-start | bytes 196616 | tf_op jit(solution)/shard_map/ppermute | solution.py:231
  19.9 7.0 %collective-permute-start.5 = (bf16[128,128]{1,0:T(8,128)(2,1)S(1)}, bf16[128,128]{1,0:T(8,128)(2,1)S(1)}, u32[]{:S(2)}, u32[]{:S(2)}) collective-permute-start(bf16[128,128]{1,0:T(8,128)(2,1)S(1)} %layers.4.refs_1_), channel_id=1, source_target_pairs={{0,12},{4,8},{8,4},{12,0},{1,13},{5,9},{9,5},{13,1},{2,14},{6,10},... | collective-permute-start | bytes 98312 | tf_op jit(solution)/shard_map/ppermute | solution.py:181
  22.0 4.9 %collective-permute-start.6 = (bf16[128,128]{1,0:T(8,128)(2,1)S(1)}, bf16[128,128]{1,0:T(8,128)(2,1)S(1)}, u32[]{:S(2)}, u32[]{:S(2)}) collective-permute-start(bf16[128,128]{1,0:T(8,128)(2,1)S(1)} %layers.5.refs_1_), channel_id=1, source_target_pairs={{0,8},{4,12},{8,0},{12,4},{1,9},{5,13},{9,1},{13,5},{2,10},{6,14},... | collective-permute-start | bytes 98312 | tf_op jit(solution)/shard_map/ppermute | solution.py:181
  22.4 4.6 %collective-permute-start.8 = (bf16[128,128]{1,0:T(8,128)(2,1)S(1)}, bf16[128,128]{1,0:T(8,128)(2,1)S(1)}, u32[]{:S(2)}, u32[]{:S(2)}) collective-permute-start(bf16[128,128]{1,0:T(8,128)(2,1)S(1)} %layers.7), channel_id=1, source_target_pairs={{0,4},{4,0},{8,12},{12,8},{1,5},{5,1},{9,13},{13,9},{2,6},{6,2},{1... | collective-permute-start | bytes 98312 | tf_op jit(solution)/shard_map/ppermute | solution.py:181

commit v6 on v5

--- a/solution.py
+++ b/solution.py
@@ -31,7 +31,9 @@
 
 
 def features_kernel(chunks, *refs):
-    sources, feats, targets, sems = refs[:6], refs[6], refs[7:13], refs[13]
+    sources, feats, (queries, eigen, basis_in, basis_out) = refs[:8], refs[8], refs[9:13]
+    targets = (*refs[13:17], basis_in, basis_out, queries, eigen)
+    sems = refs[17]
     tokens, width = targets[0].shape
     rank = targets[2].shape[0]
     step = width // chunks
@@ -52,6 +54,8 @@
         for chunk in range(chunks):
             copy(rows, chunk).start()
         copy(basis).start()
+    for which in (6, 7):
+        copy(which).start()
     for place, (rows, proj, basis) in enumerate(sides):
         copy(proj).wait()
         total = None
@@ -67,11 +71,13 @@
             preferred_element_type=F32,
         )
         feats[place * rank:(place + 1) * rank, :] = turned.astype(BF16)
-
-
-def pack_kernel(order, *refs):
-    for offset, ref in zip(order, refs):
-        refs[-1][offset] = ref[...]
+    for which in (6, 7):
+        copy(which).wait()
+
+
+def pack_kernel(count, *refs):
+    for i, ref in enumerate(refs[:count]):
+        refs[-1][i] = ref[...]
 
 
 def score_block(feats, weights, rank):
@@ -94,7 +100,8 @@
     return total.T
 
 
-def queries_kernel(queries, basis_in, basis_out, eigen, weights, half):
+def queries_kernel(queries, basis_in, basis_out, eigen, *refs):
+    weights, half = refs[-2:]
     rank = basis_in.shape[0]
     width = PACK * rank
     groups = rank // PACK
@@ -116,15 +123,16 @@
         weights[:, part * width:(part + 1) * width] = (turned * scale).astype(BF16)
 
 
-def scores_kernel(layer_size, rank, offsets, weights, mine, theirs, *refs):
+def scores_kernel(layer_size, rank, offsets, places, weights, *refs):
     own, away, scores = refs[-layer_size - 1], refs[-layer_size:-1], refs[-1]
     layer, core = lax.axis_index("layer"), lax.axis_index("sub")
-    rows, half = own.shape[1], mine.shape[2]
-    for i, offset in enumerate(offsets):
-        feats = jnp.concatenate([mine[offset], theirs[offset]], axis=1)
+    rows, half = own.shape[1], refs[0].shape[2]
+    for i, (offset, (pair, place)) in enumerate(zip(offsets, places)):
+        feats = jnp.concatenate([refs[2 * pair][place], refs[2 * pair + 1][place]], axis=1)
         scores[...] = score_block(feats, weights, rank)
+        held = 1 - core if offset else core
         for k, block in enumerate((own, *away)):
-            first = lax.rem(lax.rem(layer + k, layer_size) * rows + core * half, 2 * half)
+            first = lax.rem(lax.rem(layer + k, layer_size) * rows + held * half, 2 * half)
             block[i] = scores[pl.ds(pl.multiple_of(first, rows), rows), :].astype(block.dtype)
 
 
@@ -153,37 +161,43 @@
     anywhere = pl.BlockSpec(memory_space=pl.ANY)
     params = pltpu.CompilerParams(vmem_limit_bytes=32 << 20)
 
-    feats = pl.pallas_call(
+    sources = (inputs, out_grads, proj_in, proj_out, basis_in, basis_out, queries, eigen)
+    feats, queries, eigen, basis_in, basis_out = pl.pallas_call(
         functools.partial(features_kernel, chunks),
-        out_shape=jax.ShapeDtypeStruct((2 * rank, half), BF16),
-        in_specs=[hbm] * 6,
-        out_specs=vmem,
+        out_shape=[
+            jax.ShapeDtypeStruct((2 * rank, half), BF16),
+            jax.ShapeDtypeStruct((count, entries), BF16),
+            *[jax.ShapeDtypeStruct((rank, rank), F32)] * 3,
+        ],
+        in_specs=[hbm] * len(sources),
+        out_specs=[vmem] * 5,
         scratch_shapes=[
             pltpu.VMEM((half, width), BF16),
             pltpu.VMEM((half, width), BF16),
             pltpu.VMEM((rank, width), BF16),
             pltpu.VMEM((rank, width), BF16),
-            pltpu.VMEM((rank, rank), F32),
-            pltpu.VMEM((rank, rank), F32),
-            pltpu.SemaphoreType.DMA((6, chunks)),
+            pltpu.SemaphoreType.DMA((len(sources), chunks)),
         ],
         compiler_params=params,
         cost_estimate=pl.CostEstimate(
             flops=4 * half * rank * width, bytes_accessed=4 * width * (half + rank), transcendentals=0
         ),
         name="features",
-    )(*[
-        pltpu.with_memory_space_constraint(value, pltpu.HBM)
-        for value in (inputs, out_grads, proj_in, proj_out, basis_in, basis_out)
-    ])
+    )(*[pltpu.with_memory_space_constraint(value, pltpu.HBM) for value in sources])
 
     def exchange(value, offset):
         return lax.ppermute(value, "train", [(j, j ^ offset) for j in range(train_size)])
 
+    def exchange_across(value, offset):
+        pairs = [(2 * j + s, 2 * (j ^ offset) + 1 - s) for j in range(train_size) for s in range(2)]
+        return lax.ppermute(value, ("train", "sub"), pairs)
+
     middle = train_size // 2
-    order = (0, *range(1, middle), *range(train_size - 1, middle - 1, -1))
-    gathered = [exchange(feats, offset) if offset else feats for offset in order]
-
+    far, near = tuple(range(train_size - 1, middle - 1, -1)), tuple(range(middle))
+    gathered = {offset: exchange_across(feats, offset) for offset in range(train_size - 1, 0, -1)}
+    gathered[0] = feats
+
+    halves = {}
     weights = pl.pallas_call(
         queries_kernel,
         out_shape=jax.ShapeDtypeStruct((count, entries), BF16),
@@ -195,28 +209,38 @@
             flops=4 * PACK * count * entries * rank, bytes_accessed=4 * count * entries, transcendentals=0
         ),
         name="queries",
-    )(queries[0], basis_in[0], basis_out[0], eigen[0])
-
-    mine = pl.pallas_call(
-        functools.partial(pack_kernel, order),
-        out_shape=jax.ShapeDtypeStruct((train_size, 2 * rank, half), BF16),
-        in_specs=[vmem] * train_size + [anywhere],
-        out_specs=vmem,
-        compiler_params=params,
-        name="pack",
-    )(*gathered, weights)
-    theirs = lax.ppermute(mine, "sub", [(0, 1), (1, 0)])
+    )(queries, basis_in, basis_out, eigen)
+
+    def swapped(offsets, after):
+        mine = pl.pallas_call(
+            functools.partial(pack_kernel, len(offsets)),
+            out_shape=jax.ShapeDtypeStruct((len(offsets), 2 * rank, half), BF16),
+            in_specs=[vmem] * len(offsets) + [anywhere] * len(after),
+            out_specs=vmem,
+            compiler_params=params,
+            name="pack",
+        )(*[gathered[offset] for offset in offsets], *after)
+        theirs = lax.ppermute(mine, "sub", [(0, 1), (1, 0)])
+        halves.update({offset: (mine, theirs, place) for place, offset in enumerate(offsets)})
+
+    for offsets in ((*near, *far),):
+        swapped(offsets, [weights])
 
     rows = tokens // layer_size
 
     def scored(offsets, after):
+        pairs = list({id(halves[offset][0]): halves[offset][:2] for offset in offsets}.values())
+        places = [
+            (next(i for i, pair in enumerate(pairs) if pair[0] is halves[offset][0]), halves[offset][2])
+            for offset in offsets
+        ]
         own, *away = pl.pallas_call(
-            functools.partial(scores_kernel, layer_size, rank, offsets),
+            functools.partial(scores_kernel, layer_size, rank, offsets, places),
             out_shape=[
                 jax.ShapeDtypeStruct((len(offsets), rows, count), BF16 if k else F32)
                 for k in range(layer_size)
             ],
-            in_specs=[vmem] * 3 + [anywhere] * len(after),
+            in_specs=[vmem] * (1 + 2 * len(pairs)) + [anywhere] * len(after),
             out_specs=[vmem] * layer_size,
             scratch_shapes=[pltpu.VMEM((tokens, count), F32)],
             compiler_params=params,
@@ -226,7 +250,7 @@
                 transcendentals=0,
             ),
             name="scores",
-        )(weights, mine, theirs, *after)
+        )(weights, *[half for pair in pairs for half in pair], *after)
         return own, [
             lax.ppermute(block, "layer", [(l, (l + k) % layer_size) for l in range(layer_size)])
             for k, block in enumerate(away, 1)
@@ -242,15 +266,16 @@
             name="layers",
         )(own, *others, *after)
 
-    far, near = tuple(range(train_size - 1, middle - 1, -1)), tuple(range(middle))
-    far_terms = scored(far, [])
-    near_terms = scored(near, far_terms[:1])
+    terms, after = {}, []
+    for offsets in (far, near):
+        own, others = scored(offsets, after)
+        terms.update({offset: (which, offset, own, others) for which, offset in enumerate(offsets)})
+        after = [own]
     arrived, after = {}, []
-    for offsets, terms in ((far, far_terms), (near, near_terms)):
-        for which, offset in enumerate(offsets):
-            block = summed(which, offset, *terms, after)
-            after = [block]
-            arrived[offset] = exchange(block, offset) if offset else block
+    for offset in (*far, *near):
+        block = summed(*terms[offset], after)
+        after = [block]
+        arrived[offset] = exchange(block, offset) if offset else block
 
     total = pl.pallas_call(
         functools.partial(place_kernel, train_size),

time: 27.8 us -> 27.6 us (level)
  waiting for transfers between devices: 7.21 us -> 6.52 us
  starting transfers between devices: 12.3 us -> 12.9 us
    ppermute x1 -> x4, starting transfers between devices: 0.07 us -> 6.12 us  [the longest x3 5.4 us: exchange_across(): return lax.ppermute(value, ('train', 'sub'), pairs)]
    ppermute x6 -> x3, starting transfers between devices: 10.1 us -> 4.56 us  [exchange(): lax.ppermute(value, 'train', [(j, j ^ offset) for j in range(train_size)])]
    ppermute x6 -> x3, waiting for transfers between devices: 4.34 us -> 2.69 us  [exchange(): lax.ppermute(value, 'train', [(j, j ^ offset) for j in range(train_size)])]
    ppermute x1 -> x4, waiting for transfers between devices: 1.33 us -> 2.41 us  [the longest x3 1.42 us: exchange_across(): return lax.ppermute(value, ('train', 'sub'), pairs)]
where the time goes in v6:
time: 27.6 us; the launch traced here: 27.5 us
  starting transfers between devices  12.9 us (47%)
  Pallas kernels  7.99 us (29%)
  waiting for transfers between devices  6.52 us (24%)
    ppermute x3, starting transfers between devices, exchange_across(): return lax.ppermute(value, ('train', 'sub'), pairs)  5.4 us
    ppermute x3, starting transfers between devices, exchange(): lax.ppermute(value, 'train', [(j, j ^ offset) for j in range(train_size)])  4.56 us
    pallas_call x1, Pallas kernels, body(): pl.pallas_call(functools.partial(features_kernel, chunks), out_shape=[jax...  3.44 us
    ppermute x3, waiting for transfers between devices, exchange(): lax.ppermute(value, 'train', [(j, j ^ offset) for j in range(train_size)])  2.69 us
    ppermute x2, starting transfers between devices, scored(): lax.ppermute(block, 'layer', [(l, (l + k) % layer_size) for l in range(la...  2.17 us
    pallas_call x1, Pallas kernels, body(): pl.pallas_call(queries_kernel, out_shape=jax.ShapeDtypeStruct((count, ent...  2.11 us
    pallas_call x2, Pallas kernels, scored(): pl.pallas_call(functools.partial(scores_kernel, layer_size, rank, offsets...  1.65 us
    ppermute x3, waiting for transfers between devices, exchange_across(): return lax.ppermute(value, ('train', 'sub'), pairs)  1.42 us
  transfers between devices with their start and end apart: 9, of which 5 were waited for; matrix products, arithmetic and copies ran while one was open for 0% of the time, Pallas kernels for 11%

profile of v6, /device:TPU:0, one launch (start us, length us, event | category | flops | bytes accessed | tf_op | source)
XLA Modules:
  0.0 27.5 jit_solution(10000170954997636927)
XLA Ops:
  0.0 3.4 %features.1 = (bf16[128,128]{1,0:T(8,128)(2,1)S(1)}, bf16[128,4096]{1,0:T(8,128)(2,1)S(1)}, f32[64,64]{1,0:T(8,128)S(1)}, f32[64,64]{1,0:T(8,128)S(1)}, f32[64,64]{1,0:T(8,128)S(1)}) custom-call(bf16[1,256,4096]{2,1,0:T(8,128)(2,1)} %refs_0_.1, bf16[1,256,4096]{2,1,0:T(8,128)(2,1)} %refs_1_.1, bf16[1,64,4096]{2,1,0:T(8,128)(2,1)} %refs_2_.1, ...), custom_call_target="tpu_custom_call" | custom-call | flops 134217728 | bytes 3145728 | tf_op jit(solution)/shard_map/features/pallas_call | solution.py:165
  3.4 3.5 %collective-permute-start.2 = (bf16[128,128]{1,0:T(8,128)(2,1)S(1)}, bf16[128,128]{1,0:T(8,128)(2,1)S(1)}, u32[]{:S(2)}, u32[]{:S(2)}) collective-permute-start(bf16[128,128]{1,0:T(8,128)(2,1)S(1)} %get-tuple-element.18.refs_0_), channel_id=1, source_target_pairs={{0,9},{1,8},{4,13},{5,12},{8,1},{9,0},{12,5},{13,4},{2,11},{3,10},... | collective-permute-start | bytes 98312 | tf_op jit(solution)/shard_map/ppermute | solution.py:193
  7.0 1.6 %collective-permute-start.1 = (bf16[128,128]{1,0:T(8,128)(2,1)S(1)}, bf16[128,128]{1,0:T(8,128)(2,1)S(1)}, u32[]{:S(2)}, u32[]{:S(2)}) collective-permute-start(bf16[128,128]{1,0:T(8,128)(2,1)S(1)} %get-tuple-element.18.refs_0_), channel_id=1, source_target_pairs={{0,13},{1,12},{4,9},{5,8},{8,5},{9,4},{12,1},{13,0},{2,15},{3,14},... | collective-permute-start | bytes 98312 | tf_op jit(solution)/shard_map/ppermute | solution.py:193
  8.6 0.2 collective-permute-start
  8.8 2.1 %queries.1.refs_4_.weights = bf16[128,4096]{1,0:T(8,128)(2,1)S(1)} custom-call(bf16[128,4096]{1,0:T(8,128)(2,1)S(1)} %get-tuple-element.14.queries, f32[64,64]{1,0:T(8,128)S(1)} %get-tuple-element.15.basis_in, f32[64,64]{1,0:T(8,128)S(1)} %get-tuple-element.16.basis_out, f32[64,64]{1,0:T(8,128)S(1)} %get-tuple-element.17.eigen), custom_call_target="tpu_custom_call" | custom-call | flops 536870912 | bytes 2097152 | tf_op jit(solution)/shard_map/queries/pallas_call | solution.py:201
  11.0 0.0 collective-permute-done.2.refs_3_
  11.0 1.3 %collective-permute-done.1.refs_2_ = bf16[128,128]{1,0:T(8,128)(2,1)S(1)} collective-permute-done((bf16[128,128]{1,0:T(8,128)(2,1)S(1)}, bf16[128,128]{1,0:T(8,128)(2,1)S(1)}, u32[]{:S(2)}, u32[]{:S(2)}) %collective-permute-start.1) | collective-permute-done | bytes 32800 | tf_op jit(solution)/shard_map/ppermute | solution.py:193
  12.2 0.2 collective-permute-done.refs_1_
  12.4 0.7 %collective-permute-start.3 = (bf16[4,128,128]{2,1,0:T(8,128)(2,1)S(1)}, bf16[4,128,128]{2,1,0:T(8,128)(2,1)S(1)}, u32[]{:S(2)}, u32[]{:S(2)}) collective-permute-start(bf16[4,128,128]{2,1,0:T(8,128)(2,1)S(1)} %pack.1.refs_0_), channel_id=1, source_target_pairs={{0,1},{1,0},{2,3},{3,2},{4,5},{5,4},{6,7},{7,6},{8,9},{9,8},{10,11... | collective-permute-start | bytes 393224 | tf_op jit(solution)/shard_map/ppermute | solution.py:223
  13.1 1.0 %collective-permute-done.3.refs_1_ = bf16[4,128,128]{2,1,0:T(8,128)(2,1)S(1)} collective-permute-done((bf16[4,128,128]{2,1,0:T(8,128)(2,1)S(1)}, bf16[4,128,128]{2,1,0:T(8,128)(2,1)S(1)}, u32[]{:S(2)}, u32[]{:S(2)}) %collective-permute-start.3) | collective-permute-done | bytes 131104 | tf_op jit(solution)/shard_map/ppermute | solution.py:223
  14.1 0.8 %scores.2 = (f32[2,128,128]{2,1,0:T(8,128)S(1)}, bf16[2,128,128]{2,1,0:T(8,128)(2,1)S(1)}) custom-call(bf16[128,4096]{1,0:T(8,128)(2,1)S(1)} %queries.1.refs_4_.weights, bf16[4,128,128]{2,1,0:T(8,128)(2,1)S(1)} %pack.1.refs_0_, bf16[4,128,128]{2,1,0:T(8,128)(2,1)S(1)} %collective-permute-done.3.refs_1_), custom_call_target="tpu_custom_call" | custom-call | flops 536870912 | bytes 1048576 | tf_op jit(solution)/shard_map/scores/pallas_call | solution.py:237
  15.0 1.6 %collective-permute-start.4 = (bf16[2,128,128]{2,1,0:T(8,128)(2,1)S(1)}, bf16[2,128,128]{2,1,0:T(8,128)(2,1)S(1)}, u32[]{:S(2)}, u32[]{:S(2)}) collective-permute-start(bf16[2,128,128]{2,1,0:T(8,128)(2,1)S(1)} %get-tuple-element.20), channel_id=1, source_target_pairs={{0,2},{2,0},{1,3},{3,1},{4,6},{6,4},{5,7},{7,5},{8,10},{10,8},{9,1... | collective-permute-start | bytes 196616 | tf_op jit(solution)/shard_map/ppermute | solution.py:255
  16.5 0.8 %scores.3 = (f32[2,128,128]{2,1,0:T(8,128)S(1)}, bf16[2,128,128]{2,1,0:T(8,128)(2,1)S(1)}) custom-call(bf16[128,4096]{1,0:T(8,128)(2,1)S(1)} %queries.1.refs_4_.weights, bf16[4,128,128]{2,1,0:T(8,128)(2,1)S(1)} %pack.1.refs_0_, bf16[4,128,128]{2,1,0:T(8,128)(2,1)S(1)} %collective-permute-done.3.refs_1_, f32[2,128,128]{2,1,0:T(8,128)S(1)} %get-tuple-element.19.own.refs_2_), custom_call_target="tpu_custom_call" | custom-call | flops 536870912 | bytes 1048576 | tf_op jit(solution)/shard_map/scores/pallas_call | solution.py:237
  17.4 0.6 %collective-permute-start.7 = (bf16[2,128,128]{2,1,0:T(8,128)(2,1)S(1)}, bf16[2,128,128]{2,1,0:T(8,128)(2,1)S(1)}, u32[]{:S(2)}, u32[]{:S(2)}) collective-permute-start(bf16[2,128,128]{2,1,0:T(8,128)(2,1)S(1)} %get-tuple-element.22), channel_id=1, source_target_pairs={{0,2},{2,0},{1,3},{3,1},{4,6},{6,4},{5,7},{7,5},{8,10},{10,8},{9,1... | collective-permute-start | bytes 196616 | tf_op jit(solution)/shard_map/ppermute | solution.py:255
  18.0 1.4 %collective-permute-done.4.refs_0_ = bf16[2,128,128]{2,1,0:T(8,128)(2,1)S(1)} collective-permute-done((bf16[2,128,128]{2,1,0:T(8,128)(2,1)S(1)}, bf16[2,128,128]{2,1,0:T(8,128)(2,1)S(1)}, u32[]{:S(2)}, u32[]{:S(2)}) %collective-permute-start.4) | collective-permute-done | bytes 65568 | tf_op jit(solution)/shard_map/ppermute | solution.py:255
  19.4 2.4 %collective-permute-start.5 = (bf16[128,128]{1,0:T(8,128)(2,1)S(1)}, bf16[128,128]{1,0:T(8,128)(2,1)S(1)}, u32[]{:S(2)}, u32[]{:S(2)}) collective-permute-start(bf16[128,128]{1,0:T(8,128)(2,1)S(1)} %layers.4.refs_1_), channel_id=1, source_target_pairs={{0,12},{4,8},{8,4},{12,0},{1,13},{5,9},{9,5},{13,1},{2,14},{6,10},... | collective-permute-start | bytes 98312 | tf_op jit(solution)/shard_map/ppermute | solution.py:189
  21.8 0.1 collective-permute-start.6
  21.9 0.0 collective-permute-done.7.refs_0_
  22.0 2.1 %collective-permute-start.8 = (bf16[128,128]{1,0:T(8,128)(2,1)S(1)}, bf16[128,128]{1,0:T(8,128)(2,1)S(1)}, u32[]{:S(2)}, u32[]{:S(2)}) collective-permute-start(bf16[128,128]{1,0:T(8,128)(2,1)S(1)} %layers.7), channel_id=1, source_target_pairs={{0,4},{4,0},{8,12},{12,8},{1,5},{5,1},{9,13},{13,9},{2,6},{6,2},{1... | collective-permute-start | bytes 98312 | tf_op jit(solution)/shard_map/ppermute | solution.py:189
  24.0 2.7 %collective-permute-done.6.refs_1_ = bf16[128,128]{1,0:T(8,128)(2,1)S(1)} collective-permute-done((bf16[128,128]{1,0:T(8,128)(2,1)S(1)}, bf16[128,128]{1,0:T(8,128)(2,1)S(1)}, u32[]{:S(2)}, u32[]{:S(2)}) %collective-permute-start.6) | collective-permute-done | bytes 32800 | tf_op jit(solution)/shard_map/ppermute | solution.py:189
  26.7 0.0 collective-permute-done.5.refs_0_
  26.7 0.0 collective-permute-done.8.refs_2_
  26.7 0.7 %place.1 = f32[512,128]{1,0:T(8,128)} custom-call(bf16[128,128]{1,0:T(8,128)(2,1)S(1)} %collective-permute-done.5.refs_0_, bf16[128,128]{1,0:T(8,128)(2,1)S(1)} %collective-permute-done.6.refs_1_, bf16[128,128]{1,0:T(8,128)(2,1)S(1)} %collective-permute-done.8.refs_2_, f32[128,128]{1,0:T(8,128)S(1)} %layers.6.refs_1_.refs_3_), custom_call_target="tpu_custom_call" | custom-call | tf_op jit(solution)/shard_map/place/pallas_call | solution.py:280
  (5 shorter events, 0.0 us)
Async XLA Ops:
  3.4 7.5 %collective-permute-start.2 = (bf16[128,128]{1,0:T(8,128)(2,1)S(1)}, bf16[128,128]{1,0:T(8,128)(2,1)S(1)}, u32[]{:S(2)}, u32[]{:S(2)}) collective-permute-start(bf16[128,128]{1,0:T(8,128)(2,1)S(1)} %get-tuple-element.18.refs_0_), channel_id=1, source_target_pairs={{0,9},{1,8},{4,13},{5,12},{8,1},{9,0},{12,5},{13,4},{2,11},{3,10},... | collective-permute-start | bytes 98312 | tf_op jit(solution)/shard_map/ppermute | solution.py:193
  7.0 5.2 %collective-permute-start.1 = (bf16[128,128]{1,0:T(8,128)(2,1)S(1)}, bf16[128,128]{1,0:T(8,128)(2,1)S(1)}, u32[]{:S(2)}, u32[]{:S(2)}) collective-permute-start(bf16[128,128]{1,0:T(8,128)(2,1)S(1)} %get-tuple-element.18.refs_0_), channel_id=1, source_target_pairs={{0,13},{1,12},{4,9},{5,8},{8,5},{9,4},{12,1},{13,0},{2,15},{3,14},... | collective-permute-start | bytes 98312 | tf_op jit(solution)/shard_map/ppermute | solution.py:193
  8.6 3.8 %collective-permute-start = (bf16[128,128]{1,0:T(8,128)(2,1)S(1)}, bf16[128,128]{1,0:T(8,128)(2,1)S(1)}, u32[]{:S(2)}, u32[]{:S(2)}) collective-permute-start(bf16[128,128]{1,0:T(8,128)(2,1)S(1)} %get-tuple-element.18.refs_0_), channel_id=1, source_target_pairs={{0,5},{1,4},{4,1},{5,0},{8,13},{9,12},{12,9},{13,8},{2,7},{3,6},{6... | collective-permute-start | bytes 98312 | tf_op jit(solution)/shard_map/ppermute | solution.py:193
  12.4 1.7 %collective-permute-start.3 = (bf16[4,128,128]{2,1,0:T(8,128)(2,1)S(1)}, bf16[4,128,128]{2,1,0:T(8,128)(2,1)S(1)}, u32[]{:S(2)}, u32[]{:S(2)}) collective-permute-start(bf16[4,128,128]{2,1,0:T(8,128)(2,1)S(1)} %pack.1.refs_0_), channel_id=1, source_target_pairs={{0,1},{1,0},{2,3},{3,2},{4,5},{5,4},{6,7},{7,6},{8,9},{9,8},{10,11... | collective-permute-start | bytes 393224 | tf_op jit(solution)/shard_map/ppermute | solution.py:223
  15.0 4.4 %collective-permute-start.4 = (bf16[2,128,128]{2,1,0:T(8,128)(2,1)S(1)}, bf16[2,128,128]{2,1,0:T(8,128)(2,1)S(1)}, u32[]{:S(2)}, u32[]{:S(2)}) collective-permute-start(bf16[2,128,128]{2,1,0:T(8,128)(2,1)S(1)} %get-tuple-element.20), channel_id=1, source_target_pairs={{0,2},{2,0},{1,3},{3,1},{4,6},{6,4},{5,7},{7,5},{8,10},{10,8},{9,1... | collective-permute-start | bytes 196616 | tf_op jit(solution)/shard_map/ppermute | solution.py:255
  17.4 4.6 %collective-permute-start.7 = (bf16[2,128,128]{2,1,0:T(8,128)(2,1)S(1)}, bf16[2,128,128]{2,1,0:T(8,128)(2,1)S(1)}, u32[]{:S(2)}, u32[]{:S(2)}) collective-permute-start(bf16[2,128,128]{2,1,0:T(8,128)(2,1)S(1)} %get-tuple-element.22), channel_id=1, source_target_pairs={{0,2},{2,0},{1,3},{3,1},{4,6},{6,4},{5,7},{7,5},{8,10},{10,8},{9,1... | collective-permute-start | bytes 196616 | tf_op jit(solution)/shard_map/ppermute | solution.py:255
  19.4 7.3 %collective-permute-start.5 = (bf16[128,128]{1,0:T(8,128)(2,1)S(1)}, bf16[128,128]{1,0:T(8,128)(2,1)S(1)}, u32[]{:S(2)}, u32[]{:S(2)}) collective-permute-start(bf16[128,128]{1,0:T(8,128)(2,1)S(1)} %layers.4.refs_1_), channel_id=1, source_target_pairs={{0,12},{4,8},{8,4},{12,0},{1,13},{5,9},{9,5},{13,1},{2,14},{6,10},... | collective-permute-start | bytes 98312 | tf_op jit(solution)/shard_map/ppermute | solution.py:189
  21.8 4.9 %collective-permute-start.6 = (bf16[128,128]{1,0:T(8,128)(2,1)S(1)}, bf16[128,128]{1,0:T(8,128)(2,1)S(1)}, u32[]{:S(2)}, u32[]{:S(2)}) collective-permute-start(bf16[128,128]{1,0:T(8,128)(2,1)S(1)} %layers.5.refs_1_), channel_id=1, source_target_pairs={{0,8},{4,12},{8,0},{12,4},{1,9},{5,13},{9,1},{13,5},{2,10},{6,14},... | collective-permute-start | bytes 98312 | tf_op jit(solution)/shard_map/ppermute | solution.py:189
  22.0 4.8 %collective-permute-start.8 = (bf16[128,128]{1,0:T(8,128)(2,1)S(1)}, bf16[128,128]{1,0:T(8,128)(2,1)S(1)}, u32[]{:S(2)}, u32[]{:S(2)}) collective-permute-start(bf16[128,128]{1,0:T(8,128)(2,1)S(1)} %layers.7), channel_id=1, source_target_pairs={{0,4},{4,0},{8,12},{12,8},{1,5},{5,1},{9,13},{13,9},{2,6},{6,2},{1... | collective-permute-start | bytes 98312 | tf_op jit(solution)/shard_map/ppermute | solution.py:189

commit v7 on v6

--- a/solution.py
+++ b/solution.py
@@ -123,12 +123,12 @@
         weights[:, part * width:(part + 1) * width] = (turned * scale).astype(BF16)
 
 
-def scores_kernel(layer_size, rank, offsets, places, weights, *refs):
+def scores_kernel(layer_size, rank, offsets, places, weights, mine, theirs, *refs):
     own, away, scores = refs[-layer_size - 1], refs[-layer_size:-1], refs[-1]
     layer, core = lax.axis_index("layer"), lax.axis_index("sub")
-    rows, half = own.shape[1], refs[0].shape[2]
-    for i, (offset, (pair, place)) in enumerate(zip(offsets, places)):
-        feats = jnp.concatenate([refs[2 * pair][place], refs[2 * pair + 1][place]], axis=1)
+    rows, half = own.shape[1], mine.shape[2]
+    for i, (offset, place) in enumerate(zip(offsets, places)):
+        feats = jnp.concatenate([mine[place], theirs[place]], axis=1)
         scores[...] = score_block(feats, weights, rank)
         held = 1 - core if offset else core
         for k, block in enumerate((own, *away)):
@@ -143,10 +143,14 @@
     refs[-1][...] = total.astype(refs[-1].dtype)
 
 
+def keep_kernel(block, *refs):
+    refs[-1][...] = block[...].astype(F32)
+
+
 def place_kernel(train_size, *refs):
-    arrived, out = refs[:-1], refs[-1]
+    blocks, out = refs[:-1], refs[-1]
     here = lax.axis_index("train")
-    for offset, block in enumerate(reversed(arrived)):
+    for offset, block in zip((0, *range(train_size - 1, 0, -1)), blocks):
         out[pl.ds(here ^ offset, block.shape[0], stride=train_size), :] = block[...].astype(F32)
 
 
@@ -156,7 +160,7 @@
     count, entries = queries.shape[1:]
     rank = proj_in.shape[1]
     half = tokens // 2
-    chunks = 2
+    chunks = 1
     vmem, hbm = pl.BlockSpec(memory_space=pltpu.VMEM), pl.BlockSpec(memory_space=pltpu.HBM)
     anywhere = pl.BlockSpec(memory_space=pl.ANY)
     params = pltpu.CompilerParams(vmem_limit_bytes=32 << 20)
@@ -192,12 +196,8 @@
         pairs = [(2 * j + s, 2 * (j ^ offset) + 1 - s) for j in range(train_size) for s in range(2)]
         return lax.ppermute(value, ("train", "sub"), pairs)
 
-    middle = train_size // 2
-    far, near = tuple(range(train_size - 1, middle - 1, -1)), tuple(range(middle))
     gathered = {offset: exchange_across(feats, offset) for offset in range(train_size - 1, 0, -1)}
-    gathered[0] = feats
-
-    halves = {}
+
     weights = pl.pallas_call(
         queries_kernel,
         out_shape=jax.ShapeDtypeStruct((count, entries), BF16),
@@ -211,36 +211,19 @@
         name="queries",
     )(queries, basis_in, basis_out, eigen)
 
-    def swapped(offsets, after):
-        mine = pl.pallas_call(
-            functools.partial(pack_kernel, len(offsets)),
-            out_shape=jax.ShapeDtypeStruct((len(offsets), 2 * rank, half), BF16),
-            in_specs=[vmem] * len(offsets) + [anywhere] * len(after),
-            out_specs=vmem,
-            compiler_params=params,
-            name="pack",
-        )(*[gathered[offset] for offset in offsets], *after)
-        theirs = lax.ppermute(mine, "sub", [(0, 1), (1, 0)])
-        halves.update({offset: (mine, theirs, place) for place, offset in enumerate(offsets)})
-
-    for offsets in ((*near, *far),):
-        swapped(offsets, [weights])
+    def over_cores(value):
+        return lax.ppermute(value, "sub", [(0, 1), (1, 0)])
 
     rows = tokens // layer_size
 
-    def scored(offsets, after):
-        pairs = list({id(halves[offset][0]): halves[offset][:2] for offset in offsets}.values())
-        places = [
-            (next(i for i, pair in enumerate(pairs) if pair[0] is halves[offset][0]), halves[offset][2])
-            for offset in offsets
-        ]
+    def scored(offsets, places, mine, theirs, after):
         own, *away = pl.pallas_call(
             functools.partial(scores_kernel, layer_size, rank, offsets, places),
             out_shape=[
                 jax.ShapeDtypeStruct((len(offsets), rows, count), BF16 if k else F32)
                 for k in range(layer_size)
             ],
-            in_specs=[vmem] * (1 + 2 * len(pairs)) + [anywhere] * len(after),
+            in_specs=[vmem] * 3 + [anywhere] * len(after),
             out_specs=[vmem] * layer_size,
             scratch_shapes=[pltpu.VMEM((tokens, count), F32)],
             compiler_params=params,
@@ -250,7 +233,7 @@
                 transcendentals=0,
             ),
             name="scores",
-        )(weights, *[half for pair in pairs for half in pair], *after)
+        )(weights, mine, theirs, *after)
         return own, [
             lax.ppermute(block, "layer", [(l, (l + k) % layer_size) for l in range(layer_size)])
             for k, block in enumerate(away, 1)
@@ -266,16 +249,47 @@
             name="layers",
         )(own, *others, *after)
 
+    def kept(block, after):
+        return pl.pallas_call(
+            keep_kernel,
+            out_shape=jax.ShapeDtypeStruct(block.shape, F32),
+            in_specs=[vmem] + [anywhere] * len(after),
+            out_specs=vmem,
+            compiler_params=params,
+            name="keep",
+        )(block, *after)
+
+    own, others = scored((0,), (0,), feats[None], over_cores(feats[None]), [])
+    order = (1, *range(train_size - 1, 1, -1))
+    mine = pl.pallas_call(
+        functools.partial(pack_kernel, len(order)),
+        out_shape=jax.ShapeDtypeStruct((len(order), 2 * rank, half), BF16),
+        in_specs=[vmem] * len(order) + [anywhere],
+        out_specs=vmem,
+        compiler_params=params,
+        name="pack",
+    )(*[gathered[offset] for offset in order], own)
+    theirs = over_cores(mine)
+
+    size = -(-(train_size - 1) // 3)
+    groups = [tuple(range(last, max(last - size, 0), -1)) for last in range(train_size - 1, 0, -size)]
     terms, after = {}, []
-    for offsets in (far, near):
-        own, others = scored(offsets, after)
-        terms.update({offset: (which, offset, own, others) for which, offset in enumerate(offsets)})
-        after = [own]
-    arrived, after = {}, []
-    for offset in (*far, *near):
+    for offsets in groups:
+        places = [order.index(offset) for offset in offsets]
+        mine_terms, their_terms = scored(offsets, places, mine, theirs, after)
+        terms.update({offset: (which, offset, mine_terms, their_terms) for which, offset in enumerate(offsets)})
+        after = [mine_terms]
+    home = summed(0, 0, own, others, after)
+    arrived, after = {}, [home]
+    for offset in range(train_size - 1, 0, -1):
         block = summed(*terms[offset], after)
         after = [block]
-        arrived[offset] = exchange(block, offset) if offset else block
+        arrived[offset] = exchange(block, offset)
+    blocks, after = [home], []
+    for offset in range(train_size - 1, 1, -1):
+        blocks.append(kept(arrived[offset], after))
+        after = blocks[-1:]
+    blocks.append(arrived[1])
 
     total = pl.pallas_call(
         functools.partial(place_kernel, train_size),
@@ -284,7 +298,7 @@
         out_specs=vmem,
         compiler_params=params,
         name="place",
-    )(*[arrived[offset] for offset in reversed(range(train_size))])
+    )(*blocks)
     return total.reshape(rows, train_size, 1, count)
 
 

time: 27.6 us -> 28 us (1.014)
  waiting for transfers between devices: 6.52 us -> 3.9 us
  starting transfers between devices: 12.9 us -> 15.5 us
  Pallas kernels: 7.99 us -> 8.36 us
    ppermute x2 -> x4, starting transfers between devices: 2.17 us -> 4.68 us  [scored(): lax.ppermute(block, 'layer', [(l, (l + k) % layer_size) for l in range(la...]
    ppermute x2 -> x4, waiting for transfers between devices: 1.42 us -> 0.01 us  [scored(): lax.ppermute(block, 'layer', [(l, (l + k) % layer_size) for l in range(la...]
    ppermute x1 -> x2, waiting for transfers between devices: 0.99 us -> 0.01 us  [over_cores(): return lax.ppermute(value, 'sub', [(0, 1), (1, 0)])]
    ppermute x3, waiting for transfers between devices: 1.42 us -> 0.85 us  [exchange_across(): return lax.ppermute(value, ('train', 'sub'), pairs)]
    pallas_call x2 -> x4, Pallas kernels: 1.65 us -> 2.1 us  [scored(): pl.pallas_call(functools.partial(scores_kernel, layer_size, rank, offsets...]
    ppermute x3, waiting for transfers between devices: 2.69 us -> 3.03 us  [exchange(): lax.ppermute(value, 'train', [(j, j ^ offset) for j in range(train_size)])]
    ppermute x1 -> x2, starting transfers between devices: 0.73 us -> 0.74 us  [over_cores(): return lax.ppermute(value, 'sub', [(0, 1), (1, 0)])]
  transfers between devices with their start and end apart: 9 -> 12, of which waited for: 5 -> 5; matrix products, arithmetic and copies ran while one was open for 0% -> 0% of each run, Pallas kernels for 11% -> 15%
where the time goes in v7:
time: 28 us; the launch traced here: 27.8 us
  starting transfers between devices  15.5 us (55%)
  Pallas kernels  8.36 us (30%)
  waiting for transfers between devices  3.9 us (14%)
    ppermute x3, starting transfers between devices, exchange_across(): return lax.ppermute(value, ('train', 'sub'), pairs)  5.4 us
    ppermute x4, starting transfers between devices, scored(): lax.ppermute(block, 'layer', [(l, (l + k) % layer_size) for l in range(la...  4.68 us
    ppermute x3, starting transfers between devices, exchange(): lax.ppermute(value, 'train', [(j, j ^ offset) for j in range(train_size)])  4.67 us
    pallas_call x1, Pallas kernels, body(): pl.pallas_call(functools.partial(features_kernel, chunks), out_shape=[jax...  3.35 us
    ppermute x3, waiting for transfers between devices, exchange(): lax.ppermute(value, 'train', [(j, j ^ offset) for j in range(train_size)])  3.03 us
    pallas_call x1, Pallas kernels, body(): pl.pallas_call(queries_kernel, out_shape=jax.ShapeDtypeStruct((count, ent...  2.12 us
    pallas_call x4, Pallas kernels, scored(): pl.pallas_call(functools.partial(scores_kernel, layer_size, rank, offsets...  2.1 us
    ppermute x3, waiting for transfers between devices, exchange_across(): return lax.ppermute(value, ('train', 'sub'), pairs)  0.85 us
  transfers between devices with their start and end apart: 12, of which 5 were waited for; matrix products, arithmetic and copies ran while one was open for 0% of the time, Pallas kernels for 15%

profile of v7, /device:TPU:0, one launch (start us, length us, event | category | flops | bytes accessed | tf_op | source)
XLA Modules:
  0.0 27.8 jit_solution(14273857609067412945)
XLA Ops:
  0.0 3.4 %features.1 = (bf16[128,128]{1,0:T(8,128)(2,1)S(1)}, bf16[128,4096]{1,0:T(8,128)(2,1)S(1)}, f32[64,64]{1,0:T(8,128)S(1)}, f32[64,64]{1,0:T(8,128)S(1)}, f32[64,64]{1,0:T(8,128)S(1)}) custom-call(bf16[1,256,4096]{2,1,0:T(8,128)(2,1)} %refs_0_.1, bf16[1,256,4096]{2,1,0:T(8,128)(2,1)} %refs_1_.1, bf16[1,64,4096]{2,1,0:T(8,128)(2,1)} %refs_2_.1, ...), custom_call_target="tpu_custom_call" | custom-call | flops 134217728 | bytes 3145728 | tf_op jit(solution)/shard_map/features/pallas_call | solution.py:169
  3.4 3.5 %collective-permute-start.4 = (bf16[128,128]{1,0:T(8,128)(2,1)S(1)}, bf16[128,128]{1,0:T(8,128)(2,1)S(1)}, u32[]{:S(2)}, u32[]{:S(2)}) collective-permute-start(bf16[128,128]{1,0:T(8,128)(2,1)S(1)} %get-tuple-element.22), channel_id=1, source_target_pairs={{0,9},{1,8},{4,13},{5,12},{8,1},{9,0},{12,5},{13,4},{2,11},{3,10},... | collective-permute-start | bytes 98312 | tf_op jit(solution)/shard_map/ppermute | solution.py:197
  6.9 1.6 %collective-permute-start.3 = (bf16[128,128]{1,0:T(8,128)(2,1)S(1)}, bf16[128,128]{1,0:T(8,128)(2,1)S(1)}, u32[]{:S(2)}, u32[]{:S(2)}) collective-permute-start(bf16[128,128]{1,0:T(8,128)(2,1)S(1)} %get-tuple-element.22), channel_id=1, source_target_pairs={{0,13},{1,12},{4,9},{5,8},{8,5},{9,4},{12,1},{13,0},{2,15},{3,14},... | collective-permute-start | bytes 98312 | tf_op jit(solution)/shard_map/ppermute | solution.py:197
  8.5 0.2 collective-permute-start.2
  8.8 0.0 collective-permute-start
  8.8 2.1 %queries.1.weights = bf16[128,4096]{1,0:T(8,128)(2,1)S(1)} custom-call(bf16[128,4096]{1,0:T(8,128)(2,1)S(1)} %get-tuple-element.18.queries, f32[64,64]{1,0:T(8,128)S(1)} %get-tuple-element.19.basis_in, f32[64,64]{1,0:T(8,128)S(1)} %get-tuple-element.20.basis_out, f32[64,64]{1,0:T(8,128)S(1)} %get-tuple-element.21.eigen), custom_call_target="tpu_custom_call" | custom-call | flops 536870912 | bytes 2097152 | tf_op jit(solution)/shard_map/queries/pallas_call | solution.py:201
  10.9 0.0 collective-permute-done.theirs
  10.9 0.5 %scores.4 = (f32[1,128,128]{2,1,0:T(8,128)S(1)}, bf16[1,128,128]{2,1,0:T(8,128)(2,1)S(1)}) custom-call(bf16[128,4096]{1,0:T(8,128)(2,1)S(1)} %queries.1.weights, bf16[1,128,128]{2,1,0:T(8,128)(2,1)S(1)} %bitcast.5, bf16[1,128,128]{2,1,0:T(8,128)(2,1)S(1)} %collective-permute-done.theirs), custom_call_target="tpu_custom_call" | custom-call | flops 268435456 | bytes 1048576 | tf_op jit(solution)/shard_map/scores/pallas_call | solution.py:220
  11.4 0.0 collective-permute-done.4.refs_2_
  11.4 0.7 %collective-permute-done.3.refs_1_ = bf16[128,128]{1,0:T(8,128)(2,1)S(1)} collective-permute-done((bf16[128,128]{1,0:T(8,128)(2,1)S(1)}, bf16[128,128]{1,0:T(8,128)(2,1)S(1)}, u32[]{:S(2)}, u32[]{:S(2)}) %collective-permute-start.3) | collective-permute-done | bytes 32800 | tf_op jit(solution)/shard_map/ppermute | solution.py:197
  12.1 0.1 collective-permute-done.2.refs_0_
  12.3 0.7 %collective-permute-start.5 = (bf16[3,128,128]{2,1,0:T(8,128)(2,1)S(1)}, bf16[3,128,128]{2,1,0:T(8,128)(2,1)S(1)}, u32[]{:S(2)}, u32[]{:S(2)}) collective-permute-start(bf16[3,128,128]{2,1,0:T(8,128)(2,1)S(1)} %pack.1.mine), channel_id=1, source_target_pairs={{0,1},{1,0},{2,3},{3,2},{4,5},{5,4},{6,7},{7,6},{8,9},{9,8},{10,11... | collective-permute-start | bytes 294920 | tf_op jit(solution)/shard_map/ppermute | solution.py:215
  13.0 1.5 %collective-permute-start.1 = (bf16[1,128,128]{2,1,0:T(8,128)(2,1)S(1)}, bf16[1,128,128]{2,1,0:T(8,128)(2,1)S(1)}, u32[]{:S(2)}, u32[]{:S(2)}) collective-permute-start(bf16[1,128,128]{2,1,0:T(8,128)(2,1)S(1)} %get-tuple-element.24), channel_id=1, source_target_pairs={{0,2},{2,0},{1,3},{3,1},{4,6},{6,4},{5,7},{7,5},{8,10},{10,8},{9,1... | collective-permute-start | bytes 98312 | tf_op jit(solution)/shard_map/ppermute | solution.py:238
  14.5 0.0 collective-permute-done.5.theirs
  14.5 0.5 %scores.5 = (f32[1,128,128]{2,1,0:T(8,128)S(1)}, bf16[1,128,128]{2,1,0:T(8,128)(2,1)S(1)}) custom-call(bf16[128,4096]{1,0:T(8,128)(2,1)S(1)} %queries.1.weights, bf16[3,128,128]{2,1,0:T(8,128)(2,1)S(1)} %pack.1.mine, bf16[3,128,128]{2,1,0:T(8,128)(2,1)S(1)} %collective-permute-done.5.theirs), custom_call_target="tpu_custom_call" | custom-call | flops 268435456 | bytes 1048576 | tf_op jit(solution)/shard_map/scores/pallas_call | solution.py:220
  15.1 1.0 %collective-permute-start.6 = (bf16[1,128,128]{2,1,0:T(8,128)(2,1)S(1)}, bf16[1,128,128]{2,1,0:T(8,128)(2,1)S(1)}, u32[]{:S(2)}, u32[]{:S(2)}) collective-permute-start(bf16[1,128,128]{2,1,0:T(8,128)(2,1)S(1)} %get-tuple-element.28), channel_id=1, source_target_pairs={{0,2},{2,0},{1,3},{3,1},{4,6},{6,4},{5,7},{7,5},{8,10},{10,8},{9,1... | collective-permute-start | bytes 98312 | tf_op jit(solution)/shard_map/ppermute | solution.py:238
  16.1 0.5 %scores.6 = (f32[1,128,128]{2,1,0:T(8,128)S(1)}, bf16[1,128,128]{2,1,0:T(8,128)(2,1)S(1)}) custom-call(bf16[128,4096]{1,0:T(8,128)(2,1)S(1)} %queries.1.weights, bf16[3,128,128]{2,1,0:T(8,128)(2,1)S(1)} %pack.1.mine, bf16[3,128,128]{2,1,0:T(8,128)(2,1)S(1)} %collective-permute-done.5.theirs, f32[1,128,128]{2,1,0:T(8,128)S(1)} %get-tuple-element.25.refs_0_.own), custom_call_target="tpu_custom_call" | custom-call | flops 268435456 | bytes 1048576 | tf_op jit(solution)/shard_map/scores/pallas_call | solution.py:220
  16.6 1.1 %collective-permute-start.8 = (bf16[1,128,128]{2,1,0:T(8,128)(2,1)S(1)}, bf16[1,128,128]{2,1,0:T(8,128)(2,1)S(1)}, u32[]{:S(2)}, u32[]{:S(2)}) collective-permute-start(bf16[1,128,128]{2,1,0:T(8,128)(2,1)S(1)} %get-tuple-element.29), channel_id=1, source_target_pairs={{0,2},{2,0},{1,3},{3,1},{4,6},{6,4},{5,7},{7,5},{8,10},{10,8},{9,1... | collective-permute-start | bytes 98312 | tf_op jit(solution)/shard_map/ppermute | solution.py:238
  17.8 0.5 %scores.7 = (f32[1,128,128]{2,1,0:T(8,128)S(1)}, bf16[1,128,128]{2,1,0:T(8,128)(2,1)S(1)}) custom-call(bf16[128,4096]{1,0:T(8,128)(2,1)S(1)} %queries.1.weights, bf16[3,128,128]{2,1,0:T(8,128)(2,1)S(1)} %pack.1.mine, bf16[3,128,128]{2,1,0:T(8,128)(2,1)S(1)} %collective-permute-done.5.theirs, f32[1,128,128]{2,1,0:T(8,128)S(1)} %get-tuple-element.26.refs_0_.own), custom_call_target="tpu_custom_call" | custom-call | flops 268435456 | bytes 1048576 | tf_op jit(solution)/shard_map/scores/pallas_call | solution.py:220
  18.3 1.0 %collective-permute-start.10 = (bf16[1,128,128]{2,1,0:T(8,128)(2,1)S(1)}, bf16[1,128,128]{2,1,0:T(8,128)(2,1)S(1)}, u32[]{:S(2)}, u32[]{:S(2)}) collective-permute-start(bf16[1,128,128]{2,1,0:T(8,128)(2,1)S(1)} %get-tuple-element.30), channel_id=1, source_target_pairs={{0,2},{2,0},{1,3},{3,1},{4,6},{6,4},{5,7},{7,5},{8,10},{10,8},{9,1... | collective-permute-start | bytes 98312 | tf_op jit(solution)/shard_map/ppermute | solution.py:238
  19.3 0.0 collective-permute-done.1.refs_0_
  19.3 0.0 collective-permute-done.6.refs_0_
  19.4 2.5 %collective-permute-start.7 = (bf16[128,128]{1,0:T(8,128)(2,1)S(1)}, bf16[128,128]{1,0:T(8,128)(2,1)S(1)}, u32[]{:S(2)}, u32[]{:S(2)}) collective-permute-start(bf16[128,128]{1,0:T(8,128)(2,1)S(1)} %layers.5.refs_1_), channel_id=1, source_target_pairs={{0,12},{4,8},{8,4},{12,0},{1,13},{5,9},{9,5},{13,1},{2,14},{6,10},... | collective-permute-start | bytes 98312 | tf_op jit(solution)/shard_map/ppermute | solution.py:193
  21.9 0.0 collective-permute-done.8.refs_0_
  21.9 0.9 %collective-permute-start.9 = (bf16[128,128]{1,0:T(8,128)(2,1)S(1)}, bf16[128,128]{1,0:T(8,128)(2,1)S(1)}, u32[]{:S(2)}, u32[]{:S(2)}) collective-permute-start(bf16[128,128]{1,0:T(8,128)(2,1)S(1)} %layers.6.refs_1_), channel_id=1, source_target_pairs={{0,8},{4,12},{8,0},{12,4},{1,9},{5,13},{9,1},{13,5},{2,10},{6,14},... | collective-permute-start | bytes 98312 | tf_op jit(solution)/shard_map/ppermute | solution.py:193
  22.8 0.0 collective-permute-done.10.refs_0_
  22.8 1.3 %collective-permute-start.11 = (bf16[128,128]{1,0:T(8,128)(2,1)S(1)}, bf16[128,128]{1,0:T(8,128)(2,1)S(1)}, u32[]{:S(2)}, u32[]{:S(2)}) collective-permute-start(bf16[128,128]{1,0:T(8,128)(2,1)S(1)} %layers.7), channel_id=1, source_target_pairs={{0,4},{4,0},{8,12},{12,8},{1,5},{5,1},{9,13},{13,9},{2,6},{6,2},{1... | collective-permute-start | bytes 98312 | tf_op jit(solution)/shard_map/ppermute | solution.py:193
  24.1 1.1 %collective-permute-done.7.block = bf16[128,128]{1,0:T(8,128)(2,1)S(1)} collective-permute-done((bf16[128,128]{1,0:T(8,128)(2,1)S(1)}, bf16[128,128]{1,0:T(8,128)(2,1)S(1)}, u32[]{:S(2)}, u32[]{:S(2)}) %collective-permute-start.7) | collective-permute-done | bytes 32800 | tf_op jit(solution)/shard_map/ppermute | solution.py:193
  25.2 1.7 %collective-permute-done.9.block = bf16[128,128]{1,0:T(8,128)(2,1)S(1)} collective-permute-done((bf16[128,128]{1,0:T(8,128)(2,1)S(1)}, bf16[128,128]{1,0:T(8,128)(2,1)S(1)}, u32[]{:S(2)}, u32[]{:S(2)}) %collective-permute-start.9) | collective-permute-done | bytes 32800 | tf_op jit(solution)/shard_map/ppermute | solution.py:193
  26.9 0.2 collective-permute-done.11.refs_3_
  27.1 0.7 %place.1 = f32[512,128]{1,0:T(8,128)} custom-call(f32[128,128]{1,0:T(8,128)S(1)} %layers.4.refs_1_.refs_0_, f32[128,128]{1,0:T(8,128)S(1)} %keep.2.refs_0_.refs_1_, f32[128,128]{1,0:T(8,128)S(1)} %keep.3.refs_2_, bf16[128,128]{1,0:T(8,128)(2,1)S(1)} %collective-permute-done.11.refs_3_), custom_call_target="tpu_custom_call" | custom-call | tf_op jit(solution)/shard_map/place/pallas_call | solution.py:294
  (7 shorter events, 0.1 us)
Async XLA Ops:
  3.4 8.1 %collective-permute-start.4 = (bf16[128,128]{1,0:T(8,128)(2,1)S(1)}, bf16[128,128]{1,0:T(8,128)(2,1)S(1)}, u32[]{:S(2)}, u32[]{:S(2)}) collective-permute-start(bf16[128,128]{1,0:T(8,128)(2,1)S(1)} %get-tuple-element.22), channel_id=1, source_target_pairs={{0,9},{1,8},{4,13},{5,12},{8,1},{9,0},{12,5},{13,4},{2,11},{3,10},... | collective-permute-start | bytes 98312 | tf_op jit(solution)/shard_map/ppermute | solution.py:197
  6.9 5.2 %collective-permute-start.3 = (bf16[128,128]{1,0:T(8,128)(2,1)S(1)}, bf16[128,128]{1,0:T(8,128)(2,1)S(1)}, u32[]{:S(2)}, u32[]{:S(2)}) collective-permute-start(bf16[128,128]{1,0:T(8,128)(2,1)S(1)} %get-tuple-element.22), channel_id=1, source_target_pairs={{0,13},{1,12},{4,9},{5,8},{8,5},{9,4},{12,1},{13,0},{2,15},{3,14},... | collective-permute-start | bytes 98312 | tf_op jit(solution)/shard_map/ppermute | solution.py:197
  8.5 3.8 %collective-permute-start.2 = (bf16[128,128]{1,0:T(8,128)(2,1)S(1)}, bf16[128,128]{1,0:T(8,128)(2,1)S(1)}, u32[]{:S(2)}, u32[]{:S(2)}) collective-permute-start(bf16[128,128]{1,0:T(8,128)(2,1)S(1)} %get-tuple-element.22), channel_id=1, source_target_pairs={{0,5},{1,4},{4,1},{5,0},{8,13},{9,12},{12,9},{13,8},{2,7},{3,6},{6... | collective-permute-start | bytes 98312 | tf_op jit(solution)/shard_map/ppermute | solution.py:197
  8.8 2.1 %collective-permute-start = (bf16[1,128,128]{2,1,0:T(8,128)(2,1)S(1)}, bf16[1,128,128]{2,1,0:T(8,128)(2,1)S(1)}, u32[]{:S(2)}, u32[]{:S(2)}) collective-permute-start(bf16[1,128,128]{2,1,0:T(8,128)(2,1)S(1)} %bitcast.4), channel_id=1, source_target_pairs={{0,1},{1,0},{2,3},{3,2},{4,5},{5,4},{6,7},{7,6},{8,9},{9,8},{10,11... | collective-permute-start | bytes 98312 | tf_op jit(solution)/shard_map/ppermute | solution.py:215
  12.3 2.2 %collective-permute-start.5 = (bf16[3,128,128]{2,1,0:T(8,128)(2,1)S(1)}, bf16[3,128,128]{2,1,0:T(8,128)(2,1)S(1)}, u32[]{:S(2)}, u32[]{:S(2)}) collective-permute-start(bf16[3,128,128]{2,1,0:T(8,128)(2,1)S(1)} %pack.1.mine), channel_id=1, source_target_pairs={{0,1},{1,0},{2,3},{3,2},{4,5},{5,4},{6,7},{7,6},{8,9},{9,8},{10,11... | collective-permute-start | bytes 294920 | tf_op jit(solution)/shard_map/ppermute | solution.py:215
  13.0 6.3 %collective-permute-start.1 = (bf16[1,128,128]{2,1,0:T(8,128)(2,1)S(1)}, bf16[1,128,128]{2,1,0:T(8,128)(2,1)S(1)}, u32[]{:S(2)}, u32[]{:S(2)}) collective-permute-start(bf16[1,128,128]{2,1,0:T(8,128)(2,1)S(1)} %get-tuple-element.24), channel_id=1, source_target_pairs={{0,2},{2,0},{1,3},{3,1},{4,6},{6,4},{5,7},{7,5},{8,10},{10,8},{9,1... | collective-permute-start | bytes 98312 | tf_op jit(solution)/shard_map/ppermute | solution.py:238
  15.1 4.3 %collective-permute-start.6 = (bf16[1,128,128]{2,1,0:T(8,128)(2,1)S(1)}, bf16[1,128,128]{2,1,0:T(8,128)(2,1)S(1)}, u32[]{:S(2)}, u32[]{:S(2)}) collective-permute-start(bf16[1,128,128]{2,1,0:T(8,128)(2,1)S(1)} %get-tuple-element.28), channel_id=1, source_target_pairs={{0,2},{2,0},{1,3},{3,1},{4,6},{6,4},{5,7},{7,5},{8,10},{10,8},{9,1... | collective-permute-start | bytes 98312 | tf_op jit(solution)/shard_map/ppermute | solution.py:238
  16.6 5.2 %collective-permute-start.8 = (bf16[1,128,128]{2,1,0:T(8,128)(2,1)S(1)}, bf16[1,128,128]{2,1,0:T(8,128)(2,1)S(1)}, u32[]{:S(2)}, u32[]{:S(2)}) collective-permute-start(bf16[1,128,128]{2,1,0:T(8,128)(2,1)S(1)} %get-tuple-element.29), channel_id=1, source_target_pairs={{0,2},{2,0},{1,3},{3,1},{4,6},{6,4},{5,7},{7,5},{8,10},{10,8},{9,1... | collective-permute-start | bytes 98312 | tf_op jit(solution)/shard_map/ppermute | solution.py:238
  18.3 4.5 %collective-permute-start.10 = (bf16[1,128,128]{2,1,0:T(8,128)(2,1)S(1)}, bf16[1,128,128]{2,1,0:T(8,128)(2,1)S(1)}, u32[]{:S(2)}, u32[]{:S(2)}) collective-permute-start(bf16[1,128,128]{2,1,0:T(8,128)(2,1)S(1)} %get-tuple-element.30), channel_id=1, source_target_pairs={{0,2},{2,0},{1,3},{3,1},{4,6},{6,4},{5,7},{7,5},{8,10},{10,8},{9,1... | collective-permute-start | bytes 98312 | tf_op jit(solution)/shard_map/ppermute | solution.py:238
  19.4 5.8 %collective-permute-start.7 = (bf16[128,128]{1,0:T(8,128)(2,1)S(1)}, bf16[128,128]{1,0:T(8,128)(2,1)S(1)}, u32[]{:S(2)}, u32[]{:S(2)}) collective-permute-start(bf16[128,128]{1,0:T(8,128)(2,1)S(1)} %layers.5.refs_1_), channel_id=1, source_target_pairs={{0,12},{4,8},{8,4},{12,0},{1,13},{5,9},{9,5},{13,1},{2,14},{6,10},... | collective-permute-start | bytes 98312 | tf_op jit(solution)/shard_map/ppermute | solution.py:193
  21.9 5.0 %collective-permute-start.9 = (bf16[128,128]{1,0:T(8,128)(2,1)S(1)}, bf16[128,128]{1,0:T(8,128)(2,1)S(1)}, u32[]{:S(2)}, u32[]{:S(2)}) collective-permute-start(bf16[128,128]{1,0:T(8,128)(2,1)S(1)} %layers.6.refs_1_), channel_id=1, source_target_pairs={{0,8},{4,12},{8,0},{12,4},{1,9},{5,13},{9,1},{13,5},{2,10},{6,14},... | collective-permute-start | bytes 98312 | tf_op jit(solution)/shard_map/ppermute | solution.py:193
  22.8 4.3 %collective-permute-start.11 = (bf16[128,128]{1,0:T(8,128)(2,1)S(1)}, bf16[128,128]{1,0:T(8,128)(2,1)S(1)}, u32[]{:S(2)}, u32[]{:S(2)}) collective-permute-start(bf16[128,128]{1,0:T(8,128)(2,1)S(1)} %layers.7), channel_id=1, source_target_pairs={{0,4},{4,0},{8,12},{12,8},{1,5},{5,1},{9,13},{13,9},{2,6},{6,2},{1... | collective-permute-start | bytes 98312 | tf_op jit(solution)/shard_map/ppermute | solution.py:193

commit v8 on v6

--- a/solution.py
+++ b/solution.py
@@ -31,48 +31,48 @@
 
 
 def features_kernel(chunks, *refs):
-    sources, feats, (queries, eigen, basis_in, basis_out) = refs[:8], refs[8], refs[9:13]
-    targets = (*refs[13:17], basis_in, basis_out, queries, eigen)
-    sems = refs[17]
-    tokens, width = targets[0].shape
-    rank = targets[2].shape[0]
-    step = width // chunks
-    first = pl.multiple_of(lax.axis_index("sub") * tokens, tokens)
-
-    def copy(which, chunk=None):
-        source, target = sources[which].at[0], targets[which]
-        if chunk is None:
-            return pltpu.make_async_copy(source, target, sems.at[which, 0])
-        columns = pl.ds(chunk * step, step)
-        return pltpu.make_async_copy(
-            source.at[pl.ds(first, tokens), columns], target.at[:, columns], sems.at[which, chunk]
-        )
-
-    sides = ((0, 2, 4), (1, 3, 5))
-    for rows, proj, basis in sides:
-        copy(proj).start()
-        for chunk in range(chunks):
-            copy(rows, chunk).start()
-        copy(basis).start()
-    for which in (6, 7):
-        copy(which).start()
-    for place, (rows, proj, basis) in enumerate(sides):
-        copy(proj).wait()
-        total = None
-        for chunk in range(chunks):
-            copy(rows, chunk).wait()
-            columns = slice(chunk * step, (chunk + 1) * step)
-            term = nt(targets[proj][:, columns], targets[rows][:, columns])
-            total = term if total is None else total + term
-        copy(basis).wait()
-        turned = jnp.dot(
-            two_terms(targets[basis][...].T),
-            jnp.concatenate([total.astype(BF16)] * 2, axis=0),
-            preferred_element_type=F32,
-        )
-        feats[place * rank:(place + 1) * rank, :] = turned.astype(BF16)
-    for which in (6, 7):
-        copy(which).wait()
+    sides, (queries_hbm, eigen_hbm) = (refs[0:3], refs[3:6]), refs[6:8]
+    feats, queries, eigen, basis_in, basis_out, rows, proj, sems = refs[8:]
+    core = lax.axis_index("sub")
+    step = rows.shape[1] // chunks
+
+    def part(chunk):
+        return pl.ds(chunk * step, step)
+
+    for side, (rows_hbm, proj_hbm, _) in enumerate(sides):
+        @pl.when(core == side)
+        def _():
+            for chunk in range(chunks):
+                for number, (source, target) in enumerate(((proj_hbm, proj), (rows_hbm, rows))):
+                    pltpu.make_async_copy(
+                        source.at[0, :, part(chunk)], target.at[:, part(chunk)], sems.at[number, chunk]
+                    ).start()
+
+    others = [
+        pltpu.make_async_copy(source.at[0], target, sems.at[2 + number, 0])
+        for number, (source, target) in enumerate((
+            (sides[0][2], basis_in), (sides[1][2], basis_out), (eigen_hbm, eigen), (queries_hbm, queries)
+        ))
+    ]
+    for copy in others:
+        copy.start()
+    total = None
+    for chunk in range(chunks):
+        for number, (source, target) in enumerate(((sides[0][1], proj), (sides[0][0], rows))):
+            pltpu.make_async_copy(
+                source.at[0, :, part(chunk)], target.at[:, part(chunk)], sems.at[number, chunk]
+            ).wait()
+        columns = slice(chunk * step, (chunk + 1) * step)
+        term = nt(proj[:, columns], rows[:, columns])
+        total = term if total is None else total + term
+    for copy in others:
+        copy.wait()
+    basis = jnp.where(core == 0, basis_in[...], basis_out[...])
+    feats[...] = jnp.dot(
+        two_terms(basis.T),
+        jnp.concatenate([total.astype(BF16)] * 2, axis=0),
+        preferred_element_type=F32,
+    ).astype(BF16)
 
 
 def pack_kernel(count, *refs):
@@ -80,10 +80,10 @@
         refs[-1][i] = ref[...]
 
 
-def score_block(feats, weights, rank):
-    tokens = feats.shape[1]
-    side_in = feats[:rank, :].astype(F32)
-    side_out = feats[rank:, :].reshape(rank // 16, 16, tokens)
+def score_block(side_in, side_out, weights):
+    rank, tokens = side_in.shape
+    side_in = side_in.astype(F32)
+    side_out = side_out.reshape(rank // 16, 16, tokens)
     total = None
     for part in range(rank // PACK):
         products = []
@@ -123,17 +123,19 @@
         weights[:, part * width:(part + 1) * width] = (turned * scale).astype(BF16)
 
 
-def scores_kernel(layer_size, rank, offsets, places, weights, *refs):
+def scores_kernel(layer_size, offsets, places, weights, mine, theirs, *refs):
     own, away, scores = refs[-layer_size - 1], refs[-layer_size:-1], refs[-1]
     layer, core = lax.axis_index("layer"), lax.axis_index("sub")
-    rows, half = own.shape[1], refs[0].shape[2]
-    for i, (offset, (pair, place)) in enumerate(zip(offsets, places)):
-        feats = jnp.concatenate([refs[2 * pair][place], refs[2 * pair + 1][place]], axis=1)
-        scores[...] = score_block(feats, weights, rank)
-        held = 1 - core if offset else core
+    rows = own.shape[1]
+    for i, (offset, place) in enumerate(zip(offsets, places)):
+        here, there = mine[place], theirs[place]
+        mine_in = (core == 0) == (offset == 0)
+        scores[...] = score_block(
+            jnp.where(mine_in, here, there), jnp.where(mine_in, there, here), weights
+        )
         for k, block in enumerate((own, *away)):
-            first = lax.rem(lax.rem(layer + k, layer_size) * rows + held * half, 2 * half)
-            block[i] = scores[pl.ds(pl.multiple_of(first, rows), rows), :].astype(block.dtype)
+            first = pl.multiple_of(lax.rem(layer + k, layer_size) * rows, rows)
+            block[i] = scores[pl.ds(first, rows), :].astype(block.dtype)
 
 
 def layers_kernel(layer_size, which, own, *refs):
@@ -155,32 +157,29 @@
     tokens, width = inputs.shape[1:]
     count, entries = queries.shape[1:]
     rank = proj_in.shape[1]
-    half = tokens // 2
     chunks = 2
     vmem, hbm = pl.BlockSpec(memory_space=pltpu.VMEM), pl.BlockSpec(memory_space=pltpu.HBM)
     anywhere = pl.BlockSpec(memory_space=pl.ANY)
     params = pltpu.CompilerParams(vmem_limit_bytes=32 << 20)
 
-    sources = (inputs, out_grads, proj_in, proj_out, basis_in, basis_out, queries, eigen)
+    sources = (inputs, proj_in, basis_in, out_grads, proj_out, basis_out, queries, eigen)
     feats, queries, eigen, basis_in, basis_out = pl.pallas_call(
         functools.partial(features_kernel, chunks),
         out_shape=[
-            jax.ShapeDtypeStruct((2 * rank, half), BF16),
+            jax.ShapeDtypeStruct((rank, tokens), BF16),
             jax.ShapeDtypeStruct((count, entries), BF16),
             *[jax.ShapeDtypeStruct((rank, rank), F32)] * 3,
         ],
         in_specs=[hbm] * len(sources),
         out_specs=[vmem] * 5,
         scratch_shapes=[
-            pltpu.VMEM((half, width), BF16),
-            pltpu.VMEM((half, width), BF16),
+            pltpu.VMEM((tokens, width), BF16),
             pltpu.VMEM((rank, width), BF16),
-            pltpu.VMEM((rank, width), BF16),
-            pltpu.SemaphoreType.DMA((len(sources), chunks)),
+            pltpu.SemaphoreType.DMA((6, chunks)),
         ],
         compiler_params=params,
         cost_estimate=pl.CostEstimate(
-            flops=4 * half * rank * width, bytes_accessed=4 * width * (half + rank), transcendentals=0
+            flops=2 * tokens * rank * width, bytes_accessed=2 * width * (tokens + rank), transcendentals=0
         ),
         name="features",
     )(*[pltpu.with_memory_space_constraint(value, pltpu.HBM) for value in sources])
@@ -197,7 +196,6 @@
     gathered = {offset: exchange_across(feats, offset) for offset in range(train_size - 1, 0, -1)}
     gathered[0] = feats
 
-    halves = {}
     weights = pl.pallas_call(
         queries_kernel,
         out_shape=jax.ShapeDtypeStruct((count, entries), BF16),
@@ -211,36 +209,28 @@
         name="queries",
     )(queries, basis_in, basis_out, eigen)
 
-    def swapped(offsets, after):
-        mine = pl.pallas_call(
-            functools.partial(pack_kernel, len(offsets)),
-            out_shape=jax.ShapeDtypeStruct((len(offsets), 2 * rank, half), BF16),
-            in_specs=[vmem] * len(offsets) + [anywhere] * len(after),
-            out_specs=vmem,
-            compiler_params=params,
-            name="pack",
-        )(*[gathered[offset] for offset in offsets], *after)
-        theirs = lax.ppermute(mine, "sub", [(0, 1), (1, 0)])
-        halves.update({offset: (mine, theirs, place) for place, offset in enumerate(offsets)})
-
-    for offsets in ((*near, *far),):
-        swapped(offsets, [weights])
+    order = (*near, *far)
+    mine = pl.pallas_call(
+        functools.partial(pack_kernel, len(order)),
+        out_shape=jax.ShapeDtypeStruct((len(order), rank, tokens), BF16),
+        in_specs=[vmem] * len(order) + [anywhere],
+        out_specs=vmem,
+        compiler_params=params,
+        name="pack",
+    )(*[gathered[offset] for offset in order], weights)
+    theirs = lax.ppermute(mine, "sub", [(0, 1), (1, 0)])
 
     rows = tokens // layer_size
 
     def scored(offsets, after):
-        pairs = list({id(halves[offset][0]): halves[offset][:2] for offset in offsets}.values())
-        places = [
-            (next(i for i, pair in enumerate(pairs) if pair[0] is halves[offset][0]), halves[offset][2])
-            for offset in offsets
-        ]
+        places = [order.index(offset) for offset in offsets]
         own, *away = pl.pallas_call(
-            functools.partial(scores_kernel, layer_size, rank, offsets, places),
+            functools.partial(scores_kernel, layer_size, offsets, places),
             out_shape=[
                 jax.ShapeDtypeStruct((len(offsets), rows, count), BF16 if k else F32)
                 for k in range(layer_size)
             ],
-            in_specs=[vmem] * (1 + 2 * len(pairs)) + [anywhere] * len(after),
+            in_specs=[vmem] * 3 + [anywhere] * len(after),
             out_specs=[vmem] * layer_size,
             scratch_shapes=[pltpu.VMEM((tokens, count), F32)],
             compiler_params=params,
@@ -250,7 +240,7 @@
                 transcendentals=0,
             ),
             name="scores",
-        )(weights, *[half for pair in pairs for half in pair], *after)
+        )(weights, mine, theirs, *after)
         return own, [
             lax.ppermute(block, "layer", [(l, (l + k) % layer_size) for l in range(layer_size)])
             for k, block in enumerate(away, 1)

time: 27.6 us -> 27 us (0.978)
  Pallas kernels: 7.99 us -> 7.51 us
    pallas_call x1, Pallas kernels: 3.44 us -> 2.85 us  [body(): pl.pallas_call(functools.partial(features_kernel, chunks), out_shape=[jax...]
where the time goes in v8:
time: 27 us; the launch traced here: 26.9 us
  starting transfers between devices  12.9 us (48%)
  Pallas kernels  7.51 us (28%)
  waiting for transfers between devices  6.45 us (24%)
    ppermute x3, starting transfers between devices, exchange_across(): return lax.ppermute(value, ('train', 'sub'), pairs)  5.4 us
    ppermute x3, starting transfers between devices, exchange(): lax.ppermute(value, 'train', [(j, j ^ offset) for j in range(train_size)])  4.56 us
    pallas_call x1, Pallas kernels, body(): pl.pallas_call(functools.partial(features_kernel, chunks), out_shape=[jax...  2.85 us
    ppermute x3, waiting for transfers between devices, exchange(): lax.ppermute(value, 'train', [(j, j ^ offset) for j in range(train_size)])  2.69 us
    ppermute x2, starting transfers between devices, scored(): lax.ppermute(block, 'layer', [(l, (l + k) % layer_size) for l in range(la...  2.17 us
    pallas_call x1, Pallas kernels, body(): pl.pallas_call(queries_kernel, out_shape=jax.ShapeDtypeStruct((count, ent...  2.12 us
    pallas_call x2, Pallas kernels, scored(): pl.pallas_call(functools.partial(scores_kernel, layer_size, offsets, plac...  1.76 us
    ppermute x3, waiting for transfers between devices, exchange_across(): return lax.ppermute(value, ('train', 'sub'), pairs)  1.4 us
  transfers between devices with their start and end apart: 9, of which 5 were waited for; matrix products, arithmetic and copies ran while one was open for 0% of the time, Pallas kernels for 11%

profile of v8, /device:TPU:0, one launch (start us, length us, event | category | flops | bytes accessed | tf_op | source)
XLA Modules:
  0.0 26.9 jit_solution(8707387002520076912)
XLA Ops:
  0.0 2.9 %features.1 = (bf16[64,256]{1,0:T(8,128)(2,1)S(1)}, bf16[128,4096]{1,0:T(8,128)(2,1)S(1)}, f32[64,64]{1,0:T(8,128)S(1)}, f32[64,64]{1,0:T(8,128)S(1)}, f32[64,64]{1,0:T(8,128)S(1)}) custom-call(bf16[1,256,4096]{2,1,0:T(8,128)(2,1)} %refs_0_.1, bf16[1,64,4096]{2,1,0:T(8,128)(2,1)} %refs_1_.1, f32[1,64,64]{2,1,0:T(8,128)} %refs_2_.1, ...), custom_call_target="tpu_custom_call" | custom-call | flops 134217728 | bytes 2621440 | tf_op jit(solution)/shard_map/features/pallas_call | solution.py:166
  2.9 3.5 %collective-permute-start.2 = (bf16[64,256]{1,0:T(8,128)(2,1)S(1)}, bf16[64,256]{1,0:T(8,128)(2,1)S(1)}, u32[]{:S(2)}, u32[]{:S(2)}) collective-permute-start(bf16[64,256]{1,0:T(8,128)(2,1)S(1)} %get-tuple-element.18.refs_0_), channel_id=1, source_target_pairs={{0,9},{1,8},{4,13},{5,12},{8,1},{9,0},{12,5},{13,4},{2,11},{3,10},... | collective-permute-start | bytes 98312 | tf_op jit(solution)/shard_map/ppermute | solution.py:192
  6.4 1.6 %collective-permute-start.1 = (bf16[64,256]{1,0:T(8,128)(2,1)S(1)}, bf16[64,256]{1,0:T(8,128)(2,1)S(1)}, u32[]{:S(2)}, u32[]{:S(2)}) collective-permute-start(bf16[64,256]{1,0:T(8,128)(2,1)S(1)} %get-tuple-element.18.refs_0_), channel_id=1, source_target_pairs={{0,13},{1,12},{4,9},{5,8},{8,5},{9,4},{12,1},{13,0},{2,15},{3,14},... | collective-permute-start | bytes 98312 | tf_op jit(solution)/shard_map/ppermute | solution.py:192
  8.0 0.2 collective-permute-start
  8.3 2.1 %queries.1.refs_4_.weights = bf16[128,4096]{1,0:T(8,128)(2,1)S(1)} custom-call(bf16[128,4096]{1,0:T(8,128)(2,1)S(1)} %get-tuple-element.14.queries, f32[64,64]{1,0:T(8,128)S(1)} %get-tuple-element.15.basis_in, f32[64,64]{1,0:T(8,128)S(1)} %get-tuple-element.16.basis_out, f32[64,64]{1,0:T(8,128)S(1)} %get-tuple-element.17.eigen), custom_call_target="tpu_custom_call" | custom-call | flops 536870912 | bytes 2097152 | tf_op jit(solution)/shard_map/queries/pallas_call | solution.py:199
  10.4 0.0 collective-permute-done.2.refs_3_
  10.4 1.3 %collective-permute-done.1.refs_2_ = bf16[64,256]{1,0:T(8,128)(2,1)S(1)} collective-permute-done((bf16[64,256]{1,0:T(8,128)(2,1)S(1)}, bf16[64,256]{1,0:T(8,128)(2,1)S(1)}, u32[]{:S(2)}, u32[]{:S(2)}) %collective-permute-start.1) | collective-permute-done | bytes 32800 | tf_op jit(solution)/shard_map/ppermute | solution.py:192
  11.6 0.1 collective-permute-done.refs_1_
  11.8 0.7 %collective-permute-start.3 = (bf16[4,64,256]{2,1,0:T(8,128)(2,1)S(1)}, bf16[4,64,256]{2,1,0:T(8,128)(2,1)S(1)}, u32[]{:S(2)}, u32[]{:S(2)}) collective-permute-start(bf16[4,64,256]{2,1,0:T(8,128)(2,1)S(1)} %pack.1.mine), channel_id=1, source_target_pairs={{0,1},{1,0},{2,3},{3,2},{4,5},{5,4},{6,7},{7,6},{8,9},{9,8},{10,11... | collective-permute-start | bytes 393224 | tf_op jit(solution)/shard_map/ppermute | solution.py:221
  12.5 1.0 %collective-permute-done.3.theirs = bf16[4,64,256]{2,1,0:T(8,128)(2,1)S(1)} collective-permute-done((bf16[4,64,256]{2,1,0:T(8,128)(2,1)S(1)}, bf16[4,64,256]{2,1,0:T(8,128)(2,1)S(1)}, u32[]{:S(2)}, u32[]{:S(2)}) %collective-permute-start.3) | collective-permute-done | bytes 131104 | tf_op jit(solution)/shard_map/ppermute | solution.py:221
  13.5 0.9 %scores.2 = (f32[2,128,128]{2,1,0:T(8,128)S(1)}, bf16[2,128,128]{2,1,0:T(8,128)(2,1)S(1)}) custom-call(bf16[128,4096]{1,0:T(8,128)(2,1)S(1)} %queries.1.refs_4_.weights, bf16[4,64,256]{2,1,0:T(8,128)(2,1)S(1)} %pack.1.mine, bf16[4,64,256]{2,1,0:T(8,128)(2,1)S(1)} %collective-permute-done.3.theirs), custom_call_target="tpu_custom_call" | custom-call | flops 536870912 | bytes 1048576 | tf_op jit(solution)/shard_map/scores/pallas_call | solution.py:227
  14.4 1.6 %collective-permute-start.4 = (bf16[2,128,128]{2,1,0:T(8,128)(2,1)S(1)}, bf16[2,128,128]{2,1,0:T(8,128)(2,1)S(1)}, u32[]{:S(2)}, u32[]{:S(2)}) collective-permute-start(bf16[2,128,128]{2,1,0:T(8,128)(2,1)S(1)} %get-tuple-element.20), channel_id=1, source_target_pairs={{0,2},{2,0},{1,3},{3,1},{4,6},{6,4},{5,7},{7,5},{8,10},{10,8},{9,1... | collective-permute-start | bytes 196616 | tf_op jit(solution)/shard_map/ppermute | solution.py:245
  16.0 0.9 %scores.3 = (f32[2,128,128]{2,1,0:T(8,128)S(1)}, bf16[2,128,128]{2,1,0:T(8,128)(2,1)S(1)}) custom-call(bf16[128,4096]{1,0:T(8,128)(2,1)S(1)} %queries.1.refs_4_.weights, bf16[4,64,256]{2,1,0:T(8,128)(2,1)S(1)} %pack.1.mine, bf16[4,64,256]{2,1,0:T(8,128)(2,1)S(1)} %collective-permute-done.3.theirs, f32[2,128,128]{2,1,0:T(8,128)S(1)} %get-tuple-element.19.own.refs_0_), custom_call_target="tpu_custom_call" | custom-call | flops 536870912 | bytes 1048576 | tf_op jit(solution)/shard_map/scores/pallas_call | solution.py:227
  16.9 0.6 %collective-permute-start.7 = (bf16[2,128,128]{2,1,0:T(8,128)(2,1)S(1)}, bf16[2,128,128]{2,1,0:T(8,128)(2,1)S(1)}, u32[]{:S(2)}, u32[]{:S(2)}) collective-permute-start(bf16[2,128,128]{2,1,0:T(8,128)(2,1)S(1)} %get-tuple-element.22), channel_id=1, source_target_pairs={{0,2},{2,0},{1,3},{3,1},{4,6},{6,4},{5,7},{7,5},{8,10},{10,8},{9,1... | collective-permute-start | bytes 196616 | tf_op jit(solution)/shard_map/ppermute | solution.py:245
  17.5 1.4 %collective-permute-done.4.refs_0_ = bf16[2,128,128]{2,1,0:T(8,128)(2,1)S(1)} collective-permute-done((bf16[2,128,128]{2,1,0:T(8,128)(2,1)S(1)}, bf16[2,128,128]{2,1,0:T(8,128)(2,1)S(1)}, u32[]{:S(2)}, u32[]{:S(2)}) %collective-permute-start.4) | collective-permute-done | bytes 65568 | tf_op jit(solution)/shard_map/ppermute | solution.py:245
  18.9 2.4 %collective-permute-start.5 = (bf16[128,128]{1,0:T(8,128)(2,1)S(1)}, bf16[128,128]{1,0:T(8,128)(2,1)S(1)}, u32[]{:S(2)}, u32[]{:S(2)}) collective-permute-start(bf16[128,128]{1,0:T(8,128)(2,1)S(1)} %layers.4.refs_1_), channel_id=1, source_target_pairs={{0,12},{4,8},{8,4},{12,0},{1,13},{5,9},{9,5},{13,1},{2,14},{6,10},... | collective-permute-start | bytes 98312 | tf_op jit(solution)/shard_map/ppermute | solution.py:188
  21.3 0.1 collective-permute-start.6
  21.4 0.0 collective-permute-done.7.refs_0_
  21.4 2.1 %collective-permute-start.8 = (bf16[128,128]{1,0:T(8,128)(2,1)S(1)}, bf16[128,128]{1,0:T(8,128)(2,1)S(1)}, u32[]{:S(2)}, u32[]{:S(2)}) collective-permute-start(bf16[128,128]{1,0:T(8,128)(2,1)S(1)} %layers.7), channel_id=1, source_target_pairs={{0,4},{4,0},{8,12},{12,8},{1,5},{5,1},{9,13},{13,9},{2,6},{6,2},{1... | collective-permute-start | bytes 98312 | tf_op jit(solution)/shard_map/ppermute | solution.py:188
  23.5 2.7 %collective-permute-done.6.refs_1_ = bf16[128,128]{1,0:T(8,128)(2,1)S(1)} collective-permute-done((bf16[128,128]{1,0:T(8,128)(2,1)S(1)}, bf16[128,128]{1,0:T(8,128)(2,1)S(1)}, u32[]{:S(2)}, u32[]{:S(2)}) %collective-permute-start.6) | collective-permute-done | bytes 32800 | tf_op jit(solution)/shard_map/ppermute | solution.py:188
  26.2 0.0 collective-permute-done.5.refs_0_
  26.2 0.0 collective-permute-done.8.refs_2_
  26.2 0.7 %place.1 = f32[512,128]{1,0:T(8,128)} custom-call(bf16[128,128]{1,0:T(8,128)(2,1)S(1)} %collective-permute-done.5.refs_0_, bf16[128,128]{1,0:T(8,128)(2,1)S(1)} %collective-permute-done.6.refs_1_, bf16[128,128]{1,0:T(8,128)(2,1)S(1)} %collective-permute-done.8.refs_2_, f32[128,128]{1,0:T(8,128)S(1)} %layers.6.refs_1_.refs_3_), custom_call_target="tpu_custom_call" | custom-call | tf_op jit(solution)/shard_map/place/pallas_call | solution.py:270
  (5 shorter events, 0.0 us)
Async XLA Ops:
  2.9 7.5 %collective-permute-start.2 = (bf16[64,256]{1,0:T(8,128)(2,1)S(1)}, bf16[64,256]{1,0:T(8,128)(2,1)S(1)}, u32[]{:S(2)}, u32[]{:S(2)}) collective-permute-start(bf16[64,256]{1,0:T(8,128)(2,1)S(1)} %get-tuple-element.18.refs_0_), channel_id=1, source_target_pairs={{0,9},{1,8},{4,13},{5,12},{8,1},{9,0},{12,5},{13,4},{2,11},{3,10},... | collective-permute-start | bytes 98312 | tf_op jit(solution)/shard_map/ppermute | solution.py:192
  6.4 5.2 %collective-permute-start.1 = (bf16[64,256]{1,0:T(8,128)(2,1)S(1)}, bf16[64,256]{1,0:T(8,128)(2,1)S(1)}, u32[]{:S(2)}, u32[]{:S(2)}) collective-permute-start(bf16[64,256]{1,0:T(8,128)(2,1)S(1)} %get-tuple-element.18.refs_0_), channel_id=1, source_target_pairs={{0,13},{1,12},{4,9},{5,8},{8,5},{9,4},{12,1},{13,0},{2,15},{3,14},... | collective-permute-start | bytes 98312 | tf_op jit(solution)/shard_map/ppermute | solution.py:192
  8.0 3.8 %collective-permute-start = (bf16[64,256]{1,0:T(8,128)(2,1)S(1)}, bf16[64,256]{1,0:T(8,128)(2,1)S(1)}, u32[]{:S(2)}, u32[]{:S(2)}) collective-permute-start(bf16[64,256]{1,0:T(8,128)(2,1)S(1)} %get-tuple-element.18.refs_0_), channel_id=1, source_target_pairs={{0,5},{1,4},{4,1},{5,0},{8,13},{9,12},{12,9},{13,8},{2,7},{3,6},{6... | collective-permute-start | bytes 98312 | tf_op jit(solution)/shard_map/ppermute | solution.py:192
  11.8 1.7 %collective-permute-start.3 = (bf16[4,64,256]{2,1,0:T(8,128)(2,1)S(1)}, bf16[4,64,256]{2,1,0:T(8,128)(2,1)S(1)}, u32[]{:S(2)}, u32[]{:S(2)}) collective-permute-start(bf16[4,64,256]{2,1,0:T(8,128)(2,1)S(1)} %pack.1.mine), channel_id=1, source_target_pairs={{0,1},{1,0},{2,3},{3,2},{4,5},{5,4},{6,7},{7,6},{8,9},{9,8},{10,11... | collective-permute-start | bytes 393224 | tf_op jit(solution)/shard_map/ppermute | solution.py:221
  14.4 4.4 %collective-permute-start.4 = (bf16[2,128,128]{2,1,0:T(8,128)(2,1)S(1)}, bf16[2,128,128]{2,1,0:T(8,128)(2,1)S(1)}, u32[]{:S(2)}, u32[]{:S(2)}) collective-permute-start(bf16[2,128,128]{2,1,0:T(8,128)(2,1)S(1)} %get-tuple-element.20), channel_id=1, source_target_pairs={{0,2},{2,0},{1,3},{3,1},{4,6},{6,4},{5,7},{7,5},{8,10},{10,8},{9,1... | collective-permute-start | bytes 196616 | tf_op jit(solution)/shard_map/ppermute | solution.py:245
  16.9 4.5 %collective-permute-start.7 = (bf16[2,128,128]{2,1,0:T(8,128)(2,1)S(1)}, bf16[2,128,128]{2,1,0:T(8,128)(2,1)S(1)}, u32[]{:S(2)}, u32[]{:S(2)}) collective-permute-start(bf16[2,128,128]{2,1,0:T(8,128)(2,1)S(1)} %get-tuple-element.22), channel_id=1, source_target_pairs={{0,2},{2,0},{1,3},{3,1},{4,6},{6,4},{5,7},{7,5},{8,10},{10,8},{9,1... | collective-permute-start | bytes 196616 | tf_op jit(solution)/shard_map/ppermute | solution.py:245
  18.9 7.3 %collective-permute-start.5 = (bf16[128,128]{1,0:T(8,128)(2,1)S(1)}, bf16[128,128]{1,0:T(8,128)(2,1)S(1)}, u32[]{:S(2)}, u32[]{:S(2)}) collective-permute-start(bf16[128,128]{1,0:T(8,128)(2,1)S(1)} %layers.4.refs_1_), channel_id=1, source_target_pairs={{0,12},{4,8},{8,4},{12,0},{1,13},{5,9},{9,5},{13,1},{2,14},{6,10},... | collective-permute-start | bytes 98312 | tf_op jit(solution)/shard_map/ppermute | solution.py:188
  21.3 4.9 %collective-permute-start.6 = (bf16[128,128]{1,0:T(8,128)(2,1)S(1)}, bf16[128,128]{1,0:T(8,128)(2,1)S(1)}, u32[]{:S(2)}, u32[]{:S(2)}) collective-permute-start(bf16[128,128]{1,0:T(8,128)(2,1)S(1)} %layers.5.refs_1_), channel_id=1, source_target_pairs={{0,8},{4,12},{8,0},{12,4},{1,9},{5,13},{9,1},{13,5},{2,10},{6,14},... | collective-permute-start | bytes 98312 | tf_op jit(solution)/shard_map/ppermute | solution.py:188
  21.4 4.8 %collective-permute-start.8 = (bf16[128,128]{1,0:T(8,128)(2,1)S(1)}, bf16[128,128]{1,0:T(8,128)(2,1)S(1)}, u32[]{:S(2)}, u32[]{:S(2)}) collective-permute-start(bf16[128,128]{1,0:T(8,128)(2,1)S(1)} %layers.7), channel_id=1, source_target_pairs={{0,4},{4,0},{8,12},{12,8},{1,5},{5,1},{9,13},{13,9},{2,6},{6,2},{1... | collective-permute-start | bytes 98312 | tf_op jit(solution)/shard_map/ppermute | solution.py:188

commit v9 on v8

--- a/solution.py
+++ b/solution.py
@@ -10,6 +10,31 @@
 F32 = jnp.float32
 BF16 = jnp.bfloat16
 PACK = 4
+
+
+def plan(train_size):
+    if train_size == 4:
+        return FEATURE_ROUNDS, SCORE_ROUNDS, FIRST
+    rounds = [
+        tuple((j, j ^ offset) for j in range(train_size)) for offset in range(train_size - 1, 0, -1)
+    ]
+    return rounds, rounds, train_size // 2
+
+
+FEATURE_ROUNDS = [((3, 1), (2, 0)), ((1, 0),), ((3, 0), (0, 2), (1, 3), (2, 1)), ((0, 3), (3, 2)), ((0, 1), (2, 3), (1, 2))]
+SCORE_ROUNDS = [((3, 0), (1, 2)), ((2, 0), (0, 2), (3, 1)), ((2, 1), (1, 0), (0, 3)), ((1, 3), (0, 1), (3, 2)), ((2, 3),)]
+FIRST = 3
+
+
+def lookup(index, values):
+    found = jnp.int32(values[0])
+    for place, value in enumerate(values[1:], 1):
+        found = jnp.where(index == place, jnp.int32(value), found)
+    return found
+
+
+def sources_of(pairs, train_size):
+    return [next((s for s, d in pairs if d == j), -1) for j in range(train_size)]
 
 
 def nt(left, right):
@@ -75,9 +100,20 @@
     ).astype(BF16)
 
 
-def pack_kernel(count, *refs):
-    for i, ref in enumerate(refs[:count]):
-        refs[-1][i] = ref[...]
+def pack_kernel(rounds, *refs):
+    own, arrivals, out = refs[0], refs[1:1 + len(rounds)], refs[-1]
+    train_size = out.shape[0]
+    here = lax.axis_index("train")
+    out[here] = own[...]
+    for pairs, arrival in zip(rounds, arrivals):
+        sources = sources_of(pairs, train_size)
+        source = lookup(here, sources)
+        if min(sources) >= 0:
+            out[source] = arrival[...]
+        else:
+            @pl.when(source >= 0)
+            def _():
+                out[source] = arrival[...]
 
 
 def score_block(side_in, side_out, weights):
@@ -123,13 +159,14 @@
         weights[:, part * width:(part + 1) * width] = (turned * scale).astype(BF16)
 
 
-def scores_kernel(layer_size, offsets, places, weights, mine, theirs, *refs):
+def scores_kernel(layer_size, targets, weights, mine, theirs, *refs):
     own, away, scores = refs[-layer_size - 1], refs[-layer_size:-1], refs[-1]
-    layer, core = lax.axis_index("layer"), lax.axis_index("sub")
+    place, layer, core = (lax.axis_index(name) for name in ("train", "layer", "sub"))
     rows = own.shape[1]
-    for i, (offset, place) in enumerate(zip(offsets, places)):
-        here, there = mine[place], theirs[place]
-        mine_in = (core == 0) == (offset == 0)
+    for i, target in enumerate(targets):
+        slot = lookup(place, target)
+        here, there = mine[slot], theirs[slot]
+        mine_in = (core == 0) == (slot == place)
         scores[...] = score_block(
             jnp.where(mine_in, here, there), jnp.where(mine_in, there, here), weights
         )
@@ -138,18 +175,32 @@
             block[i] = scores[pl.ds(first, rows), :].astype(block.dtype)
 
 
-def layers_kernel(layer_size, which, own, *refs):
+def layers_kernel(layer_size, places, own, *refs):
+    which = places[0] if len(set(places)) == 1 else lookup(lax.axis_index("train"), places)
     total = own[which]
     for other in refs[:layer_size - 1]:
         total = total + other[which].astype(F32)
     refs[-1][...] = total.astype(refs[-1].dtype)
 
 
-def place_kernel(train_size, *refs):
-    arrived, out = refs[:-1], refs[-1]
+def keep_kernel(block, *refs):
+    refs[-1][...] = block[...]
+
+
+def place_kernel(train_size, rounds, own, *refs):
+    arrivals, out = refs[:-1], refs[-1]
     here = lax.axis_index("train")
-    for offset, block in enumerate(reversed(arrived)):
-        out[pl.ds(here ^ offset, block.shape[0], stride=train_size), :] = block[...].astype(F32)
+    rows = own.shape[0]
+    out[pl.ds(here, rows, stride=train_size), :] = own[...]
+    for pairs, arrival in zip(rounds, arrivals):
+        sources = sources_of(pairs, train_size)
+        source = lookup(here, sources)
+        if min(sources) >= 0:
+            out[pl.ds(source, rows, stride=train_size), :] = arrival[...].astype(F32)
+        else:
+            @pl.when(source >= 0)
+            def _():
+                out[pl.ds(source, rows, stride=train_size), :] = arrival[...].astype(F32)
 
 
 def body(inputs, out_grads, proj_in, proj_out, basis_in, basis_out, eigen, queries):
@@ -184,17 +235,29 @@
         name="features",
     )(*[pltpu.with_memory_space_constraint(value, pltpu.HBM) for value in sources])
 
-    def exchange(value, offset):
-        return lax.ppermute(value, "train", [(j, j ^ offset) for j in range(train_size)])
-
-    def exchange_across(value, offset):
-        pairs = [(2 * j + s, 2 * (j ^ offset) + 1 - s) for j in range(train_size) for s in range(2)]
-        return lax.ppermute(value, ("train", "sub"), pairs)
-
-    middle = train_size // 2
-    far, near = tuple(range(train_size - 1, middle - 1, -1)), tuple(range(middle))
-    gathered = {offset: exchange_across(feats, offset) for offset in range(train_size - 1, 0, -1)}
-    gathered[0] = feats
+    feature_rounds, score_rounds, first = plan(train_size)
+
+    def kept(block, after):
+        return pl.pallas_call(
+            keep_kernel,
+            out_shape=jax.ShapeDtypeStruct(block.shape, block.dtype),
+            in_specs=[vmem] + [anywhere] * len(after),
+            out_specs=vmem,
+            compiler_params=params,
+            name="keep",
+        )(block, *after)
+
+    def in_order(blocks):
+        ordered = []
+        for block in blocks[:-1]:
+            ordered.append(kept(block, ordered[-1:]))
+        return ordered + blocks[-1:]
+
+    def across(pairs):
+        cores = [(2 * s + c, 2 * d + 1 - c) for s, d in pairs for c in range(2)]
+        return lax.ppermute(feats, ("train", "sub"), cores)
+
+    gathered = [across(pairs) for pairs in feature_rounds]
 
     weights = pl.pallas_call(
         queries_kernel,
@@ -209,25 +272,23 @@
         name="queries",
     )(queries, basis_in, basis_out, eigen)
 
-    order = (*near, *far)
     mine = pl.pallas_call(
-        functools.partial(pack_kernel, len(order)),
-        out_shape=jax.ShapeDtypeStruct((len(order), rank, tokens), BF16),
-        in_specs=[vmem] * len(order) + [anywhere],
+        functools.partial(pack_kernel, feature_rounds[::-1]),
+        out_shape=jax.ShapeDtypeStruct((train_size, rank, tokens), BF16),
+        in_specs=[vmem] * (1 + len(gathered)) + [anywhere],
         out_specs=vmem,
         compiler_params=params,
         name="pack",
-    )(*[gathered[offset] for offset in order], weights)
+    )(feats, *gathered[::-1], weights)
     theirs = lax.ppermute(mine, "sub", [(0, 1), (1, 0)])
 
     rows = tokens // layer_size
 
-    def scored(offsets, after):
-        places = [order.index(offset) for offset in offsets]
+    def scored(targets, after):
         own, *away = pl.pallas_call(
-            functools.partial(scores_kernel, layer_size, offsets, places),
+            functools.partial(scores_kernel, layer_size, targets),
             out_shape=[
-                jax.ShapeDtypeStruct((len(offsets), rows, count), BF16 if k else F32)
+                jax.ShapeDtypeStruct((len(targets), rows, count), BF16 if k else F32)
                 for k in range(layer_size)
             ],
             in_specs=[vmem] * 3 + [anywhere] * len(after),
@@ -235,7 +296,7 @@
             scratch_shapes=[pltpu.VMEM((tokens, count), F32)],
             compiler_params=params,
             cost_estimate=pl.CostEstimate(
-                flops=2 * len(offsets) * tokens * entries * count,
+                flops=2 * len(targets) * tokens * entries * count,
                 bytes_accessed=2 * count * entries,
                 transcendentals=0,
             ),
@@ -246,35 +307,49 @@
             for k, block in enumerate(away, 1)
         ]
 
-    def summed(which, offset, own, others, after):
+    def summed(places, dtype, own, others, after):
         return pl.pallas_call(
-            functools.partial(layers_kernel, layer_size, which),
-            out_shape=jax.ShapeDtypeStruct((rows, count), BF16 if offset else F32),
+            functools.partial(layers_kernel, layer_size, places),
+            out_shape=jax.ShapeDtypeStruct((rows, count), dtype),
             in_specs=[vmem] * layer_size + [anywhere] * len(after),
             out_specs=vmem,
             compiler_params=params,
             name="layers",
         )(own, *others, *after)
 
-    terms, after = {}, []
-    for offsets in (far, near):
-        own, others = scored(offsets, after)
-        terms.update({offset: (which, offset, own, others) for which, offset in enumerate(offsets)})
-        after = [own]
-    arrived, after = {}, []
-    for offset in (*far, *near):
-        block = summed(*terms[offset], after)
+    def table(rounds, lead):
+        lists = [lead(j) + [d for pairs in rounds for s, d in pairs if s == j] for j in range(train_size)]
+        length = max(len(targets) for targets in lists)
+        return lists, [
+            [targets[i] if i < len(targets) else j for j, targets in enumerate(lists)] for i in range(length)
+        ]
+
+    first_lists, first_targets = table(score_rounds[:first], lambda j: [])
+    last_lists, last_targets = table(score_rounds[first:], lambda j: [j])
+    first_terms = scored(first_targets, [])
+    last_terms = scored(last_targets, first_terms[:1])
+    arrivals, after = [], []
+    for number, pairs in enumerate(score_rounds):
+        lists, terms = (first_lists, first_terms) if number < first else (last_lists, last_terms)
+        if number == first:
+            home = summed([0] * train_size, F32, *last_terms, after)
+            after = [home]
+        targets = dict(pairs)
+        places = [lists[j].index(targets[j]) if j in targets else 0 for j in range(train_size)]
+        block = summed(places, BF16, *terms, after)
         after = [block]
-        arrived[offset] = exchange(block, offset) if offset else block
+        arrivals.append(lax.ppermute(block, "train", pairs))
+    if first >= len(score_rounds):
+        home = summed([0] * train_size, F32, *last_terms, after)
 
     total = pl.pallas_call(
-        functools.partial(place_kernel, train_size),
+        functools.partial(place_kernel, train_size, score_rounds),
         out_shape=jax.ShapeDtypeStruct((rows * train_size, count), F32),
-        in_specs=[vmem] * train_size,
+        in_specs=[vmem] * (1 + len(arrivals)),
         out_specs=vmem,
         compiler_params=params,
         name="place",
-    )(*[arrived[offset] for offset in reversed(range(train_size))])
+    )(home, *in_order(arrivals))
     return total.reshape(rows, train_size, 1, count)
 
 

time: 27 us -> 38.2 us (1.41)
  the two profiles are of different devices: /device:TPU:0 before, /device:TPU:26 now
where the time goes in v9:
time: 38.2 us; the launch traced here: 37.9 us
  starting transfers between devices  21.1 us (55%)
  waiting for transfers between devices  9.05 us (24%)
  Pallas kernels  7.59 us (20%)
    ppermute x5, starting transfers between devices, body(): arrivals.append(lax.ppermute(block, 'train', pairs))  11.2 us
    ppermute x5, starting transfers between devices, across(): return lax.ppermute(feats, ('train', 'sub'), cores)  6.94 us
    ppermute x5, waiting for transfers between devices, body(): arrivals.append(lax.ppermute(block, 'train', pairs))  4.46 us
    pallas_call x1, Pallas kernels, body(): pl.pallas_call(functools.partial(features_kernel, chunks), out_shape=[jax...  2.85 us
    ppermute x2, starting transfers between devices, scored(): lax.ppermute(block, 'layer', [(l, (l + k) % layer_size) for l in range(la...  2.17 us
    pallas_call x1, Pallas kernels, body(): pl.pallas_call(queries_kernel, out_shape=jax.ShapeDtypeStruct((count, ent...  2.11 us
    ppermute x2, waiting for transfers between devices, scored(): lax.ppermute(block, 'layer', [(l, (l + k) % layer_size) for l in range(la...  1.82 us
    ppermute x5, waiting for transfers between devices, across(): return lax.ppermute(feats, ('train', 'sub'), cores)  1.79 us
  transfers between devices with their start and end apart: 13, of which 7 were waited for; matrix products, arithmetic and copies ran while one was open for 0% of the time, Pallas kernels for 8%

profile of v9, /device:TPU:26, one launch (start us, length us, event | category | flops | bytes accessed | tf_op | source)
XLA Modules:
  0.0 37.9 jit_solution(5248339312236421159)
XLA Ops:
  0.0 2.8 %features.1 = (bf16[64,256]{1,0:T(8,128)(2,1)S(1)}, bf16[128,4096]{1,0:T(8,128)(2,1)S(1)}, f32[64,64]{1,0:T(8,128)S(1)}, f32[64,64]{1,0:T(8,128)S(1)}, f32[64,64]{1,0:T(8,128)S(1)}) custom-call(bf16[1,256,4096]{2,1,0:T(8,128)(2,1)} %refs_0_.1, bf16[1,64,4096]{2,1,0:T(8,128)(2,1)} %refs_1_.1, f32[1,64,64]{2,1,0:T(8,128)} %refs_2_.1, ...), custom_call_target="tpu_custom_call" | custom-call | flops 134217728 | bytes 2621440 | tf_op jit(solution)/shard_map/features/pallas_call | solution.py:217
  2.9 1.7 %collective-permute-start.4 = (bf16[64,256]{1,0:T(8,128)(2,1)S(1)}, bf16[64,256]{1,0:T(8,128)(2,1)S(1)}, u32[]{:S(2)}, u32[]{:S(2)}) collective-permute-start(bf16[64,256]{1,0:T(8,128)(2,1)S(1)} %get-tuple-element.18.refs_0_), channel_id=1, source_target_pairs={{12,5},{13,4},{8,1},{9,0},{14,7},{15,6},{10,3},{11,2},{28,21},{29,... | collective-permute-start | bytes 98312 | tf_op jit(solution)/shard_map/ppermute | solution.py:258
  4.5 0.7 %collective-permute-start.3 = (bf16[64,256]{1,0:T(8,128)(2,1)S(1)}, bf16[64,256]{1,0:T(8,128)(2,1)S(1)}, u32[]{:S(2)}, u32[]{:S(2)}) collective-permute-start(bf16[64,256]{1,0:T(8,128)(2,1)S(1)} %get-tuple-element.18.refs_0_), channel_id=1, source_target_pairs={{4,1},{5,0},{6,3},{7,2},{20,17},{21,16},{22,19},{23,18}} | collective-permute-start | bytes 98312 | tf_op jit(solution)/shard_map/ppermute | solution.py:258
  5.2 0.1 collective-permute-start.2
  5.3 3.2 %collective-permute-start.1 = (bf16[64,256]{1,0:T(8,128)(2,1)S(1)}, bf16[64,256]{1,0:T(8,128)(2,1)S(1)}, u32[]{:S(2)}, u32[]{:S(2)}) collective-permute-start(bf16[64,256]{1,0:T(8,128)(2,1)S(1)} %get-tuple-element.18.refs_0_), channel_id=1, source_target_pairs={{0,13},{1,12},{12,9},{13,8},{2,15},{3,14},{14,11},{15,10},{16,29},... | collective-permute-start | bytes 98312 | tf_op jit(solution)/shard_map/ppermute | solution.py:258
  8.5 1.3 %collective-permute-start = (bf16[64,256]{1,0:T(8,128)(2,1)S(1)}, bf16[64,256]{1,0:T(8,128)(2,1)S(1)}, u32[]{:S(2)}, u32[]{:S(2)}) collective-permute-start(bf16[64,256]{1,0:T(8,128)(2,1)S(1)} %get-tuple-element.18.refs_0_), channel_id=1, source_target_pairs={{0,5},{1,4},{8,13},{9,12},{4,9},{5,8},{2,7},{3,6},{10,15},{11,14},... | collective-permute-start | bytes 98312 | tf_op jit(solution)/shard_map/ppermute | solution.py:258
  9.8 2.1 %queries.1.refs_6_.weights = bf16[128,4096]{1,0:T(8,128)(2,1)S(1)} custom-call(bf16[128,4096]{1,0:T(8,128)(2,1)S(1)} %get-tuple-element.14.queries, f32[64,64]{1,0:T(8,128)S(1)} %get-tuple-element.15.basis_in, f32[64,64]{1,0:T(8,128)S(1)} %get-tuple-element.16.basis_out, f32[64,64]{1,0:T(8,128)S(1)} %get-tuple-element.17.eigen), custom_call_target="tpu_custom_call" | custom-call | flops 536870912 | bytes 2097152 | tf_op jit(solution)/shard_map/queries/pallas_call | solution.py:262
  12.0 0.0 collective-permute-done.4.refs_5_
  12.0 0.0 collective-permute-done.3.refs_4_
  12.0 0.0 collective-permute-done.2.refs_3_
  12.0 0.3 collective-permute-done.1.refs_2_
  12.3 1.5 %collective-permute-done.refs_1_ = bf16[64,256]{1,0:T(8,128)(2,1)S(1)} collective-permute-done((bf16[64,256]{1,0:T(8,128)(2,1)S(1)}, bf16[64,256]{1,0:T(8,128)(2,1)S(1)}, u32[]{:S(2)}, u32[]{:S(2)}) %collective-permute-start) | collective-permute-done | bytes 32800 | tf_op jit(solution)/shard_map/ppermute | solution.py:258
  13.8 0.7 %collective-permute-start.5 = (bf16[4,64,256]{2,1,0:T(8,128)(2,1)S(1)}, bf16[4,64,256]{2,1,0:T(8,128)(2,1)S(1)}, u32[]{:S(2)}, u32[]{:S(2)}) collective-permute-start(bf16[4,64,256]{2,1,0:T(8,128)(2,1)S(1)} %pack.1.mine), channel_id=1, source_target_pairs={{0,1},{1,0},{2,3},{3,2},{4,5},{5,4},{6,7},{7,6},{8,9},{9,8},{10,11... | collective-permute-start | bytes 393224 | tf_op jit(solution)/shard_map/ppermute | solution.py:283
  14.5 1.0 %collective-permute-done.5.theirs = bf16[4,64,256]{2,1,0:T(8,128)(2,1)S(1)} collective-permute-done((bf16[4,64,256]{2,1,0:T(8,128)(2,1)S(1)}, bf16[4,64,256]{2,1,0:T(8,128)(2,1)S(1)}, u32[]{:S(2)}, u32[]{:S(2)}) %collective-permute-start.5) | collective-permute-done | bytes 131104 | tf_op jit(solution)/shard_map/ppermute | solution.py:283
  15.5 0.9 %scores.2 = (f32[2,128,128]{2,1,0:T(8,128)S(1)}, bf16[2,128,128]{2,1,0:T(8,128)(2,1)S(1)}) custom-call(bf16[128,4096]{1,0:T(8,128)(2,1)S(1)} %queries.1.refs_6_.weights, bf16[4,64,256]{2,1,0:T(8,128)(2,1)S(1)} %pack.1.mine, bf16[4,64,256]{2,1,0:T(8,128)(2,1)S(1)} %collective-permute-done.5.theirs), custom_call_target="tpu_custom_call" | custom-call | flops 536870912 | bytes 1048576 | tf_op jit(solution)/shard_map/scores/pallas_call | solution.py:288
  16.4 0.4 collective-permute-start.7
  16.8 0.9 %scores.3 = (f32[2,128,128]{2,1,0:T(8,128)S(1)}, bf16[2,128,128]{2,1,0:T(8,128)(2,1)S(1)}) custom-call(bf16[128,4096]{1,0:T(8,128)(2,1)S(1)} %queries.1.refs_6_.weights, bf16[4,64,256]{2,1,0:T(8,128)(2,1)S(1)} %pack.1.mine, bf16[4,64,256]{2,1,0:T(8,128)(2,1)S(1)} %collective-permute-done.5.theirs, f32[2,128,128]{2,1,0:T(8,128)S(1)} %get-tuple-element.19.refs_0_.own), custom_call_target="tpu_custom_call" | custom-call | flops 536870912 | bytes 1048576 | tf_op jit(solution)/shard_map/scores/pallas_call | solution.py:288
  17.7 1.8 %collective-permute-start.6 = (bf16[2,128,128]{2,1,0:T(8,128)(2,1)S(1)}, bf16[2,128,128]{2,1,0:T(8,128)(2,1)S(1)}, u32[]{:S(2)}, u32[]{:S(2)}) collective-permute-start(bf16[2,128,128]{2,1,0:T(8,128)(2,1)S(1)} %get-tuple-element.21), channel_id=1, source_target_pairs={{0,2},{2,0},{1,3},{3,1},{4,6},{6,4},{5,7},{7,5},{8,10},{10,8},{9,1... | collective-permute-start | bytes 196616 | tf_op jit(solution)/shard_map/ppermute | solution.py:306
  19.5 1.8 %collective-permute-done.7.refs_0_ = bf16[2,128,128]{2,1,0:T(8,128)(2,1)S(1)} collective-permute-done((bf16[2,128,128]{2,1,0:T(8,128)(2,1)S(1)}, bf16[2,128,128]{2,1,0:T(8,128)(2,1)S(1)}, u32[]{:S(2)}, u32[]{:S(2)}) %collective-permute-start.7) | collective-permute-done | bytes 65568 | tf_op jit(solution)/shard_map/ppermute | solution.py:306
  21.3 2.5 %collective-permute-start.8 = (bf16[128,128]{1,0:T(8,128)(2,1)S(1)}, bf16[128,128]{1,0:T(8,128)(2,1)S(1)}, u32[]{:S(2)}, u32[]{:S(2)}) collective-permute-start(bf16[128,128]{1,0:T(8,128)(2,1)S(1)} %layers.6.refs_1_), channel_id=1, source_target_pairs={{12,0},{4,8},{13,1},{5,9},{14,2},{6,10},{15,3},{7,11},{28,16},{20,... | collective-permute-start | bytes 98312 | tf_op jit(solution)/shard_map/ppermute | solution.py:341
  23.8 3.7 %collective-permute-start.9 = (bf16[128,128]{1,0:T(8,128)(2,1)S(1)}, bf16[128,128]{1,0:T(8,128)(2,1)S(1)}, u32[]{:S(2)}, u32[]{:S(2)}) collective-permute-start(bf16[128,128]{1,0:T(8,128)(2,1)S(1)} %layers.7.refs_1_), channel_id=1, source_target_pairs={{8,0},{0,8},{12,4},{9,1},{1,9},{13,5},{10,2},{2,10},{14,6},{11,3},... | collective-permute-start | bytes 98312 | tf_op jit(solution)/shard_map/ppermute | solution.py:341
  27.5 1.3 %collective-permute-start.10 = (bf16[128,128]{1,0:T(8,128)(2,1)S(1)}, bf16[128,128]{1,0:T(8,128)(2,1)S(1)}, u32[]{:S(2)}, u32[]{:S(2)}) collective-permute-start(bf16[128,128]{1,0:T(8,128)(2,1)S(1)} %layers.8.refs_1_), channel_id=1, source_target_pairs={{8,4},{4,0},{0,12},{9,5},{5,1},{1,13},{10,6},{6,2},{2,14},{11,7},{... | collective-permute-start | bytes 98312 | tf_op jit(solution)/shard_map/ppermute | solution.py:341
  28.8 0.0 collective-permute-done.6.refs_0_
  28.9 2.5 %collective-permute-start.11 = (bf16[128,128]{1,0:T(8,128)(2,1)S(1)}, bf16[128,128]{1,0:T(8,128)(2,1)S(1)}, u32[]{:S(2)}, u32[]{:S(2)}) collective-permute-start(bf16[128,128]{1,0:T(8,128)(2,1)S(1)} %layers.10.refs_1_), channel_id=1, source_target_pairs={{4,12},{0,4},{12,8},{5,13},{1,5},{13,9},{6,14},{2,6},{14,10},{7,15... | collective-permute-start | bytes 98312 | tf_op jit(solution)/shard_map/ppermute | solution.py:341
  31.4 1.3 %collective-permute-start.12 = (bf16[128,128]{1,0:T(8,128)(2,1)S(1)}, bf16[128,128]{1,0:T(8,128)(2,1)S(1)}, u32[]{:S(2)}, u32[]{:S(2)}) collective-permute-start(bf16[128,128]{1,0:T(8,128)(2,1)S(1)} %layers.11), channel_id=1, source_target_pairs={{8,12},{9,13},{10,14},{11,15},{24,28},{25,29},{26,30},{27,31}} | collective-permute-start | bytes 98312 | tf_op jit(solution)/shard_map/ppermute | solution.py:341
  32.7 0.0 collective-permute-done.8.block
  32.7 0.0 collective-permute-done.9.block
  32.7 2.4 %collective-permute-done.10.block = bf16[128,128]{1,0:T(8,128)(2,1)S(1)} collective-permute-done((bf16[128,128]{1,0:T(8,128)(2,1)S(1)}, bf16[128,128]{1,0:T(8,128)(2,1)S(1)}, u32[]{:S(2)}, u32[]{:S(2)}) %collective-permute-start.10) | collective-permute-done | bytes 32800 | tf_op jit(solution)/shard_map/ppermute | solution.py:341
  35.1 0.5 %collective-permute-done.11.block = bf16[128,128]{1,0:T(8,128)(2,1)S(1)} collective-permute-done((bf16[128,128]{1,0:T(8,128)(2,1)S(1)}, bf16[128,128]{1,0:T(8,128)(2,1)S(1)}, u32[]{:S(2)}, u32[]{:S(2)}) %collective-permute-start.11) | collective-permute-done | bytes 32800 | tf_op jit(solution)/shard_map/ppermute | solution.py:341
  35.6 1.6 %collective-permute-done.12.refs_4_ = bf16[128,128]{1,0:T(8,128)(2,1)S(1)} collective-permute-done((bf16[128,128]{1,0:T(8,128)(2,1)S(1)}, bf16[128,128]{1,0:T(8,128)(2,1)S(1)}, u32[]{:S(2)}, u32[]{:S(2)}) %collective-permute-start.12) | collective-permute-done | bytes 32800 | tf_op jit(solution)/shard_map/ppermute | solution.py:341
  37.2 0.7 %place.1 = f32[512,128]{1,0:T(8,128)} custom-call(f32[128,128]{1,0:T(8,128)S(1)} %layers.9.refs_1_.own, bf16[128,128]{1,0:T(8,128)(2,1)S(1)} %keep.4.refs_0_, bf16[128,128]{1,0:T(8,128)(2,1)S(1)} %keep.5.refs_0_.refs_1_, bf16[128,128]{1,0:T(8,128)(2,1)S(1)} %keep.6.refs_0_.refs_2_, bf16[128,128]{1,0:T(8,128)(2,1)S(1)} %keep.7.refs_3_, ...), custom_call_target="tpu_custom_call" | custom-call | tf_op jit(solution)/shard_map/place/pallas_call | solution.py:345
  (11 shorter events, 0.1 us)
Async XLA Ops:
  2.9 9.1 %collective-permute-start.4 = (bf16[64,256]{1,0:T(8,128)(2,1)S(1)}, bf16[64,256]{1,0:T(8,128)(2,1)S(1)}, u32[]{:S(2)}, u32[]{:S(2)}) collective-permute-start(bf16[64,256]{1,0:T(8,128)(2,1)S(1)} %get-tuple-element.18.refs_0_), channel_id=1, source_target_pairs={{12,5},{13,4},{8,1},{9,0},{14,7},{15,6},{10,3},{11,2},{28,21},{29,... | collective-permute-start | bytes 98312 | tf_op jit(solution)/shard_map/ppermute | solution.py:258
  4.5 7.4 %collective-permute-start.3 = (bf16[64,256]{1,0:T(8,128)(2,1)S(1)}, bf16[64,256]{1,0:T(8,128)(2,1)S(1)}, u32[]{:S(2)}, u32[]{:S(2)}) collective-permute-start(bf16[64,256]{1,0:T(8,128)(2,1)S(1)} %get-tuple-element.18.refs_0_), channel_id=1, source_target_pairs={{4,1},{5,0},{6,3},{7,2},{20,17},{21,16},{22,19},{23,18}} | collective-permute-start | bytes 98312 | tf_op jit(solution)/shard_map/ppermute | solution.py:258
  5.2 6.8 %collective-permute-start.2 = (bf16[64,256]{1,0:T(8,128)(2,1)S(1)}, bf16[64,256]{1,0:T(8,128)(2,1)S(1)}, u32[]{:S(2)}, u32[]{:S(2)}) collective-permute-start(bf16[64,256]{1,0:T(8,128)(2,1)S(1)} %get-tuple-element.18.refs_0_), channel_id=1, source_target_pairs={{12,1},{13,0},{0,9},{1,8},{4,13},{5,12},{8,5},{9,4},{14,3},{15,2},... | collective-permute-start | bytes 98312 | tf_op jit(solution)/shard_map/ppermute | solution.py:258
  5.3 7.0 %collective-permute-start.1 = (bf16[64,256]{1,0:T(8,128)(2,1)S(1)}, bf16[64,256]{1,0:T(8,128)(2,1)S(1)}, u32[]{:S(2)}, u32[]{:S(2)}) collective-permute-start(bf16[64,256]{1,0:T(8,128)(2,1)S(1)} %get-tuple-element.18.refs_0_), channel_id=1, source_target_pairs={{0,13},{1,12},{12,9},{13,8},{2,15},{3,14},{14,11},{15,10},{16,29},... | collective-permute-start | bytes 98312 | tf_op jit(solution)/shard_map/ppermute | solution.py:258
  8.5 5.2 %collective-permute-start = (bf16[64,256]{1,0:T(8,128)(2,1)S(1)}, bf16[64,256]{1,0:T(8,128)(2,1)S(1)}, u32[]{:S(2)}, u32[]{:S(2)}) collective-permute-start(bf16[64,256]{1,0:T(8,128)(2,1)S(1)} %get-tuple-element.18.refs_0_), channel_id=1, source_target_pairs={{0,5},{1,4},{8,13},{9,12},{4,9},{5,8},{2,7},{3,6},{10,15},{11,14},... | collective-permute-start | bytes 98312 | tf_op jit(solution)/shard_map/ppermute | solution.py:258
  13.8 1.7 %collective-permute-start.5 = (bf16[4,64,256]{2,1,0:T(8,128)(2,1)S(1)}, bf16[4,64,256]{2,1,0:T(8,128)(2,1)S(1)}, u32[]{:S(2)}, u32[]{:S(2)}) collective-permute-start(bf16[4,64,256]{2,1,0:T(8,128)(2,1)S(1)} %pack.1.mine), channel_id=1, source_target_pairs={{0,1},{1,0},{2,3},{3,2},{4,5},{5,4},{6,7},{7,6},{8,9},{9,8},{10,11... | collective-permute-start | bytes 393224 | tf_op jit(solution)/shard_map/ppermute | solution.py:283
  16.4 4.9 %collective-permute-start.7 = (bf16[2,128,128]{2,1,0:T(8,128)(2,1)S(1)}, bf16[2,128,128]{2,1,0:T(8,128)(2,1)S(1)}, u32[]{:S(2)}, u32[]{:S(2)}) collective-permute-start(bf16[2,128,128]{2,1,0:T(8,128)(2,1)S(1)} %get-tuple-element.22), channel_id=1, source_target_pairs={{0,2},{2,0},{1,3},{3,1},{4,6},{6,4},{5,7},{7,5},{8,10},{10,8},{9,1... | collective-permute-start | bytes 196616 | tf_op jit(solution)/shard_map/ppermute | solution.py:306
  17.7 11.2 %collective-permute-start.6 = (bf16[2,128,128]{2,1,0:T(8,128)(2,1)S(1)}, bf16[2,128,128]{2,1,0:T(8,128)(2,1)S(1)}, u32[]{:S(2)}, u32[]{:S(2)}) collective-permute-start(bf16[2,128,128]{2,1,0:T(8,128)(2,1)S(1)} %get-tuple-element.21), channel_id=1, source_target_pairs={{0,2},{2,0},{1,3},{3,1},{4,6},{6,4},{5,7},{7,5},{8,10},{10,8},{9,1... | collective-permute-start | bytes 196616 | tf_op jit(solution)/shard_map/ppermute | solution.py:306
  21.3 11.4 %collective-permute-start.8 = (bf16[128,128]{1,0:T(8,128)(2,1)S(1)}, bf16[128,128]{1,0:T(8,128)(2,1)S(1)}, u32[]{:S(2)}, u32[]{:S(2)}) collective-permute-start(bf16[128,128]{1,0:T(8,128)(2,1)S(1)} %layers.6.refs_1_), channel_id=1, source_target_pairs={{12,0},{4,8},{13,1},{5,9},{14,2},{6,10},{15,3},{7,11},{28,16},{20,... | collective-permute-start | bytes 98312 | tf_op jit(solution)/shard_map/ppermute | solution.py:341
  23.8 8.9 %collective-permute-start.9 = (bf16[128,128]{1,0:T(8,128)(2,1)S(1)}, bf16[128,128]{1,0:T(8,128)(2,1)S(1)}, u32[]{:S(2)}, u32[]{:S(2)}) collective-permute-start(bf16[128,128]{1,0:T(8,128)(2,1)S(1)} %layers.7.refs_1_), channel_id=1, source_target_pairs={{8,0},{0,8},{12,4},{9,1},{1,9},{13,5},{10,2},{2,10},{14,6},{11,3},... | collective-permute-start | bytes 98312 | tf_op jit(solution)/shard_map/ppermute | solution.py:341
  27.5 7.6 %collective-permute-start.10 = (bf16[128,128]{1,0:T(8,128)(2,1)S(1)}, bf16[128,128]{1,0:T(8,128)(2,1)S(1)}, u32[]{:S(2)}, u32[]{:S(2)}) collective-permute-start(bf16[128,128]{1,0:T(8,128)(2,1)S(1)} %layers.8.refs_1_), channel_id=1, source_target_pairs={{8,4},{4,0},{0,12},{9,5},{5,1},{1,13},{10,6},{6,2},{2,14},{11,7},{... | collective-permute-start | bytes 98312 | tf_op jit(solution)/shard_map/ppermute | solution.py:341
  28.9 6.7 %collective-permute-start.11 = (bf16[128,128]{1,0:T(8,128)(2,1)S(1)}, bf16[128,128]{1,0:T(8,128)(2,1)S(1)}, u32[]{:S(2)}, u32[]{:S(2)}) collective-permute-start(bf16[128,128]{1,0:T(8,128)(2,1)S(1)} %layers.10.refs_1_), channel_id=1, source_target_pairs={{4,12},{0,4},{12,8},{5,13},{1,5},{13,9},{6,14},{2,6},{14,10},{7,15... | collective-permute-start | bytes 98312 | tf_op jit(solution)/shard_map/ppermute | solution.py:341
  31.4 5.8 %collective-permute-start.12 = (bf16[128,128]{1,0:T(8,128)(2,1)S(1)}, bf16[128,128]{1,0:T(8,128)(2,1)S(1)}, u32[]{:S(2)}, u32[]{:S(2)}) collective-permute-start(bf16[128,128]{1,0:T(8,128)(2,1)S(1)} %layers.11), channel_id=1, source_target_pairs={{8,12},{9,13},{10,14},{11,15},{24,28},{25,29},{26,30},{27,31}} | collective-permute-start | bytes 98312 | tf_op jit(solution)/shard_map/ppermute | solution.py:341

commit v10 on v8

--- a/solution.py
+++ b/solution.py
@@ -65,7 +65,7 @@
         columns = slice(chunk * step, (chunk + 1) * step)
         term = nt(proj[:, columns], rows[:, columns])
         total = term if total is None else total + term
-    for copy in others:
+    for copy in others[:2]:
         copy.wait()
     basis = jnp.where(core == 0, basis_in[...], basis_out[...])
     feats[...] = jnp.dot(
@@ -73,6 +73,8 @@
         jnp.concatenate([total.astype(BF16)] * 2, axis=0),
         preferred_element_type=F32,
     ).astype(BF16)
+    for copy in others[2:]:
+        copy.wait()
 
 
 def pack_kernel(count, *refs):
@@ -145,11 +147,20 @@
     refs[-1][...] = total.astype(refs[-1].dtype)
 
 
-def place_kernel(train_size, *refs):
-    arrived, out = refs[:-1], refs[-1]
+def place_kernel(train_size, pieces, *refs):
+    arrived, out, staged, sems = refs[:train_size], *refs[train_size:]
     here = lax.axis_index("train")
-    for offset, block in enumerate(reversed(arrived)):
-        out[pl.ds(here ^ offset, block.shape[0], stride=train_size), :] = block[...].astype(F32)
+    step = arrived[0].shape[0] // pieces
+    copies = []
+    for piece in range(pieces):
+        rows = pl.ds(piece * step * train_size, step * train_size)
+        for offset, block in enumerate(reversed(arrived)):
+            first = piece * step * train_size + (here ^ offset)
+            staged[pl.ds(first, step, stride=train_size), :] = block[piece * step:(piece + 1) * step, :].astype(F32)
+        copies.append(pltpu.make_async_copy(staged.at[rows, :], out.at[rows, :], sems.at[piece]))
+        copies[-1].start()
+    for copy in copies:
+        copy.wait()
 
 
 def body(inputs, out_grads, proj_in, proj_out, basis_in, basis_out, eigen, queries):
@@ -157,7 +168,7 @@
     tokens, width = inputs.shape[1:]
     count, entries = queries.shape[1:]
     rank = proj_in.shape[1]
-    chunks = 2
+    chunks = 4
     vmem, hbm = pl.BlockSpec(memory_space=pltpu.VMEM), pl.BlockSpec(memory_space=pltpu.HBM)
     anywhere = pl.BlockSpec(memory_space=pl.ANY)
     params = pltpu.CompilerParams(vmem_limit_bytes=32 << 20)
@@ -267,11 +278,13 @@
         after = [block]
         arrived[offset] = exchange(block, offset) if offset else block
 
+    pieces = 2
     total = pl.pallas_call(
-        functools.partial(place_kernel, train_size),
+        functools.partial(place_kernel, train_size, pieces),
         out_shape=jax.ShapeDtypeStruct((rows * train_size, count), F32),
         in_specs=[vmem] * train_size,
-        out_specs=vmem,
+        out_specs=hbm,
+        scratch_shapes=[pltpu.VMEM((rows * train_size, count), F32), pltpu.SemaphoreType.DMA((pieces,))],
         compiler_params=params,
         name="place",
     )(*[arrived[offset] for offset in reversed(range(train_size))])

time: 27 us -> 27.4 us (1.015)
  Pallas kernels: 7.51 us -> 7.83 us
    pallas_call x1, Pallas kernels: 2.85 us -> 3.18 us  [body(): pl.pallas_call(functools.partial(features_kernel, chunks), out_shape=[jax...]
where the time goes in v10:
time: 27.4 us; the launch traced here: 27.2 us
  starting transfers between devices  12.9 us (47%)
  Pallas kernels  7.83 us (29%)
  waiting for transfers between devices  6.47 us (24%)
    ppermute x3, starting transfers between devices, exchange_across(): return lax.ppermute(value, ('train', 'sub'), pairs)  5.4 us
    ppermute x3, starting transfers between devices, exchange(): lax.ppermute(value, 'train', [(j, j ^ offset) for j in range(train_size)])  4.56 us
    pallas_call x1, Pallas kernels, body(): pl.pallas_call(functools.partial(features_kernel, chunks), out_shape=[jax...  3.18 us
    ppermute x3, waiting for transfers between devices, exchange(): lax.ppermute(value, 'train', [(j, j ^ offset) for j in range(train_size)])  2.68 us
    ppermute x2, starting transfers between devices, scored(): lax.ppermute(block, 'layer', [(l, (l + k) % layer_size) for l in range(la...  2.17 us
    pallas_call x1, Pallas kernels, body(): pl.pallas_call(queries_kernel, out_shape=jax.ShapeDtypeStruct((count, ent...  2.11 us
    pallas_call x2, Pallas kernels, scored(): pl.pallas_call(functools.partial(scores_kernel, layer_size, offsets, plac...  1.76 us
    ppermute x3, waiting for transfers between devices, exchange_across(): return lax.ppermute(value, ('train', 'sub'), pairs)  1.42 us
  transfers between devices with their start and end apart: 9, of which 5 were waited for; matrix products, arithmetic and copies ran while one was open for 0% of the time, Pallas kernels for 11%

profile of v10, /device:TPU:0, one launch (start us, length us, event | category | flops | bytes accessed | tf_op | source)
XLA Modules:
  0.0 27.2 jit_solution(10022711038702539710)
XLA Ops:
  0.0 3.2 %features.1 = (bf16[64,256]{1,0:T(8,128)(2,1)S(1)}, bf16[128,4096]{1,0:T(8,128)(2,1)S(1)}, f32[64,64]{1,0:T(8,128)S(1)}, f32[64,64]{1,0:T(8,128)S(1)}, f32[64,64]{1,0:T(8,128)S(1)}) custom-call(bf16[1,256,4096]{2,1,0:T(8,128)(2,1)} %refs_0_.1, bf16[1,64,4096]{2,1,0:T(8,128)(2,1)} %refs_1_.1, f32[1,64,64]{2,1,0:T(8,128)} %refs_2_.1, ...), custom_call_target="tpu_custom_call" | custom-call | flops 134217728 | bytes 2621440 | tf_op jit(solution)/shard_map/features/pallas_call | solution.py:177
  3.2 3.5 %collective-permute-start.2 = (bf16[64,256]{1,0:T(8,128)(2,1)S(1)}, bf16[64,256]{1,0:T(8,128)(2,1)S(1)}, u32[]{:S(2)}, u32[]{:S(2)}) collective-permute-start(bf16[64,256]{1,0:T(8,128)(2,1)S(1)} %get-tuple-element.18.refs_0_), channel_id=1, source_target_pairs={{0,9},{1,8},{4,13},{5,12},{8,1},{9,0},{12,5},{13,4},{2,11},{3,10},... | collective-permute-start | bytes 98312 | tf_op jit(solution)/shard_map/ppermute | solution.py:203
  6.7 1.6 %collective-permute-start.1 = (bf16[64,256]{1,0:T(8,128)(2,1)S(1)}, bf16[64,256]{1,0:T(8,128)(2,1)S(1)}, u32[]{:S(2)}, u32[]{:S(2)}) collective-permute-start(bf16[64,256]{1,0:T(8,128)(2,1)S(1)} %get-tuple-element.18.refs_0_), channel_id=1, source_target_pairs={{0,13},{1,12},{4,9},{5,8},{8,5},{9,4},{12,1},{13,0},{2,15},{3,14},... | collective-permute-start | bytes 98312 | tf_op jit(solution)/shard_map/ppermute | solution.py:203
  8.4 0.2 collective-permute-start
  8.6 2.1 %queries.1.refs_4_.weights = bf16[128,4096]{1,0:T(8,128)(2,1)S(1)} custom-call(bf16[128,4096]{1,0:T(8,128)(2,1)S(1)} %get-tuple-element.14.queries, f32[64,64]{1,0:T(8,128)S(1)} %get-tuple-element.15.basis_in, f32[64,64]{1,0:T(8,128)S(1)} %get-tuple-element.16.basis_out, f32[64,64]{1,0:T(8,128)S(1)} %get-tuple-element.17.eigen), custom_call_target="tpu_custom_call" | custom-call | flops 536870912 | bytes 2097152 | tf_op jit(solution)/shard_map/queries/pallas_call | solution.py:210
  10.7 0.0 collective-permute-done.2.refs_3_
  10.7 1.3 %collective-permute-done.1.refs_2_ = bf16[64,256]{1,0:T(8,128)(2,1)S(1)} collective-permute-done((bf16[64,256]{1,0:T(8,128)(2,1)S(1)}, bf16[64,256]{1,0:T(8,128)(2,1)S(1)}, u32[]{:S(2)}, u32[]{:S(2)}) %collective-permute-start.1) | collective-permute-done | bytes 32800 | tf_op jit(solution)/shard_map/ppermute | solution.py:203
  12.0 0.2 collective-permute-done.refs_1_
  12.2 0.7 %collective-permute-start.3 = (bf16[4,64,256]{2,1,0:T(8,128)(2,1)S(1)}, bf16[4,64,256]{2,1,0:T(8,128)(2,1)S(1)}, u32[]{:S(2)}, u32[]{:S(2)}) collective-permute-start(bf16[4,64,256]{2,1,0:T(8,128)(2,1)S(1)} %pack.1.mine), channel_id=1, source_target_pairs={{0,1},{1,0},{2,3},{3,2},{4,5},{5,4},{6,7},{7,6},{8,9},{9,8},{10,11... | collective-permute-start | bytes 393224 | tf_op jit(solution)/shard_map/ppermute | solution.py:232
  12.9 1.0 %collective-permute-done.3.theirs = bf16[4,64,256]{2,1,0:T(8,128)(2,1)S(1)} collective-permute-done((bf16[4,64,256]{2,1,0:T(8,128)(2,1)S(1)}, bf16[4,64,256]{2,1,0:T(8,128)(2,1)S(1)}, u32[]{:S(2)}, u32[]{:S(2)}) %collective-permute-start.3) | collective-permute-done | bytes 131104 | tf_op jit(solution)/shard_map/ppermute | solution.py:232
  13.9 0.9 %scores.2 = (f32[2,128,128]{2,1,0:T(8,128)S(1)}, bf16[2,128,128]{2,1,0:T(8,128)(2,1)S(1)}) custom-call(bf16[128,4096]{1,0:T(8,128)(2,1)S(1)} %queries.1.refs_4_.weights, bf16[4,64,256]{2,1,0:T(8,128)(2,1)S(1)} %pack.1.mine, bf16[4,64,256]{2,1,0:T(8,128)(2,1)S(1)} %collective-permute-done.3.theirs), custom_call_target="tpu_custom_call" | custom-call | flops 536870912 | bytes 1048576 | tf_op jit(solution)/shard_map/scores/pallas_call | solution.py:238
  14.8 1.6 %collective-permute-start.4 = (bf16[2,128,128]{2,1,0:T(8,128)(2,1)S(1)}, bf16[2,128,128]{2,1,0:T(8,128)(2,1)S(1)}, u32[]{:S(2)}, u32[]{:S(2)}) collective-permute-start(bf16[2,128,128]{2,1,0:T(8,128)(2,1)S(1)} %get-tuple-element.20), channel_id=1, source_target_pairs={{0,2},{2,0},{1,3},{3,1},{4,6},{6,4},{5,7},{7,5},{8,10},{10,8},{9,1... | collective-permute-start | bytes 196616 | tf_op jit(solution)/shard_map/ppermute | solution.py:256
  16.3 0.9 %scores.3 = (f32[2,128,128]{2,1,0:T(8,128)S(1)}, bf16[2,128,128]{2,1,0:T(8,128)(2,1)S(1)}) custom-call(bf16[128,4096]{1,0:T(8,128)(2,1)S(1)} %queries.1.refs_4_.weights, bf16[4,64,256]{2,1,0:T(8,128)(2,1)S(1)} %pack.1.mine, bf16[4,64,256]{2,1,0:T(8,128)(2,1)S(1)} %collective-permute-done.3.theirs, f32[2,128,128]{2,1,0:T(8,128)S(1)} %get-tuple-element.19.own.refs_0_), custom_call_target="tpu_custom_call" | custom-call | flops 536870912 | bytes 1048576 | tf_op jit(solution)/shard_map/scores/pallas_call | solution.py:238
  17.2 0.6 %collective-permute-start.7 = (bf16[2,128,128]{2,1,0:T(8,128)(2,1)S(1)}, bf16[2,128,128]{2,1,0:T(8,128)(2,1)S(1)}, u32[]{:S(2)}, u32[]{:S(2)}) collective-permute-start(bf16[2,128,128]{2,1,0:T(8,128)(2,1)S(1)} %get-tuple-element.22), channel_id=1, source_target_pairs={{0,2},{2,0},{1,3},{3,1},{4,6},{6,4},{5,7},{7,5},{8,10},{10,8},{9,1... | collective-permute-start | bytes 196616 | tf_op jit(solution)/shard_map/ppermute | solution.py:256
  17.8 1.4 %collective-permute-done.4.refs_0_ = bf16[2,128,128]{2,1,0:T(8,128)(2,1)S(1)} collective-permute-done((bf16[2,128,128]{2,1,0:T(8,128)(2,1)S(1)}, bf16[2,128,128]{2,1,0:T(8,128)(2,1)S(1)}, u32[]{:S(2)}, u32[]{:S(2)}) %collective-permute-start.4) | collective-permute-done | bytes 65568 | tf_op jit(solution)/shard_map/ppermute | solution.py:256
  19.2 2.4 %collective-permute-start.5 = (bf16[128,128]{1,0:T(8,128)(2,1)S(1)}, bf16[128,128]{1,0:T(8,128)(2,1)S(1)}, u32[]{:S(2)}, u32[]{:S(2)}) collective-permute-start(bf16[128,128]{1,0:T(8,128)(2,1)S(1)} %layers.4.refs_1_), channel_id=1, source_target_pairs={{0,12},{4,8},{8,4},{12,0},{1,13},{5,9},{9,5},{13,1},{2,14},{6,10},... | collective-permute-start | bytes 98312 | tf_op jit(solution)/shard_map/ppermute | solution.py:199
  21.6 0.1 collective-permute-start.6
  21.7 0.0 collective-permute-done.7.refs_0_
  21.7 2.1 %collective-permute-start.8 = (bf16[128,128]{1,0:T(8,128)(2,1)S(1)}, bf16[128,128]{1,0:T(8,128)(2,1)S(1)}, u32[]{:S(2)}, u32[]{:S(2)}) collective-permute-start(bf16[128,128]{1,0:T(8,128)(2,1)S(1)} %layers.7), channel_id=1, source_target_pairs={{0,4},{4,0},{8,12},{12,8},{1,5},{5,1},{9,13},{13,9},{2,6},{6,2},{1... | collective-permute-start | bytes 98312 | tf_op jit(solution)/shard_map/ppermute | solution.py:199
  23.8 2.7 %collective-permute-done.6.refs_1_ = bf16[128,128]{1,0:T(8,128)(2,1)S(1)} collective-permute-done((bf16[128,128]{1,0:T(8,128)(2,1)S(1)}, bf16[128,128]{1,0:T(8,128)(2,1)S(1)}, u32[]{:S(2)}, u32[]{:S(2)}) %collective-permute-start.6) | collective-permute-done | bytes 32800 | tf_op jit(solution)/shard_map/ppermute | solution.py:199
  26.5 0.0 collective-permute-done.5.refs_0_
  26.5 0.0 collective-permute-done.8.refs_2_
  26.5 0.7 %place.1 = f32[512,128]{1,0:T(8,128)} custom-call(bf16[128,128]{1,0:T(8,128)(2,1)S(1)} %collective-permute-done.5.refs_0_, bf16[128,128]{1,0:T(8,128)(2,1)S(1)} %collective-permute-done.6.refs_1_, bf16[128,128]{1,0:T(8,128)(2,1)S(1)} %collective-permute-done.8.refs_2_, f32[128,128]{1,0:T(8,128)S(1)} %layers.6.refs_1_.refs_3_), custom_call_target="tpu_custom_call" | custom-call | tf_op jit(solution)/shard_map/place/pallas_call | solution.py:282
  (5 shorter events, 0.0 us)
Async XLA Ops:
  3.2 7.5 %collective-permute-start.2 = (bf16[64,256]{1,0:T(8,128)(2,1)S(1)}, bf16[64,256]{1,0:T(8,128)(2,1)S(1)}, u32[]{:S(2)}, u32[]{:S(2)}) collective-permute-start(bf16[64,256]{1,0:T(8,128)(2,1)S(1)} %get-tuple-element.18.refs_0_), channel_id=1, source_target_pairs={{0,9},{1,8},{4,13},{5,12},{8,1},{9,0},{12,5},{13,4},{2,11},{3,10},... | collective-permute-start | bytes 98312 | tf_op jit(solution)/shard_map/ppermute | solution.py:203
  6.7 5.2 %collective-permute-start.1 = (bf16[64,256]{1,0:T(8,128)(2,1)S(1)}, bf16[64,256]{1,0:T(8,128)(2,1)S(1)}, u32[]{:S(2)}, u32[]{:S(2)}) collective-permute-start(bf16[64,256]{1,0:T(8,128)(2,1)S(1)} %get-tuple-element.18.refs_0_), channel_id=1, source_target_pairs={{0,13},{1,12},{4,9},{5,8},{8,5},{9,4},{12,1},{13,0},{2,15},{3,14},... | collective-permute-start | bytes 98312 | tf_op jit(solution)/shard_map/ppermute | solution.py:203
  8.4 3.8 %collective-permute-start = (bf16[64,256]{1,0:T(8,128)(2,1)S(1)}, bf16[64,256]{1,0:T(8,128)(2,1)S(1)}, u32[]{:S(2)}, u32[]{:S(2)}) collective-permute-start(bf16[64,256]{1,0:T(8,128)(2,1)S(1)} %get-tuple-element.18.refs_0_), channel_id=1, source_target_pairs={{0,5},{1,4},{4,1},{5,0},{8,13},{9,12},{12,9},{13,8},{2,7},{3,6},{6... | collective-permute-start | bytes 98312 | tf_op jit(solution)/shard_map/ppermute | solution.py:203
  12.2 1.7 %collective-permute-start.3 = (bf16[4,64,256]{2,1,0:T(8,128)(2,1)S(1)}, bf16[4,64,256]{2,1,0:T(8,128)(2,1)S(1)}, u32[]{:S(2)}, u32[]{:S(2)}) collective-permute-start(bf16[4,64,256]{2,1,0:T(8,128)(2,1)S(1)} %pack.1.mine), channel_id=1, source_target_pairs={{0,1},{1,0},{2,3},{3,2},{4,5},{5,4},{6,7},{7,6},{8,9},{9,8},{10,11... | collective-permute-start | bytes 393224 | tf_op jit(solution)/shard_map/ppermute | solution.py:232
  14.8 4.4 %collective-permute-start.4 = (bf16[2,128,128]{2,1,0:T(8,128)(2,1)S(1)}, bf16[2,128,128]{2,1,0:T(8,128)(2,1)S(1)}, u32[]{:S(2)}, u32[]{:S(2)}) collective-permute-start(bf16[2,128,128]{2,1,0:T(8,128)(2,1)S(1)} %get-tuple-element.20), channel_id=1, source_target_pairs={{0,2},{2,0},{1,3},{3,1},{4,6},{6,4},{5,7},{7,5},{8,10},{10,8},{9,1... | collective-permute-start | bytes 196616 | tf_op jit(solution)/shard_map/ppermute | solution.py:256
  17.2 4.5 %collective-permute-start.7 = (bf16[2,128,128]{2,1,0:T(8,128)(2,1)S(1)}, bf16[2,128,128]{2,1,0:T(8,128)(2,1)S(1)}, u32[]{:S(2)}, u32[]{:S(2)}) collective-permute-start(bf16[2,128,128]{2,1,0:T(8,128)(2,1)S(1)} %get-tuple-element.22), channel_id=1, source_target_pairs={{0,2},{2,0},{1,3},{3,1},{4,6},{6,4},{5,7},{7,5},{8,10},{10,8},{9,1... | collective-permute-start | bytes 196616 | tf_op jit(solution)/shard_map/ppermute | solution.py:256
  19.2 7.3 %collective-permute-start.5 = (bf16[128,128]{1,0:T(8,128)(2,1)S(1)}, bf16[128,128]{1,0:T(8,128)(2,1)S(1)}, u32[]{:S(2)}, u32[]{:S(2)}) collective-permute-start(bf16[128,128]{1,0:T(8,128)(2,1)S(1)} %layers.4.refs_1_), channel_id=1, source_target_pairs={{0,12},{4,8},{8,4},{12,0},{1,13},{5,9},{9,5},{13,1},{2,14},{6,10},... | collective-permute-start | bytes 98312 | tf_op jit(solution)/shard_map/ppermute | solution.py:199
  21.6 4.9 %collective-permute-start.6 = (bf16[128,128]{1,0:T(8,128)(2,1)S(1)}, bf16[128,128]{1,0:T(8,128)(2,1)S(1)}, u32[]{:S(2)}, u32[]{:S(2)}) collective-permute-start(bf16[128,128]{1,0:T(8,128)(2,1)S(1)} %layers.5.refs_1_), channel_id=1, source_target_pairs={{0,8},{4,12},{8,0},{12,4},{1,9},{5,13},{9,1},{13,5},{2,10},{6,14},... | collective-permute-start | bytes 98312 | tf_op jit(solution)/shard_map/ppermute | solution.py:199
  21.7 4.8 %collective-permute-start.8 = (bf16[128,128]{1,0:T(8,128)(2,1)S(1)}, bf16[128,128]{1,0:T(8,128)(2,1)S(1)}, u32[]{:S(2)}, u32[]{:S(2)}) collective-permute-start(bf16[128,128]{1,0:T(8,128)(2,1)S(1)} %layers.7), channel_id=1, source_target_pairs={{0,4},{4,0},{8,12},{12,8},{1,5},{5,1},{9,13},{13,9},{2,6},{6,2},{1... | collective-permute-start | bytes 98312 | tf_op jit(solution)/shard_map/ppermute | solution.py:199

commit v11 on v8

--- a/solution.py
+++ b/solution.py
@@ -31,45 +31,36 @@
 
 
 def features_kernel(chunks, *refs):
-    sides, (queries_hbm, eigen_hbm) = (refs[0:3], refs[3:6]), refs[6:8]
-    feats, queries, eigen, basis_in, basis_out, rows, proj, sems = refs[8:]
+    sides, (feats, rows, proj, basis, sems) = (refs[0:3], refs[3:6]), refs[6:]
     core = lax.axis_index("sub")
     step = rows.shape[1] // chunks
 
-    def part(chunk):
-        return pl.ds(chunk * step, step)
-
-    for side, (rows_hbm, proj_hbm, _) in enumerate(sides):
-        @pl.when(core == side)
+    def copies(side):
+        rows_hbm, proj_hbm, basis_hbm = side
+        pairs = [(proj_hbm.at[0], proj)]
+        for chunk in range(chunks):
+            part = pl.ds(chunk * step, step)
+            pairs.append((rows_hbm.at[0, :, part], rows.at[:, part]))
+        pairs.append((basis_hbm.at[0], basis))
+        return [pltpu.make_async_copy(*pair, sems.at[i]) for i, pair in enumerate(pairs)]
+
+    for number, side in enumerate(sides):
+        @pl.when(core == number)
         def _():
-            for chunk in range(chunks):
-                for number, (source, target) in enumerate(((proj_hbm, proj), (rows_hbm, rows))):
-                    pltpu.make_async_copy(
-                        source.at[0, :, part(chunk)], target.at[:, part(chunk)], sems.at[number, chunk]
-                    ).start()
-
-    others = [
-        pltpu.make_async_copy(source.at[0], target, sems.at[2 + number, 0])
-        for number, (source, target) in enumerate((
-            (sides[0][2], basis_in), (sides[1][2], basis_out), (eigen_hbm, eigen), (queries_hbm, queries)
-        ))
-    ]
-    for copy in others:
-        copy.start()
+            for copy in copies(side):
+                copy.start()
+
+    waits = copies(sides[0])
+    waits[0].wait()
     total = None
     for chunk in range(chunks):
-        for number, (source, target) in enumerate(((sides[0][1], proj), (sides[0][0], rows))):
-            pltpu.make_async_copy(
-                source.at[0, :, part(chunk)], target.at[:, part(chunk)], sems.at[number, chunk]
-            ).wait()
+        waits[1 + chunk].wait()
         columns = slice(chunk * step, (chunk + 1) * step)
         term = nt(proj[:, columns], rows[:, columns])
         total = term if total is None else total + term
-    for copy in others:
-        copy.wait()
-    basis = jnp.where(core == 0, basis_in[...], basis_out[...])
+    waits[-1].wait()
     feats[...] = jnp.dot(
-        two_terms(basis.T),
+        two_terms(basis[...].T),
         jnp.concatenate([total.astype(BF16)] * 2, axis=0),
         preferred_element_type=F32,
     ).astype(BF16)
@@ -162,20 +153,17 @@
     anywhere = pl.BlockSpec(memory_space=pl.ANY)
     params = pltpu.CompilerParams(vmem_limit_bytes=32 << 20)
 
-    sources = (inputs, proj_in, basis_in, out_grads, proj_out, basis_out, queries, eigen)
-    feats, queries, eigen, basis_in, basis_out = pl.pallas_call(
+    sources = (inputs, proj_in, basis_in, out_grads, proj_out, basis_out)
+    feats = pl.pallas_call(
         functools.partial(features_kernel, chunks),
-        out_shape=[
-            jax.ShapeDtypeStruct((rank, tokens), BF16),
-            jax.ShapeDtypeStruct((count, entries), BF16),
-            *[jax.ShapeDtypeStruct((rank, rank), F32)] * 3,
-        ],
+        out_shape=jax.ShapeDtypeStruct((rank, tokens), BF16),
         in_specs=[hbm] * len(sources),
-        out_specs=[vmem] * 5,
+        out_specs=vmem,
         scratch_shapes=[
             pltpu.VMEM((tokens, width), BF16),
             pltpu.VMEM((rank, width), BF16),
-            pltpu.SemaphoreType.DMA((6, chunks)),
+            pltpu.VMEM((rank, rank), F32),
+            pltpu.SemaphoreType.DMA((chunks + 2,)),
         ],
         compiler_params=params,
         cost_estimate=pl.CostEstimate(
@@ -207,7 +195,7 @@
             flops=4 * PACK * count * entries * rank, bytes_accessed=4 * count * entries, transcendentals=0
         ),
         name="queries",
-    )(queries, basis_in, basis_out, eigen)
+    )(queries[0], basis_in[0], basis_out[0], eigen[0])
 
     order = (*near, *far)
     mine = pl.pallas_call(

time: 27 us -> 27.1 us (level)
  no operation moved by 1% of the time
where the time goes in v11:
time: 27.1 us; the launch traced here: 26.9 us
  starting transfers between devices  12.9 us (48%)
  Pallas kernels  7.52 us (28%)
  waiting for transfers between devices  6.44 us (24%)
    ppermute x3, starting transfers between devices, exchange_across(): return lax.ppermute(value, ('train', 'sub'), pairs)  5.42 us
    ppermute x3, starting transfers between devices, exchange(): lax.ppermute(value, 'train', [(j, j ^ offset) for j in range(train_size)])  4.56 us
    pallas_call x1, Pallas kernels, body(): pl.pallas_call(functools.partial(features_kernel, chunks), out_shape=jax....  2.86 us
    ppermute x3, waiting for transfers between devices, exchange(): lax.ppermute(value, 'train', [(j, j ^ offset) for j in range(train_size)])  2.69 us
    ppermute x2, starting transfers between devices, scored(): lax.ppermute(block, 'layer', [(l, (l + k) % layer_size) for l in range(la...  2.18 us
    pallas_call x1, Pallas kernels, body(): pl.pallas_call(queries_kernel, out_shape=jax.ShapeDtypeStruct((count, ent...  2.11 us
    pallas_call x2, Pallas kernels, scored(): pl.pallas_call(functools.partial(scores_kernel, layer_size, offsets, plac...  1.76 us
    ppermute x3, waiting for transfers between devices, exchange_across(): return lax.ppermute(value, ('train', 'sub'), pairs)  1.39 us
  transfers between devices with their start and end apart: 9, of which 5 were waited for; matrix products, arithmetic and copies ran while one was open for 0% of the time, Pallas kernels for 11%

profile of v11, /device:TPU:0, one launch (start us, length us, event | category | flops | bytes accessed | tf_op | source)
XLA Modules:
  0.0 26.9 jit_solution(2820251438652494324)
XLA Ops:
  0.0 0.0 copy-start.2
  0.0 0.0 copy-start.1
  0.0 0.0 copy-start
  0.0 0.0 copy-start.3
  0.0 2.9 %features.1.refs_0_ = bf16[64,256]{1,0:T(8,128)(2,1)S(1)} custom-call(bf16[1,256,4096]{2,1,0:T(8,128)(2,1)} %refs_0_.1, bf16[1,64,4096]{2,1,0:T(8,128)(2,1)} %refs_1_.1, f32[1,64,64]{2,1,0:T(8,128)} %refs_2_.1, bf16[1,256,4096]{2,1,0:T(8,128)(2,1)} %refs_3_.1, bf16[1,64,4096]{2,1,0:T(8,128)(2,1)} %refs_4_.1, f32[1,64,64]{2,1,0:T(8,128)} %refs_5_.1), custom_call_target="tpu_custom_call" | custom-call | flops 134217728 | bytes 2621440 | tf_op jit(solution)/shard_map/features/pallas_call | solution.py:157
  2.9 3.6 %collective-permute-start.2 = (bf16[64,256]{1,0:T(8,128)(2,1)S(1)}, bf16[64,256]{1,0:T(8,128)(2,1)S(1)}, u32[]{:S(2)}, u32[]{:S(2)}) collective-permute-start(bf16[64,256]{1,0:T(8,128)(2,1)S(1)} %features.1.refs_0_), channel_id=1, source_target_pairs={{0,9},{1,8},{4,13},{5,12},{8,1},{9,0},{12,5},{13,4},{2,11},{3,10},... | collective-permute-start | bytes 98312 | tf_op jit(solution)/shard_map/ppermute | solution.py:180
  6.4 1.6 %collective-permute-start.1 = (bf16[64,256]{1,0:T(8,128)(2,1)S(1)}, bf16[64,256]{1,0:T(8,128)(2,1)S(1)}, u32[]{:S(2)}, u32[]{:S(2)}) collective-permute-start(bf16[64,256]{1,0:T(8,128)(2,1)S(1)} %features.1.refs_0_), channel_id=1, source_target_pairs={{0,13},{1,12},{4,9},{5,8},{8,5},{9,4},{12,1},{13,0},{2,15},{3,14},... | collective-permute-start | bytes 98312 | tf_op jit(solution)/shard_map/ppermute | solution.py:180
  8.1 0.2 collective-permute-start
  8.3 0.0 copy-done.2
  8.3 0.0 copy-done.1
  8.3 0.0 copy-done
  8.3 0.0 copy-done.3
  8.3 2.1 %queries.1.refs_4_.weights = bf16[128,4096]{1,0:T(8,128)(2,1)S(1)} custom-call(bf16[128,4096]{1,0:T(8,128)(2,1)S(1)} %bitcast.7, f32[64,64]{1,0:T(8,128)S(1)} %bitcast.8, f32[64,64]{1,0:T(8,128)S(1)} %bitcast.9, f32[64,64]{1,0:T(8,128)S(1)} %bitcast.10), custom_call_target="tpu_custom_call" | custom-call | flops 536870912 | bytes 2097152 | tf_op jit(solution)/shard_map/queries/pallas_call | solution.py:187
  10.4 0.0 collective-permute-done.2.refs_3_
  10.4 1.2 %collective-permute-done.1.refs_2_ = bf16[64,256]{1,0:T(8,128)(2,1)S(1)} collective-permute-done((bf16[64,256]{1,0:T(8,128)(2,1)S(1)}, bf16[64,256]{1,0:T(8,128)(2,1)S(1)}, u32[]{:S(2)}, u32[]{:S(2)}) %collective-permute-start.1) | collective-permute-done | bytes 32800 | tf_op jit(solution)/shard_map/ppermute | solution.py:180
  11.7 0.1 collective-permute-done.refs_1_
  11.8 0.7 %collective-permute-start.3 = (bf16[4,64,256]{2,1,0:T(8,128)(2,1)S(1)}, bf16[4,64,256]{2,1,0:T(8,128)(2,1)S(1)}, u32[]{:S(2)}, u32[]{:S(2)}) collective-permute-start(bf16[4,64,256]{2,1,0:T(8,128)(2,1)S(1)} %pack.1.mine), channel_id=1, source_target_pairs={{0,1},{1,0},{2,3},{3,2},{4,5},{5,4},{6,7},{7,6},{8,9},{9,8},{10,11... | collective-permute-start | bytes 393224 | tf_op jit(solution)/shard_map/ppermute | solution.py:209
  12.6 1.0 %collective-permute-done.3.theirs = bf16[4,64,256]{2,1,0:T(8,128)(2,1)S(1)} collective-permute-done((bf16[4,64,256]{2,1,0:T(8,128)(2,1)S(1)}, bf16[4,64,256]{2,1,0:T(8,128)(2,1)S(1)}, u32[]{:S(2)}, u32[]{:S(2)}) %collective-permute-start.3) | collective-permute-done | bytes 131104 | tf_op jit(solution)/shard_map/ppermute | solution.py:209
  13.6 0.9 %scores.2 = (f32[2,128,128]{2,1,0:T(8,128)S(1)}, bf16[2,128,128]{2,1,0:T(8,128)(2,1)S(1)}) custom-call(bf16[128,4096]{1,0:T(8,128)(2,1)S(1)} %queries.1.refs_4_.weights, bf16[4,64,256]{2,1,0:T(8,128)(2,1)S(1)} %pack.1.mine, bf16[4,64,256]{2,1,0:T(8,128)(2,1)S(1)} %collective-permute-done.3.theirs), custom_call_target="tpu_custom_call" | custom-call | flops 536870912 | bytes 1048576 | tf_op jit(solution)/shard_map/scores/pallas_call | solution.py:215
  14.4 1.6 %collective-permute-start.4 = (bf16[2,128,128]{2,1,0:T(8,128)(2,1)S(1)}, bf16[2,128,128]{2,1,0:T(8,128)(2,1)S(1)}, u32[]{:S(2)}, u32[]{:S(2)}) collective-permute-start(bf16[2,128,128]{2,1,0:T(8,128)(2,1)S(1)} %get-tuple-element.10), channel_id=1, source_target_pairs={{0,2},{2,0},{1,3},{3,1},{4,6},{6,4},{5,7},{7,5},{8,10},{10,8},{9,1... | collective-permute-start | bytes 196616 | tf_op jit(solution)/shard_map/ppermute | solution.py:233
  16.0 0.9 %scores.3 = (f32[2,128,128]{2,1,0:T(8,128)S(1)}, bf16[2,128,128]{2,1,0:T(8,128)(2,1)S(1)}) custom-call(bf16[128,4096]{1,0:T(8,128)(2,1)S(1)} %queries.1.refs_4_.weights, bf16[4,64,256]{2,1,0:T(8,128)(2,1)S(1)} %pack.1.mine, bf16[4,64,256]{2,1,0:T(8,128)(2,1)S(1)} %collective-permute-done.3.theirs, f32[2,128,128]{2,1,0:T(8,128)S(1)} %get-tuple-element.9.own.refs_0_), custom_call_target="tpu_custom_call" | custom-call | flops 536870912 | bytes 1048576 | tf_op jit(solution)/shard_map/scores/pallas_call | solution.py:215
  16.9 0.6 %collective-permute-start.7 = (bf16[2,128,128]{2,1,0:T(8,128)(2,1)S(1)}, bf16[2,128,128]{2,1,0:T(8,128)(2,1)S(1)}, u32[]{:S(2)}, u32[]{:S(2)}) collective-permute-start(bf16[2,128,128]{2,1,0:T(8,128)(2,1)S(1)} %get-tuple-element.12), channel_id=1, source_target_pairs={{0,2},{2,0},{1,3},{3,1},{4,6},{6,4},{5,7},{7,5},{8,10},{10,8},{9,1... | collective-permute-start | bytes 196616 | tf_op jit(solution)/shard_map/ppermute | solution.py:233
  17.5 1.4 %collective-permute-done.4.refs_0_ = bf16[2,128,128]{2,1,0:T(8,128)(2,1)S(1)} collective-permute-done((bf16[2,128,128]{2,1,0:T(8,128)(2,1)S(1)}, bf16[2,128,128]{2,1,0:T(8,128)(2,1)S(1)}, u32[]{:S(2)}, u32[]{:S(2)}) %collective-permute-start.4) | collective-permute-done | bytes 65568 | tf_op jit(solution)/shard_map/ppermute | solution.py:233
  18.9 2.4 %collective-permute-start.5 = (bf16[128,128]{1,0:T(8,128)(2,1)S(1)}, bf16[128,128]{1,0:T(8,128)(2,1)S(1)}, u32[]{:S(2)}, u32[]{:S(2)}) collective-permute-start(bf16[128,128]{1,0:T(8,128)(2,1)S(1)} %layers.4.refs_1_), channel_id=1, source_target_pairs={{0,12},{4,8},{8,4},{12,0},{1,13},{5,9},{9,5},{13,1},{2,14},{6,10},... | collective-permute-start | bytes 98312 | tf_op jit(solution)/shard_map/ppermute | solution.py:176
  21.3 0.1 collective-permute-start.6
  21.4 0.0 collective-permute-done.7.refs_0_
  21.4 2.1 %collective-permute-start.8 = (bf16[128,128]{1,0:T(8,128)(2,1)S(1)}, bf16[128,128]{1,0:T(8,128)(2,1)S(1)}, u32[]{:S(2)}, u32[]{:S(2)}) collective-permute-start(bf16[128,128]{1,0:T(8,128)(2,1)S(1)} %layers.7), channel_id=1, source_target_pairs={{0,4},{4,0},{8,12},{12,8},{1,5},{5,1},{9,13},{13,9},{2,6},{6,2},{1... | collective-permute-start | bytes 98312 | tf_op jit(solution)/shard_map/ppermute | solution.py:176
  23.5 2.7 %collective-permute-done.6.refs_1_ = bf16[128,128]{1,0:T(8,128)(2,1)S(1)} collective-permute-done((bf16[128,128]{1,0:T(8,128)(2,1)S(1)}, bf16[128,128]{1,0:T(8,128)(2,1)S(1)}, u32[]{:S(2)}, u32[]{:S(2)}) %collective-permute-start.6) | collective-permute-done | bytes 32800 | tf_op jit(solution)/shard_map/ppermute | solution.py:176
  26.2 0.0 collective-permute-done.5.refs_0_
  26.2 0.0 collective-permute-done.8.refs_2_
  26.2 0.7 %place.1 = f32[512,128]{1,0:T(8,128)} custom-call(bf16[128,128]{1,0:T(8,128)(2,1)S(1)} %collective-permute-done.5.refs_0_, bf16[128,128]{1,0:T(8,128)(2,1)S(1)} %collective-permute-done.6.refs_1_, bf16[128,128]{1,0:T(8,128)(2,1)S(1)} %collective-permute-done.8.refs_2_, f32[128,128]{1,0:T(8,128)S(1)} %layers.6.refs_1_.refs_3_), custom_call_target="tpu_custom_call" | custom-call | tf_op jit(solution)/shard_map/place/pallas_call | solution.py:258
  (5 shorter events, 0.0 us)
Async XLA Ops:
  0.0 8.3 %copy-start.2 = (f32[1,64,64]{2,1,0:T(8,128)S(1)}, f32[1,64,64]{2,1,0:T(8,128)}, u32[]{:S(2)}) copy-start(f32[1,64,64]{2,1,0:T(8,128)} %refs_5_.1) | copy-start | bytes 49156
  0.0 8.3 %copy-start.1 = (f32[1,64,64]{2,1,0:T(8,128)S(1)}, f32[1,64,64]{2,1,0:T(8,128)}, u32[]{:S(2)}) copy-start(f32[1,64,64]{2,1,0:T(8,128)} %refs_2_.1) | copy-start | bytes 49156
  0.0 8.3 %copy-start = (bf16[1,128,4096]{2,1,0:T(8,128)(2,1)S(1)}, bf16[1,128,4096]{2,1,0:T(8,128)(2,1)}, u32[]{:S(2)}) copy-start(bf16[1,128,4096]{2,1,0:T(8,128)(2,1)} %param.15) | copy-start | bytes 3145732
  0.0 8.3 %copy-start.3 = (f32[1,64,64]{2,1,0:T(8,128)S(1)}, f32[1,64,64]{2,1,0:T(8,128)}, u32[]{:S(2)}) copy-start(f32[1,64,64]{2,1,0:T(8,128)} %param.14) | copy-start | bytes 49156
  2.9 7.6 %collective-permute-start.2 = (bf16[64,256]{1,0:T(8,128)(2,1)S(1)}, bf16[64,256]{1,0:T(8,128)(2,1)S(1)}, u32[]{:S(2)}, u32[]{:S(2)}) collective-permute-start(bf16[64,256]{1,0:T(8,128)(2,1)S(1)} %features.1.refs_0_), channel_id=1, source_target_pairs={{0,9},{1,8},{4,13},{5,12},{8,1},{9,0},{12,5},{13,4},{2,11},{3,10},... | collective-permute-start | bytes 98312 | tf_op jit(solution)/shard_map/ppermute | solution.py:180
  6.4 5.2 %collective-permute-start.1 = (bf16[64,256]{1,0:T(8,128)(2,1)S(1)}, bf16[64,256]{1,0:T(8,128)(2,1)S(1)}, u32[]{:S(2)}, u32[]{:S(2)}) collective-permute-start(bf16[64,256]{1,0:T(8,128)(2,1)S(1)} %features.1.refs_0_), channel_id=1, source_target_pairs={{0,13},{1,12},{4,9},{5,8},{8,5},{9,4},{12,1},{13,0},{2,15},{3,14},... | collective-permute-start | bytes 98312 | tf_op jit(solution)/shard_map/ppermute | solution.py:180
  8.1 3.8 %collective-permute-start = (bf16[64,256]{1,0:T(8,128)(2,1)S(1)}, bf16[64,256]{1,0:T(8,128)(2,1)S(1)}, u32[]{:S(2)}, u32[]{:S(2)}) collective-permute-start(bf16[64,256]{1,0:T(8,128)(2,1)S(1)} %features.1.refs_0_), channel_id=1, source_target_pairs={{0,5},{1,4},{4,1},{5,0},{8,13},{9,12},{12,9},{13,8},{2,7},{3,6},{6... | collective-permute-start | bytes 98312 | tf_op jit(solution)/shard_map/ppermute | solution.py:180
  11.8 1.7 %collective-permute-start.3 = (bf16[4,64,256]{2,1,0:T(8,128)(2,1)S(1)}, bf16[4,64,256]{2,1,0:T(8,128)(2,1)S(1)}, u32[]{:S(2)}, u32[]{:S(2)}) collective-permute-start(bf16[4,64,256]{2,1,0:T(8,128)(2,1)S(1)} %pack.1.mine), channel_id=1, source_target_pairs={{0,1},{1,0},{2,3},{3,2},{4,5},{5,4},{6,7},{7,6},{8,9},{9,8},{10,11... | collective-permute-start | bytes 393224 | tf_op jit(solution)/shard_map/ppermute | solution.py:209
  14.4 4.4 %collective-permute-start.4 = (bf16[2,128,128]{2,1,0:T(8,128)(2,1)S(1)}, bf16[2,128,128]{2,1,0:T(8,128)(2,1)S(1)}, u32[]{:S(2)}, u32[]{:S(2)}) collective-permute-start(bf16[2,128,128]{2,1,0:T(8,128)(2,1)S(1)} %get-tuple-element.10), channel_id=1, source_target_pairs={{0,2},{2,0},{1,3},{3,1},{4,6},{6,4},{5,7},{7,5},{8,10},{10,8},{9,1... | collective-permute-start | bytes 196616 | tf_op jit(solution)/shard_map/ppermute | solution.py:233
  16.9 4.5 %collective-permute-start.7 = (bf16[2,128,128]{2,1,0:T(8,128)(2,1)S(1)}, bf16[2,128,128]{2,1,0:T(8,128)(2,1)S(1)}, u32[]{:S(2)}, u32[]{:S(2)}) collective-permute-start(bf16[2,128,128]{2,1,0:T(8,128)(2,1)S(1)} %get-tuple-element.12), channel_id=1, source_target_pairs={{0,2},{2,0},{1,3},{3,1},{4,6},{6,4},{5,7},{7,5},{8,10},{10,8},{9,1... | collective-permute-start | bytes 196616 | tf_op jit(solution)/shard_map/ppermute | solution.py:233
  18.9 7.3 %collective-permute-start.5 = (bf16[128,128]{1,0:T(8,128)(2,1)S(1)}, bf16[128,128]{1,0:T(8,128)(2,1)S(1)}, u32[]{:S(2)}, u32[]{:S(2)}) collective-permute-start(bf16[128,128]{1,0:T(8,128)(2,1)S(1)} %layers.4.refs_1_), channel_id=1, source_target_pairs={{0,12},{4,8},{8,4},{12,0},{1,13},{5,9},{9,5},{13,1},{2,14},{6,10},... | collective-permute-start | bytes 98312 | tf_op jit(solution)/shard_map/ppermute | solution.py:176
  21.3 4.9 %collective-permute-start.6 = (bf16[128,128]{1,0:T(8,128)(2,1)S(1)}, bf16[128,128]{1,0:T(8,128)(2,1)S(1)}, u32[]{:S(2)}, u32[]{:S(2)}) collective-permute-start(bf16[128,128]{1,0:T(8,128)(2,1)S(1)} %layers.5.refs_1_), channel_id=1, source_target_pairs={{0,8},{4,12},{8,0},{12,4},{1,9},{5,13},{9,1},{13,5},{2,10},{6,14},... | collective-permute-start | bytes 98312 | tf_op jit(solution)/shard_map/ppermute | solution.py:176
  21.4 4.8 %collective-permute-start.8 = (bf16[128,128]{1,0:T(8,128)(2,1)S(1)}, bf16[128,128]{1,0:T(8,128)(2,1)S(1)}, u32[]{:S(2)}, u32[]{:S(2)}) collective-permute-start(bf16[128,128]{1,0:T(8,128)(2,1)S(1)} %layers.7), channel_id=1, source_target_pairs={{0,4},{4,0},{8,12},{12,8},{1,5},{5,1},{9,13},{13,9},{2,6},{6,2},{1... | collective-permute-start | bytes 98312 | tf_op jit(solution)/shard_map/ppermute | solution.py:176

commit v12 on v11

--- a/solution.py
+++ b/solution.py
@@ -33,14 +33,14 @@
 def features_kernel(chunks, *refs):
     sides, (feats, rows, proj, basis, sems) = (refs[0:3], refs[3:6]), refs[6:]
     core = lax.axis_index("sub")
-    step = rows.shape[1] // chunks
+    step = rows.shape[0] // chunks
 
     def copies(side):
         rows_hbm, proj_hbm, basis_hbm = side
         pairs = [(proj_hbm.at[0], proj)]
         for chunk in range(chunks):
             part = pl.ds(chunk * step, step)
-            pairs.append((rows_hbm.at[0, :, part], rows.at[:, part]))
+            pairs.append((rows_hbm.at[0, part], rows.at[part]))
         pairs.append((basis_hbm.at[0], basis))
         return [pltpu.make_async_copy(*pair, sems.at[i]) for i, pair in enumerate(pairs)]
 
@@ -52,16 +52,15 @@
 
     waits = copies(sides[0])
     waits[0].wait()
-    total = None
+    totals = []
     for chunk in range(chunks):
         waits[1 + chunk].wait()
-        columns = slice(chunk * step, (chunk + 1) * step)
-        term = nt(proj[:, columns], rows[:, columns])
-        total = term if total is None else total + term
+        totals.append(nt(proj[...], rows[chunk * step:(chunk + 1) * step, :]).astype(BF16))
+    total = jnp.concatenate(totals, axis=1)
     waits[-1].wait()
     feats[...] = jnp.dot(
         two_terms(basis[...].T),
-        jnp.concatenate([total.astype(BF16)] * 2, axis=0),
+        jnp.concatenate([total] * 2, axis=0),
         preferred_element_type=F32,
     ).astype(BF16)
 

time: 27.1 us -> 27.4 us (1.011)
  no operation moved by 1% of the time
where the time goes in v12:
time: 27.4 us; the launch traced here: 27.2 us
  starting transfers between devices  12.9 us (47%)
  Pallas kernels  7.79 us (28%)
  waiting for transfers between devices  6.44 us (24%)
    ppermute x3, starting transfers between devices, exchange_across(): return lax.ppermute(value, ('train', 'sub'), pairs)  5.41 us
    ppermute x3, starting transfers between devices, exchange(): lax.ppermute(value, 'train', [(j, j ^ offset) for j in range(train_size)])  4.56 us
    pallas_call x1, Pallas kernels, body(): pl.pallas_call(functools.partial(features_kernel, chunks), out_shape=jax....  3.13 us
    ppermute x3, waiting for transfers between devices, exchange(): lax.ppermute(value, 'train', [(j, j ^ offset) for j in range(train_size)])  2.68 us
    ppermute x2, starting transfers between devices, scored(): lax.ppermute(block, 'layer', [(l, (l + k) % layer_size) for l in range(la...  2.17 us
    pallas_call x1, Pallas kernels, body(): pl.pallas_call(queries_kernel, out_shape=jax.ShapeDtypeStruct((count, ent...  2.11 us
    pallas_call x2, Pallas kernels, scored(): pl.pallas_call(functools.partial(scores_kernel, layer_size, offsets, plac...  1.76 us
    ppermute x3, waiting for transfers between devices, exchange_across(): return lax.ppermute(value, ('train', 'sub'), pairs)  1.4 us
  transfers between devices with their start and end apart: 9, of which 5 were waited for; matrix products, arithmetic and copies ran while one was open for 0% of the time, Pallas kernels for 11%

profile of v12, /device:TPU:0, one launch (start us, length us, event | category | flops | bytes accessed | tf_op | source)
XLA Modules:
  0.0 27.2 jit_solution(10897160274544863420)
XLA Ops:
  0.0 0.0 copy-start.2
  0.0 0.0 copy-start.1
  0.0 0.0 copy-start
  0.0 0.0 copy-start.3
  0.0 3.1 %features.1.refs_0_ = bf16[64,256]{1,0:T(8,128)(2,1)S(1)} custom-call(bf16[1,256,4096]{2,1,0:T(8,128)(2,1)} %refs_0_.1, bf16[1,64,4096]{2,1,0:T(8,128)(2,1)} %refs_1_.1, f32[1,64,64]{2,1,0:T(8,128)} %refs_2_.1, bf16[1,256,4096]{2,1,0:T(8,128)(2,1)} %refs_3_.1, bf16[1,64,4096]{2,1,0:T(8,128)(2,1)} %refs_4_.1, f32[1,64,64]{2,1,0:T(8,128)} %refs_5_.1), custom_call_target="tpu_custom_call" | custom-call | flops 134217728 | bytes 2621440 | tf_op jit(solution)/shard_map/features/pallas_call | solution.py:156
  3.1 3.6 %collective-permute-start.2 = (bf16[64,256]{1,0:T(8,128)(2,1)S(1)}, bf16[64,256]{1,0:T(8,128)(2,1)S(1)}, u32[]{:S(2)}, u32[]{:S(2)}) collective-permute-start(bf16[64,256]{1,0:T(8,128)(2,1)S(1)} %features.1.refs_0_), channel_id=1, source_target_pairs={{0,9},{1,8},{4,13},{5,12},{8,1},{9,0},{12,5},{13,4},{2,11},{3,10},... | collective-permute-start | bytes 98312 | tf_op jit(solution)/shard_map/ppermute | solution.py:179
  6.7 1.6 %collective-permute-start.1 = (bf16[64,256]{1,0:T(8,128)(2,1)S(1)}, bf16[64,256]{1,0:T(8,128)(2,1)S(1)}, u32[]{:S(2)}, u32[]{:S(2)}) collective-permute-start(bf16[64,256]{1,0:T(8,128)(2,1)S(1)} %features.1.refs_0_), channel_id=1, source_target_pairs={{0,13},{1,12},{4,9},{5,8},{8,5},{9,4},{12,1},{13,0},{2,15},{3,14},... | collective-permute-start | bytes 98312 | tf_op jit(solution)/shard_map/ppermute | solution.py:179
  8.3 0.2 collective-permute-start
  8.6 0.0 copy-done.2
  8.6 0.0 copy-done.1
  8.6 0.0 copy-done
  8.6 0.0 copy-done.3
  8.6 2.1 %queries.1.refs_4_.weights = bf16[128,4096]{1,0:T(8,128)(2,1)S(1)} custom-call(bf16[128,4096]{1,0:T(8,128)(2,1)S(1)} %bitcast.7, f32[64,64]{1,0:T(8,128)S(1)} %bitcast.8, f32[64,64]{1,0:T(8,128)S(1)} %bitcast.9, f32[64,64]{1,0:T(8,128)S(1)} %bitcast.10), custom_call_target="tpu_custom_call" | custom-call | flops 536870912 | bytes 2097152 | tf_op jit(solution)/shard_map/queries/pallas_call | solution.py:186
  10.7 0.0 collective-permute-done.2.refs_3_
  10.7 1.2 %collective-permute-done.1.refs_2_ = bf16[64,256]{1,0:T(8,128)(2,1)S(1)} collective-permute-done((bf16[64,256]{1,0:T(8,128)(2,1)S(1)}, bf16[64,256]{1,0:T(8,128)(2,1)S(1)}, u32[]{:S(2)}, u32[]{:S(2)}) %collective-permute-start.1) | collective-permute-done | bytes 32800 | tf_op jit(solution)/shard_map/ppermute | solution.py:179
  12.0 0.1 collective-permute-done.refs_1_
  12.1 0.7 %collective-permute-start.3 = (bf16[4,64,256]{2,1,0:T(8,128)(2,1)S(1)}, bf16[4,64,256]{2,1,0:T(8,128)(2,1)S(1)}, u32[]{:S(2)}, u32[]{:S(2)}) collective-permute-start(bf16[4,64,256]{2,1,0:T(8,128)(2,1)S(1)} %pack.1.mine), channel_id=1, source_target_pairs={{0,1},{1,0},{2,3},{3,2},{4,5},{5,4},{6,7},{7,6},{8,9},{9,8},{10,11... | collective-permute-start | bytes 393224 | tf_op jit(solution)/shard_map/ppermute | solution.py:208
  12.9 1.0 %collective-permute-done.3.theirs = bf16[4,64,256]{2,1,0:T(8,128)(2,1)S(1)} collective-permute-done((bf16[4,64,256]{2,1,0:T(8,128)(2,1)S(1)}, bf16[4,64,256]{2,1,0:T(8,128)(2,1)S(1)}, u32[]{:S(2)}, u32[]{:S(2)}) %collective-permute-start.3) | collective-permute-done | bytes 131104 | tf_op jit(solution)/shard_map/ppermute | solution.py:208
  13.8 0.9 %scores.2 = (f32[2,128,128]{2,1,0:T(8,128)S(1)}, bf16[2,128,128]{2,1,0:T(8,128)(2,1)S(1)}) custom-call(bf16[128,4096]{1,0:T(8,128)(2,1)S(1)} %queries.1.refs_4_.weights, bf16[4,64,256]{2,1,0:T(8,128)(2,1)S(1)} %pack.1.mine, bf16[4,64,256]{2,1,0:T(8,128)(2,1)S(1)} %collective-permute-done.3.theirs), custom_call_target="tpu_custom_call" | custom-call | flops 536870912 | bytes 1048576 | tf_op jit(solution)/shard_map/scores/pallas_call | solution.py:214
  14.7 1.6 %collective-permute-start.4 = (bf16[2,128,128]{2,1,0:T(8,128)(2,1)S(1)}, bf16[2,128,128]{2,1,0:T(8,128)(2,1)S(1)}, u32[]{:S(2)}, u32[]{:S(2)}) collective-permute-start(bf16[2,128,128]{2,1,0:T(8,128)(2,1)S(1)} %get-tuple-element.10), channel_id=1, source_target_pairs={{0,2},{2,0},{1,3},{3,1},{4,6},{6,4},{5,7},{7,5},{8,10},{10,8},{9,1... | collective-permute-start | bytes 196616 | tf_op jit(solution)/shard_map/ppermute | solution.py:232
  16.3 0.9 %scores.3 = (f32[2,128,128]{2,1,0:T(8,128)S(1)}, bf16[2,128,128]{2,1,0:T(8,128)(2,1)S(1)}) custom-call(bf16[128,4096]{1,0:T(8,128)(2,1)S(1)} %queries.1.refs_4_.weights, bf16[4,64,256]{2,1,0:T(8,128)(2,1)S(1)} %pack.1.mine, bf16[4,64,256]{2,1,0:T(8,128)(2,1)S(1)} %collective-permute-done.3.theirs, f32[2,128,128]{2,1,0:T(8,128)S(1)} %get-tuple-element.9.own.refs_0_), custom_call_target="tpu_custom_call" | custom-call | flops 536870912 | bytes 1048576 | tf_op jit(solution)/shard_map/scores/pallas_call | solution.py:214
  17.2 0.6 %collective-permute-start.7 = (bf16[2,128,128]{2,1,0:T(8,128)(2,1)S(1)}, bf16[2,128,128]{2,1,0:T(8,128)(2,1)S(1)}, u32[]{:S(2)}, u32[]{:S(2)}) collective-permute-start(bf16[2,128,128]{2,1,0:T(8,128)(2,1)S(1)} %get-tuple-element.12), channel_id=1, source_target_pairs={{0,2},{2,0},{1,3},{3,1},{4,6},{6,4},{5,7},{7,5},{8,10},{10,8},{9,1... | collective-permute-start | bytes 196616 | tf_op jit(solution)/shard_map/ppermute | solution.py:232
  17.8 1.4 %collective-permute-done.4.refs_0_ = bf16[2,128,128]{2,1,0:T(8,128)(2,1)S(1)} collective-permute-done((bf16[2,128,128]{2,1,0:T(8,128)(2,1)S(1)}, bf16[2,128,128]{2,1,0:T(8,128)(2,1)S(1)}, u32[]{:S(2)}, u32[]{:S(2)}) %collective-permute-start.4) | collective-permute-done | bytes 65568 | tf_op jit(solution)/shard_map/ppermute | solution.py:232
  19.2 2.4 %collective-permute-start.5 = (bf16[128,128]{1,0:T(8,128)(2,1)S(1)}, bf16[128,128]{1,0:T(8,128)(2,1)S(1)}, u32[]{:S(2)}, u32[]{:S(2)}) collective-permute-start(bf16[128,128]{1,0:T(8,128)(2,1)S(1)} %layers.4.refs_1_), channel_id=1, source_target_pairs={{0,12},{4,8},{8,4},{12,0},{1,13},{5,9},{9,5},{13,1},{2,14},{6,10},... | collective-permute-start | bytes 98312 | tf_op jit(solution)/shard_map/ppermute | solution.py:175
  21.6 0.1 collective-permute-start.6
  21.7 0.0 collective-permute-done.7.refs_0_
  21.7 2.1 %collective-permute-start.8 = (bf16[128,128]{1,0:T(8,128)(2,1)S(1)}, bf16[128,128]{1,0:T(8,128)(2,1)S(1)}, u32[]{:S(2)}, u32[]{:S(2)}) collective-permute-start(bf16[128,128]{1,0:T(8,128)(2,1)S(1)} %layers.7), channel_id=1, source_target_pairs={{0,4},{4,0},{8,12},{12,8},{1,5},{5,1},{9,13},{13,9},{2,6},{6,2},{1... | collective-permute-start | bytes 98312 | tf_op jit(solution)/shard_map/ppermute | solution.py:175
  23.8 2.7 %collective-permute-done.6.refs_1_ = bf16[128,128]{1,0:T(8,128)(2,1)S(1)} collective-permute-done((bf16[128,128]{1,0:T(8,128)(2,1)S(1)}, bf16[128,128]{1,0:T(8,128)(2,1)S(1)}, u32[]{:S(2)}, u32[]{:S(2)}) %collective-permute-start.6) | collective-permute-done | bytes 32800 | tf_op jit(solution)/shard_map/ppermute | solution.py:175
  26.5 0.0 collective-permute-done.5.refs_0_
  26.5 0.0 collective-permute-done.8.refs_2_
  26.5 0.7 %place.1 = f32[512,128]{1,0:T(8,128)} custom-call(bf16[128,128]{1,0:T(8,128)(2,1)S(1)} %collective-permute-done.5.refs_0_, bf16[128,128]{1,0:T(8,128)(2,1)S(1)} %collective-permute-done.6.refs_1_, bf16[128,128]{1,0:T(8,128)(2,1)S(1)} %collective-permute-done.8.refs_2_, f32[128,128]{1,0:T(8,128)S(1)} %layers.6.refs_1_.refs_3_), custom_call_target="tpu_custom_call" | custom-call | tf_op jit(solution)/shard_map/place/pallas_call | solution.py:257
  (5 shorter events, 0.0 us)
Async XLA Ops:
  0.0 8.6 %copy-start.2 = (f32[1,64,64]{2,1,0:T(8,128)S(1)}, f32[1,64,64]{2,1,0:T(8,128)}, u32[]{:S(2)}) copy-start(f32[1,64,64]{2,1,0:T(8,128)} %refs_5_.1) | copy-start | bytes 49156
  0.0 8.6 %copy-start.1 = (f32[1,64,64]{2,1,0:T(8,128)S(1)}, f32[1,64,64]{2,1,0:T(8,128)}, u32[]{:S(2)}) copy-start(f32[1,64,64]{2,1,0:T(8,128)} %refs_2_.1) | copy-start | bytes 49156
  0.0 8.6 %copy-start = (bf16[1,128,4096]{2,1,0:T(8,128)(2,1)S(1)}, bf16[1,128,4096]{2,1,0:T(8,128)(2,1)}, u32[]{:S(2)}) copy-start(bf16[1,128,4096]{2,1,0:T(8,128)(2,1)} %param.15) | copy-start | bytes 3145732
  0.0 8.6 %copy-start.3 = (f32[1,64,64]{2,1,0:T(8,128)S(1)}, f32[1,64,64]{2,1,0:T(8,128)}, u32[]{:S(2)}) copy-start(f32[1,64,64]{2,1,0:T(8,128)} %param.14) | copy-start | bytes 49156
  3.1 7.6 %collective-permute-start.2 = (bf16[64,256]{1,0:T(8,128)(2,1)S(1)}, bf16[64,256]{1,0:T(8,128)(2,1)S(1)}, u32[]{:S(2)}, u32[]{:S(2)}) collective-permute-start(bf16[64,256]{1,0:T(8,128)(2,1)S(1)} %features.1.refs_0_), channel_id=1, source_target_pairs={{0,9},{1,8},{4,13},{5,12},{8,1},{9,0},{12,5},{13,4},{2,11},{3,10},... | collective-permute-start | bytes 98312 | tf_op jit(solution)/shard_map/ppermute | solution.py:179
  6.7 5.2 %collective-permute-start.1 = (bf16[64,256]{1,0:T(8,128)(2,1)S(1)}, bf16[64,256]{1,0:T(8,128)(2,1)S(1)}, u32[]{:S(2)}, u32[]{:S(2)}) collective-permute-start(bf16[64,256]{1,0:T(8,128)(2,1)S(1)} %features.1.refs_0_), channel_id=1, source_target_pairs={{0,13},{1,12},{4,9},{5,8},{8,5},{9,4},{12,1},{13,0},{2,15},{3,14},... | collective-permute-start | bytes 98312 | tf_op jit(solution)/shard_map/ppermute | solution.py:179
  8.3 3.8 %collective-permute-start = (bf16[64,256]{1,0:T(8,128)(2,1)S(1)}, bf16[64,256]{1,0:T(8,128)(2,1)S(1)}, u32[]{:S(2)}, u32[]{:S(2)}) collective-permute-start(bf16[64,256]{1,0:T(8,128)(2,1)S(1)} %features.1.refs_0_), channel_id=1, source_target_pairs={{0,5},{1,4},{4,1},{5,0},{8,13},{9,12},{12,9},{13,8},{2,7},{3,6},{6... | collective-permute-start | bytes 98312 | tf_op jit(solution)/shard_map/ppermute | solution.py:179
  12.1 1.7 %collective-permute-start.3 = (bf16[4,64,256]{2,1,0:T(8,128)(2,1)S(1)}, bf16[4,64,256]{2,1,0:T(8,128)(2,1)S(1)}, u32[]{:S(2)}, u32[]{:S(2)}) collective-permute-start(bf16[4,64,256]{2,1,0:T(8,128)(2,1)S(1)} %pack.1.mine), channel_id=1, source_target_pairs={{0,1},{1,0},{2,3},{3,2},{4,5},{5,4},{6,7},{7,6},{8,9},{9,8},{10,11... | collective-permute-start | bytes 393224 | tf_op jit(solution)/shard_map/ppermute | solution.py:208
  14.7 4.4 %collective-permute-start.4 = (bf16[2,128,128]{2,1,0:T(8,128)(2,1)S(1)}, bf16[2,128,128]{2,1,0:T(8,128)(2,1)S(1)}, u32[]{:S(2)}, u32[]{:S(2)}) collective-permute-start(bf16[2,128,128]{2,1,0:T(8,128)(2,1)S(1)} %get-tuple-element.10), channel_id=1, source_target_pairs={{0,2},{2,0},{1,3},{3,1},{4,6},{6,4},{5,7},{7,5},{8,10},{10,8},{9,1... | collective-permute-start | bytes 196616 | tf_op jit(solution)/shard_map/ppermute | solution.py:232
  17.2 4.5 %collective-permute-start.7 = (bf16[2,128,128]{2,1,0:T(8,128)(2,1)S(1)}, bf16[2,128,128]{2,1,0:T(8,128)(2,1)S(1)}, u32[]{:S(2)}, u32[]{:S(2)}) collective-permute-start(bf16[2,128,128]{2,1,0:T(8,128)(2,1)S(1)} %get-tuple-element.12), channel_id=1, source_target_pairs={{0,2},{2,0},{1,3},{3,1},{4,6},{6,4},{5,7},{7,5},{8,10},{10,8},{9,1... | collective-permute-start | bytes 196616 | tf_op jit(solution)/shard_map/ppermute | solution.py:232
  19.2 7.3 %collective-permute-start.5 = (bf16[128,128]{1,0:T(8,128)(2,1)S(1)}, bf16[128,128]{1,0:T(8,128)(2,1)S(1)}, u32[]{:S(2)}, u32[]{:S(2)}) collective-permute-start(bf16[128,128]{1,0:T(8,128)(2,1)S(1)} %layers.4.refs_1_), channel_id=1, source_target_pairs={{0,12},{4,8},{8,4},{12,0},{1,13},{5,9},{9,5},{13,1},{2,14},{6,10},... | collective-permute-start | bytes 98312 | tf_op jit(solution)/shard_map/ppermute | solution.py:175
  21.6 4.9 %collective-permute-start.6 = (bf16[128,128]{1,0:T(8,128)(2,1)S(1)}, bf16[128,128]{1,0:T(8,128)(2,1)S(1)}, u32[]{:S(2)}, u32[]{:S(2)}) collective-permute-start(bf16[128,128]{1,0:T(8,128)(2,1)S(1)} %layers.5.refs_1_), channel_id=1, source_target_pairs={{0,8},{4,12},{8,0},{12,4},{1,9},{5,13},{9,1},{13,5},{2,10},{6,14},... | collective-permute-start | bytes 98312 | tf_op jit(solution)/shard_map/ppermute | solution.py:175
  21.7 4.8 %collective-permute-start.8 = (bf16[128,128]{1,0:T(8,128)(2,1)S(1)}, bf16[128,128]{1,0:T(8,128)(2,1)S(1)}, u32[]{:S(2)}, u32[]{:S(2)}) collective-permute-start(bf16[128,128]{1,0:T(8,128)(2,1)S(1)} %layers.7), channel_id=1, source_target_pairs={{0,4},{4,0},{8,12},{12,8},{1,5},{5,1},{9,13},{13,9},{2,6},{6,2},{1... | collective-permute-start | bytes 98312 | tf_op jit(solution)/shard_map/ppermute | solution.py:175

commit v13 on v11

--- a/solution.py
+++ b/solution.py
@@ -56,13 +56,11 @@
     for chunk in range(chunks):
         waits[1 + chunk].wait()
         columns = slice(chunk * step, (chunk + 1) * step)
-        term = nt(proj[:, columns], rows[:, columns])
+        term = nt(rows[:, columns], proj[:, columns])
         total = term if total is None else total + term
     waits[-1].wait()
-    feats[...] = jnp.dot(
-        two_terms(basis[...].T),
-        jnp.concatenate([total.astype(BF16)] * 2, axis=0),
-        preferred_element_type=F32,
+    feats[...] = nt(
+        two_terms(basis[...].T), jnp.concatenate([total.astype(BF16)] * 2, axis=1)
     ).astype(BF16)
 
 

time: 27.1 us -> 27 us (level)
  no operation moved by 1% of the time
where the time goes in v13:
time: 27 us; the launch traced here: 26.9 us
  starting transfers between devices  12.9 us (48%)
  Pallas kernels  7.47 us (28%)
  waiting for transfers between devices  6.44 us (24%)
    ppermute x3, starting transfers between devices, exchange_across(): return lax.ppermute(value, ('train', 'sub'), pairs)  5.42 us
    ppermute x3, starting transfers between devices, exchange(): lax.ppermute(value, 'train', [(j, j ^ offset) for j in range(train_size)])  4.56 us
    pallas_call x1, Pallas kernels, body(): pl.pallas_call(functools.partial(features_kernel, chunks), out_shape=jax....  2.81 us
    ppermute x3, waiting for transfers between devices, exchange(): lax.ppermute(value, 'train', [(j, j ^ offset) for j in range(train_size)])  2.7 us
    ppermute x2, starting transfers between devices, scored(): lax.ppermute(block, 'layer', [(l, (l + k) % layer_size) for l in range(la...  2.17 us
    pallas_call x1, Pallas kernels, body(): pl.pallas_call(queries_kernel, out_shape=jax.ShapeDtypeStruct((count, ent...  2.12 us
    pallas_call x2, Pallas kernels, scored(): pl.pallas_call(functools.partial(scores_kernel, layer_size, offsets, plac...  1.76 us
    ppermute x3, waiting for transfers between devices, exchange_across(): return lax.ppermute(value, ('train', 'sub'), pairs)  1.39 us
  transfers between devices with their start and end apart: 9, of which 5 were waited for; matrix products, arithmetic and copies ran while one was open for 0% of the time, Pallas kernels for 11%

profile of v13, /device:TPU:0, one launch (start us, length us, event | category | flops | bytes accessed | tf_op | source)
XLA Modules:
  0.0 26.9 jit_solution(17995444134482406449)
XLA Ops:
  0.0 0.0 copy-start.2
  0.0 0.0 copy-start.1
  0.0 0.0 copy-start
  0.0 0.0 copy-start.3
  0.0 2.8 %features.1.refs_0_ = bf16[64,256]{1,0:T(8,128)(2,1)S(1)} custom-call(bf16[1,256,4096]{2,1,0:T(8,128)(2,1)} %refs_0_.1, bf16[1,64,4096]{2,1,0:T(8,128)(2,1)} %refs_1_.1, f32[1,64,64]{2,1,0:T(8,128)} %refs_2_.1, bf16[1,256,4096]{2,1,0:T(8,128)(2,1)} %refs_3_.1, bf16[1,64,4096]{2,1,0:T(8,128)(2,1)} %refs_4_.1, f32[1,64,64]{2,1,0:T(8,128)} %refs_5_.1), custom_call_target="tpu_custom_call" | custom-call | flops 134217728 | bytes 2621440 | tf_op jit(solution)/shard_map/features/pallas_call | solution.py:155
  2.8 3.6 %collective-permute-start.2 = (bf16[64,256]{1,0:T(8,128)(2,1)S(1)}, bf16[64,256]{1,0:T(8,128)(2,1)S(1)}, u32[]{:S(2)}, u32[]{:S(2)}) collective-permute-start(bf16[64,256]{1,0:T(8,128)(2,1)S(1)} %features.1.refs_0_), channel_id=1, source_target_pairs={{0,9},{1,8},{4,13},{5,12},{8,1},{9,0},{12,5},{13,4},{2,11},{3,10},... | collective-permute-start | bytes 98312 | tf_op jit(solution)/shard_map/ppermute | solution.py:178
  6.4 1.6 %collective-permute-start.1 = (bf16[64,256]{1,0:T(8,128)(2,1)S(1)}, bf16[64,256]{1,0:T(8,128)(2,1)S(1)}, u32[]{:S(2)}, u32[]{:S(2)}) collective-permute-start(bf16[64,256]{1,0:T(8,128)(2,1)S(1)} %features.1.refs_0_), channel_id=1, source_target_pairs={{0,13},{1,12},{4,9},{5,8},{8,5},{9,4},{12,1},{13,0},{2,15},{3,14},... | collective-permute-start | bytes 98312 | tf_op jit(solution)/shard_map/ppermute | solution.py:178
  8.0 0.2 collective-permute-start
  8.2 0.0 copy-done.2
  8.3 0.0 copy-done.1
  8.3 0.0 copy-done
  8.3 0.0 copy-done.3
  8.3 2.1 %queries.1.refs_4_.weights = bf16[128,4096]{1,0:T(8,128)(2,1)S(1)} custom-call(bf16[128,4096]{1,0:T(8,128)(2,1)S(1)} %bitcast.7, f32[64,64]{1,0:T(8,128)S(1)} %bitcast.8, f32[64,64]{1,0:T(8,128)S(1)} %bitcast.9, f32[64,64]{1,0:T(8,128)S(1)} %bitcast.10), custom_call_target="tpu_custom_call" | custom-call | flops 536870912 | bytes 2097152 | tf_op jit(solution)/shard_map/queries/pallas_call | solution.py:185
  10.4 0.0 collective-permute-done.2.refs_3_
  10.4 1.2 %collective-permute-done.1.refs_2_ = bf16[64,256]{1,0:T(8,128)(2,1)S(1)} collective-permute-done((bf16[64,256]{1,0:T(8,128)(2,1)S(1)}, bf16[64,256]{1,0:T(8,128)(2,1)S(1)}, u32[]{:S(2)}, u32[]{:S(2)}) %collective-permute-start.1) | collective-permute-done | bytes 32800 | tf_op jit(solution)/shard_map/ppermute | solution.py:178
  11.6 0.1 collective-permute-done.refs_1_
  11.8 0.7 %collective-permute-start.3 = (bf16[4,64,256]{2,1,0:T(8,128)(2,1)S(1)}, bf16[4,64,256]{2,1,0:T(8,128)(2,1)S(1)}, u32[]{:S(2)}, u32[]{:S(2)}) collective-permute-start(bf16[4,64,256]{2,1,0:T(8,128)(2,1)S(1)} %pack.1.mine), channel_id=1, source_target_pairs={{0,1},{1,0},{2,3},{3,2},{4,5},{5,4},{6,7},{7,6},{8,9},{9,8},{10,11... | collective-permute-start | bytes 393224 | tf_op jit(solution)/shard_map/ppermute | solution.py:207
  12.5 1.0 %collective-permute-done.3.theirs = bf16[4,64,256]{2,1,0:T(8,128)(2,1)S(1)} collective-permute-done((bf16[4,64,256]{2,1,0:T(8,128)(2,1)S(1)}, bf16[4,64,256]{2,1,0:T(8,128)(2,1)S(1)}, u32[]{:S(2)}, u32[]{:S(2)}) %collective-permute-start.3) | collective-permute-done | bytes 131104 | tf_op jit(solution)/shard_map/ppermute | solution.py:207
  13.5 0.9 %scores.2 = (f32[2,128,128]{2,1,0:T(8,128)S(1)}, bf16[2,128,128]{2,1,0:T(8,128)(2,1)S(1)}) custom-call(bf16[128,4096]{1,0:T(8,128)(2,1)S(1)} %queries.1.refs_4_.weights, bf16[4,64,256]{2,1,0:T(8,128)(2,1)S(1)} %pack.1.mine, bf16[4,64,256]{2,1,0:T(8,128)(2,1)S(1)} %collective-permute-done.3.theirs), custom_call_target="tpu_custom_call" | custom-call | flops 536870912 | bytes 1048576 | tf_op jit(solution)/shard_map/scores/pallas_call | solution.py:213
  14.4 1.6 %collective-permute-start.4 = (bf16[2,128,128]{2,1,0:T(8,128)(2,1)S(1)}, bf16[2,128,128]{2,1,0:T(8,128)(2,1)S(1)}, u32[]{:S(2)}, u32[]{:S(2)}) collective-permute-start(bf16[2,128,128]{2,1,0:T(8,128)(2,1)S(1)} %get-tuple-element.10), channel_id=1, source_target_pairs={{0,2},{2,0},{1,3},{3,1},{4,6},{6,4},{5,7},{7,5},{8,10},{10,8},{9,1... | collective-permute-start | bytes 196616 | tf_op jit(solution)/shard_map/ppermute | solution.py:231
  16.0 0.9 %scores.3 = (f32[2,128,128]{2,1,0:T(8,128)S(1)}, bf16[2,128,128]{2,1,0:T(8,128)(2,1)S(1)}) custom-call(bf16[128,4096]{1,0:T(8,128)(2,1)S(1)} %queries.1.refs_4_.weights, bf16[4,64,256]{2,1,0:T(8,128)(2,1)S(1)} %pack.1.mine, bf16[4,64,256]{2,1,0:T(8,128)(2,1)S(1)} %collective-permute-done.3.theirs, f32[2,128,128]{2,1,0:T(8,128)S(1)} %get-tuple-element.9.own.refs_0_), custom_call_target="tpu_custom_call" | custom-call | flops 536870912 | bytes 1048576 | tf_op jit(solution)/shard_map/scores/pallas_call | solution.py:213
  16.9 0.6 %collective-permute-start.7 = (bf16[2,128,128]{2,1,0:T(8,128)(2,1)S(1)}, bf16[2,128,128]{2,1,0:T(8,128)(2,1)S(1)}, u32[]{:S(2)}, u32[]{:S(2)}) collective-permute-start(bf16[2,128,128]{2,1,0:T(8,128)(2,1)S(1)} %get-tuple-element.12), channel_id=1, source_target_pairs={{0,2},{2,0},{1,3},{3,1},{4,6},{6,4},{5,7},{7,5},{8,10},{10,8},{9,1... | collective-permute-start | bytes 196616 | tf_op jit(solution)/shard_map/ppermute | solution.py:231
  17.5 1.4 %collective-permute-done.4.refs_0_ = bf16[2,128,128]{2,1,0:T(8,128)(2,1)S(1)} collective-permute-done((bf16[2,128,128]{2,1,0:T(8,128)(2,1)S(1)}, bf16[2,128,128]{2,1,0:T(8,128)(2,1)S(1)}, u32[]{:S(2)}, u32[]{:S(2)}) %collective-permute-start.4) | collective-permute-done | bytes 65568 | tf_op jit(solution)/shard_map/ppermute | solution.py:231
  18.8 2.4 %collective-permute-start.5 = (bf16[128,128]{1,0:T(8,128)(2,1)S(1)}, bf16[128,128]{1,0:T(8,128)(2,1)S(1)}, u32[]{:S(2)}, u32[]{:S(2)}) collective-permute-start(bf16[128,128]{1,0:T(8,128)(2,1)S(1)} %layers.4.refs_1_), channel_id=1, source_target_pairs={{0,12},{4,8},{8,4},{12,0},{1,13},{5,9},{9,5},{13,1},{2,14},{6,10},... | collective-permute-start | bytes 98312 | tf_op jit(solution)/shard_map/ppermute | solution.py:174
  21.3 0.1 collective-permute-start.6
  21.4 0.0 collective-permute-done.7.refs_0_
  21.4 2.1 %collective-permute-start.8 = (bf16[128,128]{1,0:T(8,128)(2,1)S(1)}, bf16[128,128]{1,0:T(8,128)(2,1)S(1)}, u32[]{:S(2)}, u32[]{:S(2)}) collective-permute-start(bf16[128,128]{1,0:T(8,128)(2,1)S(1)} %layers.7), channel_id=1, source_target_pairs={{0,4},{4,0},{8,12},{12,8},{1,5},{5,1},{9,13},{13,9},{2,6},{6,2},{1... | collective-permute-start | bytes 98312 | tf_op jit(solution)/shard_map/ppermute | solution.py:174
  23.5 2.7 %collective-permute-done.6.refs_1_ = bf16[128,128]{1,0:T(8,128)(2,1)S(1)} collective-permute-done((bf16[128,128]{1,0:T(8,128)(2,1)S(1)}, bf16[128,128]{1,0:T(8,128)(2,1)S(1)}, u32[]{:S(2)}, u32[]{:S(2)}) %collective-permute-start.6) | collective-permute-done | bytes 32800 | tf_op jit(solution)/shard_map/ppermute | solution.py:174
  26.2 0.0 collective-permute-done.5.refs_0_
  26.2 0.0 collective-permute-done.8.refs_2_
  26.2 0.7 %place.1 = f32[512,128]{1,0:T(8,128)} custom-call(bf16[128,128]{1,0:T(8,128)(2,1)S(1)} %collective-permute-done.5.refs_0_, bf16[128,128]{1,0:T(8,128)(2,1)S(1)} %collective-permute-done.6.refs_1_, bf16[128,128]{1,0:T(8,128)(2,1)S(1)} %collective-permute-done.8.refs_2_, f32[128,128]{1,0:T(8,128)S(1)} %layers.6.refs_1_.refs_3_), custom_call_target="tpu_custom_call" | custom-call | tf_op jit(solution)/shard_map/place/pallas_call | solution.py:256
  (5 shorter events, 0.0 us)
Async XLA Ops:
  0.0 8.3 %copy-start.2 = (f32[1,64,64]{2,1,0:T(8,128)S(1)}, f32[1,64,64]{2,1,0:T(8,128)}, u32[]{:S(2)}) copy-start(f32[1,64,64]{2,1,0:T(8,128)} %refs_5_.1) | copy-start | bytes 49156
  0.0 8.3 %copy-start.1 = (f32[1,64,64]{2,1,0:T(8,128)S(1)}, f32[1,64,64]{2,1,0:T(8,128)}, u32[]{:S(2)}) copy-start(f32[1,64,64]{2,1,0:T(8,128)} %refs_2_.1) | copy-start | bytes 49156
  0.0 8.3 %copy-start = (bf16[1,128,4096]{2,1,0:T(8,128)(2,1)S(1)}, bf16[1,128,4096]{2,1,0:T(8,128)(2,1)}, u32[]{:S(2)}) copy-start(bf16[1,128,4096]{2,1,0:T(8,128)(2,1)} %param.15) | copy-start | bytes 3145732
  0.0 8.3 %copy-start.3 = (f32[1,64,64]{2,1,0:T(8,128)S(1)}, f32[1,64,64]{2,1,0:T(8,128)}, u32[]{:S(2)}) copy-start(f32[1,64,64]{2,1,0:T(8,128)} %param.14) | copy-start | bytes 49156
  2.8 7.6 %collective-permute-start.2 = (bf16[64,256]{1,0:T(8,128)(2,1)S(1)}, bf16[64,256]{1,0:T(8,128)(2,1)S(1)}, u32[]{:S(2)}, u32[]{:S(2)}) collective-permute-start(bf16[64,256]{1,0:T(8,128)(2,1)S(1)} %features.1.refs_0_), channel_id=1, source_target_pairs={{0,9},{1,8},{4,13},{5,12},{8,1},{9,0},{12,5},{13,4},{2,11},{3,10},... | collective-permute-start | bytes 98312 | tf_op jit(solution)/shard_map/ppermute | solution.py:178
  6.4 5.2 %collective-permute-start.1 = (bf16[64,256]{1,0:T(8,128)(2,1)S(1)}, bf16[64,256]{1,0:T(8,128)(2,1)S(1)}, u32[]{:S(2)}, u32[]{:S(2)}) collective-permute-start(bf16[64,256]{1,0:T(8,128)(2,1)S(1)} %features.1.refs_0_), channel_id=1, source_target_pairs={{0,13},{1,12},{4,9},{5,8},{8,5},{9,4},{12,1},{13,0},{2,15},{3,14},... | collective-permute-start | bytes 98312 | tf_op jit(solution)/shard_map/ppermute | solution.py:178
  8.0 3.8 %collective-permute-start = (bf16[64,256]{1,0:T(8,128)(2,1)S(1)}, bf16[64,256]{1,0:T(8,128)(2,1)S(1)}, u32[]{:S(2)}, u32[]{:S(2)}) collective-permute-start(bf16[64,256]{1,0:T(8,128)(2,1)S(1)} %features.1.refs_0_), channel_id=1, source_target_pairs={{0,5},{1,4},{4,1},{5,0},{8,13},{9,12},{12,9},{13,8},{2,7},{3,6},{6... | collective-permute-start | bytes 98312 | tf_op jit(solution)/shard_map/ppermute | solution.py:178
  11.8 1.7 %collective-permute-start.3 = (bf16[4,64,256]{2,1,0:T(8,128)(2,1)S(1)}, bf16[4,64,256]{2,1,0:T(8,128)(2,1)S(1)}, u32[]{:S(2)}, u32[]{:S(2)}) collective-permute-start(bf16[4,64,256]{2,1,0:T(8,128)(2,1)S(1)} %pack.1.mine), channel_id=1, source_target_pairs={{0,1},{1,0},{2,3},{3,2},{4,5},{5,4},{6,7},{7,6},{8,9},{9,8},{10,11... | collective-permute-start | bytes 393224 | tf_op jit(solution)/shard_map/ppermute | solution.py:207
  14.4 4.4 %collective-permute-start.4 = (bf16[2,128,128]{2,1,0:T(8,128)(2,1)S(1)}, bf16[2,128,128]{2,1,0:T(8,128)(2,1)S(1)}, u32[]{:S(2)}, u32[]{:S(2)}) collective-permute-start(bf16[2,128,128]{2,1,0:T(8,128)(2,1)S(1)} %get-tuple-element.10), channel_id=1, source_target_pairs={{0,2},{2,0},{1,3},{3,1},{4,6},{6,4},{5,7},{7,5},{8,10},{10,8},{9,1... | collective-permute-start | bytes 196616 | tf_op jit(solution)/shard_map/ppermute | solution.py:231
  16.9 4.5 %collective-permute-start.7 = (bf16[2,128,128]{2,1,0:T(8,128)(2,1)S(1)}, bf16[2,128,128]{2,1,0:T(8,128)(2,1)S(1)}, u32[]{:S(2)}, u32[]{:S(2)}) collective-permute-start(bf16[2,128,128]{2,1,0:T(8,128)(2,1)S(1)} %get-tuple-element.12), channel_id=1, source_target_pairs={{0,2},{2,0},{1,3},{3,1},{4,6},{6,4},{5,7},{7,5},{8,10},{10,8},{9,1... | collective-permute-start | bytes 196616 | tf_op jit(solution)/shard_map/ppermute | solution.py:231
  18.8 7.3 %collective-permute-start.5 = (bf16[128,128]{1,0:T(8,128)(2,1)S(1)}, bf16[128,128]{1,0:T(8,128)(2,1)S(1)}, u32[]{:S(2)}, u32[]{:S(2)}) collective-permute-start(bf16[128,128]{1,0:T(8,128)(2,1)S(1)} %layers.4.refs_1_), channel_id=1, source_target_pairs={{0,12},{4,8},{8,4},{12,0},{1,13},{5,9},{9,5},{13,1},{2,14},{6,10},... | collective-permute-start | bytes 98312 | tf_op jit(solution)/shard_map/ppermute | solution.py:174
  21.3 4.9 %collective-permute-start.6 = (bf16[128,128]{1,0:T(8,128)(2,1)S(1)}, bf16[128,128]{1,0:T(8,128)(2,1)S(1)}, u32[]{:S(2)}, u32[]{:S(2)}) collective-permute-start(bf16[128,128]{1,0:T(8,128)(2,1)S(1)} %layers.5.refs_1_), channel_id=1, source_target_pairs={{0,8},{4,12},{8,0},{12,4},{1,9},{5,13},{9,1},{13,5},{2,10},{6,14},... | collective-permute-start | bytes 98312 | tf_op jit(solution)/shard_map/ppermute | solution.py:174
  21.4 4.8 %collective-permute-start.8 = (bf16[128,128]{1,0:T(8,128)(2,1)S(1)}, bf16[128,128]{1,0:T(8,128)(2,1)S(1)}, u32[]{:S(2)}, u32[]{:S(2)}) collective-permute-start(bf16[128,128]{1,0:T(8,128)(2,1)S(1)} %layers.7), channel_id=1, source_target_pairs={{0,4},{4,0},{8,12},{12,8},{1,5},{5,1},{9,13},{13,9},{2,6},{6,2},{1... | collective-permute-start | bytes 98312 | tf_op jit(solution)/shard_map/ppermute | solution.py:174

commit v14 on v9

--- a/solution.py
+++ b/solution.py
@@ -21,9 +21,9 @@
     return rounds, rounds, train_size // 2
 
 
-FEATURE_ROUNDS = [((3, 1), (2, 0)), ((1, 0),), ((3, 0), (0, 2), (1, 3), (2, 1)), ((0, 3), (3, 2)), ((0, 1), (2, 3), (1, 2))]
-SCORE_ROUNDS = [((3, 0), (1, 2)), ((2, 0), (0, 2), (3, 1)), ((2, 1), (1, 0), (0, 3)), ((1, 3), (0, 1), (3, 2)), ((2, 3),)]
-FIRST = 3
+FEATURE_ROUNDS = [((0, 2), (1, 3), (2, 0), (3, 1)), ((0, 3), (1, 2), (2, 1), (3, 0)), ((0, 1), (1, 0), (2, 3), (3, 2))]
+SCORE_ROUNDS = [((0, 1), (1, 2), (2, 3), (3, 0)), ((0, 2), (1, 3), (2, 0), (3, 1)), ((0, 3), (1, 0), (2, 1), (3, 2))]
+FIRST = 2
 
 
 def lookup(index, values):
@@ -208,7 +208,7 @@
     tokens, width = inputs.shape[1:]
     count, entries = queries.shape[1:]
     rank = proj_in.shape[1]
-    chunks = 2
+    chunks = 1
     vmem, hbm = pl.BlockSpec(memory_space=pltpu.VMEM), pl.BlockSpec(memory_space=pltpu.HBM)
     anywhere = pl.BlockSpec(memory_space=pl.ANY)
     params = pltpu.CompilerParams(vmem_limit_bytes=32 << 20)

time: 38.2 us -> 26.8 us (0.70)
  the two profiles are of different devices: /device:TPU:26 before, /device:TPU:0 now
where the time goes in v14:
time: 26.8 us; the launch traced here: 26.6 us
  starting transfers between devices  13.1 us (49%)
  Pallas kernels  7.51 us (28%)
  waiting for transfers between devices  5.95 us (22%)
    ppermute x3, starting transfers between devices, across(): return lax.ppermute(feats, ('train', 'sub'), cores)  5.4 us
    ppermute x3, starting transfers between devices, body(): arrivals.append(lax.ppermute(block, 'train', pairs))  4.8 us
    pallas_call x1, Pallas kernels, body(): pl.pallas_call(functools.partial(features_kernel, chunks), out_shape=[jax...  2.86 us
    ppermute x3, waiting for transfers between devices, body(): arrivals.append(lax.ppermute(block, 'train', pairs))  2.18 us
    ppermute x2, starting transfers between devices, scored(): lax.ppermute(block, 'layer', [(l, (l + k) % layer_size) for l in range(la...  2.17 us
    pallas_call x1, Pallas kernels, body(): pl.pallas_call(queries_kernel, out_shape=jax.ShapeDtypeStruct((count, ent...  2.11 us
    pallas_call x2, Pallas kernels, scored(): pl.pallas_call(functools.partial(scores_kernel, layer_size, targets), out...  1.75 us
    ppermute x3, waiting for transfers between devices, across(): return lax.ppermute(feats, ('train', 'sub'), cores)  1.41 us
  transfers between devices with their start and end apart: 9, of which 6 were waited for; matrix products, arithmetic and copies ran while one was open for 0% of the time, Pallas kernels for 11%

profile of v14, /device:TPU:0, one launch (start us, length us, event | category | flops | bytes accessed | tf_op | source)
XLA Modules:
  0.0 26.6 jit_solution(8476494824020680237)
XLA Ops:
  0.0 2.9 %features.1 = (bf16[64,256]{1,0:T(8,128)(2,1)S(1)}, bf16[128,4096]{1,0:T(8,128)(2,1)S(1)}, f32[64,64]{1,0:T(8,128)S(1)}, f32[64,64]{1,0:T(8,128)S(1)}, f32[64,64]{1,0:T(8,128)S(1)}) custom-call(bf16[1,256,4096]{2,1,0:T(8,128)(2,1)} %refs_0_.1, bf16[1,64,4096]{2,1,0:T(8,128)(2,1)} %refs_1_.1, f32[1,64,64]{2,1,0:T(8,128)} %refs_2_.1, ...), custom_call_target="tpu_custom_call" | custom-call | flops 134217728 | bytes 2621440 | tf_op jit(solution)/shard_map/features/pallas_call | solution.py:217
  2.9 3.5 %collective-permute-start.2 = (bf16[64,256]{1,0:T(8,128)(2,1)S(1)}, bf16[64,256]{1,0:T(8,128)(2,1)S(1)}, u32[]{:S(2)}, u32[]{:S(2)}) collective-permute-start(bf16[64,256]{1,0:T(8,128)(2,1)S(1)} %get-tuple-element.18.refs_0_), channel_id=1, source_target_pairs={{0,9},{1,8},{4,13},{5,12},{8,1},{9,0},{12,5},{13,4},{2,11},{3,10},... | collective-permute-start | bytes 98312 | tf_op jit(solution)/shard_map/ppermute | solution.py:258
  6.4 1.6 %collective-permute-start.1 = (bf16[64,256]{1,0:T(8,128)(2,1)S(1)}, bf16[64,256]{1,0:T(8,128)(2,1)S(1)}, u32[]{:S(2)}, u32[]{:S(2)}) collective-permute-start(bf16[64,256]{1,0:T(8,128)(2,1)S(1)} %get-tuple-element.18.refs_0_), channel_id=1, source_target_pairs={{0,13},{1,12},{4,9},{5,8},{8,5},{9,4},{12,1},{13,0},{2,15},{3,14},... | collective-permute-start | bytes 98312 | tf_op jit(solution)/shard_map/ppermute | solution.py:258
  8.0 0.2 collective-permute-start
  8.3 2.1 %queries.1.refs_4_.weights = bf16[128,4096]{1,0:T(8,128)(2,1)S(1)} custom-call(bf16[128,4096]{1,0:T(8,128)(2,1)S(1)} %get-tuple-element.14.queries, f32[64,64]{1,0:T(8,128)S(1)} %get-tuple-element.15.basis_in, f32[64,64]{1,0:T(8,128)S(1)} %get-tuple-element.16.basis_out, f32[64,64]{1,0:T(8,128)S(1)} %get-tuple-element.17.eigen), custom_call_target="tpu_custom_call" | custom-call | flops 536870912 | bytes 2097152 | tf_op jit(solution)/shard_map/queries/pallas_call | solution.py:262
  10.4 0.0 collective-permute-done.2.refs_3_
  10.4 1.3 %collective-permute-done.1.refs_2_ = bf16[64,256]{1,0:T(8,128)(2,1)S(1)} collective-permute-done((bf16[64,256]{1,0:T(8,128)(2,1)S(1)}, bf16[64,256]{1,0:T(8,128)(2,1)S(1)}, u32[]{:S(2)}, u32[]{:S(2)}) %collective-permute-start.1) | collective-permute-done | bytes 32800 | tf_op jit(solution)/shard_map/ppermute | solution.py:258
  11.7 0.2 collective-permute-done.refs_1_
  11.8 0.7 %collective-permute-start.3 = (bf16[4,64,256]{2,1,0:T(8,128)(2,1)S(1)}, bf16[4,64,256]{2,1,0:T(8,128)(2,1)S(1)}, u32[]{:S(2)}, u32[]{:S(2)}) collective-permute-start(bf16[4,64,256]{2,1,0:T(8,128)(2,1)S(1)} %pack.1.mine), channel_id=1, source_target_pairs={{0,1},{1,0},{2,3},{3,2},{4,5},{5,4},{6,7},{7,6},{8,9},{9,8},{10,11... | collective-permute-start | bytes 393224 | tf_op jit(solution)/shard_map/ppermute | solution.py:283
  12.6 1.0 %collective-permute-done.3.theirs = bf16[4,64,256]{2,1,0:T(8,128)(2,1)S(1)} collective-permute-done((bf16[4,64,256]{2,1,0:T(8,128)(2,1)S(1)}, bf16[4,64,256]{2,1,0:T(8,128)(2,1)S(1)}, u32[]{:S(2)}, u32[]{:S(2)}) %collective-permute-start.3) | collective-permute-done | bytes 131104 | tf_op jit(solution)/shard_map/ppermute | solution.py:283
  13.6 0.9 %scores.2 = (f32[2,128,128]{2,1,0:T(8,128)S(1)}, bf16[2,128,128]{2,1,0:T(8,128)(2,1)S(1)}) custom-call(bf16[128,4096]{1,0:T(8,128)(2,1)S(1)} %queries.1.refs_4_.weights, bf16[4,64,256]{2,1,0:T(8,128)(2,1)S(1)} %pack.1.mine, bf16[4,64,256]{2,1,0:T(8,128)(2,1)S(1)} %collective-permute-done.3.theirs), custom_call_target="tpu_custom_call" | custom-call | flops 536870912 | bytes 1048576 | tf_op jit(solution)/shard_map/scores/pallas_call | solution.py:288
  14.4 1.6 %collective-permute-start.5 = (bf16[2,128,128]{2,1,0:T(8,128)(2,1)S(1)}, bf16[2,128,128]{2,1,0:T(8,128)(2,1)S(1)}, u32[]{:S(2)}, u32[]{:S(2)}) collective-permute-start(bf16[2,128,128]{2,1,0:T(8,128)(2,1)S(1)} %get-tuple-element.22), channel_id=1, source_target_pairs={{0,2},{2,0},{1,3},{3,1},{4,6},{6,4},{5,7},{7,5},{8,10},{10,8},{9,1... | collective-permute-start | bytes 196616 | tf_op jit(solution)/shard_map/ppermute | solution.py:306
  16.0 0.9 %scores.3 = (f32[2,128,128]{2,1,0:T(8,128)S(1)}, bf16[2,128,128]{2,1,0:T(8,128)(2,1)S(1)}) custom-call(bf16[128,4096]{1,0:T(8,128)(2,1)S(1)} %queries.1.refs_4_.weights, bf16[4,64,256]{2,1,0:T(8,128)(2,1)S(1)} %pack.1.mine, bf16[4,64,256]{2,1,0:T(8,128)(2,1)S(1)} %collective-permute-done.3.theirs, f32[2,128,128]{2,1,0:T(8,128)S(1)} %get-tuple-element.19.refs_0_.own), custom_call_target="tpu_custom_call" | custom-call | flops 536870912 | bytes 1048576 | tf_op jit(solution)/shard_map/scores/pallas_call | solution.py:288
  16.9 0.6 %collective-permute-start.4 = (bf16[2,128,128]{2,1,0:T(8,128)(2,1)S(1)}, bf16[2,128,128]{2,1,0:T(8,128)(2,1)S(1)}, u32[]{:S(2)}, u32[]{:S(2)}) collective-permute-start(bf16[2,128,128]{2,1,0:T(8,128)(2,1)S(1)} %get-tuple-element.21), channel_id=1, source_target_pairs={{0,2},{2,0},{1,3},{3,1},{4,6},{6,4},{5,7},{7,5},{8,10},{10,8},{9,1... | collective-permute-start | bytes 196616 | tf_op jit(solution)/shard_map/ppermute | solution.py:306
  17.5 1.4 %collective-permute-done.5.refs_0_ = bf16[2,128,128]{2,1,0:T(8,128)(2,1)S(1)} collective-permute-done((bf16[2,128,128]{2,1,0:T(8,128)(2,1)S(1)}, bf16[2,128,128]{2,1,0:T(8,128)(2,1)S(1)}, u32[]{:S(2)}, u32[]{:S(2)}) %collective-permute-start.5) | collective-permute-done | bytes 65568 | tf_op jit(solution)/shard_map/ppermute | solution.py:306
  18.9 0.1 collective-permute-start.6
  19.0 3.0 %collective-permute-start.7 = (bf16[128,128]{1,0:T(8,128)(2,1)S(1)}, bf16[128,128]{1,0:T(8,128)(2,1)S(1)}, u32[]{:S(2)}, u32[]{:S(2)}) collective-permute-start(bf16[128,128]{1,0:T(8,128)(2,1)S(1)} %layers.5.refs_1_), channel_id=1, source_target_pairs={{0,8},{4,12},{8,0},{12,4},{1,9},{5,13},{9,1},{13,5},{2,10},{6,14},... | collective-permute-start | bytes 98312 | tf_op jit(solution)/shard_map/ppermute | solution.py:341
  21.9 0.0 collective-permute-done.4.refs_0_
  21.9 1.8 %collective-permute-start.8 = (bf16[128,128]{1,0:T(8,128)(2,1)S(1)}, bf16[128,128]{1,0:T(8,128)(2,1)S(1)}, u32[]{:S(2)}, u32[]{:S(2)}) collective-permute-start(bf16[128,128]{1,0:T(8,128)(2,1)S(1)} %layers.7), channel_id=1, source_target_pairs={{0,12},{4,0},{8,4},{12,8},{1,13},{5,1},{9,5},{13,9},{2,14},{6,2},{... | collective-permute-start | bytes 98312 | tf_op jit(solution)/shard_map/ppermute | solution.py:341
  23.7 0.9 %collective-permute-done.6.block = bf16[128,128]{1,0:T(8,128)(2,1)S(1)} collective-permute-done((bf16[128,128]{1,0:T(8,128)(2,1)S(1)}, bf16[128,128]{1,0:T(8,128)(2,1)S(1)}, u32[]{:S(2)}, u32[]{:S(2)}) %collective-permute-start.6) | collective-permute-done | bytes 32800 | tf_op jit(solution)/shard_map/ppermute | solution.py:341
  24.6 0.0 collective-permute-done.7.block
  24.7 1.3 %collective-permute-done.8.refs_2_ = bf16[128,128]{1,0:T(8,128)(2,1)S(1)} collective-permute-done((bf16[128,128]{1,0:T(8,128)(2,1)S(1)}, bf16[128,128]{1,0:T(8,128)(2,1)S(1)}, u32[]{:S(2)}, u32[]{:S(2)}) %collective-permute-start.8) | collective-permute-done | bytes 32800 | tf_op jit(solution)/shard_map/ppermute | solution.py:341
  25.9 0.7 %place.1 = f32[512,128]{1,0:T(8,128)} custom-call(f32[128,128]{1,0:T(8,128)S(1)} %layers.6.refs_1_.own, bf16[128,128]{1,0:T(8,128)(2,1)S(1)} %keep.2.refs_0_, bf16[128,128]{1,0:T(8,128)(2,1)S(1)} %keep.3.refs_1_, bf16[128,128]{1,0:T(8,128)(2,1)S(1)} %collective-permute-done.8.refs_2_), custom_call_target="tpu_custom_call" | custom-call | tf_op jit(solution)/shard_map/place/pallas_call | solution.py:345
  (7 shorter events, 0.1 us)
Async XLA Ops:
  2.9 7.5 %collective-permute-start.2 = (bf16[64,256]{1,0:T(8,128)(2,1)S(1)}, bf16[64,256]{1,0:T(8,128)(2,1)S(1)}, u32[]{:S(2)}, u32[]{:S(2)}) collective-permute-start(bf16[64,256]{1,0:T(8,128)(2,1)S(1)} %get-tuple-element.18.refs_0_), channel_id=1, source_target_pairs={{0,9},{1,8},{4,13},{5,12},{8,1},{9,0},{12,5},{13,4},{2,11},{3,10},... | collective-permute-start | bytes 98312 | tf_op jit(solution)/shard_map/ppermute | solution.py:258
  6.4 5.2 %collective-permute-start.1 = (bf16[64,256]{1,0:T(8,128)(2,1)S(1)}, bf16[64,256]{1,0:T(8,128)(2,1)S(1)}, u32[]{:S(2)}, u32[]{:S(2)}) collective-permute-start(bf16[64,256]{1,0:T(8,128)(2,1)S(1)} %get-tuple-element.18.refs_0_), channel_id=1, source_target_pairs={{0,13},{1,12},{4,9},{5,8},{8,5},{9,4},{12,1},{13,0},{2,15},{3,14},... | collective-permute-start | bytes 98312 | tf_op jit(solution)/shard_map/ppermute | solution.py:258
  8.0 3.8 %collective-permute-start = (bf16[64,256]{1,0:T(8,128)(2,1)S(1)}, bf16[64,256]{1,0:T(8,128)(2,1)S(1)}, u32[]{:S(2)}, u32[]{:S(2)}) collective-permute-start(bf16[64,256]{1,0:T(8,128)(2,1)S(1)} %get-tuple-element.18.refs_0_), channel_id=1, source_target_pairs={{0,5},{1,4},{4,1},{5,0},{8,13},{9,12},{12,9},{13,8},{2,7},{3,6},{6... | collective-permute-start | bytes 98312 | tf_op jit(solution)/shard_map/ppermute | solution.py:258
  11.8 1.7 %collective-permute-start.3 = (bf16[4,64,256]{2,1,0:T(8,128)(2,1)S(1)}, bf16[4,64,256]{2,1,0:T(8,128)(2,1)S(1)}, u32[]{:S(2)}, u32[]{:S(2)}) collective-permute-start(bf16[4,64,256]{2,1,0:T(8,128)(2,1)S(1)} %pack.1.mine), channel_id=1, source_target_pairs={{0,1},{1,0},{2,3},{3,2},{4,5},{5,4},{6,7},{7,6},{8,9},{9,8},{10,11... | collective-permute-start | bytes 393224 | tf_op jit(solution)/shard_map/ppermute | solution.py:283
  14.4 4.4 %collective-permute-start.5 = (bf16[2,128,128]{2,1,0:T(8,128)(2,1)S(1)}, bf16[2,128,128]{2,1,0:T(8,128)(2,1)S(1)}, u32[]{:S(2)}, u32[]{:S(2)}) collective-permute-start(bf16[2,128,128]{2,1,0:T(8,128)(2,1)S(1)} %get-tuple-element.22), channel_id=1, source_target_pairs={{0,2},{2,0},{1,3},{3,1},{4,6},{6,4},{5,7},{7,5},{8,10},{10,8},{9,1... | collective-permute-start | bytes 196616 | tf_op jit(solution)/shard_map/ppermute | solution.py:306
  16.9 5.0 %collective-permute-start.4 = (bf16[2,128,128]{2,1,0:T(8,128)(2,1)S(1)}, bf16[2,128,128]{2,1,0:T(8,128)(2,1)S(1)}, u32[]{:S(2)}, u32[]{:S(2)}) collective-permute-start(bf16[2,128,128]{2,1,0:T(8,128)(2,1)S(1)} %get-tuple-element.21), channel_id=1, source_target_pairs={{0,2},{2,0},{1,3},{3,1},{4,6},{6,4},{5,7},{7,5},{8,10},{10,8},{9,1... | collective-permute-start | bytes 196616 | tf_op jit(solution)/shard_map/ppermute | solution.py:306
  18.9 5.8 %collective-permute-start.6 = (bf16[128,128]{1,0:T(8,128)(2,1)S(1)}, bf16[128,128]{1,0:T(8,128)(2,1)S(1)}, u32[]{:S(2)}, u32[]{:S(2)}) collective-permute-start(bf16[128,128]{1,0:T(8,128)(2,1)S(1)} %layers.4.refs_1_), channel_id=1, source_target_pairs={{0,4},{4,8},{8,12},{12,0},{1,5},{5,9},{9,13},{13,1},{2,6},{6,10},{... | collective-permute-start | bytes 98312 | tf_op jit(solution)/shard_map/ppermute | solution.py:341
  19.0 5.7 %collective-permute-start.7 = (bf16[128,128]{1,0:T(8,128)(2,1)S(1)}, bf16[128,128]{1,0:T(8,128)(2,1)S(1)}, u32[]{:S(2)}, u32[]{:S(2)}) collective-permute-start(bf16[128,128]{1,0:T(8,128)(2,1)S(1)} %layers.5.refs_1_), channel_id=1, source_target_pairs={{0,8},{4,12},{8,0},{12,4},{1,9},{5,13},{9,1},{13,5},{2,10},{6,14},... | collective-permute-start | bytes 98312 | tf_op jit(solution)/shard_map/ppermute | solution.py:341
  21.9 4.0 %collective-permute-start.8 = (bf16[128,128]{1,0:T(8,128)(2,1)S(1)}, bf16[128,128]{1,0:T(8,128)(2,1)S(1)}, u32[]{:S(2)}, u32[]{:S(2)}) collective-permute-start(bf16[128,128]{1,0:T(8,128)(2,1)S(1)} %layers.7), channel_id=1, source_target_pairs={{0,12},{4,0},{8,4},{12,8},{1,13},{5,1},{9,5},{13,9},{2,14},{6,2},{... | collective-permute-start | bytes 98312 | tf_op jit(solution)/shard_map/ppermute | solution.py:341

commit v15 on v14

--- a/solution.py
+++ b/solution.py
@@ -56,8 +56,8 @@
 
 
 def features_kernel(chunks, *refs):
-    sides, (queries_hbm, eigen_hbm) = (refs[0:3], refs[3:6]), refs[6:8]
-    feats, queries, eigen, basis_in, basis_out, rows, proj, sems = refs[8:]
+    sides, eigen_hbm = (refs[0:3], refs[3:6]), refs[6]
+    feats, eigen, basis_in, basis_out, rows, proj, sems = refs[7:]
     core = lax.axis_index("sub")
     step = rows.shape[1] // chunks
 
@@ -76,7 +76,7 @@
     others = [
         pltpu.make_async_copy(source.at[0], target, sems.at[2 + number, 0])
         for number, (source, target) in enumerate((
-            (sides[0][2], basis_in), (sides[1][2], basis_out), (eigen_hbm, eigen), (queries_hbm, queries)
+            (sides[0][2], basis_in), (sides[1][2], basis_out), (eigen_hbm, eigen)
         ))
     ]
     for copy in others:
@@ -136,13 +136,22 @@
     return total.T
 
 
-def queries_kernel(queries, basis_in, basis_out, eigen, *refs):
-    weights, half = refs[-2:]
+def queries_kernel(pieces, queries_hbm, basis_in, basis_out, eigen, weights, queries, half, sems):
     rank = basis_in.shape[0]
     width = PACK * rank
     groups = rank // PACK
+    step = queries.shape[1] // pieces
+    copies = []
+    for piece in range(pieces):
+        columns = pl.ds(piece * step, step)
+        copies.append(
+            pltpu.make_async_copy(queries_hbm.at[0, :, columns], queries.at[:, columns], sems.at[piece])
+        )
+        copies[-1].start()
     right = block_diagonal(basis_in[...].T).astype(BF16)
     for part in range(groups):
+        if part * width % step == 0:
+            copies[part * width // step].wait()
         half[part * width:(part + 1) * width, :] = nt(
             right, queries[:, part * width:(part + 1) * width]
         )
@@ -213,20 +222,19 @@
     anywhere = pl.BlockSpec(memory_space=pl.ANY)
     params = pltpu.CompilerParams(vmem_limit_bytes=32 << 20)
 
-    sources = (inputs, proj_in, basis_in, out_grads, proj_out, basis_out, queries, eigen)
-    feats, queries, eigen, basis_in, basis_out = pl.pallas_call(
+    sources = (inputs, proj_in, basis_in, out_grads, proj_out, basis_out, eigen)
+    feats, eigen, basis_in, basis_out = pl.pallas_call(
         functools.partial(features_kernel, chunks),
         out_shape=[
             jax.ShapeDtypeStruct((rank, tokens), BF16),
-            jax.ShapeDtypeStruct((count, entries), BF16),
             *[jax.ShapeDtypeStruct((rank, rank), F32)] * 3,
         ],
         in_specs=[hbm] * len(sources),
-        out_specs=[vmem] * 5,
+        out_specs=[vmem] * 4,
         scratch_shapes=[
             pltpu.VMEM((tokens, width), BF16),
             pltpu.VMEM((rank, width), BF16),
-            pltpu.SemaphoreType.DMA((6, chunks)),
+            pltpu.SemaphoreType.DMA((5, chunks)),
         ],
         compiler_params=params,
         cost_estimate=pl.CostEstimate(
@@ -259,27 +267,32 @@
 
     gathered = [across(pairs) for pairs in feature_rounds]
 
+    pieces = 4
     weights = pl.pallas_call(
-        queries_kernel,
+        functools.partial(queries_kernel, pieces),
         out_shape=jax.ShapeDtypeStruct((count, entries), BF16),
-        in_specs=[vmem] * 4,
+        in_specs=[hbm] + [vmem] * 3,
         out_specs=vmem,
-        scratch_shapes=[pltpu.VMEM((entries, count), F32)],
+        scratch_shapes=[
+            pltpu.VMEM((count, entries), BF16),
+            pltpu.VMEM((entries, count), F32),
+            pltpu.SemaphoreType.DMA((pieces,)),
+        ],
         compiler_params=params,
         cost_estimate=pl.CostEstimate(
             flops=4 * PACK * count * entries * rank, bytes_accessed=4 * count * entries, transcendentals=0
         ),
         name="queries",
-    )(queries, basis_in, basis_out, eigen)
+    )(pltpu.with_memory_space_constraint(queries, pltpu.HBM), basis_in, basis_out, eigen)
 
     mine = pl.pallas_call(
-        functools.partial(pack_kernel, feature_rounds[::-1]),
+        functools.partial(pack_kernel, feature_rounds),
         out_shape=jax.ShapeDtypeStruct((train_size, rank, tokens), BF16),
         in_specs=[vmem] * (1 + len(gathered)) + [anywhere],
         out_specs=vmem,
         compiler_params=params,
         name="pack",
-    )(feats, *gathered[::-1], weights)
+    )(feats, *gathered, weights)
     theirs = lax.ppermute(mine, "sub", [(0, 1), (1, 0)])
 
     rows = tokens // layer_size

time: 26.8 us -> 26.9 us (level)
  waiting for transfers between devices: 5.95 us -> 4.03 us
  Pallas kernels: 7.51 us -> 8.93 us
  starting transfers between devices: 13.1 us -> 13.7 us
    pallas_call x2, Pallas kernels: 2.13 us -> 3.56 us  [the longest x1 3.54 us: body(): pl.pallas_call(functools.partial(queries_kernel, pieces), out_shape=jax.S...]
    ppermute x3, waiting for transfers between devices: 1.41 us -> 0.01 us  [across(): return lax.ppermute(feats, ('train', 'sub'), cores)]
    ppermute x3, starting transfers between devices: 4.8 us -> 5.4 us  [body(): arrivals.append(lax.ppermute(block, 'train', pairs))]
    ppermute x3, waiting for transfers between devices: 2.18 us -> 1.66 us  [body(): arrivals.append(lax.ppermute(block, 'train', pairs))]
  transfers between devices with their start and end apart: 9 -> 9, of which waited for: 6 -> 5; matrix products, arithmetic and copies ran while one was open for 0% -> 0% of each run, Pallas kernels for 11% -> 17%
where the time goes in v15:
time: 26.9 us; the launch traced here: 26.7 us
  starting transfers between devices  13.7 us (51%)
  Pallas kernels  8.93 us (33%)
  waiting for transfers between devices  4.03 us (15%)
    ppermute x3, starting transfers between devices, across(): return lax.ppermute(feats, ('train', 'sub'), cores)  5.4 us
    ppermute x3, starting transfers between devices, body(): arrivals.append(lax.ppermute(block, 'train', pairs))  5.4 us
    pallas_call x1, Pallas kernels, body(): pl.pallas_call(functools.partial(queries_kernel, pieces), out_shape=jax.S...  3.54 us
    pallas_call x1, Pallas kernels, body(): pl.pallas_call(functools.partial(features_kernel, chunks), out_shape=[jax...  2.85 us
    ppermute x2, starting transfers between devices, scored(): lax.ppermute(block, 'layer', [(l, (l + k) % layer_size) for l in range(la...  2.17 us
    pallas_call x2, Pallas kernels, scored(): pl.pallas_call(functools.partial(scores_kernel, layer_size, targets), out...  1.74 us
    ppermute x3, waiting for transfers between devices, body(): arrivals.append(lax.ppermute(block, 'train', pairs))  1.66 us
    ppermute x2, waiting for transfers between devices, scored(): lax.ppermute(block, 'layer', [(l, (l + k) % layer_size) for l in range(la...  1.38 us
  transfers between devices with their start and end apart: 9, of which 5 were waited for; matrix products, arithmetic and copies ran while one was open for 0% of the time, Pallas kernels for 17%

profile of v15, /device:TPU:0, one launch (start us, length us, event | category | flops | bytes accessed | tf_op | source)
XLA Modules:
  0.0 26.7 jit_solution(2723795190331303168)
XLA Ops:
  0.0 2.8 %features.1 = (bf16[64,256]{1,0:T(8,128)(2,1)S(1)}, f32[64,64]{1,0:T(8,128)S(1)}, f32[64,64]{1,0:T(8,128)S(1)}, f32[64,64]{1,0:T(8,128)S(1)}) custom-call(bf16[1,256,4096]{2,1,0:T(8,128)(2,1)} %refs_0_.1, bf16[1,64,4096]{2,1,0:T(8,128)(2,1)} %refs_1_.1, f32[1,64,64]{2,1,0:T(8,128)} %refs_2_.1, bf16[1,256,4096]{2,1,0:T(8,128)(2,1)} %refs_3_.1, ...), custom_call_target="tpu_custom_call" | custom-call | flops 134217728 | bytes 2621440 | tf_op jit(solution)/shard_map/features/pallas_call | solution.py:226
  2.9 3.5 %collective-permute-start = (bf16[64,256]{1,0:T(8,128)(2,1)S(1)}, bf16[64,256]{1,0:T(8,128)(2,1)S(1)}, u32[]{:S(2)}, u32[]{:S(2)}) collective-permute-start(bf16[64,256]{1,0:T(8,128)(2,1)S(1)} %get-tuple-element.16.refs_0_), channel_id=1, source_target_pairs={{0,9},{1,8},{4,13},{5,12},{8,1},{9,0},{12,5},{13,4},{2,11},{3,10},... | collective-permute-start | bytes 98312 | tf_op jit(solution)/shard_map/ppermute | solution.py:266
  6.4 1.6 %collective-permute-start.1 = (bf16[64,256]{1,0:T(8,128)(2,1)S(1)}, bf16[64,256]{1,0:T(8,128)(2,1)S(1)}, u32[]{:S(2)}, u32[]{:S(2)}) collective-permute-start(bf16[64,256]{1,0:T(8,128)(2,1)S(1)} %get-tuple-element.16.refs_0_), channel_id=1, source_target_pairs={{0,13},{1,12},{4,9},{5,8},{8,5},{9,4},{12,1},{13,0},{2,15},{3,14},... | collective-permute-start | bytes 98312 | tf_op jit(solution)/shard_map/ppermute | solution.py:266
  8.0 0.2 collective-permute-start.2
  8.3 3.5 %queries.1.refs_4_.weights = bf16[128,4096]{1,0:T(8,128)(2,1)S(1)} custom-call(bf16[1,128,4096]{2,1,0:T(8,128)(2,1)} %queries_hbm.1, f32[64,64]{1,0:T(8,128)S(1)} %get-tuple-element.13.basis_in, f32[64,64]{1,0:T(8,128)S(1)} %get-tuple-element.14.basis_out, f32[64,64]{1,0:T(8,128)S(1)} %get-tuple-element.15.eigen), custom_call_target="tpu_custom_call" | custom-call | flops 536870912 | bytes 2097152 | tf_op jit(solution)/shard_map/queries/pallas_call | solution.py:271
  11.8 0.0 collective-permute-done.refs_1_
  11.8 0.0 collective-permute-done.1.refs_2_
  11.8 0.0 collective-permute-done.2.refs_3_
  11.9 0.7 %collective-permute-start.3 = (bf16[4,64,256]{2,1,0:T(8,128)(2,1)S(1)}, bf16[4,64,256]{2,1,0:T(8,128)(2,1)S(1)}, u32[]{:S(2)}, u32[]{:S(2)}) collective-permute-start(bf16[4,64,256]{2,1,0:T(8,128)(2,1)S(1)} %pack.1.mine), channel_id=1, source_target_pairs={{0,1},{1,0},{2,3},{3,2},{4,5},{5,4},{6,7},{7,6},{8,9},{9,8},{10,11... | collective-permute-start | bytes 393224 | tf_op jit(solution)/shard_map/ppermute | solution.py:296
  12.6 1.0 %collective-permute-done.3.theirs = bf16[4,64,256]{2,1,0:T(8,128)(2,1)S(1)} collective-permute-done((bf16[4,64,256]{2,1,0:T(8,128)(2,1)S(1)}, bf16[4,64,256]{2,1,0:T(8,128)(2,1)S(1)}, u32[]{:S(2)}, u32[]{:S(2)}) %collective-permute-start.3) | collective-permute-done | bytes 131104 | tf_op jit(solution)/shard_map/ppermute | solution.py:296
  13.5 0.9 %scores.2 = (f32[2,128,128]{2,1,0:T(8,128)S(1)}, bf16[2,128,128]{2,1,0:T(8,128)(2,1)S(1)}) custom-call(bf16[128,4096]{1,0:T(8,128)(2,1)S(1)} %queries.1.refs_4_.weights, bf16[4,64,256]{2,1,0:T(8,128)(2,1)S(1)} %pack.1.mine, bf16[4,64,256]{2,1,0:T(8,128)(2,1)S(1)} %collective-permute-done.3.theirs), custom_call_target="tpu_custom_call" | custom-call | flops 536870912 | bytes 1048576 | tf_op jit(solution)/shard_map/scores/pallas_call | solution.py:301
  14.4 1.6 %collective-permute-start.5 = (bf16[2,128,128]{2,1,0:T(8,128)(2,1)S(1)}, bf16[2,128,128]{2,1,0:T(8,128)(2,1)S(1)}, u32[]{:S(2)}, u32[]{:S(2)}) collective-permute-start(bf16[2,128,128]{2,1,0:T(8,128)(2,1)S(1)} %get-tuple-element.20), channel_id=1, source_target_pairs={{0,2},{2,0},{1,3},{3,1},{4,6},{6,4},{5,7},{7,5},{8,10},{10,8},{9,1... | collective-permute-start | bytes 196616 | tf_op jit(solution)/shard_map/ppermute | solution.py:319
  16.0 0.9 %scores.3 = (f32[2,128,128]{2,1,0:T(8,128)S(1)}, bf16[2,128,128]{2,1,0:T(8,128)(2,1)S(1)}) custom-call(bf16[128,4096]{1,0:T(8,128)(2,1)S(1)} %queries.1.refs_4_.weights, bf16[4,64,256]{2,1,0:T(8,128)(2,1)S(1)} %pack.1.mine, bf16[4,64,256]{2,1,0:T(8,128)(2,1)S(1)} %collective-permute-done.3.theirs, f32[2,128,128]{2,1,0:T(8,128)S(1)} %get-tuple-element.17.refs_0_.own), custom_call_target="tpu_custom_call" | custom-call | flops 536870912 | bytes 1048576 | tf_op jit(solution)/shard_map/scores/pallas_call | solution.py:301
  16.9 0.6 %collective-permute-start.4 = (bf16[2,128,128]{2,1,0:T(8,128)(2,1)S(1)}, bf16[2,128,128]{2,1,0:T(8,128)(2,1)S(1)}, u32[]{:S(2)}, u32[]{:S(2)}) collective-permute-start(bf16[2,128,128]{2,1,0:T(8,128)(2,1)S(1)} %get-tuple-element.19), channel_id=1, source_target_pairs={{0,2},{2,0},{1,3},{3,1},{4,6},{6,4},{5,7},{7,5},{8,10},{10,8},{9,1... | collective-permute-start | bytes 196616 | tf_op jit(solution)/shard_map/ppermute | solution.py:319
  17.5 1.4 %collective-permute-done.5.refs_0_ = bf16[2,128,128]{2,1,0:T(8,128)(2,1)S(1)} collective-permute-done((bf16[2,128,128]{2,1,0:T(8,128)(2,1)S(1)}, bf16[2,128,128]{2,1,0:T(8,128)(2,1)S(1)}, u32[]{:S(2)}, u32[]{:S(2)}) %collective-permute-start.5) | collective-permute-done | bytes 65568 | tf_op jit(solution)/shard_map/ppermute | solution.py:319
  18.9 1.3 %collective-permute-start.6 = (bf16[128,128]{1,0:T(8,128)(2,1)S(1)}, bf16[128,128]{1,0:T(8,128)(2,1)S(1)}, u32[]{:S(2)}, u32[]{:S(2)}) collective-permute-start(bf16[128,128]{1,0:T(8,128)(2,1)S(1)} %layers.4.refs_1_), channel_id=1, source_target_pairs={{0,4},{4,8},{8,12},{12,0},{1,5},{5,9},{9,13},{13,1},{2,6},{6,10},{... | collective-permute-start | bytes 98312 | tf_op jit(solution)/shard_map/ppermute | solution.py:354
  20.2 1.8 %collective-permute-start.7 = (bf16[128,128]{1,0:T(8,128)(2,1)S(1)}, bf16[128,128]{1,0:T(8,128)(2,1)S(1)}, u32[]{:S(2)}, u32[]{:S(2)}) collective-permute-start(bf16[128,128]{1,0:T(8,128)(2,1)S(1)} %layers.5.refs_1_), channel_id=1, source_target_pairs={{0,8},{4,12},{8,0},{12,4},{1,9},{5,13},{9,1},{13,5},{2,10},{6,14},... | collective-permute-start | bytes 98312 | tf_op jit(solution)/shard_map/ppermute | solution.py:354
  22.0 0.0 collective-permute-done.4.refs_0_
  22.0 2.3 %collective-permute-start.8 = (bf16[128,128]{1,0:T(8,128)(2,1)S(1)}, bf16[128,128]{1,0:T(8,128)(2,1)S(1)}, u32[]{:S(2)}, u32[]{:S(2)}) collective-permute-start(bf16[128,128]{1,0:T(8,128)(2,1)S(1)} %layers.7), channel_id=1, source_target_pairs={{0,12},{4,0},{8,4},{12,8},{1,13},{5,1},{9,5},{13,9},{2,14},{6,2},{... | collective-permute-start | bytes 98312 | tf_op jit(solution)/shard_map/ppermute | solution.py:354
  24.3 0.7 %collective-permute-done.6.block = bf16[128,128]{1,0:T(8,128)(2,1)S(1)} collective-permute-done((bf16[128,128]{1,0:T(8,128)(2,1)S(1)}, bf16[128,128]{1,0:T(8,128)(2,1)S(1)}, u32[]{:S(2)}, u32[]{:S(2)}) %collective-permute-start.6) | collective-permute-done | bytes 32800 | tf_op jit(solution)/shard_map/ppermute | solution.py:354
  25.0 0.5 %collective-permute-done.7.block = bf16[128,128]{1,0:T(8,128)(2,1)S(1)} collective-permute-done((bf16[128,128]{1,0:T(8,128)(2,1)S(1)}, bf16[128,128]{1,0:T(8,128)(2,1)S(1)}, u32[]{:S(2)}, u32[]{:S(2)}) %collective-permute-start.7) | collective-permute-done | bytes 32800 | tf_op jit(solution)/shard_map/ppermute | solution.py:354
  25.5 0.5 %collective-permute-done.8.refs_2_ = bf16[128,128]{1,0:T(8,128)(2,1)S(1)} collective-permute-done((bf16[128,128]{1,0:T(8,128)(2,1)S(1)}, bf16[128,128]{1,0:T(8,128)(2,1)S(1)}, u32[]{:S(2)}, u32[]{:S(2)}) %collective-permute-start.8) | collective-permute-done | bytes 32800 | tf_op jit(solution)/shard_map/ppermute | solution.py:354
  26.0 0.7 %place.1 = f32[512,128]{1,0:T(8,128)} custom-call(f32[128,128]{1,0:T(8,128)S(1)} %layers.6.refs_1_.own, bf16[128,128]{1,0:T(8,128)(2,1)S(1)} %keep.2.refs_0_, bf16[128,128]{1,0:T(8,128)(2,1)S(1)} %keep.3.refs_1_, bf16[128,128]{1,0:T(8,128)(2,1)S(1)} %collective-permute-done.8.refs_2_), custom_call_target="tpu_custom_call" | custom-call | tf_op jit(solution)/shard_map/place/pallas_call | solution.py:358
  (7 shorter events, 0.1 us)
Async XLA Ops:
  2.9 9.0 %collective-permute-start = (bf16[64,256]{1,0:T(8,128)(2,1)S(1)}, bf16[64,256]{1,0:T(8,128)(2,1)S(1)}, u32[]{:S(2)}, u32[]{:S(2)}) collective-permute-start(bf16[64,256]{1,0:T(8,128)(2,1)S(1)} %get-tuple-element.16.refs_0_), channel_id=1, source_target_pairs={{0,9},{1,8},{4,13},{5,12},{8,1},{9,0},{12,5},{13,4},{2,11},{3,10},... | collective-permute-start | bytes 98312 | tf_op jit(solution)/shard_map/ppermute | solution.py:266
  6.4 5.4 %collective-permute-start.1 = (bf16[64,256]{1,0:T(8,128)(2,1)S(1)}, bf16[64,256]{1,0:T(8,128)(2,1)S(1)}, u32[]{:S(2)}, u32[]{:S(2)}) collective-permute-start(bf16[64,256]{1,0:T(8,128)(2,1)S(1)} %get-tuple-element.16.refs_0_), channel_id=1, source_target_pairs={{0,13},{1,12},{4,9},{5,8},{8,5},{9,4},{12,1},{13,0},{2,15},{3,14},... | collective-permute-start | bytes 98312 | tf_op jit(solution)/shard_map/ppermute | solution.py:266
  8.0 3.8 %collective-permute-start.2 = (bf16[64,256]{1,0:T(8,128)(2,1)S(1)}, bf16[64,256]{1,0:T(8,128)(2,1)S(1)}, u32[]{:S(2)}, u32[]{:S(2)}) collective-permute-start(bf16[64,256]{1,0:T(8,128)(2,1)S(1)} %get-tuple-element.16.refs_0_), channel_id=1, source_target_pairs={{0,5},{1,4},{4,1},{5,0},{8,13},{9,12},{12,9},{13,8},{2,7},{3,6},{6... | collective-permute-start | bytes 98312 | tf_op jit(solution)/shard_map/ppermute | solution.py:266
  11.9 1.7 %collective-permute-start.3 = (bf16[4,64,256]{2,1,0:T(8,128)(2,1)S(1)}, bf16[4,64,256]{2,1,0:T(8,128)(2,1)S(1)}, u32[]{:S(2)}, u32[]{:S(2)}) collective-permute-start(bf16[4,64,256]{2,1,0:T(8,128)(2,1)S(1)} %pack.1.mine), channel_id=1, source_target_pairs={{0,1},{1,0},{2,3},{3,2},{4,5},{5,4},{6,7},{7,6},{8,9},{9,8},{10,11... | collective-permute-start | bytes 393224 | tf_op jit(solution)/shard_map/ppermute | solution.py:296
  14.4 4.4 %collective-permute-start.5 = (bf16[2,128,128]{2,1,0:T(8,128)(2,1)S(1)}, bf16[2,128,128]{2,1,0:T(8,128)(2,1)S(1)}, u32[]{:S(2)}, u32[]{:S(2)}) collective-permute-start(bf16[2,128,128]{2,1,0:T(8,128)(2,1)S(1)} %get-tuple-element.20), channel_id=1, source_target_pairs={{0,2},{2,0},{1,3},{3,1},{4,6},{6,4},{5,7},{7,5},{8,10},{10,8},{9,1... | collective-permute-start | bytes 196616 | tf_op jit(solution)/shard_map/ppermute | solution.py:319
  16.9 5.1 %collective-permute-start.4 = (bf16[2,128,128]{2,1,0:T(8,128)(2,1)S(1)}, bf16[2,128,128]{2,1,0:T(8,128)(2,1)S(1)}, u32[]{:S(2)}, u32[]{:S(2)}) collective-permute-start(bf16[2,128,128]{2,1,0:T(8,128)(2,1)S(1)} %get-tuple-element.19), channel_id=1, source_target_pairs={{0,2},{2,0},{1,3},{3,1},{4,6},{6,4},{5,7},{7,5},{8,10},{10,8},{9,1... | collective-permute-start | bytes 196616 | tf_op jit(solution)/shard_map/ppermute | solution.py:319
  18.9 6.1 %collective-permute-start.6 = (bf16[128,128]{1,0:T(8,128)(2,1)S(1)}, bf16[128,128]{1,0:T(8,128)(2,1)S(1)}, u32[]{:S(2)}, u32[]{:S(2)}) collective-permute-start(bf16[128,128]{1,0:T(8,128)(2,1)S(1)} %layers.4.refs_1_), channel_id=1, source_target_pairs={{0,4},{4,8},{8,12},{12,0},{1,5},{5,9},{9,13},{13,1},{2,6},{6,10},{... | collective-permute-start | bytes 98312 | tf_op jit(solution)/shard_map/ppermute | solution.py:354
  20.2 5.2 %collective-permute-start.7 = (bf16[128,128]{1,0:T(8,128)(2,1)S(1)}, bf16[128,128]{1,0:T(8,128)(2,1)S(1)}, u32[]{:S(2)}, u32[]{:S(2)}) collective-permute-start(bf16[128,128]{1,0:T(8,128)(2,1)S(1)} %layers.5.refs_1_), channel_id=1, source_target_pairs={{0,8},{4,12},{8,0},{12,4},{1,9},{5,13},{9,1},{13,5},{2,10},{6,14},... | collective-permute-start | bytes 98312 | tf_op jit(solution)/shard_map/ppermute | solution.py:354
  22.0 4.0 %collective-permute-start.8 = (bf16[128,128]{1,0:T(8,128)(2,1)S(1)}, bf16[128,128]{1,0:T(8,128)(2,1)S(1)}, u32[]{:S(2)}, u32[]{:S(2)}) collective-permute-start(bf16[128,128]{1,0:T(8,128)(2,1)S(1)} %layers.7), channel_id=1, source_target_pairs={{0,12},{4,0},{8,4},{12,8},{1,13},{5,1},{9,5},{13,9},{2,14},{6,2},{... | collective-permute-start | bytes 98312 | tf_op jit(solution)/shard_map/ppermute | solution.py:354

commit v16 on v14

--- a/solution.py
+++ b/solution.py
@@ -59,38 +59,32 @@
     sides, (queries_hbm, eigen_hbm) = (refs[0:3], refs[3:6]), refs[6:8]
     feats, queries, eigen, basis_in, basis_out, rows, proj, sems = refs[8:]
     core = lax.axis_index("sub")
-    step = rows.shape[1] // chunks
-
-    def part(chunk):
-        return pl.ds(chunk * step, step)
+    step = rows.shape[0] // chunks
+
+    def copies(rows_hbm, proj_hbm):
+        pieces = [pl.ds(chunk * step, step) for chunk in range(chunks)]
+        pairs = [(rows_hbm.at[0, piece], rows.at[piece]) for piece in pieces]
+        pairs.append((proj_hbm.at[0], proj))
+        return [pltpu.make_async_copy(*pair, sems.at[0, i]) for i, pair in enumerate(pairs)]
 
     for side, (rows_hbm, proj_hbm, _) in enumerate(sides):
         @pl.when(core == side)
         def _():
-            for chunk in range(chunks):
-                for number, (source, target) in enumerate(((proj_hbm, proj), (rows_hbm, rows))):
-                    pltpu.make_async_copy(
-                        source.at[0, :, part(chunk)], target.at[:, part(chunk)], sems.at[number, chunk]
-                    ).start()
+            for copy in copies(rows_hbm, proj_hbm):
+                copy.start()
 
     others = [
-        pltpu.make_async_copy(source.at[0], target, sems.at[2 + number, 0])
+        pltpu.make_async_copy(source.at[0], target, sems.at[1, number])
         for number, (source, target) in enumerate((
             (sides[0][2], basis_in), (sides[1][2], basis_out), (eigen_hbm, eigen), (queries_hbm, queries)
         ))
     ]
     for copy in others:
         copy.start()
-    total = None
-    for chunk in range(chunks):
-        for number, (source, target) in enumerate(((sides[0][1], proj), (sides[0][0], rows))):
-            pltpu.make_async_copy(
-                source.at[0, :, part(chunk)], target.at[:, part(chunk)], sems.at[number, chunk]
-            ).wait()
-        columns = slice(chunk * step, (chunk + 1) * step)
-        term = nt(proj[:, columns], rows[:, columns])
-        total = term if total is None else total + term
-    for copy in others:
+    for copy in copies(*sides[0][:2]):
+        copy.wait()
+    total = nt(proj[...], rows[...])
+    for copy in others[:2]:
         copy.wait()
     basis = jnp.where(core == 0, basis_in[...], basis_out[...])
     feats[...] = jnp.dot(
@@ -98,6 +92,8 @@
         jnp.concatenate([total.astype(BF16)] * 2, axis=0),
         preferred_element_type=F32,
     ).astype(BF16)
+    for copy in others[2:]:
+        copy.wait()
 
 
 def pack_kernel(rounds, *refs):
@@ -208,7 +204,7 @@
     tokens, width = inputs.shape[1:]
     count, entries = queries.shape[1:]
     rank = proj_in.shape[1]
-    chunks = 1
+    chunks = 4
     vmem, hbm = pl.BlockSpec(memory_space=pltpu.VMEM), pl.BlockSpec(memory_space=pltpu.HBM)
     anywhere = pl.BlockSpec(memory_space=pl.ANY)
     params = pltpu.CompilerParams(vmem_limit_bytes=32 << 20)
@@ -226,7 +222,7 @@
         scratch_shapes=[
             pltpu.VMEM((tokens, width), BF16),
             pltpu.VMEM((rank, width), BF16),
-            pltpu.SemaphoreType.DMA((6, chunks)),
+            pltpu.SemaphoreType.DMA((2, chunks + 1)),
         ],
         compiler_params=params,
         cost_estimate=pl.CostEstimate(

time: 26.8 us -> 26.7 us (level)
  no operation moved by 1% of the time
where the time goes in v16:
time: 26.7 us; the launch traced here: 26.6 us
  starting transfers between devices  13.1 us (49%)
  Pallas kernels  7.45 us (28%)
  waiting for transfers between devices  5.95 us (22%)
    ppermute x3, starting transfers between devices, across(): return lax.ppermute(feats, ('train', 'sub'), cores)  5.4 us
    ppermute x3, starting transfers between devices, body(): arrivals.append(lax.ppermute(block, 'train', pairs))  4.8 us
    pallas_call x1, Pallas kernels, body(): pl.pallas_call(functools.partial(features_kernel, chunks), out_shape=[jax...  2.8 us
    ppermute x3, waiting for transfers between devices, body(): arrivals.append(lax.ppermute(block, 'train', pairs))  2.18 us
    ppermute x2, starting transfers between devices, scored(): lax.ppermute(block, 'layer', [(l, (l + k) % layer_size) for l in range(la...  2.17 us
    pallas_call x1, Pallas kernels, body(): pl.pallas_call(queries_kernel, out_shape=jax.ShapeDtypeStruct((count, ent...  2.11 us
    pallas_call x2, Pallas kernels, scored(): pl.pallas_call(functools.partial(scores_kernel, layer_size, targets), out...  1.74 us
    ppermute x3, waiting for transfers between devices, across(): return lax.ppermute(feats, ('train', 'sub'), cores)  1.41 us
  transfers between devices with their start and end apart: 9, of which 6 were waited for; matrix products, arithmetic and copies ran while one was open for 0% of the time, Pallas kernels for 11%

profile of v16, /device:TPU:0, one launch (start us, length us, event | category | flops | bytes accessed | tf_op | source)
XLA Modules:
  0.0 26.6 jit_solution(1179470971778374896)
XLA Ops:
  0.0 2.8 %features.1 = (bf16[64,256]{1,0:T(8,128)(2,1)S(1)}, bf16[128,4096]{1,0:T(8,128)(2,1)S(1)}, f32[64,64]{1,0:T(8,128)S(1)}, f32[64,64]{1,0:T(8,128)S(1)}, f32[64,64]{1,0:T(8,128)S(1)}) custom-call(bf16[1,256,4096]{2,1,0:T(8,128)(2,1)} %refs_0_.1, bf16[1,64,4096]{2,1,0:T(8,128)(2,1)} %refs_1_.1, f32[1,64,64]{2,1,0:T(8,128)} %refs_2_.1, ...), custom_call_target="tpu_custom_call" | custom-call | flops 134217728 | bytes 2621440 | tf_op jit(solution)/shard_map/features/pallas_call | solution.py:213
  2.8 3.5 %collective-permute-start.2 = (bf16[64,256]{1,0:T(8,128)(2,1)S(1)}, bf16[64,256]{1,0:T(8,128)(2,1)S(1)}, u32[]{:S(2)}, u32[]{:S(2)}) collective-permute-start(bf16[64,256]{1,0:T(8,128)(2,1)S(1)} %get-tuple-element.18.refs_0_), channel_id=1, source_target_pairs={{0,9},{1,8},{4,13},{5,12},{8,1},{9,0},{12,5},{13,4},{2,11},{3,10},... | collective-permute-start | bytes 98312 | tf_op jit(solution)/shard_map/ppermute | solution.py:254
  6.3 1.6 %collective-permute-start.1 = (bf16[64,256]{1,0:T(8,128)(2,1)S(1)}, bf16[64,256]{1,0:T(8,128)(2,1)S(1)}, u32[]{:S(2)}, u32[]{:S(2)}) collective-permute-start(bf16[64,256]{1,0:T(8,128)(2,1)S(1)} %get-tuple-element.18.refs_0_), channel_id=1, source_target_pairs={{0,13},{1,12},{4,9},{5,8},{8,5},{9,4},{12,1},{13,0},{2,15},{3,14},... | collective-permute-start | bytes 98312 | tf_op jit(solution)/shard_map/ppermute | solution.py:254
  8.0 0.2 collective-permute-start
  8.2 2.1 %queries.1.refs_4_.weights = bf16[128,4096]{1,0:T(8,128)(2,1)S(1)} custom-call(bf16[128,4096]{1,0:T(8,128)(2,1)S(1)} %get-tuple-element.14.queries, f32[64,64]{1,0:T(8,128)S(1)} %get-tuple-element.15.basis_in, f32[64,64]{1,0:T(8,128)S(1)} %get-tuple-element.16.basis_out, f32[64,64]{1,0:T(8,128)S(1)} %get-tuple-element.17.eigen), custom_call_target="tpu_custom_call" | custom-call | flops 536870912 | bytes 2097152 | tf_op jit(solution)/shard_map/queries/pallas_call | solution.py:258
  10.3 0.0 collective-permute-done.2.refs_3_
  10.3 1.3 %collective-permute-done.1.refs_2_ = bf16[64,256]{1,0:T(8,128)(2,1)S(1)} collective-permute-done((bf16[64,256]{1,0:T(8,128)(2,1)S(1)}, bf16[64,256]{1,0:T(8,128)(2,1)S(1)}, u32[]{:S(2)}, u32[]{:S(2)}) %collective-permute-start.1) | collective-permute-done | bytes 32800 | tf_op jit(solution)/shard_map/ppermute | solution.py:254
  11.6 0.1 collective-permute-done.refs_1_
  11.8 0.7 %collective-permute-start.3 = (bf16[4,64,256]{2,1,0:T(8,128)(2,1)S(1)}, bf16[4,64,256]{2,1,0:T(8,128)(2,1)S(1)}, u32[]{:S(2)}, u32[]{:S(2)}) collective-permute-start(bf16[4,64,256]{2,1,0:T(8,128)(2,1)S(1)} %pack.1.mine), channel_id=1, source_target_pairs={{0,1},{1,0},{2,3},{3,2},{4,5},{5,4},{6,7},{7,6},{8,9},{9,8},{10,11... | collective-permute-start | bytes 393224 | tf_op jit(solution)/shard_map/ppermute | solution.py:279
  12.5 1.0 %collective-permute-done.3.theirs = bf16[4,64,256]{2,1,0:T(8,128)(2,1)S(1)} collective-permute-done((bf16[4,64,256]{2,1,0:T(8,128)(2,1)S(1)}, bf16[4,64,256]{2,1,0:T(8,128)(2,1)S(1)}, u32[]{:S(2)}, u32[]{:S(2)}) %collective-permute-start.3) | collective-permute-done | bytes 131104 | tf_op jit(solution)/shard_map/ppermute | solution.py:279
  13.5 0.9 %scores.2 = (f32[2,128,128]{2,1,0:T(8,128)S(1)}, bf16[2,128,128]{2,1,0:T(8,128)(2,1)S(1)}) custom-call(bf16[128,4096]{1,0:T(8,128)(2,1)S(1)} %queries.1.refs_4_.weights, bf16[4,64,256]{2,1,0:T(8,128)(2,1)S(1)} %pack.1.mine, bf16[4,64,256]{2,1,0:T(8,128)(2,1)S(1)} %collective-permute-done.3.theirs), custom_call_target="tpu_custom_call" | custom-call | flops 536870912 | bytes 1048576 | tf_op jit(solution)/shard_map/scores/pallas_call | solution.py:284
  14.4 1.6 %collective-permute-start.5 = (bf16[2,128,128]{2,1,0:T(8,128)(2,1)S(1)}, bf16[2,128,128]{2,1,0:T(8,128)(2,1)S(1)}, u32[]{:S(2)}, u32[]{:S(2)}) collective-permute-start(bf16[2,128,128]{2,1,0:T(8,128)(2,1)S(1)} %get-tuple-element.22), channel_id=1, source_target_pairs={{0,2},{2,0},{1,3},{3,1},{4,6},{6,4},{5,7},{7,5},{8,10},{10,8},{9,1... | collective-permute-start | bytes 196616 | tf_op jit(solution)/shard_map/ppermute | solution.py:302
  15.9 0.9 %scores.3 = (f32[2,128,128]{2,1,0:T(8,128)S(1)}, bf16[2,128,128]{2,1,0:T(8,128)(2,1)S(1)}) custom-call(bf16[128,4096]{1,0:T(8,128)(2,1)S(1)} %queries.1.refs_4_.weights, bf16[4,64,256]{2,1,0:T(8,128)(2,1)S(1)} %pack.1.mine, bf16[4,64,256]{2,1,0:T(8,128)(2,1)S(1)} %collective-permute-done.3.theirs, f32[2,128,128]{2,1,0:T(8,128)S(1)} %get-tuple-element.19.refs_0_.own), custom_call_target="tpu_custom_call" | custom-call | flops 536870912 | bytes 1048576 | tf_op jit(solution)/shard_map/scores/pallas_call | solution.py:284
  16.8 0.6 %collective-permute-start.4 = (bf16[2,128,128]{2,1,0:T(8,128)(2,1)S(1)}, bf16[2,128,128]{2,1,0:T(8,128)(2,1)S(1)}, u32[]{:S(2)}, u32[]{:S(2)}) collective-permute-start(bf16[2,128,128]{2,1,0:T(8,128)(2,1)S(1)} %get-tuple-element.21), channel_id=1, source_target_pairs={{0,2},{2,0},{1,3},{3,1},{4,6},{6,4},{5,7},{7,5},{8,10},{10,8},{9,1... | collective-permute-start | bytes 196616 | tf_op jit(solution)/shard_map/ppermute | solution.py:302
  17.4 1.4 %collective-permute-done.5.refs_0_ = bf16[2,128,128]{2,1,0:T(8,128)(2,1)S(1)} collective-permute-done((bf16[2,128,128]{2,1,0:T(8,128)(2,1)S(1)}, bf16[2,128,128]{2,1,0:T(8,128)(2,1)S(1)}, u32[]{:S(2)}, u32[]{:S(2)}) %collective-permute-start.5) | collective-permute-done | bytes 65568 | tf_op jit(solution)/shard_map/ppermute | solution.py:302
  18.8 0.1 collective-permute-start.6
  18.9 3.0 %collective-permute-start.7 = (bf16[128,128]{1,0:T(8,128)(2,1)S(1)}, bf16[128,128]{1,0:T(8,128)(2,1)S(1)}, u32[]{:S(2)}, u32[]{:S(2)}) collective-permute-start(bf16[128,128]{1,0:T(8,128)(2,1)S(1)} %layers.5.refs_1_), channel_id=1, source_target_pairs={{0,8},{4,12},{8,0},{12,4},{1,9},{5,13},{9,1},{13,5},{2,10},{6,14},... | collective-permute-start | bytes 98312 | tf_op jit(solution)/shard_map/ppermute | solution.py:337
  21.9 0.0 collective-permute-done.4.refs_0_
  21.9 1.8 %collective-permute-start.8 = (bf16[128,128]{1,0:T(8,128)(2,1)S(1)}, bf16[128,128]{1,0:T(8,128)(2,1)S(1)}, u32[]{:S(2)}, u32[]{:S(2)}) collective-permute-start(bf16[128,128]{1,0:T(8,128)(2,1)S(1)} %layers.7), channel_id=1, source_target_pairs={{0,12},{4,0},{8,4},{12,8},{1,13},{5,1},{9,5},{13,9},{2,14},{6,2},{... | collective-permute-start | bytes 98312 | tf_op jit(solution)/shard_map/ppermute | solution.py:337
  23.7 0.9 %collective-permute-done.6.block = bf16[128,128]{1,0:T(8,128)(2,1)S(1)} collective-permute-done((bf16[128,128]{1,0:T(8,128)(2,1)S(1)}, bf16[128,128]{1,0:T(8,128)(2,1)S(1)}, u32[]{:S(2)}, u32[]{:S(2)}) %collective-permute-start.6) | collective-permute-done | bytes 32800 | tf_op jit(solution)/shard_map/ppermute | solution.py:337
  24.6 0.0 collective-permute-done.7.block
  24.6 1.3 %collective-permute-done.8.refs_2_ = bf16[128,128]{1,0:T(8,128)(2,1)S(1)} collective-permute-done((bf16[128,128]{1,0:T(8,128)(2,1)S(1)}, bf16[128,128]{1,0:T(8,128)(2,1)S(1)}, u32[]{:S(2)}, u32[]{:S(2)}) %collective-permute-start.8) | collective-permute-done | bytes 32800 | tf_op jit(solution)/shard_map/ppermute | solution.py:337
  25.9 0.7 %place.1 = f32[512,128]{1,0:T(8,128)} custom-call(f32[128,128]{1,0:T(8,128)S(1)} %layers.6.refs_1_.own, bf16[128,128]{1,0:T(8,128)(2,1)S(1)} %keep.2.refs_0_, bf16[128,128]{1,0:T(8,128)(2,1)S(1)} %keep.3.refs_1_, bf16[128,128]{1,0:T(8,128)(2,1)S(1)} %collective-permute-done.8.refs_2_), custom_call_target="tpu_custom_call" | custom-call | tf_op jit(solution)/shard_map/place/pallas_call | solution.py:341
  (7 shorter events, 0.1 us)
Async XLA Ops:
  2.8 7.5 %collective-permute-start.2 = (bf16[64,256]{1,0:T(8,128)(2,1)S(1)}, bf16[64,256]{1,0:T(8,128)(2,1)S(1)}, u32[]{:S(2)}, u32[]{:S(2)}) collective-permute-start(bf16[64,256]{1,0:T(8,128)(2,1)S(1)} %get-tuple-element.18.refs_0_), channel_id=1, source_target_pairs={{0,9},{1,8},{4,13},{5,12},{8,1},{9,0},{12,5},{13,4},{2,11},{3,10},... | collective-permute-start | bytes 98312 | tf_op jit(solution)/shard_map/ppermute | solution.py:254
  6.3 5.2 %collective-permute-start.1 = (bf16[64,256]{1,0:T(8,128)(2,1)S(1)}, bf16[64,256]{1,0:T(8,128)(2,1)S(1)}, u32[]{:S(2)}, u32[]{:S(2)}) collective-permute-start(bf16[64,256]{1,0:T(8,128)(2,1)S(1)} %get-tuple-element.18.refs_0_), channel_id=1, source_target_pairs={{0,13},{1,12},{4,9},{5,8},{8,5},{9,4},{12,1},{13,0},{2,15},{3,14},... | collective-permute-start | bytes 98312 | tf_op jit(solution)/shard_map/ppermute | solution.py:254
  8.0 3.8 %collective-permute-start = (bf16[64,256]{1,0:T(8,128)(2,1)S(1)}, bf16[64,256]{1,0:T(8,128)(2,1)S(1)}, u32[]{:S(2)}, u32[]{:S(2)}) collective-permute-start(bf16[64,256]{1,0:T(8,128)(2,1)S(1)} %get-tuple-element.18.refs_0_), channel_id=1, source_target_pairs={{0,5},{1,4},{4,1},{5,0},{8,13},{9,12},{12,9},{13,8},{2,7},{3,6},{6... | collective-permute-start | bytes 98312 | tf_op jit(solution)/shard_map/ppermute | solution.py:254
  11.8 1.7 %collective-permute-start.3 = (bf16[4,64,256]{2,1,0:T(8,128)(2,1)S(1)}, bf16[4,64,256]{2,1,0:T(8,128)(2,1)S(1)}, u32[]{:S(2)}, u32[]{:S(2)}) collective-permute-start(bf16[4,64,256]{2,1,0:T(8,128)(2,1)S(1)} %pack.1.mine), channel_id=1, source_target_pairs={{0,1},{1,0},{2,3},{3,2},{4,5},{5,4},{6,7},{7,6},{8,9},{9,8},{10,11... | collective-permute-start | bytes 393224 | tf_op jit(solution)/shard_map/ppermute | solution.py:279
  14.4 4.4 %collective-permute-start.5 = (bf16[2,128,128]{2,1,0:T(8,128)(2,1)S(1)}, bf16[2,128,128]{2,1,0:T(8,128)(2,1)S(1)}, u32[]{:S(2)}, u32[]{:S(2)}) collective-permute-start(bf16[2,128,128]{2,1,0:T(8,128)(2,1)S(1)} %get-tuple-element.22), channel_id=1, source_target_pairs={{0,2},{2,0},{1,3},{3,1},{4,6},{6,4},{5,7},{7,5},{8,10},{10,8},{9,1... | collective-permute-start | bytes 196616 | tf_op jit(solution)/shard_map/ppermute | solution.py:302
  16.8 5.0 %collective-permute-start.4 = (bf16[2,128,128]{2,1,0:T(8,128)(2,1)S(1)}, bf16[2,128,128]{2,1,0:T(8,128)(2,1)S(1)}, u32[]{:S(2)}, u32[]{:S(2)}) collective-permute-start(bf16[2,128,128]{2,1,0:T(8,128)(2,1)S(1)} %get-tuple-element.21), channel_id=1, source_target_pairs={{0,2},{2,0},{1,3},{3,1},{4,6},{6,4},{5,7},{7,5},{8,10},{10,8},{9,1... | collective-permute-start | bytes 196616 | tf_op jit(solution)/shard_map/ppermute | solution.py:302
  18.8 5.8 %collective-permute-start.6 = (bf16[128,128]{1,0:T(8,128)(2,1)S(1)}, bf16[128,128]{1,0:T(8,128)(2,1)S(1)}, u32[]{:S(2)}, u32[]{:S(2)}) collective-permute-start(bf16[128,128]{1,0:T(8,128)(2,1)S(1)} %layers.4.refs_1_), channel_id=1, source_target_pairs={{0,4},{4,8},{8,12},{12,0},{1,5},{5,9},{9,13},{13,1},{2,6},{6,10},{... | collective-permute-start | bytes 98312 | tf_op jit(solution)/shard_map/ppermute | solution.py:337
  18.9 5.7 %collective-permute-start.7 = (bf16[128,128]{1,0:T(8,128)(2,1)S(1)}, bf16[128,128]{1,0:T(8,128)(2,1)S(1)}, u32[]{:S(2)}, u32[]{:S(2)}) collective-permute-start(bf16[128,128]{1,0:T(8,128)(2,1)S(1)} %layers.5.refs_1_), channel_id=1, source_target_pairs={{0,8},{4,12},{8,0},{12,4},{1,9},{5,13},{9,1},{13,5},{2,10},{6,14},... | collective-permute-start | bytes 98312 | tf_op jit(solution)/shard_map/ppermute | solution.py:337
  21.9 4.0 %collective-permute-start.8 = (bf16[128,128]{1,0:T(8,128)(2,1)S(1)}, bf16[128,128]{1,0:T(8,128)(2,1)S(1)}, u32[]{:S(2)}, u32[]{:S(2)}) collective-permute-start(bf16[128,128]{1,0:T(8,128)(2,1)S(1)} %layers.7), channel_id=1, source_target_pairs={{0,12},{4,0},{8,4},{12,8},{1,13},{5,1},{9,5},{13,9},{2,14},{6,2},{... | collective-permute-start | bytes 98312 | tf_op jit(solution)/shard_map/ppermute | solution.py:337

commit v17 on v16

--- a/solution.py
+++ b/solution.py
@@ -117,12 +117,13 @@
     side_in = side_in.astype(F32)
     side_out = side_out.reshape(rank // 16, 16, tokens)
     total = None
-    for part in range(rank // PACK):
+    span = rank // 4
+    for part in range(4):
         products = []
-        for b in range(part * PACK, (part + 1) * PACK):
+        for b in range(part * span, (part + 1) * span):
             row = jnp.broadcast_to(side_in[b:b + 1, :], (16, tokens)).astype(BF16)
             products.append((side_out * row[None]).reshape(rank, tokens))
-        width = PACK * rank
+        width = span * rank
         term = jnp.dot(
             weights[:, part * width:(part + 1) * width],
             jnp.concatenate(products, axis=0),

time: 26.7 us -> 26.7 us (level)
  no operation moved by 1% of the time
where the time goes in v17:
time: 26.7 us; the launch traced here: 26.6 us
  starting transfers between devices  13.1 us (49%)
  Pallas kernels  7.45 us (28%)
  waiting for transfers between devices  5.95 us (22%)
    ppermute x3, starting transfers between devices, across(): return lax.ppermute(feats, ('train', 'sub'), cores)  5.4 us
    ppermute x3, starting transfers between devices, body(): arrivals.append(lax.ppermute(block, 'train', pairs))  4.8 us
    pallas_call x1, Pallas kernels, body(): pl.pallas_call(functools.partial(features_kernel, chunks), out_shape=[jax...  2.8 us
    ppermute x3, waiting for transfers between devices, body(): arrivals.append(lax.ppermute(block, 'train', pairs))  2.18 us
    ppermute x2, starting transfers between devices, scored(): lax.ppermute(block, 'layer', [(l, (l + k) % layer_size) for l in range(la...  2.17 us
    pallas_call x1, Pallas kernels, body(): pl.pallas_call(queries_kernel, out_shape=jax.ShapeDtypeStruct((count, ent...  2.11 us
    pallas_call x2, Pallas kernels, scored(): pl.pallas_call(functools.partial(scores_kernel, layer_size, targets), out...  1.74 us
    ppermute x3, waiting for transfers between devices, across(): return lax.ppermute(feats, ('train', 'sub'), cores)  1.41 us
  transfers between devices with their start and end apart: 9, of which 6 were waited for; matrix products, arithmetic and copies ran while one was open for 0% of the time, Pallas kernels for 11%

profile of v17, /device:TPU:0, one launch (start us, length us, event | category | flops | bytes accessed | tf_op | source)
XLA Modules:
  0.0 26.6 jit_solution(8845167715271636677)
XLA Ops:
  0.0 2.8 %features.1 = (bf16[64,256]{1,0:T(8,128)(2,1)S(1)}, bf16[128,4096]{1,0:T(8,128)(2,1)S(1)}, f32[64,64]{1,0:T(8,128)S(1)}, f32[64,64]{1,0:T(8,128)S(1)}, f32[64,64]{1,0:T(8,128)S(1)}) custom-call(bf16[1,256,4096]{2,1,0:T(8,128)(2,1)} %refs_0_.1, bf16[1,64,4096]{2,1,0:T(8,128)(2,1)} %refs_1_.1, f32[1,64,64]{2,1,0:T(8,128)} %refs_2_.1, ...), custom_call_target="tpu_custom_call" | custom-call | flops 134217728 | bytes 2621440 | tf_op jit(solution)/shard_map/features/pallas_call | solution.py:214
  2.8 3.5 %collective-permute-start.2 = (bf16[64,256]{1,0:T(8,128)(2,1)S(1)}, bf16[64,256]{1,0:T(8,128)(2,1)S(1)}, u32[]{:S(2)}, u32[]{:S(2)}) collective-permute-start(bf16[64,256]{1,0:T(8,128)(2,1)S(1)} %get-tuple-element.18.refs_0_), channel_id=1, source_target_pairs={{0,9},{1,8},{4,13},{5,12},{8,1},{9,0},{12,5},{13,4},{2,11},{3,10},... | collective-permute-start | bytes 98312 | tf_op jit(solution)/shard_map/ppermute | solution.py:255
  6.3 1.6 %collective-permute-start.1 = (bf16[64,256]{1,0:T(8,128)(2,1)S(1)}, bf16[64,256]{1,0:T(8,128)(2,1)S(1)}, u32[]{:S(2)}, u32[]{:S(2)}) collective-permute-start(bf16[64,256]{1,0:T(8,128)(2,1)S(1)} %get-tuple-element.18.refs_0_), channel_id=1, source_target_pairs={{0,13},{1,12},{4,9},{5,8},{8,5},{9,4},{12,1},{13,0},{2,15},{3,14},... | collective-permute-start | bytes 98312 | tf_op jit(solution)/shard_map/ppermute | solution.py:255
  8.0 0.2 collective-permute-start
  8.2 2.1 %queries.1.refs_4_.weights = bf16[128,4096]{1,0:T(8,128)(2,1)S(1)} custom-call(bf16[128,4096]{1,0:T(8,128)(2,1)S(1)} %get-tuple-element.14.queries, f32[64,64]{1,0:T(8,128)S(1)} %get-tuple-element.15.basis_in, f32[64,64]{1,0:T(8,128)S(1)} %get-tuple-element.16.basis_out, f32[64,64]{1,0:T(8,128)S(1)} %get-tuple-element.17.eigen), custom_call_target="tpu_custom_call" | custom-call | flops 536870912 | bytes 2097152 | tf_op jit(solution)/shard_map/queries/pallas_call | solution.py:259
  10.3 0.0 collective-permute-done.2.refs_3_
  10.3 1.3 %collective-permute-done.1.refs_2_ = bf16[64,256]{1,0:T(8,128)(2,1)S(1)} collective-permute-done((bf16[64,256]{1,0:T(8,128)(2,1)S(1)}, bf16[64,256]{1,0:T(8,128)(2,1)S(1)}, u32[]{:S(2)}, u32[]{:S(2)}) %collective-permute-start.1) | collective-permute-done | bytes 32800 | tf_op jit(solution)/shard_map/ppermute | solution.py:255
  11.6 0.1 collective-permute-done.refs_1_
  11.8 0.7 %collective-permute-start.3 = (bf16[4,64,256]{2,1,0:T(8,128)(2,1)S(1)}, bf16[4,64,256]{2,1,0:T(8,128)(2,1)S(1)}, u32[]{:S(2)}, u32[]{:S(2)}) collective-permute-start(bf16[4,64,256]{2,1,0:T(8,128)(2,1)S(1)} %pack.1.mine), channel_id=1, source_target_pairs={{0,1},{1,0},{2,3},{3,2},{4,5},{5,4},{6,7},{7,6},{8,9},{9,8},{10,11... | collective-permute-start | bytes 393224 | tf_op jit(solution)/shard_map/ppermute | solution.py:280
  12.5 1.0 %collective-permute-done.3.theirs = bf16[4,64,256]{2,1,0:T(8,128)(2,1)S(1)} collective-permute-done((bf16[4,64,256]{2,1,0:T(8,128)(2,1)S(1)}, bf16[4,64,256]{2,1,0:T(8,128)(2,1)S(1)}, u32[]{:S(2)}, u32[]{:S(2)}) %collective-permute-start.3) | collective-permute-done | bytes 131104 | tf_op jit(solution)/shard_map/ppermute | solution.py:280
  13.5 0.9 %scores.2 = (f32[2,128,128]{2,1,0:T(8,128)S(1)}, bf16[2,128,128]{2,1,0:T(8,128)(2,1)S(1)}) custom-call(bf16[128,4096]{1,0:T(8,128)(2,1)S(1)} %queries.1.refs_4_.weights, bf16[4,64,256]{2,1,0:T(8,128)(2,1)S(1)} %pack.1.mine, bf16[4,64,256]{2,1,0:T(8,128)(2,1)S(1)} %collective-permute-done.3.theirs), custom_call_target="tpu_custom_call" | custom-call | flops 536870912 | bytes 1048576 | tf_op jit(solution)/shard_map/scores/pallas_call | solution.py:285
  14.4 1.6 %collective-permute-start.5 = (bf16[2,128,128]{2,1,0:T(8,128)(2,1)S(1)}, bf16[2,128,128]{2,1,0:T(8,128)(2,1)S(1)}, u32[]{:S(2)}, u32[]{:S(2)}) collective-permute-start(bf16[2,128,128]{2,1,0:T(8,128)(2,1)S(1)} %get-tuple-element.22), channel_id=1, source_target_pairs={{0,2},{2,0},{1,3},{3,1},{4,6},{6,4},{5,7},{7,5},{8,10},{10,8},{9,1... | collective-permute-start | bytes 196616 | tf_op jit(solution)/shard_map/ppermute | solution.py:303
  15.9 0.9 %scores.3 = (f32[2,128,128]{2,1,0:T(8,128)S(1)}, bf16[2,128,128]{2,1,0:T(8,128)(2,1)S(1)}) custom-call(bf16[128,4096]{1,0:T(8,128)(2,1)S(1)} %queries.1.refs_4_.weights, bf16[4,64,256]{2,1,0:T(8,128)(2,1)S(1)} %pack.1.mine, bf16[4,64,256]{2,1,0:T(8,128)(2,1)S(1)} %collective-permute-done.3.theirs, f32[2,128,128]{2,1,0:T(8,128)S(1)} %get-tuple-element.19.refs_0_.own), custom_call_target="tpu_custom_call" | custom-call | flops 536870912 | bytes 1048576 | tf_op jit(solution)/shard_map/scores/pallas_call | solution.py:285
  16.8 0.6 %collective-permute-start.4 = (bf16[2,128,128]{2,1,0:T(8,128)(2,1)S(1)}, bf16[2,128,128]{2,1,0:T(8,128)(2,1)S(1)}, u32[]{:S(2)}, u32[]{:S(2)}) collective-permute-start(bf16[2,128,128]{2,1,0:T(8,128)(2,1)S(1)} %get-tuple-element.21), channel_id=1, source_target_pairs={{0,2},{2,0},{1,3},{3,1},{4,6},{6,4},{5,7},{7,5},{8,10},{10,8},{9,1... | collective-permute-start | bytes 196616 | tf_op jit(solution)/shard_map/ppermute | solution.py:303
  17.4 1.4 %collective-permute-done.5.refs_0_ = bf16[2,128,128]{2,1,0:T(8,128)(2,1)S(1)} collective-permute-done((bf16[2,128,128]{2,1,0:T(8,128)(2,1)S(1)}, bf16[2,128,128]{2,1,0:T(8,128)(2,1)S(1)}, u32[]{:S(2)}, u32[]{:S(2)}) %collective-permute-start.5) | collective-permute-done | bytes 65568 | tf_op jit(solution)/shard_map/ppermute | solution.py:303
  18.8 0.1 collective-permute-start.6
  18.9 3.0 %collective-permute-start.7 = (bf16[128,128]{1,0:T(8,128)(2,1)S(1)}, bf16[128,128]{1,0:T(8,128)(2,1)S(1)}, u32[]{:S(2)}, u32[]{:S(2)}) collective-permute-start(bf16[128,128]{1,0:T(8,128)(2,1)S(1)} %layers.5.refs_1_), channel_id=1, source_target_pairs={{0,8},{4,12},{8,0},{12,4},{1,9},{5,13},{9,1},{13,5},{2,10},{6,14},... | collective-permute-start | bytes 98312 | tf_op jit(solution)/shard_map/ppermute | solution.py:338
  21.9 0.0 collective-permute-done.4.refs_0_
  21.9 1.8 %collective-permute-start.8 = (bf16[128,128]{1,0:T(8,128)(2,1)S(1)}, bf16[128,128]{1,0:T(8,128)(2,1)S(1)}, u32[]{:S(2)}, u32[]{:S(2)}) collective-permute-start(bf16[128,128]{1,0:T(8,128)(2,1)S(1)} %layers.7), channel_id=1, source_target_pairs={{0,12},{4,0},{8,4},{12,8},{1,13},{5,1},{9,5},{13,9},{2,14},{6,2},{... | collective-permute-start | bytes 98312 | tf_op jit(solution)/shard_map/ppermute | solution.py:338
  23.7 0.9 %collective-permute-done.6.block = bf16[128,128]{1,0:T(8,128)(2,1)S(1)} collective-permute-done((bf16[128,128]{1,0:T(8,128)(2,1)S(1)}, bf16[128,128]{1,0:T(8,128)(2,1)S(1)}, u32[]{:S(2)}, u32[]{:S(2)}) %collective-permute-start.6) | collective-permute-done | bytes 32800 | tf_op jit(solution)/shard_map/ppermute | solution.py:338
  24.6 0.0 collective-permute-done.7.block
  24.6 1.3 %collective-permute-done.8.refs_2_ = bf16[128,128]{1,0:T(8,128)(2,1)S(1)} collective-permute-done((bf16[128,128]{1,0:T(8,128)(2,1)S(1)}, bf16[128,128]{1,0:T(8,128)(2,1)S(1)}, u32[]{:S(2)}, u32[]{:S(2)}) %collective-permute-start.8) | collective-permute-done | bytes 32800 | tf_op jit(solution)/shard_map/ppermute | solution.py:338
  25.9 0.7 %place.1 = f32[512,128]{1,0:T(8,128)} custom-call(f32[128,128]{1,0:T(8,128)S(1)} %layers.6.refs_1_.own, bf16[128,128]{1,0:T(8,128)(2,1)S(1)} %keep.2.refs_0_, bf16[128,128]{1,0:T(8,128)(2,1)S(1)} %keep.3.refs_1_, bf16[128,128]{1,0:T(8,128)(2,1)S(1)} %collective-permute-done.8.refs_2_), custom_call_target="tpu_custom_call" | custom-call | tf_op jit(solution)/shard_map/place/pallas_call | solution.py:342
  (7 shorter events, 0.1 us)
Async XLA Ops:
  2.8 7.5 %collective-permute-start.2 = (bf16[64,256]{1,0:T(8,128)(2,1)S(1)}, bf16[64,256]{1,0:T(8,128)(2,1)S(1)}, u32[]{:S(2)}, u32[]{:S(2)}) collective-permute-start(bf16[64,256]{1,0:T(8,128)(2,1)S(1)} %get-tuple-element.18.refs_0_), channel_id=1, source_target_pairs={{0,9},{1,8},{4,13},{5,12},{8,1},{9,0},{12,5},{13,4},{2,11},{3,10},... | collective-permute-start | bytes 98312 | tf_op jit(solution)/shard_map/ppermute | solution.py:255
  6.3 5.2 %collective-permute-start.1 = (bf16[64,256]{1,0:T(8,128)(2,1)S(1)}, bf16[64,256]{1,0:T(8,128)(2,1)S(1)}, u32[]{:S(2)}, u32[]{:S(2)}) collective-permute-start(bf16[64,256]{1,0:T(8,128)(2,1)S(1)} %get-tuple-element.18.refs_0_), channel_id=1, source_target_pairs={{0,13},{1,12},{4,9},{5,8},{8,5},{9,4},{12,1},{13,0},{2,15},{3,14},... | collective-permute-start | bytes 98312 | tf_op jit(solution)/shard_map/ppermute | solution.py:255
  8.0 3.8 %collective-permute-start = (bf16[64,256]{1,0:T(8,128)(2,1)S(1)}, bf16[64,256]{1,0:T(8,128)(2,1)S(1)}, u32[]{:S(2)}, u32[]{:S(2)}) collective-permute-start(bf16[64,256]{1,0:T(8,128)(2,1)S(1)} %get-tuple-element.18.refs_0_), channel_id=1, source_target_pairs={{0,5},{1,4},{4,1},{5,0},{8,13},{9,12},{12,9},{13,8},{2,7},{3,6},{6... | collective-permute-start | bytes 98312 | tf_op jit(solution)/shard_map/ppermute | solution.py:255
  11.8 1.7 %collective-permute-start.3 = (bf16[4,64,256]{2,1,0:T(8,128)(2,1)S(1)}, bf16[4,64,256]{2,1,0:T(8,128)(2,1)S(1)}, u32[]{:S(2)}, u32[]{:S(2)}) collective-permute-start(bf16[4,64,256]{2,1,0:T(8,128)(2,1)S(1)} %pack.1.mine), channel_id=1, source_target_pairs={{0,1},{1,0},{2,3},{3,2},{4,5},{5,4},{6,7},{7,6},{8,9},{9,8},{10,11... | collective-permute-start | bytes 393224 | tf_op jit(solution)/shard_map/ppermute | solution.py:280
  14.4 4.4 %collective-permute-start.5 = (bf16[2,128,128]{2,1,0:T(8,128)(2,1)S(1)}, bf16[2,128,128]{2,1,0:T(8,128)(2,1)S(1)}, u32[]{:S(2)}, u32[]{:S(2)}) collective-permute-start(bf16[2,128,128]{2,1,0:T(8,128)(2,1)S(1)} %get-tuple-element.22), channel_id=1, source_target_pairs={{0,2},{2,0},{1,3},{3,1},{4,6},{6,4},{5,7},{7,5},{8,10},{10,8},{9,1... | collective-permute-start | bytes 196616 | tf_op jit(solution)/shard_map/ppermute | solution.py:303
  16.8 5.0 %collective-permute-start.4 = (bf16[2,128,128]{2,1,0:T(8,128)(2,1)S(1)}, bf16[2,128,128]{2,1,0:T(8,128)(2,1)S(1)}, u32[]{:S(2)}, u32[]{:S(2)}) collective-permute-start(bf16[2,128,128]{2,1,0:T(8,128)(2,1)S(1)} %get-tuple-element.21), channel_id=1, source_target_pairs={{0,2},{2,0},{1,3},{3,1},{4,6},{6,4},{5,7},{7,5},{8,10},{10,8},{9,1... | collective-permute-start | bytes 196616 | tf_op jit(solution)/shard_map/ppermute | solution.py:303
  18.8 5.8 %collective-permute-start.6 = (bf16[128,128]{1,0:T(8,128)(2,1)S(1)}, bf16[128,128]{1,0:T(8,128)(2,1)S(1)}, u32[]{:S(2)}, u32[]{:S(2)}) collective-permute-start(bf16[128,128]{1,0:T(8,128)(2,1)S(1)} %layers.4.refs_1_), channel_id=1, source_target_pairs={{0,4},{4,8},{8,12},{12,0},{1,5},{5,9},{9,13},{13,1},{2,6},{6,10},{... | collective-permute-start | bytes 98312 | tf_op jit(solution)/shard_map/ppermute | solution.py:338
  18.9 5.7 %collective-permute-start.7 = (bf16[128,128]{1,0:T(8,128)(2,1)S(1)}, bf16[128,128]{1,0:T(8,128)(2,1)S(1)}, u32[]{:S(2)}, u32[]{:S(2)}) collective-permute-start(bf16[128,128]{1,0:T(8,128)(2,1)S(1)} %layers.5.refs_1_), channel_id=1, source_target_pairs={{0,8},{4,12},{8,0},{12,4},{1,9},{5,13},{9,1},{13,5},{2,10},{6,14},... | collective-permute-start | bytes 98312 | tf_op jit(solution)/shard_map/ppermute | solution.py:338
  21.9 4.0 %collective-permute-start.8 = (bf16[128,128]{1,0:T(8,128)(2,1)S(1)}, bf16[128,128]{1,0:T(8,128)(2,1)S(1)}, u32[]{:S(2)}, u32[]{:S(2)}) collective-permute-start(bf16[128,128]{1,0:T(8,128)(2,1)S(1)} %layers.7), channel_id=1, source_target_pairs={{0,12},{4,0},{8,4},{12,8},{1,13},{5,1},{9,5},{13,9},{2,14},{6,2},{... | collective-permute-start | bytes 98312 | tf_op jit(solution)/shard_map/ppermute | solution.py:338

commit v18 on v17

--- a/solution.py
+++ b/solution.py
@@ -21,7 +21,12 @@
     return rounds, rounds, train_size // 2
 
 
-FEATURE_ROUNDS = [((0, 2), (1, 3), (2, 0), (3, 1)), ((0, 3), (1, 2), (2, 1), (3, 0)), ((0, 1), (1, 0), (2, 3), (3, 2))]
+FEATURE_ROUNDS = [
+    ((0, 2), (2, 3), (3, 0), (1, 1)),
+    ((0, 3), (1, 2), (2, 0), (3, 1)),
+    ((1, 3), (2, 1), (3, 2), (0, 0)),
+    ((0, 1), (1, 0), (2, 2), (3, 3)),
+]
 SCORE_ROUNDS = [((0, 1), (1, 2), (2, 3), (3, 0)), ((0, 2), (1, 3), (2, 0), (3, 1)), ((0, 3), (1, 0), (2, 1), (3, 2))]
 FIRST = 2
 
@@ -251,7 +256,7 @@
         return ordered + blocks[-1:]
 
     def across(pairs):
-        cores = [(2 * s + c, 2 * d + 1 - c) for s, d in pairs for c in range(2)]
+        cores = [(2 * s + c, 2 * d + (c if s == d else 1 - c)) for s, d in pairs for c in range(2)]
         return lax.ppermute(feats, ("train", "sub"), cores)
 
     gathered = [across(pairs) for pairs in feature_rounds]

time: 26.7 us -> 31 us (1.16)
  starting transfers between devices: 13.1 us -> 17.6 us
    ppermute x3 -> x4, starting transfers between devices: 5.4 us -> 11.1 us  [across(): return lax.ppermute(feats, ('train', 'sub'), cores)]
    ppermute x3 -> x4, waiting for transfers between devices: 1.41 us -> 0.01 us  [across(): return lax.ppermute(feats, ('train', 'sub'), cores)]
    ppermute x3, starting transfers between devices: 4.8 us -> 3.58 us  [body(): arrivals.append(lax.ppermute(block, 'train', pairs))]
    ppermute x2, waiting for transfers between devices: 1.38 us -> 1.96 us  [scored(): lax.ppermute(block, 'layer', [(l, (l + k) % layer_size) for l in range(la...]
    ppermute x3, waiting for transfers between devices: 2.18 us -> 2.71 us  [body(): arrivals.append(lax.ppermute(block, 'train', pairs))]
  transfers between devices with their start and end apart: 9 -> 10, of which waited for: 6 -> 5; matrix products, arithmetic and copies ran while one was open for 0% -> 0% of each run, Pallas kernels for 11% -> 10%
where the time goes in v18:
time: 31 us; the launch traced here: 30.9 us
  starting transfers between devices  17.6 us (57%)
  Pallas kernels  7.46 us (24%)
  waiting for transfers between devices  5.67 us (18%)
    ppermute x4, starting transfers between devices, across(): return lax.ppermute(feats, ('train', 'sub'), cores)  11.1 us
    ppermute x3, starting transfers between devices, body(): arrivals.append(lax.ppermute(block, 'train', pairs))  3.58 us
    pallas_call x1, Pallas kernels, body(): pl.pallas_call(functools.partial(features_kernel, chunks), out_shape=[jax...  2.8 us
    ppermute x3, waiting for transfers between devices, body(): arrivals.append(lax.ppermute(block, 'train', pairs))  2.71 us
    ppermute x2, starting transfers between devices, scored(): lax.ppermute(block, 'layer', [(l, (l + k) % layer_size) for l in range(la...  2.17 us
    pallas_call x1, Pallas kernels, body(): pl.pallas_call(queries_kernel, out_shape=jax.ShapeDtypeStruct((count, ent...  2.12 us
    ppermute x2, waiting for transfers between devices, scored(): lax.ppermute(block, 'layer', [(l, (l + k) % layer_size) for l in range(la...  1.96 us
    pallas_call x2, Pallas kernels, scored(): pl.pallas_call(functools.partial(scores_kernel, layer_size, targets), out...  1.74 us
  transfers between devices with their start and end apart: 10, of which 5 were waited for; matrix products, arithmetic and copies ran while one was open for 0% of the time, Pallas kernels for 10%

profile of v18, /device:TPU:0, one launch (start us, length us, event | category | flops | bytes accessed | tf_op | source)
XLA Modules:
  0.0 30.9 jit_solution(9928925824896883800)
XLA Ops:
  0.0 2.8 %features.1 = (bf16[64,256]{1,0:T(8,128)(2,1)S(1)}, bf16[128,4096]{1,0:T(8,128)(2,1)S(1)}, f32[64,64]{1,0:T(8,128)S(1)}, f32[64,64]{1,0:T(8,128)S(1)}, f32[64,64]{1,0:T(8,128)S(1)}) custom-call(bf16[1,256,4096]{2,1,0:T(8,128)(2,1)} %refs_0_.1, bf16[1,64,4096]{2,1,0:T(8,128)(2,1)} %refs_1_.1, f32[1,64,64]{2,1,0:T(8,128)} %refs_2_.1, ...), custom_call_target="tpu_custom_call" | custom-call | flops 134217728 | bytes 2621440 | tf_op jit(solution)/shard_map/features/pallas_call | solution.py:219
  2.8 5.4 %collective-permute-start.3 = (bf16[64,256]{1,0:T(8,128)(2,1)S(1)}, bf16[64,256]{1,0:T(8,128)(2,1)S(1)}, u32[]{:S(2)}, u32[]{:S(2)}) collective-permute-start(bf16[64,256]{1,0:T(8,128)(2,1)S(1)} %get-tuple-element.18.refs_0_), channel_id=1, source_target_pairs={{0,9},{1,8},{8,13},{9,12},{12,1},{13,0},{4,4},{5,5},{2,11},{3,10},... | collective-permute-start | bytes 98312 | tf_op jit(solution)/shard_map/ppermute | solution.py:260
  8.2 1.1 %collective-permute-start.2 = (bf16[64,256]{1,0:T(8,128)(2,1)S(1)}, bf16[64,256]{1,0:T(8,128)(2,1)S(1)}, u32[]{:S(2)}, u32[]{:S(2)}) collective-permute-start(bf16[64,256]{1,0:T(8,128)(2,1)S(1)} %get-tuple-element.18.refs_0_), channel_id=1, source_target_pairs={{0,13},{1,12},{4,9},{5,8},{8,1},{9,0},{12,5},{13,4},{2,15},{3,14},... | collective-permute-start | bytes 98312 | tf_op jit(solution)/shard_map/ppermute | solution.py:260
  9.3 0.7 %collective-permute-start.1 = (bf16[64,256]{1,0:T(8,128)(2,1)S(1)}, bf16[64,256]{1,0:T(8,128)(2,1)S(1)}, u32[]{:S(2)}, u32[]{:S(2)}) collective-permute-start(bf16[64,256]{1,0:T(8,128)(2,1)S(1)} %get-tuple-element.18.refs_0_), channel_id=1, source_target_pairs={{4,13},{5,12},{8,5},{9,4},{12,9},{13,8},{0,0},{1,1},{6,15},{7,14},... | collective-permute-start | bytes 98312 | tf_op jit(solution)/shard_map/ppermute | solution.py:260
  9.9 4.0 %collective-permute-start = (bf16[64,256]{1,0:T(8,128)(2,1)S(1)}, bf16[64,256]{1,0:T(8,128)(2,1)S(1)}, u32[]{:S(2)}, u32[]{:S(2)}) collective-permute-start(bf16[64,256]{1,0:T(8,128)(2,1)S(1)} %get-tuple-element.18.refs_0_), channel_id=1, source_target_pairs={{0,5},{1,4},{4,1},{5,0},{8,8},{9,9},{12,12},{13,13},{2,7},{3,6},{6... | collective-permute-start | bytes 98312 | tf_op jit(solution)/shard_map/ppermute | solution.py:260
  14.0 2.1 %queries.1.refs_5_.weights = bf16[128,4096]{1,0:T(8,128)(2,1)S(1)} custom-call(bf16[128,4096]{1,0:T(8,128)(2,1)S(1)} %get-tuple-element.14.queries, f32[64,64]{1,0:T(8,128)S(1)} %get-tuple-element.15.basis_in, f32[64,64]{1,0:T(8,128)S(1)} %get-tuple-element.16.basis_out, f32[64,64]{1,0:T(8,128)S(1)} %get-tuple-element.17.eigen), custom_call_target="tpu_custom_call" | custom-call | flops 536870912 | bytes 2097152 | tf_op jit(solution)/shard_map/queries/pallas_call | solution.py:264
  16.1 0.0 collective-permute-done.3.refs_4_
  16.1 0.0 collective-permute-done.2.refs_3_
  16.1 0.0 collective-permute-done.1.refs_2_
  16.1 0.0 collective-permute-done.refs_1_
  16.2 0.7 %collective-permute-start.4 = (bf16[4,64,256]{2,1,0:T(8,128)(2,1)S(1)}, bf16[4,64,256]{2,1,0:T(8,128)(2,1)S(1)}, u32[]{:S(2)}, u32[]{:S(2)}) collective-permute-start(bf16[4,64,256]{2,1,0:T(8,128)(2,1)S(1)} %pack.1.mine), channel_id=1, source_target_pairs={{0,1},{1,0},{2,3},{3,2},{4,5},{5,4},{6,7},{7,6},{8,9},{9,8},{10,11... | collective-permute-start | bytes 393224 | tf_op jit(solution)/shard_map/ppermute | solution.py:285
  16.9 1.0 %collective-permute-done.4.theirs = bf16[4,64,256]{2,1,0:T(8,128)(2,1)S(1)} collective-permute-done((bf16[4,64,256]{2,1,0:T(8,128)(2,1)S(1)}, bf16[4,64,256]{2,1,0:T(8,128)(2,1)S(1)}, u32[]{:S(2)}, u32[]{:S(2)}) %collective-permute-start.4) | collective-permute-done | bytes 131104 | tf_op jit(solution)/shard_map/ppermute | solution.py:285
  17.9 0.9 %scores.2 = (f32[2,128,128]{2,1,0:T(8,128)S(1)}, bf16[2,128,128]{2,1,0:T(8,128)(2,1)S(1)}) custom-call(bf16[128,4096]{1,0:T(8,128)(2,1)S(1)} %queries.1.refs_5_.weights, bf16[4,64,256]{2,1,0:T(8,128)(2,1)S(1)} %pack.1.mine, bf16[4,64,256]{2,1,0:T(8,128)(2,1)S(1)} %collective-permute-done.4.theirs), custom_call_target="tpu_custom_call" | custom-call | flops 536870912 | bytes 1048576 | tf_op jit(solution)/shard_map/scores/pallas_call | solution.py:290
  18.7 1.6 %collective-permute-start.6 = (bf16[2,128,128]{2,1,0:T(8,128)(2,1)S(1)}, bf16[2,128,128]{2,1,0:T(8,128)(2,1)S(1)}, u32[]{:S(2)}, u32[]{:S(2)}) collective-permute-start(bf16[2,128,128]{2,1,0:T(8,128)(2,1)S(1)} %get-tuple-element.22), channel_id=1, source_target_pairs={{0,2},{2,0},{1,3},{3,1},{4,6},{6,4},{5,7},{7,5},{8,10},{10,8},{9,1... | collective-permute-start | bytes 196616 | tf_op jit(solution)/shard_map/ppermute | solution.py:308
  20.3 0.9 %scores.3 = (f32[2,128,128]{2,1,0:T(8,128)S(1)}, bf16[2,128,128]{2,1,0:T(8,128)(2,1)S(1)}) custom-call(bf16[128,4096]{1,0:T(8,128)(2,1)S(1)} %queries.1.refs_5_.weights, bf16[4,64,256]{2,1,0:T(8,128)(2,1)S(1)} %pack.1.mine, bf16[4,64,256]{2,1,0:T(8,128)(2,1)S(1)} %collective-permute-done.4.theirs, f32[2,128,128]{2,1,0:T(8,128)S(1)} %get-tuple-element.19.refs_0_.own), custom_call_target="tpu_custom_call" | custom-call | flops 536870912 | bytes 1048576 | tf_op jit(solution)/shard_map/scores/pallas_call | solution.py:290
  21.2 0.6 %collective-permute-start.5 = (bf16[2,128,128]{2,1,0:T(8,128)(2,1)S(1)}, bf16[2,128,128]{2,1,0:T(8,128)(2,1)S(1)}, u32[]{:S(2)}, u32[]{:S(2)}) collective-permute-start(bf16[2,128,128]{2,1,0:T(8,128)(2,1)S(1)} %get-tuple-element.21), channel_id=1, source_target_pairs={{0,2},{2,0},{1,3},{3,1},{4,6},{6,4},{5,7},{7,5},{8,10},{10,8},{9,1... | collective-permute-start | bytes 196616 | tf_op jit(solution)/shard_map/ppermute | solution.py:308
  21.8 1.4 %collective-permute-done.6.refs_0_ = bf16[2,128,128]{2,1,0:T(8,128)(2,1)S(1)} collective-permute-done((bf16[2,128,128]{2,1,0:T(8,128)(2,1)S(1)}, bf16[2,128,128]{2,1,0:T(8,128)(2,1)S(1)}, u32[]{:S(2)}, u32[]{:S(2)}) %collective-permute-start.6) | collective-permute-done | bytes 65568 | tf_op jit(solution)/shard_map/ppermute | solution.py:308
  23.2 1.7 %collective-permute-start.7 = (bf16[128,128]{1,0:T(8,128)(2,1)S(1)}, bf16[128,128]{1,0:T(8,128)(2,1)S(1)}, u32[]{:S(2)}, u32[]{:S(2)}) collective-permute-start(bf16[128,128]{1,0:T(8,128)(2,1)S(1)} %layers.4.refs_1_), channel_id=1, source_target_pairs={{0,4},{4,8},{8,12},{12,0},{1,5},{5,9},{9,13},{13,1},{2,6},{6,10},{... | collective-permute-start | bytes 98312 | tf_op jit(solution)/shard_map/ppermute | solution.py:343
  24.9 0.1 collective-permute-start.8
  24.9 0.6 %collective-permute-done.5.refs_0_ = bf16[2,128,128]{2,1,0:T(8,128)(2,1)S(1)} collective-permute-done((bf16[2,128,128]{2,1,0:T(8,128)(2,1)S(1)}, bf16[2,128,128]{2,1,0:T(8,128)(2,1)S(1)}, u32[]{:S(2)}, u32[]{:S(2)}) %collective-permute-start.5) | collective-permute-done | bytes 65568 | tf_op jit(solution)/shard_map/ppermute | solution.py:308
  25.6 1.8 %collective-permute-start.9 = (bf16[128,128]{1,0:T(8,128)(2,1)S(1)}, bf16[128,128]{1,0:T(8,128)(2,1)S(1)}, u32[]{:S(2)}, u32[]{:S(2)}) collective-permute-start(bf16[128,128]{1,0:T(8,128)(2,1)S(1)} %layers.7), channel_id=1, source_target_pairs={{0,12},{4,0},{8,4},{12,8},{1,13},{5,1},{9,5},{13,9},{2,14},{6,2},{... | collective-permute-start | bytes 98312 | tf_op jit(solution)/shard_map/ppermute | solution.py:343
  27.4 1.8 %collective-permute-done.7.block = bf16[128,128]{1,0:T(8,128)(2,1)S(1)} collective-permute-done((bf16[128,128]{1,0:T(8,128)(2,1)S(1)}, bf16[128,128]{1,0:T(8,128)(2,1)S(1)}, u32[]{:S(2)}, u32[]{:S(2)}) %collective-permute-start.7) | collective-permute-done | bytes 32800 | tf_op jit(solution)/shard_map/ppermute | solution.py:343
  29.2 0.9 %collective-permute-done.8.block = bf16[128,128]{1,0:T(8,128)(2,1)S(1)} collective-permute-done((bf16[128,128]{1,0:T(8,128)(2,1)S(1)}, bf16[128,128]{1,0:T(8,128)(2,1)S(1)}, u32[]{:S(2)}, u32[]{:S(2)}) %collective-permute-start.8) | collective-permute-done | bytes 32800 | tf_op jit(solution)/shard_map/ppermute | solution.py:343
  30.1 0.0 collective-permute-done.9.refs_2_
  30.1 0.7 %place.1 = f32[512,128]{1,0:T(8,128)} custom-call(f32[128,128]{1,0:T(8,128)S(1)} %layers.6.refs_1_.own, bf16[128,128]{1,0:T(8,128)(2,1)S(1)} %keep.2.refs_0_, bf16[128,128]{1,0:T(8,128)(2,1)S(1)} %keep.3.refs_1_, bf16[128,128]{1,0:T(8,128)(2,1)S(1)} %collective-permute-done.9.refs_2_), custom_call_target="tpu_custom_call" | custom-call | tf_op jit(solution)/shard_map/place/pallas_call | solution.py:347
  (7 shorter events, 0.1 us)
Async XLA Ops:
  2.8 13.3 %collective-permute-start.3 = (bf16[64,256]{1,0:T(8,128)(2,1)S(1)}, bf16[64,256]{1,0:T(8,128)(2,1)S(1)}, u32[]{:S(2)}, u32[]{:S(2)}) collective-permute-start(bf16[64,256]{1,0:T(8,128)(2,1)S(1)} %get-tuple-element.18.refs_0_), channel_id=1, source_target_pairs={{0,9},{1,8},{8,13},{9,12},{12,1},{13,0},{4,4},{5,5},{2,11},{3,10},... | collective-permute-start | bytes 98312 | tf_op jit(solution)/shard_map/ppermute | solution.py:260
  8.2 7.9 %collective-permute-start.2 = (bf16[64,256]{1,0:T(8,128)(2,1)S(1)}, bf16[64,256]{1,0:T(8,128)(2,1)S(1)}, u32[]{:S(2)}, u32[]{:S(2)}) collective-permute-start(bf16[64,256]{1,0:T(8,128)(2,1)S(1)} %get-tuple-element.18.refs_0_), channel_id=1, source_target_pairs={{0,13},{1,12},{4,9},{5,8},{8,1},{9,0},{12,5},{13,4},{2,15},{3,14},... | collective-permute-start | bytes 98312 | tf_op jit(solution)/shard_map/ppermute | solution.py:260
  9.3 6.8 %collective-permute-start.1 = (bf16[64,256]{1,0:T(8,128)(2,1)S(1)}, bf16[64,256]{1,0:T(8,128)(2,1)S(1)}, u32[]{:S(2)}, u32[]{:S(2)}) collective-permute-start(bf16[64,256]{1,0:T(8,128)(2,1)S(1)} %get-tuple-element.18.refs_0_), channel_id=1, source_target_pairs={{4,13},{5,12},{8,5},{9,4},{12,9},{13,8},{0,0},{1,1},{6,15},{7,14},... | collective-permute-start | bytes 98312 | tf_op jit(solution)/shard_map/ppermute | solution.py:260
  9.9 6.2 %collective-permute-start = (bf16[64,256]{1,0:T(8,128)(2,1)S(1)}, bf16[64,256]{1,0:T(8,128)(2,1)S(1)}, u32[]{:S(2)}, u32[]{:S(2)}) collective-permute-start(bf16[64,256]{1,0:T(8,128)(2,1)S(1)} %get-tuple-element.18.refs_0_), channel_id=1, source_target_pairs={{0,5},{1,4},{4,1},{5,0},{8,8},{9,9},{12,12},{13,13},{2,7},{3,6},{6... | collective-permute-start | bytes 98312 | tf_op jit(solution)/shard_map/ppermute | solution.py:260
  16.2 1.7 %collective-permute-start.4 = (bf16[4,64,256]{2,1,0:T(8,128)(2,1)S(1)}, bf16[4,64,256]{2,1,0:T(8,128)(2,1)S(1)}, u32[]{:S(2)}, u32[]{:S(2)}) collective-permute-start(bf16[4,64,256]{2,1,0:T(8,128)(2,1)S(1)} %pack.1.mine), channel_id=1, source_target_pairs={{0,1},{1,0},{2,3},{3,2},{4,5},{5,4},{6,7},{7,6},{8,9},{9,8},{10,11... | collective-permute-start | bytes 393224 | tf_op jit(solution)/shard_map/ppermute | solution.py:285
  18.7 4.4 %collective-permute-start.6 = (bf16[2,128,128]{2,1,0:T(8,128)(2,1)S(1)}, bf16[2,128,128]{2,1,0:T(8,128)(2,1)S(1)}, u32[]{:S(2)}, u32[]{:S(2)}) collective-permute-start(bf16[2,128,128]{2,1,0:T(8,128)(2,1)S(1)} %get-tuple-element.22), channel_id=1, source_target_pairs={{0,2},{2,0},{1,3},{3,1},{4,6},{6,4},{5,7},{7,5},{8,10},{10,8},{9,1... | collective-permute-start | bytes 196616 | tf_op jit(solution)/shard_map/ppermute | solution.py:308
  21.2 4.3 %collective-permute-start.5 = (bf16[2,128,128]{2,1,0:T(8,128)(2,1)S(1)}, bf16[2,128,128]{2,1,0:T(8,128)(2,1)S(1)}, u32[]{:S(2)}, u32[]{:S(2)}) collective-permute-start(bf16[2,128,128]{2,1,0:T(8,128)(2,1)S(1)} %get-tuple-element.21), channel_id=1, source_target_pairs={{0,2},{2,0},{1,3},{3,1},{4,6},{6,4},{5,7},{7,5},{8,10},{10,8},{9,1... | collective-permute-start | bytes 196616 | tf_op jit(solution)/shard_map/ppermute | solution.py:308
  23.2 6.0 %collective-permute-start.7 = (bf16[128,128]{1,0:T(8,128)(2,1)S(1)}, bf16[128,128]{1,0:T(8,128)(2,1)S(1)}, u32[]{:S(2)}, u32[]{:S(2)}) collective-permute-start(bf16[128,128]{1,0:T(8,128)(2,1)S(1)} %layers.4.refs_1_), channel_id=1, source_target_pairs={{0,4},{4,8},{8,12},{12,0},{1,5},{5,9},{9,13},{13,1},{2,6},{6,10},{... | collective-permute-start | bytes 98312 | tf_op jit(solution)/shard_map/ppermute | solution.py:343
  24.9 5.2 %collective-permute-start.8 = (bf16[128,128]{1,0:T(8,128)(2,1)S(1)}, bf16[128,128]{1,0:T(8,128)(2,1)S(1)}, u32[]{:S(2)}, u32[]{:S(2)}) collective-permute-start(bf16[128,128]{1,0:T(8,128)(2,1)S(1)} %layers.5.refs_1_), channel_id=1, source_target_pairs={{0,8},{4,12},{8,0},{12,4},{1,9},{5,13},{9,1},{13,5},{2,10},{6,14},... | collective-permute-start | bytes 98312 | tf_op jit(solution)/shard_map/ppermute | solution.py:343
  25.6 4.6 %collective-permute-start.9 = (bf16[128,128]{1,0:T(8,128)(2,1)S(1)}, bf16[128,128]{1,0:T(8,128)(2,1)S(1)}, u32[]{:S(2)}, u32[]{:S(2)}) collective-permute-start(bf16[128,128]{1,0:T(8,128)(2,1)S(1)} %layers.7), channel_id=1, source_target_pairs={{0,12},{4,0},{8,4},{12,8},{1,13},{5,1},{9,5},{13,9},{2,14},{6,2},{... | collective-permute-start | bytes 98312 | tf_op jit(solution)/shard_map/ppermute | solution.py:343

commit v19 on v17

--- a/solution.py
+++ b/solution.py
@@ -205,7 +205,7 @@
     tokens, width = inputs.shape[1:]
     count, entries = queries.shape[1:]
     rank = proj_in.shape[1]
-    chunks = 4
+    chunks = 8
     vmem, hbm = pl.BlockSpec(memory_space=pltpu.VMEM), pl.BlockSpec(memory_space=pltpu.HBM)
     anywhere = pl.BlockSpec(memory_space=pl.ANY)
     params = pltpu.CompilerParams(vmem_limit_bytes=32 << 20)

time: 26.7 us -> 26.8 us (level)
  no operation moved by 1% of the time
where the time goes in v19:
time: 26.8 us; the launch traced here: 26.7 us
  starting transfers between devices  13.1 us (49%)
  Pallas kernels  7.52 us (28%)
  waiting for transfers between devices  5.95 us (22%)
    ppermute x3, starting transfers between devices, across(): return lax.ppermute(feats, ('train', 'sub'), cores)  5.4 us
    ppermute x3, starting transfers between devices, body(): arrivals.append(lax.ppermute(block, 'train', pairs))  4.8 us
    pallas_call x1, Pallas kernels, body(): pl.pallas_call(functools.partial(features_kernel, chunks), out_shape=[jax...  2.87 us
    ppermute x2, starting transfers between devices, scored(): lax.ppermute(block, 'layer', [(l, (l + k) % layer_size) for l in range(la...  2.17 us
    ppermute x3, waiting for transfers between devices, body(): arrivals.append(lax.ppermute(block, 'train', pairs))  2.17 us
    pallas_call x1, Pallas kernels, body(): pl.pallas_call(queries_kernel, out_shape=jax.ShapeDtypeStruct((count, ent...  2.11 us
    pallas_call x2, Pallas kernels, scored(): pl.pallas_call(functools.partial(scores_kernel, layer_size, targets), out...  1.75 us
    ppermute x3, waiting for transfers between devices, across(): return lax.ppermute(feats, ('train', 'sub'), cores)  1.42 us
  transfers between devices with their start and end apart: 9, of which 6 were waited for; matrix products, arithmetic and copies ran while one was open for 0% of the time, Pallas kernels for 11%

profile of v19, /device:TPU:0, one launch (start us, length us, event | category | flops | bytes accessed | tf_op | source)
XLA Modules:
  0.0 26.7 jit_solution(13430325434972785927)
XLA Ops:
  0.0 2.9 %features.1 = (bf16[64,256]{1,0:T(8,128)(2,1)S(1)}, bf16[128,4096]{1,0:T(8,128)(2,1)S(1)}, f32[64,64]{1,0:T(8,128)S(1)}, f32[64,64]{1,0:T(8,128)S(1)}, f32[64,64]{1,0:T(8,128)S(1)}) custom-call(bf16[1,256,4096]{2,1,0:T(8,128)(2,1)} %refs_0_.1, bf16[1,64,4096]{2,1,0:T(8,128)(2,1)} %refs_1_.1, f32[1,64,64]{2,1,0:T(8,128)} %refs_2_.1, ...), custom_call_target="tpu_custom_call" | custom-call | flops 134217728 | bytes 2621440 | tf_op jit(solution)/shard_map/features/pallas_call | solution.py:214
  2.9 3.5 %collective-permute-start.2 = (bf16[64,256]{1,0:T(8,128)(2,1)S(1)}, bf16[64,256]{1,0:T(8,128)(2,1)S(1)}, u32[]{:S(2)}, u32[]{:S(2)}) collective-permute-start(bf16[64,256]{1,0:T(8,128)(2,1)S(1)} %get-tuple-element.18.refs_0_), channel_id=1, source_target_pairs={{0,9},{1,8},{4,13},{5,12},{8,1},{9,0},{12,5},{13,4},{2,11},{3,10},... | collective-permute-start | bytes 98312 | tf_op jit(solution)/shard_map/ppermute | solution.py:255
  6.4 1.6 %collective-permute-start.1 = (bf16[64,256]{1,0:T(8,128)(2,1)S(1)}, bf16[64,256]{1,0:T(8,128)(2,1)S(1)}, u32[]{:S(2)}, u32[]{:S(2)}) collective-permute-start(bf16[64,256]{1,0:T(8,128)(2,1)S(1)} %get-tuple-element.18.refs_0_), channel_id=1, source_target_pairs={{0,13},{1,12},{4,9},{5,8},{8,5},{9,4},{12,1},{13,0},{2,15},{3,14},... | collective-permute-start | bytes 98312 | tf_op jit(solution)/shard_map/ppermute | solution.py:255
  8.1 0.2 collective-permute-start
  8.3 2.1 %queries.1.refs_4_.weights = bf16[128,4096]{1,0:T(8,128)(2,1)S(1)} custom-call(bf16[128,4096]{1,0:T(8,128)(2,1)S(1)} %get-tuple-element.14.queries, f32[64,64]{1,0:T(8,128)S(1)} %get-tuple-element.15.basis_in, f32[64,64]{1,0:T(8,128)S(1)} %get-tuple-element.16.basis_out, f32[64,64]{1,0:T(8,128)S(1)} %get-tuple-element.17.eigen), custom_call_target="tpu_custom_call" | custom-call | flops 536870912 | bytes 2097152 | tf_op jit(solution)/shard_map/queries/pallas_call | solution.py:259
  10.4 0.0 collective-permute-done.2.refs_3_
  10.4 1.3 %collective-permute-done.1.refs_2_ = bf16[64,256]{1,0:T(8,128)(2,1)S(1)} collective-permute-done((bf16[64,256]{1,0:T(8,128)(2,1)S(1)}, bf16[64,256]{1,0:T(8,128)(2,1)S(1)}, u32[]{:S(2)}, u32[]{:S(2)}) %collective-permute-start.1) | collective-permute-done | bytes 32800 | tf_op jit(solution)/shard_map/ppermute | solution.py:255
  11.7 0.2 collective-permute-done.refs_1_
  11.8 0.7 %collective-permute-start.3 = (bf16[4,64,256]{2,1,0:T(8,128)(2,1)S(1)}, bf16[4,64,256]{2,1,0:T(8,128)(2,1)S(1)}, u32[]{:S(2)}, u32[]{:S(2)}) collective-permute-start(bf16[4,64,256]{2,1,0:T(8,128)(2,1)S(1)} %pack.1.mine), channel_id=1, source_target_pairs={{0,1},{1,0},{2,3},{3,2},{4,5},{5,4},{6,7},{7,6},{8,9},{9,8},{10,11... | collective-permute-start | bytes 393224 | tf_op jit(solution)/shard_map/ppermute | solution.py:280
  12.6 1.0 %collective-permute-done.3.theirs = bf16[4,64,256]{2,1,0:T(8,128)(2,1)S(1)} collective-permute-done((bf16[4,64,256]{2,1,0:T(8,128)(2,1)S(1)}, bf16[4,64,256]{2,1,0:T(8,128)(2,1)S(1)}, u32[]{:S(2)}, u32[]{:S(2)}) %collective-permute-start.3) | collective-permute-done | bytes 131104 | tf_op jit(solution)/shard_map/ppermute | solution.py:280
  13.6 0.9 %scores.2 = (f32[2,128,128]{2,1,0:T(8,128)S(1)}, bf16[2,128,128]{2,1,0:T(8,128)(2,1)S(1)}) custom-call(bf16[128,4096]{1,0:T(8,128)(2,1)S(1)} %queries.1.refs_4_.weights, bf16[4,64,256]{2,1,0:T(8,128)(2,1)S(1)} %pack.1.mine, bf16[4,64,256]{2,1,0:T(8,128)(2,1)S(1)} %collective-permute-done.3.theirs), custom_call_target="tpu_custom_call" | custom-call | flops 536870912 | bytes 1048576 | tf_op jit(solution)/shard_map/scores/pallas_call | solution.py:285
  14.4 1.6 %collective-permute-start.5 = (bf16[2,128,128]{2,1,0:T(8,128)(2,1)S(1)}, bf16[2,128,128]{2,1,0:T(8,128)(2,1)S(1)}, u32[]{:S(2)}, u32[]{:S(2)}) collective-permute-start(bf16[2,128,128]{2,1,0:T(8,128)(2,1)S(1)} %get-tuple-element.22), channel_id=1, source_target_pairs={{0,2},{2,0},{1,3},{3,1},{4,6},{6,4},{5,7},{7,5},{8,10},{10,8},{9,1... | collective-permute-start | bytes 196616 | tf_op jit(solution)/shard_map/ppermute | solution.py:303
  16.0 0.9 %scores.3 = (f32[2,128,128]{2,1,0:T(8,128)S(1)}, bf16[2,128,128]{2,1,0:T(8,128)(2,1)S(1)}) custom-call(bf16[128,4096]{1,0:T(8,128)(2,1)S(1)} %queries.1.refs_4_.weights, bf16[4,64,256]{2,1,0:T(8,128)(2,1)S(1)} %pack.1.mine, bf16[4,64,256]{2,1,0:T(8,128)(2,1)S(1)} %collective-permute-done.3.theirs, f32[2,128,128]{2,1,0:T(8,128)S(1)} %get-tuple-element.19.refs_0_.own), custom_call_target="tpu_custom_call" | custom-call | flops 536870912 | bytes 1048576 | tf_op jit(solution)/shard_map/scores/pallas_call | solution.py:285
  16.9 0.6 %collective-permute-start.4 = (bf16[2,128,128]{2,1,0:T(8,128)(2,1)S(1)}, bf16[2,128,128]{2,1,0:T(8,128)(2,1)S(1)}, u32[]{:S(2)}, u32[]{:S(2)}) collective-permute-start(bf16[2,128,128]{2,1,0:T(8,128)(2,1)S(1)} %get-tuple-element.21), channel_id=1, source_target_pairs={{0,2},{2,0},{1,3},{3,1},{4,6},{6,4},{5,7},{7,5},{8,10},{10,8},{9,1... | collective-permute-start | bytes 196616 | tf_op jit(solution)/shard_map/ppermute | solution.py:303
  17.5 1.4 %collective-permute-done.5.refs_0_ = bf16[2,128,128]{2,1,0:T(8,128)(2,1)S(1)} collective-permute-done((bf16[2,128,128]{2,1,0:T(8,128)(2,1)S(1)}, bf16[2,128,128]{2,1,0:T(8,128)(2,1)S(1)}, u32[]{:S(2)}, u32[]{:S(2)}) %collective-permute-start.5) | collective-permute-done | bytes 65568 | tf_op jit(solution)/shard_map/ppermute | solution.py:303
  18.9 0.1 collective-permute-start.6
  19.0 3.0 %collective-permute-start.7 = (bf16[128,128]{1,0:T(8,128)(2,1)S(1)}, bf16[128,128]{1,0:T(8,128)(2,1)S(1)}, u32[]{:S(2)}, u32[]{:S(2)}) collective-permute-start(bf16[128,128]{1,0:T(8,128)(2,1)S(1)} %layers.5.refs_1_), channel_id=1, source_target_pairs={{0,8},{4,12},{8,0},{12,4},{1,9},{5,13},{9,1},{13,5},{2,10},{6,14},... | collective-permute-start | bytes 98312 | tf_op jit(solution)/shard_map/ppermute | solution.py:338
  21.9 0.0 collective-permute-done.4.refs_0_
  22.0 1.8 %collective-permute-start.8 = (bf16[128,128]{1,0:T(8,128)(2,1)S(1)}, bf16[128,128]{1,0:T(8,128)(2,1)S(1)}, u32[]{:S(2)}, u32[]{:S(2)}) collective-permute-start(bf16[128,128]{1,0:T(8,128)(2,1)S(1)} %layers.7), channel_id=1, source_target_pairs={{0,12},{4,0},{8,4},{12,8},{1,13},{5,1},{9,5},{13,9},{2,14},{6,2},{... | collective-permute-start | bytes 98312 | tf_op jit(solution)/shard_map/ppermute | solution.py:338
  23.7 0.9 %collective-permute-done.6.block = bf16[128,128]{1,0:T(8,128)(2,1)S(1)} collective-permute-done((bf16[128,128]{1,0:T(8,128)(2,1)S(1)}, bf16[128,128]{1,0:T(8,128)(2,1)S(1)}, u32[]{:S(2)}, u32[]{:S(2)}) %collective-permute-start.6) | collective-permute-done | bytes 32800 | tf_op jit(solution)/shard_map/ppermute | solution.py:338
  24.7 0.0 collective-permute-done.7.block
  24.7 1.3 %collective-permute-done.8.refs_2_ = bf16[128,128]{1,0:T(8,128)(2,1)S(1)} collective-permute-done((bf16[128,128]{1,0:T(8,128)(2,1)S(1)}, bf16[128,128]{1,0:T(8,128)(2,1)S(1)}, u32[]{:S(2)}, u32[]{:S(2)}) %collective-permute-start.8) | collective-permute-done | bytes 32800 | tf_op jit(solution)/shard_map/ppermute | solution.py:338
  25.9 0.7 %place.1 = f32[512,128]{1,0:T(8,128)} custom-call(f32[128,128]{1,0:T(8,128)S(1)} %layers.6.refs_1_.own, bf16[128,128]{1,0:T(8,128)(2,1)S(1)} %keep.2.refs_0_, bf16[128,128]{1,0:T(8,128)(2,1)S(1)} %keep.3.refs_1_, bf16[128,128]{1,0:T(8,128)(2,1)S(1)} %collective-permute-done.8.refs_2_), custom_call_target="tpu_custom_call" | custom-call | tf_op jit(solution)/shard_map/place/pallas_call | solution.py:342
  (7 shorter events, 0.1 us)
Async XLA Ops:
  2.9 7.5 %collective-permute-start.2 = (bf16[64,256]{1,0:T(8,128)(2,1)S(1)}, bf16[64,256]{1,0:T(8,128)(2,1)S(1)}, u32[]{:S(2)}, u32[]{:S(2)}) collective-permute-start(bf16[64,256]{1,0:T(8,128)(2,1)S(1)} %get-tuple-element.18.refs_0_), channel_id=1, source_target_pairs={{0,9},{1,8},{4,13},{5,12},{8,1},{9,0},{12,5},{13,4},{2,11},{3,10},... | collective-permute-start | bytes 98312 | tf_op jit(solution)/shard_map/ppermute | solution.py:255
  6.4 5.2 %collective-permute-start.1 = (bf16[64,256]{1,0:T(8,128)(2,1)S(1)}, bf16[64,256]{1,0:T(8,128)(2,1)S(1)}, u32[]{:S(2)}, u32[]{:S(2)}) collective-permute-start(bf16[64,256]{1,0:T(8,128)(2,1)S(1)} %get-tuple-element.18.refs_0_), channel_id=1, source_target_pairs={{0,13},{1,12},{4,9},{5,8},{8,5},{9,4},{12,1},{13,0},{2,15},{3,14},... | collective-permute-start | bytes 98312 | tf_op jit(solution)/shard_map/ppermute | solution.py:255
  8.1 3.8 %collective-permute-start = (bf16[64,256]{1,0:T(8,128)(2,1)S(1)}, bf16[64,256]{1,0:T(8,128)(2,1)S(1)}, u32[]{:S(2)}, u32[]{:S(2)}) collective-permute-start(bf16[64,256]{1,0:T(8,128)(2,1)S(1)} %get-tuple-element.18.refs_0_), channel_id=1, source_target_pairs={{0,5},{1,4},{4,1},{5,0},{8,13},{9,12},{12,9},{13,8},{2,7},{3,6},{6... | collective-permute-start | bytes 98312 | tf_op jit(solution)/shard_map/ppermute | solution.py:255
  11.8 1.7 %collective-permute-start.3 = (bf16[4,64,256]{2,1,0:T(8,128)(2,1)S(1)}, bf16[4,64,256]{2,1,0:T(8,128)(2,1)S(1)}, u32[]{:S(2)}, u32[]{:S(2)}) collective-permute-start(bf16[4,64,256]{2,1,0:T(8,128)(2,1)S(1)} %pack.1.mine), channel_id=1, source_target_pairs={{0,1},{1,0},{2,3},{3,2},{4,5},{5,4},{6,7},{7,6},{8,9},{9,8},{10,11... | collective-permute-start | bytes 393224 | tf_op jit(solution)/shard_map/ppermute | solution.py:280
  14.4 4.4 %collective-permute-start.5 = (bf16[2,128,128]{2,1,0:T(8,128)(2,1)S(1)}, bf16[2,128,128]{2,1,0:T(8,128)(2,1)S(1)}, u32[]{:S(2)}, u32[]{:S(2)}) collective-permute-start(bf16[2,128,128]{2,1,0:T(8,128)(2,1)S(1)} %get-tuple-element.22), channel_id=1, source_target_pairs={{0,2},{2,0},{1,3},{3,1},{4,6},{6,4},{5,7},{7,5},{8,10},{10,8},{9,1... | collective-permute-start | bytes 196616 | tf_op jit(solution)/shard_map/ppermute | solution.py:303
  16.9 5.0 %collective-permute-start.4 = (bf16[2,128,128]{2,1,0:T(8,128)(2,1)S(1)}, bf16[2,128,128]{2,1,0:T(8,128)(2,1)S(1)}, u32[]{:S(2)}, u32[]{:S(2)}) collective-permute-start(bf16[2,128,128]{2,1,0:T(8,128)(2,1)S(1)} %get-tuple-element.21), channel_id=1, source_target_pairs={{0,2},{2,0},{1,3},{3,1},{4,6},{6,4},{5,7},{7,5},{8,10},{10,8},{9,1... | collective-permute-start | bytes 196616 | tf_op jit(solution)/shard_map/ppermute | solution.py:303
  18.9 5.8 %collective-permute-start.6 = (bf16[128,128]{1,0:T(8,128)(2,1)S(1)}, bf16[128,128]{1,0:T(8,128)(2,1)S(1)}, u32[]{:S(2)}, u32[]{:S(2)}) collective-permute-start(bf16[128,128]{1,0:T(8,128)(2,1)S(1)} %layers.4.refs_1_), channel_id=1, source_target_pairs={{0,4},{4,8},{8,12},{12,0},{1,5},{5,9},{9,13},{13,1},{2,6},{6,10},{... | collective-permute-start | bytes 98312 | tf_op jit(solution)/shard_map/ppermute | solution.py:338
  19.0 5.7 %collective-permute-start.7 = (bf16[128,128]{1,0:T(8,128)(2,1)S(1)}, bf16[128,128]{1,0:T(8,128)(2,1)S(1)}, u32[]{:S(2)}, u32[]{:S(2)}) collective-permute-start(bf16[128,128]{1,0:T(8,128)(2,1)S(1)} %layers.5.refs_1_), channel_id=1, source_target_pairs={{0,8},{4,12},{8,0},{12,4},{1,9},{5,13},{9,1},{13,5},{2,10},{6,14},... | collective-permute-start | bytes 98312 | tf_op jit(solution)/shard_map/ppermute | solution.py:338
  22.0 4.0 %collective-permute-start.8 = (bf16[128,128]{1,0:T(8,128)(2,1)S(1)}, bf16[128,128]{1,0:T(8,128)(2,1)S(1)}, u32[]{:S(2)}, u32[]{:S(2)}) collective-permute-start(bf16[128,128]{1,0:T(8,128)(2,1)S(1)} %layers.7), channel_id=1, source_target_pairs={{0,12},{4,0},{8,4},{12,8},{1,13},{5,1},{9,5},{13,9},{2,14},{6,2},{... | collective-permute-start | bytes 98312 | tf_op jit(solution)/shard_map/ppermute | solution.py:338

commit v20 on v17

--- a/solution.py
+++ b/solution.py
@@ -56,44 +56,30 @@
 
 
 def features_kernel(chunks, *refs):
-    sides, (queries_hbm, eigen_hbm) = (refs[0:3], refs[3:6]), refs[6:8]
-    feats, queries, eigen, basis_in, basis_out, rows, proj, sems = refs[8:]
+    sides, (feats, rows, proj, basis, sems) = (refs[0:3], refs[3:6]), refs[6:]
     core = lax.axis_index("sub")
     step = rows.shape[0] // chunks
 
-    def copies(rows_hbm, proj_hbm):
+    def copies(rows_hbm, proj_hbm, basis_hbm):
         pieces = [pl.ds(chunk * step, step) for chunk in range(chunks)]
         pairs = [(rows_hbm.at[0, piece], rows.at[piece]) for piece in pieces]
-        pairs.append((proj_hbm.at[0], proj))
-        return [pltpu.make_async_copy(*pair, sems.at[0, i]) for i, pair in enumerate(pairs)]
-
-    for side, (rows_hbm, proj_hbm, _) in enumerate(sides):
-        @pl.when(core == side)
+        pairs += [(proj_hbm.at[0], proj), (basis_hbm.at[0], basis)]
+        return [pltpu.make_async_copy(*pair, sems.at[i]) for i, pair in enumerate(pairs)]
+
+    for number, side in enumerate(sides):
+        @pl.when(core == number)
         def _():
-            for copy in copies(rows_hbm, proj_hbm):
+            for copy in copies(*side):
                 copy.start()
 
-    others = [
-        pltpu.make_async_copy(source.at[0], target, sems.at[1, number])
-        for number, (source, target) in enumerate((
-            (sides[0][2], basis_in), (sides[1][2], basis_out), (eigen_hbm, eigen), (queries_hbm, queries)
-        ))
-    ]
-    for copy in others:
-        copy.start()
-    for copy in copies(*sides[0][:2]):
+    for copy in copies(*sides[0]):
         copy.wait()
     total = nt(proj[...], rows[...])
-    for copy in others[:2]:
-        copy.wait()
-    basis = jnp.where(core == 0, basis_in[...], basis_out[...])
     feats[...] = jnp.dot(
-        two_terms(basis.T),
+        two_terms(basis[...].T),
         jnp.concatenate([total.astype(BF16)] * 2, axis=0),
         preferred_element_type=F32,
     ).astype(BF16)
-    for copy in others[2:]:
-        copy.wait()
 
 
 def pack_kernel(rounds, *refs):
@@ -210,20 +196,17 @@
     anywhere = pl.BlockSpec(memory_space=pl.ANY)
     params = pltpu.CompilerParams(vmem_limit_bytes=32 << 20)
 
-    sources = (inputs, proj_in, basis_in, out_grads, proj_out, basis_out, queries, eigen)
-    feats, queries, eigen, basis_in, basis_out = pl.pallas_call(
+    sources = (inputs, proj_in, basis_in, out_grads, proj_out, basis_out)
+    feats = pl.pallas_call(
         functools.partial(features_kernel, chunks),
-        out_shape=[
-            jax.ShapeDtypeStruct((rank, tokens), BF16),
-            jax.ShapeDtypeStruct((count, entries), BF16),
-            *[jax.ShapeDtypeStruct((rank, rank), F32)] * 3,
-        ],
+        out_shape=jax.ShapeDtypeStruct((rank, tokens), BF16),
         in_specs=[hbm] * len(sources),
-        out_specs=[vmem] * 5,
+        out_specs=vmem,
         scratch_shapes=[
             pltpu.VMEM((tokens, width), BF16),
             pltpu.VMEM((rank, width), BF16),
-            pltpu.SemaphoreType.DMA((2, chunks + 1)),
+            pltpu.VMEM((rank, rank), F32),
+            pltpu.SemaphoreType.DMA((chunks + 2,)),
         ],
         compiler_params=params,
         cost_estimate=pl.CostEstimate(
@@ -267,16 +250,16 @@
             flops=4 * PACK * count * entries * rank, bytes_accessed=4 * count * entries, transcendentals=0
         ),
         name="queries",
-    )(queries, basis_in, basis_out, eigen)
+    )(queries[0], basis_in[0], basis_out[0], eigen[0])
 
     mine = pl.pallas_call(
-        functools.partial(pack_kernel, feature_rounds[::-1]),
+        functools.partial(pack_kernel, feature_rounds),
         out_shape=jax.ShapeDtypeStruct((train_size, rank, tokens), BF16),
         in_specs=[vmem] * (1 + len(gathered)) + [anywhere],
         out_specs=vmem,
         compiler_params=params,
         name="pack",
-    )(feats, *gathered[::-1], weights)
+    )(feats, *gathered, weights)
     theirs = lax.ppermute(mine, "sub", [(0, 1), (1, 0)])
 
     rows = tokens // layer_size

time: 26.7 us -> 26.7 us (level)
  no operation moved by 1% of the time
where the time goes in v20:
time: 26.7 us; the launch traced here: 26.5 us
  starting transfers between devices  13.1 us (49%)
  Pallas kernels  7.37 us (28%)
  waiting for transfers between devices  5.93 us (22%)
    ppermute x3, starting transfers between devices, across(): return lax.ppermute(feats, ('train', 'sub'), cores)  5.42 us
    ppermute x3, starting transfers between devices, body(): arrivals.append(lax.ppermute(block, 'train', pairs))  4.81 us
    pallas_call x1, Pallas kernels, body(): pl.pallas_call(functools.partial(features_kernel, chunks), out_shape=jax....  2.71 us
    ppermute x3, waiting for transfers between devices, body(): arrivals.append(lax.ppermute(block, 'train', pairs))  2.17 us
    ppermute x2, starting transfers between devices, scored(): lax.ppermute(block, 'layer', [(l, (l + k) % layer_size) for l in range(la...  2.16 us
    pallas_call x1, Pallas kernels, body(): pl.pallas_call(queries_kernel, out_shape=jax.ShapeDtypeStruct((count, ent...  2.12 us
    pallas_call x2, Pallas kernels, scored(): pl.pallas_call(functools.partial(scores_kernel, layer_size, targets), out...  1.75 us
    ppermute x3, waiting for transfers between devices, across(): return lax.ppermute(feats, ('train', 'sub'), cores)  1.39 us
  transfers between devices with their start and end apart: 9, of which 6 were waited for; matrix products, arithmetic and copies ran while one was open for 0% of the time, Pallas kernels for 11%

profile of v20, /device:TPU:0, one launch (start us, length us, event | category | flops | bytes accessed | tf_op | source)
XLA Modules:
  0.0 26.5 jit_solution(14716873780374564847)
XLA Ops:
  0.0 0.0 copy-start.1
  0.0 0.0 copy-start.2
  0.0 0.0 copy-start
  0.0 0.0 copy-start.3
  0.0 2.7 %features.1.refs_0_ = bf16[64,256]{1,0:T(8,128)(2,1)S(1)} custom-call(bf16[1,256,4096]{2,1,0:T(8,128)(2,1)} %refs_0_.1, bf16[1,64,4096]{2,1,0:T(8,128)(2,1)} %refs_1_.1, f32[1,64,64]{2,1,0:T(8,128)} %refs_2_.1, bf16[1,256,4096]{2,1,0:T(8,128)(2,1)} %refs_3_.1, bf16[1,64,4096]{2,1,0:T(8,128)(2,1)} %refs_4_.1, f32[1,64,64]{2,1,0:T(8,128)} %refs_5_.1), custom_call_target="tpu_custom_call" | custom-call | flops 134217728 | bytes 2621440 | tf_op jit(solution)/shard_map/features/pallas_call | solution.py:200
  2.7 3.6 %collective-permute-start = (bf16[64,256]{1,0:T(8,128)(2,1)S(1)}, bf16[64,256]{1,0:T(8,128)(2,1)S(1)}, u32[]{:S(2)}, u32[]{:S(2)}) collective-permute-start(bf16[64,256]{1,0:T(8,128)(2,1)S(1)} %features.1.refs_0_), channel_id=1, source_target_pairs={{0,9},{1,8},{4,13},{5,12},{8,1},{9,0},{12,5},{13,4},{2,11},{3,10},... | collective-permute-start | bytes 98312 | tf_op jit(solution)/shard_map/ppermute | solution.py:238
  6.3 1.6 %collective-permute-start.1 = (bf16[64,256]{1,0:T(8,128)(2,1)S(1)}, bf16[64,256]{1,0:T(8,128)(2,1)S(1)}, u32[]{:S(2)}, u32[]{:S(2)}) collective-permute-start(bf16[64,256]{1,0:T(8,128)(2,1)S(1)} %features.1.refs_0_), channel_id=1, source_target_pairs={{0,13},{1,12},{4,9},{5,8},{8,5},{9,4},{12,1},{13,0},{2,15},{3,14},... | collective-permute-start | bytes 98312 | tf_op jit(solution)/shard_map/ppermute | solution.py:238
  7.9 0.2 collective-permute-start.2
  8.1 0.0 copy-done.1
  8.1 0.0 copy-done.2
  8.2 0.0 copy-done
  8.2 0.0 copy-done.3
  8.2 2.1 %queries.1.refs_4_.weights = bf16[128,4096]{1,0:T(8,128)(2,1)S(1)} custom-call(bf16[128,4096]{1,0:T(8,128)(2,1)S(1)} %bitcast.7, f32[64,64]{1,0:T(8,128)S(1)} %bitcast.8, f32[64,64]{1,0:T(8,128)S(1)} %bitcast.9, f32[64,64]{1,0:T(8,128)S(1)} %bitcast.10), custom_call_target="tpu_custom_call" | custom-call | flops 536870912 | bytes 2097152 | tf_op jit(solution)/shard_map/queries/pallas_call | solution.py:242
  10.3 0.0 collective-permute-done.refs_1_
  10.3 1.2 %collective-permute-done.1.refs_2_ = bf16[64,256]{1,0:T(8,128)(2,1)S(1)} collective-permute-done((bf16[64,256]{1,0:T(8,128)(2,1)S(1)}, bf16[64,256]{1,0:T(8,128)(2,1)S(1)}, u32[]{:S(2)}, u32[]{:S(2)}) %collective-permute-start.1) | collective-permute-done | bytes 32800 | tf_op jit(solution)/shard_map/ppermute | solution.py:238
  11.5 0.1 collective-permute-done.2.refs_3_
  11.7 0.7 %collective-permute-start.3 = (bf16[4,64,256]{2,1,0:T(8,128)(2,1)S(1)}, bf16[4,64,256]{2,1,0:T(8,128)(2,1)S(1)}, u32[]{:S(2)}, u32[]{:S(2)}) collective-permute-start(bf16[4,64,256]{2,1,0:T(8,128)(2,1)S(1)} %pack.1.mine), channel_id=1, source_target_pairs={{0,1},{1,0},{2,3},{3,2},{4,5},{5,4},{6,7},{7,6},{8,9},{9,8},{10,11... | collective-permute-start | bytes 393224 | tf_op jit(solution)/shard_map/ppermute | solution.py:263
  12.4 1.0 %collective-permute-done.3.theirs = bf16[4,64,256]{2,1,0:T(8,128)(2,1)S(1)} collective-permute-done((bf16[4,64,256]{2,1,0:T(8,128)(2,1)S(1)}, bf16[4,64,256]{2,1,0:T(8,128)(2,1)S(1)}, u32[]{:S(2)}, u32[]{:S(2)}) %collective-permute-start.3) | collective-permute-done | bytes 131104 | tf_op jit(solution)/shard_map/ppermute | solution.py:263
  13.4 0.9 %scores.2 = (f32[2,128,128]{2,1,0:T(8,128)S(1)}, bf16[2,128,128]{2,1,0:T(8,128)(2,1)S(1)}) custom-call(bf16[128,4096]{1,0:T(8,128)(2,1)S(1)} %queries.1.refs_4_.weights, bf16[4,64,256]{2,1,0:T(8,128)(2,1)S(1)} %pack.1.mine, bf16[4,64,256]{2,1,0:T(8,128)(2,1)S(1)} %collective-permute-done.3.theirs), custom_call_target="tpu_custom_call" | custom-call | flops 536870912 | bytes 1048576 | tf_op jit(solution)/shard_map/scores/pallas_call | solution.py:268
  14.3 1.6 %collective-permute-start.5 = (bf16[2,128,128]{2,1,0:T(8,128)(2,1)S(1)}, bf16[2,128,128]{2,1,0:T(8,128)(2,1)S(1)}, u32[]{:S(2)}, u32[]{:S(2)}) collective-permute-start(bf16[2,128,128]{2,1,0:T(8,128)(2,1)S(1)} %get-tuple-element.12), channel_id=1, source_target_pairs={{0,2},{2,0},{1,3},{3,1},{4,6},{6,4},{5,7},{7,5},{8,10},{10,8},{9,1... | collective-permute-start | bytes 196616 | tf_op jit(solution)/shard_map/ppermute | solution.py:286
  15.9 0.9 %scores.3 = (f32[2,128,128]{2,1,0:T(8,128)S(1)}, bf16[2,128,128]{2,1,0:T(8,128)(2,1)S(1)}) custom-call(bf16[128,4096]{1,0:T(8,128)(2,1)S(1)} %queries.1.refs_4_.weights, bf16[4,64,256]{2,1,0:T(8,128)(2,1)S(1)} %pack.1.mine, bf16[4,64,256]{2,1,0:T(8,128)(2,1)S(1)} %collective-permute-done.3.theirs, f32[2,128,128]{2,1,0:T(8,128)S(1)} %get-tuple-element.9.refs_0_.own), custom_call_target="tpu_custom_call" | custom-call | flops 536870912 | bytes 1048576 | tf_op jit(solution)/shard_map/scores/pallas_call | solution.py:268
  16.8 0.6 %collective-permute-start.4 = (bf16[2,128,128]{2,1,0:T(8,128)(2,1)S(1)}, bf16[2,128,128]{2,1,0:T(8,128)(2,1)S(1)}, u32[]{:S(2)}, u32[]{:S(2)}) collective-permute-start(bf16[2,128,128]{2,1,0:T(8,128)(2,1)S(1)} %get-tuple-element.11), channel_id=1, source_target_pairs={{0,2},{2,0},{1,3},{3,1},{4,6},{6,4},{5,7},{7,5},{8,10},{10,8},{9,1... | collective-permute-start | bytes 196616 | tf_op jit(solution)/shard_map/ppermute | solution.py:286
  17.3 1.4 %collective-permute-done.5.refs_0_ = bf16[2,128,128]{2,1,0:T(8,128)(2,1)S(1)} collective-permute-done((bf16[2,128,128]{2,1,0:T(8,128)(2,1)S(1)}, bf16[2,128,128]{2,1,0:T(8,128)(2,1)S(1)}, u32[]{:S(2)}, u32[]{:S(2)}) %collective-permute-start.5) | collective-permute-done | bytes 65568 | tf_op jit(solution)/shard_map/ppermute | solution.py:286
  18.7 0.1 collective-permute-start.6
  18.8 3.0 %collective-permute-start.7 = (bf16[128,128]{1,0:T(8,128)(2,1)S(1)}, bf16[128,128]{1,0:T(8,128)(2,1)S(1)}, u32[]{:S(2)}, u32[]{:S(2)}) collective-permute-start(bf16[128,128]{1,0:T(8,128)(2,1)S(1)} %layers.5.refs_1_), channel_id=1, source_target_pairs={{0,8},{4,12},{8,0},{12,4},{1,9},{5,13},{9,1},{13,5},{2,10},{6,14},... | collective-permute-start | bytes 98312 | tf_op jit(solution)/shard_map/ppermute | solution.py:321
  21.8 0.0 collective-permute-done.4.refs_0_
  21.8 1.8 %collective-permute-start.8 = (bf16[128,128]{1,0:T(8,128)(2,1)S(1)}, bf16[128,128]{1,0:T(8,128)(2,1)S(1)}, u32[]{:S(2)}, u32[]{:S(2)}) collective-permute-start(bf16[128,128]{1,0:T(8,128)(2,1)S(1)} %layers.7), channel_id=1, source_target_pairs={{0,12},{4,0},{8,4},{12,8},{1,13},{5,1},{9,5},{13,9},{2,14},{6,2},{... | collective-permute-start | bytes 98312 | tf_op jit(solution)/shard_map/ppermute | solution.py:321
  23.6 0.9 %collective-permute-done.6.block = bf16[128,128]{1,0:T(8,128)(2,1)S(1)} collective-permute-done((bf16[128,128]{1,0:T(8,128)(2,1)S(1)}, bf16[128,128]{1,0:T(8,128)(2,1)S(1)}, u32[]{:S(2)}, u32[]{:S(2)}) %collective-permute-start.6) | collective-permute-done | bytes 32800 | tf_op jit(solution)/shard_map/ppermute | solution.py:321
  24.5 0.0 collective-permute-done.7.block
  24.5 1.3 %collective-permute-done.8.refs_2_ = bf16[128,128]{1,0:T(8,128)(2,1)S(1)} collective-permute-done((bf16[128,128]{1,0:T(8,128)(2,1)S(1)}, bf16[128,128]{1,0:T(8,128)(2,1)S(1)}, u32[]{:S(2)}, u32[]{:S(2)}) %collective-permute-start.8) | collective-permute-done | bytes 32800 | tf_op jit(solution)/shard_map/ppermute | solution.py:321
  25.8 0.7 %place.1 = f32[512,128]{1,0:T(8,128)} custom-call(f32[128,128]{1,0:T(8,128)S(1)} %layers.6.refs_1_.own, bf16[128,128]{1,0:T(8,128)(2,1)S(1)} %keep.2.refs_0_, bf16[128,128]{1,0:T(8,128)(2,1)S(1)} %keep.3.refs_1_, bf16[128,128]{1,0:T(8,128)(2,1)S(1)} %collective-permute-done.8.refs_2_), custom_call_target="tpu_custom_call" | custom-call | tf_op jit(solution)/shard_map/place/pallas_call | solution.py:325
  (7 shorter events, 0.1 us)
Async XLA Ops:
  0.0 8.1 %copy-start.1 = (f32[1,64,64]{2,1,0:T(8,128)S(1)}, f32[1,64,64]{2,1,0:T(8,128)}, u32[]{:S(2)}) copy-start(f32[1,64,64]{2,1,0:T(8,128)} %refs_2_.1) | copy-start | bytes 49156
  0.0 8.1 %copy-start.2 = (f32[1,64,64]{2,1,0:T(8,128)S(1)}, f32[1,64,64]{2,1,0:T(8,128)}, u32[]{:S(2)}) copy-start(f32[1,64,64]{2,1,0:T(8,128)} %refs_5_.1) | copy-start | bytes 49156
  0.0 8.1 %copy-start = (bf16[1,128,4096]{2,1,0:T(8,128)(2,1)S(1)}, bf16[1,128,4096]{2,1,0:T(8,128)(2,1)}, u32[]{:S(2)}) copy-start(bf16[1,128,4096]{2,1,0:T(8,128)(2,1)} %param.15) | copy-start | bytes 3145732
  0.0 8.1 %copy-start.3 = (f32[1,64,64]{2,1,0:T(8,128)S(1)}, f32[1,64,64]{2,1,0:T(8,128)}, u32[]{:S(2)}) copy-start(f32[1,64,64]{2,1,0:T(8,128)} %param.14) | copy-start | bytes 49156
  2.7 7.6 %collective-permute-start = (bf16[64,256]{1,0:T(8,128)(2,1)S(1)}, bf16[64,256]{1,0:T(8,128)(2,1)S(1)}, u32[]{:S(2)}, u32[]{:S(2)}) collective-permute-start(bf16[64,256]{1,0:T(8,128)(2,1)S(1)} %features.1.refs_0_), channel_id=1, source_target_pairs={{0,9},{1,8},{4,13},{5,12},{8,1},{9,0},{12,5},{13,4},{2,11},{3,10},... | collective-permute-start | bytes 98312 | tf_op jit(solution)/shard_map/ppermute | solution.py:238
  6.3 5.2 %collective-permute-start.1 = (bf16[64,256]{1,0:T(8,128)(2,1)S(1)}, bf16[64,256]{1,0:T(8,128)(2,1)S(1)}, u32[]{:S(2)}, u32[]{:S(2)}) collective-permute-start(bf16[64,256]{1,0:T(8,128)(2,1)S(1)} %features.1.refs_0_), channel_id=1, source_target_pairs={{0,13},{1,12},{4,9},{5,8},{8,5},{9,4},{12,1},{13,0},{2,15},{3,14},... | collective-permute-start | bytes 98312 | tf_op jit(solution)/shard_map/ppermute | solution.py:238
  7.9 3.8 %collective-permute-start.2 = (bf16[64,256]{1,0:T(8,128)(2,1)S(1)}, bf16[64,256]{1,0:T(8,128)(2,1)S(1)}, u32[]{:S(2)}, u32[]{:S(2)}) collective-permute-start(bf16[64,256]{1,0:T(8,128)(2,1)S(1)} %features.1.refs_0_), channel_id=1, source_target_pairs={{0,5},{1,4},{4,1},{5,0},{8,13},{9,12},{12,9},{13,8},{2,7},{3,6},{6... | collective-permute-start | bytes 98312 | tf_op jit(solution)/shard_map/ppermute | solution.py:238
  11.7 1.7 %collective-permute-start.3 = (bf16[4,64,256]{2,1,0:T(8,128)(2,1)S(1)}, bf16[4,64,256]{2,1,0:T(8,128)(2,1)S(1)}, u32[]{:S(2)}, u32[]{:S(2)}) collective-permute-start(bf16[4,64,256]{2,1,0:T(8,128)(2,1)S(1)} %pack.1.mine), channel_id=1, source_target_pairs={{0,1},{1,0},{2,3},{3,2},{4,5},{5,4},{6,7},{7,6},{8,9},{9,8},{10,11... | collective-permute-start | bytes 393224 | tf_op jit(solution)/shard_map/ppermute | solution.py:263
  14.3 4.4 %collective-permute-start.5 = (bf16[2,128,128]{2,1,0:T(8,128)(2,1)S(1)}, bf16[2,128,128]{2,1,0:T(8,128)(2,1)S(1)}, u32[]{:S(2)}, u32[]{:S(2)}) collective-permute-start(bf16[2,128,128]{2,1,0:T(8,128)(2,1)S(1)} %get-tuple-element.12), channel_id=1, source_target_pairs={{0,2},{2,0},{1,3},{3,1},{4,6},{6,4},{5,7},{7,5},{8,10},{10,8},{9,1... | collective-permute-start | bytes 196616 | tf_op jit(solution)/shard_map/ppermute | solution.py:286
  16.8 5.0 %collective-permute-start.4 = (bf16[2,128,128]{2,1,0:T(8,128)(2,1)S(1)}, bf16[2,128,128]{2,1,0:T(8,128)(2,1)S(1)}, u32[]{:S(2)}, u32[]{:S(2)}) collective-permute-start(bf16[2,128,128]{2,1,0:T(8,128)(2,1)S(1)} %get-tuple-element.11), channel_id=1, source_target_pairs={{0,2},{2,0},{1,3},{3,1},{4,6},{6,4},{5,7},{7,5},{8,10},{10,8},{9,1... | collective-permute-start | bytes 196616 | tf_op jit(solution)/shard_map/ppermute | solution.py:286
  18.7 5.8 %collective-permute-start.6 = (bf16[128,128]{1,0:T(8,128)(2,1)S(1)}, bf16[128,128]{1,0:T(8,128)(2,1)S(1)}, u32[]{:S(2)}, u32[]{:S(2)}) collective-permute-start(bf16[128,128]{1,0:T(8,128)(2,1)S(1)} %layers.4.refs_1_), channel_id=1, source_target_pairs={{0,4},{4,8},{8,12},{12,0},{1,5},{5,9},{9,13},{13,1},{2,6},{6,10},{... | collective-permute-start | bytes 98312 | tf_op jit(solution)/shard_map/ppermute | solution.py:321
  18.8 5.7 %collective-permute-start.7 = (bf16[128,128]{1,0:T(8,128)(2,1)S(1)}, bf16[128,128]{1,0:T(8,128)(2,1)S(1)}, u32[]{:S(2)}, u32[]{:S(2)}) collective-permute-start(bf16[128,128]{1,0:T(8,128)(2,1)S(1)} %layers.5.refs_1_), channel_id=1, source_target_pairs={{0,8},{4,12},{8,0},{12,4},{1,9},{5,13},{9,1},{13,5},{2,10},{6,14},... | collective-permute-start | bytes 98312 | tf_op jit(solution)/shard_map/ppermute | solution.py:321
  21.8 4.0 %collective-permute-start.8 = (bf16[128,128]{1,0:T(8,128)(2,1)S(1)}, bf16[128,128]{1,0:T(8,128)(2,1)S(1)}, u32[]{:S(2)}, u32[]{:S(2)}) collective-permute-start(bf16[128,128]{1,0:T(8,128)(2,1)S(1)} %layers.7), channel_id=1, source_target_pairs={{0,12},{4,0},{8,4},{12,8},{1,13},{5,1},{9,5},{13,9},{2,14},{6,2},{... | collective-permute-start | bytes 98312 | tf_op jit(solution)/shard_map/ppermute | solution.py:321

commit v21 on v20

--- a/solution.py
+++ b/solution.py
@@ -191,7 +191,7 @@
     tokens, width = inputs.shape[1:]
     count, entries = queries.shape[1:]
     rank = proj_in.shape[1]
-    chunks = 4
+    chunks = 2
     vmem, hbm = pl.BlockSpec(memory_space=pltpu.VMEM), pl.BlockSpec(memory_space=pltpu.HBM)
     anywhere = pl.BlockSpec(memory_space=pl.ANY)
     params = pltpu.CompilerParams(vmem_limit_bytes=32 << 20)

time: 26.7 us -> 26.6 us (level)
  no operation moved by 1% of the time
where the time goes in v21:
time: 26.6 us; the launch traced here: 26.5 us
  starting transfers between devices  13.1 us (49%)
  Pallas kernels  7.35 us (28%)
  waiting for transfers between devices  5.93 us (22%)
    ppermute x3, starting transfers between devices, across(): return lax.ppermute(feats, ('train', 'sub'), cores)  5.42 us
    ppermute x3, starting transfers between devices, body(): arrivals.append(lax.ppermute(block, 'train', pairs))  4.8 us
    pallas_call x1, Pallas kernels, body(): pl.pallas_call(functools.partial(features_kernel, chunks), out_shape=jax....  2.69 us
    ppermute x2, starting transfers between devices, scored(): lax.ppermute(block, 'layer', [(l, (l + k) % layer_size) for l in range(la...  2.18 us
    ppermute x3, waiting for transfers between devices, body(): arrivals.append(lax.ppermute(block, 'train', pairs))  2.17 us
    pallas_call x1, Pallas kernels, body(): pl.pallas_call(queries_kernel, out_shape=jax.ShapeDtypeStruct((count, ent...  2.11 us
    pallas_call x2, Pallas kernels, scored(): pl.pallas_call(functools.partial(scores_kernel, layer_size, targets), out...  1.74 us
    ppermute x3, waiting for transfers between devices, across(): return lax.ppermute(feats, ('train', 'sub'), cores)  1.4 us
  transfers between devices with their start and end apart: 9, of which 6 were waited for; matrix products, arithmetic and copies ran while one was open for 0% of the time, Pallas kernels for 11%

profile of v21, /device:TPU:0, one launch (start us, length us, event | category | flops | bytes accessed | tf_op | source)
XLA Modules:
  0.0 26.5 jit_solution(4493529810774972938)
XLA Ops:
  0.0 0.0 copy-start.1
  0.0 0.0 copy-start.2
  0.0 0.0 copy-start
  0.0 0.0 copy-start.3
  0.0 2.7 %features.1.refs_0_ = bf16[64,256]{1,0:T(8,128)(2,1)S(1)} custom-call(bf16[1,256,4096]{2,1,0:T(8,128)(2,1)} %refs_0_.1, bf16[1,64,4096]{2,1,0:T(8,128)(2,1)} %refs_1_.1, f32[1,64,64]{2,1,0:T(8,128)} %refs_2_.1, bf16[1,256,4096]{2,1,0:T(8,128)(2,1)} %refs_3_.1, bf16[1,64,4096]{2,1,0:T(8,128)(2,1)} %refs_4_.1, f32[1,64,64]{2,1,0:T(8,128)} %refs_5_.1), custom_call_target="tpu_custom_call" | custom-call | flops 134217728 | bytes 2621440 | tf_op jit(solution)/shard_map/features/pallas_call | solution.py:200
  2.7 3.6 %collective-permute-start = (bf16[64,256]{1,0:T(8,128)(2,1)S(1)}, bf16[64,256]{1,0:T(8,128)(2,1)S(1)}, u32[]{:S(2)}, u32[]{:S(2)}) collective-permute-start(bf16[64,256]{1,0:T(8,128)(2,1)S(1)} %features.1.refs_0_), channel_id=1, source_target_pairs={{0,9},{1,8},{4,13},{5,12},{8,1},{9,0},{12,5},{13,4},{2,11},{3,10},... | collective-permute-start | bytes 98312 | tf_op jit(solution)/shard_map/ppermute | solution.py:238
  6.3 1.6 %collective-permute-start.1 = (bf16[64,256]{1,0:T(8,128)(2,1)S(1)}, bf16[64,256]{1,0:T(8,128)(2,1)S(1)}, u32[]{:S(2)}, u32[]{:S(2)}) collective-permute-start(bf16[64,256]{1,0:T(8,128)(2,1)S(1)} %features.1.refs_0_), channel_id=1, source_target_pairs={{0,13},{1,12},{4,9},{5,8},{8,5},{9,4},{12,1},{13,0},{2,15},{3,14},... | collective-permute-start | bytes 98312 | tf_op jit(solution)/shard_map/ppermute | solution.py:238
  7.9 0.2 collective-permute-start.2
  8.1 0.0 copy-done.1
  8.1 0.0 copy-done.2
  8.1 0.0 copy-done
  8.1 0.0 copy-done.3
  8.1 2.1 %queries.1.refs_4_.weights = bf16[128,4096]{1,0:T(8,128)(2,1)S(1)} custom-call(bf16[128,4096]{1,0:T(8,128)(2,1)S(1)} %bitcast.7, f32[64,64]{1,0:T(8,128)S(1)} %bitcast.8, f32[64,64]{1,0:T(8,128)S(1)} %bitcast.9, f32[64,64]{1,0:T(8,128)S(1)} %bitcast.10), custom_call_target="tpu_custom_call" | custom-call | flops 536870912 | bytes 2097152 | tf_op jit(solution)/shard_map/queries/pallas_call | solution.py:242
  10.3 0.0 collective-permute-done.refs_1_
  10.3 1.2 %collective-permute-done.1.refs_2_ = bf16[64,256]{1,0:T(8,128)(2,1)S(1)} collective-permute-done((bf16[64,256]{1,0:T(8,128)(2,1)S(1)}, bf16[64,256]{1,0:T(8,128)(2,1)S(1)}, u32[]{:S(2)}, u32[]{:S(2)}) %collective-permute-start.1) | collective-permute-done | bytes 32800 | tf_op jit(solution)/shard_map/ppermute | solution.py:238
  11.5 0.2 collective-permute-done.2.refs_3_
  11.7 0.7 %collective-permute-start.3 = (bf16[4,64,256]{2,1,0:T(8,128)(2,1)S(1)}, bf16[4,64,256]{2,1,0:T(8,128)(2,1)S(1)}, u32[]{:S(2)}, u32[]{:S(2)}) collective-permute-start(bf16[4,64,256]{2,1,0:T(8,128)(2,1)S(1)} %pack.1.mine), channel_id=1, source_target_pairs={{0,1},{1,0},{2,3},{3,2},{4,5},{5,4},{6,7},{7,6},{8,9},{9,8},{10,11... | collective-permute-start | bytes 393224 | tf_op jit(solution)/shard_map/ppermute | solution.py:263
  12.4 1.0 %collective-permute-done.3.theirs = bf16[4,64,256]{2,1,0:T(8,128)(2,1)S(1)} collective-permute-done((bf16[4,64,256]{2,1,0:T(8,128)(2,1)S(1)}, bf16[4,64,256]{2,1,0:T(8,128)(2,1)S(1)}, u32[]{:S(2)}, u32[]{:S(2)}) %collective-permute-start.3) | collective-permute-done | bytes 131104 | tf_op jit(solution)/shard_map/ppermute | solution.py:263
  13.4 0.9 %scores.2 = (f32[2,128,128]{2,1,0:T(8,128)S(1)}, bf16[2,128,128]{2,1,0:T(8,128)(2,1)S(1)}) custom-call(bf16[128,4096]{1,0:T(8,128)(2,1)S(1)} %queries.1.refs_4_.weights, bf16[4,64,256]{2,1,0:T(8,128)(2,1)S(1)} %pack.1.mine, bf16[4,64,256]{2,1,0:T(8,128)(2,1)S(1)} %collective-permute-done.3.theirs), custom_call_target="tpu_custom_call" | custom-call | flops 536870912 | bytes 1048576 | tf_op jit(solution)/shard_map/scores/pallas_call | solution.py:268
  14.3 1.6 %collective-permute-start.5 = (bf16[2,128,128]{2,1,0:T(8,128)(2,1)S(1)}, bf16[2,128,128]{2,1,0:T(8,128)(2,1)S(1)}, u32[]{:S(2)}, u32[]{:S(2)}) collective-permute-start(bf16[2,128,128]{2,1,0:T(8,128)(2,1)S(1)} %get-tuple-element.12), channel_id=1, source_target_pairs={{0,2},{2,0},{1,3},{3,1},{4,6},{6,4},{5,7},{7,5},{8,10},{10,8},{9,1... | collective-permute-start | bytes 196616 | tf_op jit(solution)/shard_map/ppermute | solution.py:286
  15.9 0.9 %scores.3 = (f32[2,128,128]{2,1,0:T(8,128)S(1)}, bf16[2,128,128]{2,1,0:T(8,128)(2,1)S(1)}) custom-call(bf16[128,4096]{1,0:T(8,128)(2,1)S(1)} %queries.1.refs_4_.weights, bf16[4,64,256]{2,1,0:T(8,128)(2,1)S(1)} %pack.1.mine, bf16[4,64,256]{2,1,0:T(8,128)(2,1)S(1)} %collective-permute-done.3.theirs, f32[2,128,128]{2,1,0:T(8,128)S(1)} %get-tuple-element.9.refs_0_.own), custom_call_target="tpu_custom_call" | custom-call | flops 536870912 | bytes 1048576 | tf_op jit(solution)/shard_map/scores/pallas_call | solution.py:268
  16.7 0.6 %collective-permute-start.4 = (bf16[2,128,128]{2,1,0:T(8,128)(2,1)S(1)}, bf16[2,128,128]{2,1,0:T(8,128)(2,1)S(1)}, u32[]{:S(2)}, u32[]{:S(2)}) collective-permute-start(bf16[2,128,128]{2,1,0:T(8,128)(2,1)S(1)} %get-tuple-element.11), channel_id=1, source_target_pairs={{0,2},{2,0},{1,3},{3,1},{4,6},{6,4},{5,7},{7,5},{8,10},{10,8},{9,1... | collective-permute-start | bytes 196616 | tf_op jit(solution)/shard_map/ppermute | solution.py:286
  17.3 1.4 %collective-permute-done.5.refs_0_ = bf16[2,128,128]{2,1,0:T(8,128)(2,1)S(1)} collective-permute-done((bf16[2,128,128]{2,1,0:T(8,128)(2,1)S(1)}, bf16[2,128,128]{2,1,0:T(8,128)(2,1)S(1)}, u32[]{:S(2)}, u32[]{:S(2)}) %collective-permute-start.5) | collective-permute-done | bytes 65568 | tf_op jit(solution)/shard_map/ppermute | solution.py:286
  18.7 0.1 collective-permute-start.6
  18.8 3.0 %collective-permute-start.7 = (bf16[128,128]{1,0:T(8,128)(2,1)S(1)}, bf16[128,128]{1,0:T(8,128)(2,1)S(1)}, u32[]{:S(2)}, u32[]{:S(2)}) collective-permute-start(bf16[128,128]{1,0:T(8,128)(2,1)S(1)} %layers.5.refs_1_), channel_id=1, source_target_pairs={{0,8},{4,12},{8,0},{12,4},{1,9},{5,13},{9,1},{13,5},{2,10},{6,14},... | collective-permute-start | bytes 98312 | tf_op jit(solution)/shard_map/ppermute | solution.py:321
  21.8 0.0 collective-permute-done.4.refs_0_
  21.8 1.8 %collective-permute-start.8 = (bf16[128,128]{1,0:T(8,128)(2,1)S(1)}, bf16[128,128]{1,0:T(8,128)(2,1)S(1)}, u32[]{:S(2)}, u32[]{:S(2)}) collective-permute-start(bf16[128,128]{1,0:T(8,128)(2,1)S(1)} %layers.7), channel_id=1, source_target_pairs={{0,12},{4,0},{8,4},{12,8},{1,13},{5,1},{9,5},{13,9},{2,14},{6,2},{... | collective-permute-start | bytes 98312 | tf_op jit(solution)/shard_map/ppermute | solution.py:321
  23.6 0.9 %collective-permute-done.6.block = bf16[128,128]{1,0:T(8,128)(2,1)S(1)} collective-permute-done((bf16[128,128]{1,0:T(8,128)(2,1)S(1)}, bf16[128,128]{1,0:T(8,128)(2,1)S(1)}, u32[]{:S(2)}, u32[]{:S(2)}) %collective-permute-start.6) | collective-permute-done | bytes 32800 | tf_op jit(solution)/shard_map/ppermute | solution.py:321
  24.5 0.0 collective-permute-done.7.block
  24.5 1.3 %collective-permute-done.8.refs_2_ = bf16[128,128]{1,0:T(8,128)(2,1)S(1)} collective-permute-done((bf16[128,128]{1,0:T(8,128)(2,1)S(1)}, bf16[128,128]{1,0:T(8,128)(2,1)S(1)}, u32[]{:S(2)}, u32[]{:S(2)}) %collective-permute-start.8) | collective-permute-done | bytes 32800 | tf_op jit(solution)/shard_map/ppermute | solution.py:321
  25.8 0.7 %place.1 = f32[512,128]{1,0:T(8,128)} custom-call(f32[128,128]{1,0:T(8,128)S(1)} %layers.6.refs_1_.own, bf16[128,128]{1,0:T(8,128)(2,1)S(1)} %keep.2.refs_0_, bf16[128,128]{1,0:T(8,128)(2,1)S(1)} %keep.3.refs_1_, bf16[128,128]{1,0:T(8,128)(2,1)S(1)} %collective-permute-done.8.refs_2_), custom_call_target="tpu_custom_call" | custom-call | tf_op jit(solution)/shard_map/place/pallas_call | solution.py:325
  (7 shorter events, 0.1 us)
Async XLA Ops:
  0.0 8.1 %copy-start.1 = (f32[1,64,64]{2,1,0:T(8,128)S(1)}, f32[1,64,64]{2,1,0:T(8,128)}, u32[]{:S(2)}) copy-start(f32[1,64,64]{2,1,0:T(8,128)} %refs_2_.1) | copy-start | bytes 49156
  0.0 8.1 %copy-start.2 = (f32[1,64,64]{2,1,0:T(8,128)S(1)}, f32[1,64,64]{2,1,0:T(8,128)}, u32[]{:S(2)}) copy-start(f32[1,64,64]{2,1,0:T(8,128)} %refs_5_.1) | copy-start | bytes 49156
  0.0 8.1 %copy-start = (bf16[1,128,4096]{2,1,0:T(8,128)(2,1)S(1)}, bf16[1,128,4096]{2,1,0:T(8,128)(2,1)}, u32[]{:S(2)}) copy-start(bf16[1,128,4096]{2,1,0:T(8,128)(2,1)} %param.15) | copy-start | bytes 3145732
  0.0 8.1 %copy-start.3 = (f32[1,64,64]{2,1,0:T(8,128)S(1)}, f32[1,64,64]{2,1,0:T(8,128)}, u32[]{:S(2)}) copy-start(f32[1,64,64]{2,1,0:T(8,128)} %param.14) | copy-start | bytes 49156
  2.7 7.6 %collective-permute-start = (bf16[64,256]{1,0:T(8,128)(2,1)S(1)}, bf16[64,256]{1,0:T(8,128)(2,1)S(1)}, u32[]{:S(2)}, u32[]{:S(2)}) collective-permute-start(bf16[64,256]{1,0:T(8,128)(2,1)S(1)} %features.1.refs_0_), channel_id=1, source_target_pairs={{0,9},{1,8},{4,13},{5,12},{8,1},{9,0},{12,5},{13,4},{2,11},{3,10},... | collective-permute-start | bytes 98312 | tf_op jit(solution)/shard_map/ppermute | solution.py:238
  6.3 5.2 %collective-permute-start.1 = (bf16[64,256]{1,0:T(8,128)(2,1)S(1)}, bf16[64,256]{1,0:T(8,128)(2,1)S(1)}, u32[]{:S(2)}, u32[]{:S(2)}) collective-permute-start(bf16[64,256]{1,0:T(8,128)(2,1)S(1)} %features.1.refs_0_), channel_id=1, source_target_pairs={{0,13},{1,12},{4,9},{5,8},{8,5},{9,4},{12,1},{13,0},{2,15},{3,14},... | collective-permute-start | bytes 98312 | tf_op jit(solution)/shard_map/ppermute | solution.py:238
  7.9 3.8 %collective-permute-start.2 = (bf16[64,256]{1,0:T(8,128)(2,1)S(1)}, bf16[64,256]{1,0:T(8,128)(2,1)S(1)}, u32[]{:S(2)}, u32[]{:S(2)}) collective-permute-start(bf16[64,256]{1,0:T(8,128)(2,1)S(1)} %features.1.refs_0_), channel_id=1, source_target_pairs={{0,5},{1,4},{4,1},{5,0},{8,13},{9,12},{12,9},{13,8},{2,7},{3,6},{6... | collective-permute-start | bytes 98312 | tf_op jit(solution)/shard_map/ppermute | solution.py:238
  11.7 1.7 %collective-permute-start.3 = (bf16[4,64,256]{2,1,0:T(8,128)(2,1)S(1)}, bf16[4,64,256]{2,1,0:T(8,128)(2,1)S(1)}, u32[]{:S(2)}, u32[]{:S(2)}) collective-permute-start(bf16[4,64,256]{2,1,0:T(8,128)(2,1)S(1)} %pack.1.mine), channel_id=1, source_target_pairs={{0,1},{1,0},{2,3},{3,2},{4,5},{5,4},{6,7},{7,6},{8,9},{9,8},{10,11... | collective-permute-start | bytes 393224 | tf_op jit(solution)/shard_map/ppermute | solution.py:263
  14.3 4.4 %collective-permute-start.5 = (bf16[2,128,128]{2,1,0:T(8,128)(2,1)S(1)}, bf16[2,128,128]{2,1,0:T(8,128)(2,1)S(1)}, u32[]{:S(2)}, u32[]{:S(2)}) collective-permute-start(bf16[2,128,128]{2,1,0:T(8,128)(2,1)S(1)} %get-tuple-element.12), channel_id=1, source_target_pairs={{0,2},{2,0},{1,3},{3,1},{4,6},{6,4},{5,7},{7,5},{8,10},{10,8},{9,1... | collective-permute-start | bytes 196616 | tf_op jit(solution)/shard_map/ppermute | solution.py:286
  16.7 5.0 %collective-permute-start.4 = (bf16[2,128,128]{2,1,0:T(8,128)(2,1)S(1)}, bf16[2,128,128]{2,1,0:T(8,128)(2,1)S(1)}, u32[]{:S(2)}, u32[]{:S(2)}) collective-permute-start(bf16[2,128,128]{2,1,0:T(8,128)(2,1)S(1)} %get-tuple-element.11), channel_id=1, source_target_pairs={{0,2},{2,0},{1,3},{3,1},{4,6},{6,4},{5,7},{7,5},{8,10},{10,8},{9,1... | collective-permute-start | bytes 196616 | tf_op jit(solution)/shard_map/ppermute | solution.py:286
  18.7 5.8 %collective-permute-start.6 = (bf16[128,128]{1,0:T(8,128)(2,1)S(1)}, bf16[128,128]{1,0:T(8,128)(2,1)S(1)}, u32[]{:S(2)}, u32[]{:S(2)}) collective-permute-start(bf16[128,128]{1,0:T(8,128)(2,1)S(1)} %layers.4.refs_1_), channel_id=1, source_target_pairs={{0,4},{4,8},{8,12},{12,0},{1,5},{5,9},{9,13},{13,1},{2,6},{6,10},{... | collective-permute-start | bytes 98312 | tf_op jit(solution)/shard_map/ppermute | solution.py:321
  18.8 5.7 %collective-permute-start.7 = (bf16[128,128]{1,0:T(8,128)(2,1)S(1)}, bf16[128,128]{1,0:T(8,128)(2,1)S(1)}, u32[]{:S(2)}, u32[]{:S(2)}) collective-permute-start(bf16[128,128]{1,0:T(8,128)(2,1)S(1)} %layers.5.refs_1_), channel_id=1, source_target_pairs={{0,8},{4,12},{8,0},{12,4},{1,9},{5,13},{9,1},{13,5},{2,10},{6,14},... | collective-permute-start | bytes 98312 | tf_op jit(solution)/shard_map/ppermute | solution.py:321
  21.8 4.0 %collective-permute-start.8 = (bf16[128,128]{1,0:T(8,128)(2,1)S(1)}, bf16[128,128]{1,0:T(8,128)(2,1)S(1)}, u32[]{:S(2)}, u32[]{:S(2)}) collective-permute-start(bf16[128,128]{1,0:T(8,128)(2,1)S(1)} %layers.7), channel_id=1, source_target_pairs={{0,12},{4,0},{8,4},{12,8},{1,13},{5,1},{9,5},{13,9},{2,14},{6,2},{... | collective-permute-start | bytes 98312 | tf_op jit(solution)/shard_map/ppermute | solution.py:321
